TPU v7x, 32 devices: a whole 2x2x4 slice. The times are simulated.
32 devices in a mesh: pole: 2 (over x), row: 8 (over z, y), col: 2 (over core).
Axes of the slice: x: 2, y: 2, z: 4, core: 2. Of those that a mesh axis runs over, the one named last changes fastest.
Arguments:
- panel: bfloat16 [4, 8, 2, 512, 128], P(('pole', 'col'), None, None, 'row'), parts along dimension 0, may hold values from -6 to 6
- tiles: bfloat16 [352, 2, 512, 512], P(('pole', 'row', 'col')), parts along dimension 0, may hold values from -0.078125 to 0.078125
- tile_slot: int32 [352], P(('pole', 'row', 'col')), parts along dimension 0, may hold values from 0 to 1
- tile_col: int32 [352], P(('pole', 'row', 'col')), parts along dimension 0, may hold values from 0 to 7
- pole_weight: float32 [4], P('pole'), parts along dimension 0, may hold values from -4 to 4
- box_orbitals: int32 [64, 256], P(('pole', 'row', 'col')), parts along dimension 0, may hold values from 0 to 8191, as said below
- box_basis: bfloat16 [64, 256, 512], P(('pole', 'row', 'col')), parts along dimension 0, may hold values from -0.375 to 0.375
- supernode_basis: bfloat16 [64, 128, 512], P(('pole', 'row', 'col')), parts along dimension 0, may hold values from -0.5 to 0.5
Outputs:
- inverse_column: float32 [32, 2, 512, 128], P(('pole', 'row'), None, 'col'), parts along dimension 0
- density: float32 [64, 512], P(('pole', 'row', 'col')), parts along dimension 0
There are 2 independent parts, one for each index of `pole`. A program takes and returns all parts, laid end to end along the dimension named above; each array names one. Nothing has to cross between parts.
Inputs may be any that keep to these rules, and one draw needn't show every extreme that they name: `box_orbitals`: let a row g be held by device r * 2 + c where r = (g // 512) // 2 and c = (g % 512) // (512 // 2). The 2 boxes of one device take at most 64 rows (counted with repeats) held by any one device, and exactly 64 from some device.
All inputs are finite; a program needn't handle non-finite values.
Results may differ from a plain program's by a relative error of at most 0.0029.
Values may be sent and summed in bfloat16 or wider, within the bound.
No kernel may reach another device: no remote copies, remote signals or barrier semaphores. Data moves between devices by JAX's collectives and lax.ppermute only.
A program may use at most 64 MiB of HBM per device.

v0:
```python
import jax
import jax.numpy as jnp
from jax import lax
from jax.sharding import PartitionSpec as P

BR_DEV = 2


def local(panel, tiles, tile_slot, tile_col, pole_weight, box_orbitals, box_basis, supernode_basis):
    gathered = lax.all_gather(panel, "row", axis=3, tiled=True)
    blocks = gathered[0]
    selector = (tile_col[:, None] == jnp.arange(blocks.shape[0], dtype=jnp.int32)[None, :]).astype(
        jnp.bfloat16
    )
    chosen = jnp.einsum(
        "tj,jcbs->tcbs", selector, blocks, preferred_element_type=jnp.float32
    ).astype(jnp.bfloat16)
    real_part = jnp.einsum(
        "tab,tbs->tas", tiles[:, 0], chosen[:, 0], preferred_element_type=jnp.float32
    )
    real_part = real_part - jnp.einsum(
        "tab,tbs->tas", tiles[:, 1], chosen[:, 1], preferred_element_type=jnp.float32
    )
    imag_part = jnp.einsum(
        "tab,tbs->tas", tiles[:, 0], chosen[:, 1], preferred_element_type=jnp.float32
    )
    imag_part = imag_part + jnp.einsum(
        "tab,tbs->tas", tiles[:, 1], chosen[:, 0], preferred_element_type=jnp.float32
    )
    products = jnp.stack([real_part, imag_part], axis=1)
    partial_value = jnp.stack(
        [
            jnp.sum(jnp.where((tile_slot == slot_row)[:, None, None, None], products, 0.0), axis=0)
            for slot_row in range(BR_DEV)
        ]
    )
    summed = lax.psum_scatter(partial_value, "col", scatter_dimension=2, tiled=True)
    inverse_column = -summed
    density_local = (
        pole_weight[0] * inverse_column[:, 1] + pole_weight[1] * inverse_column[:, 0]
    ).astype(jnp.bfloat16)
    columns = density_local.shape[2]
    density_local = density_local.reshape(-1, columns)
    block_width = tiles.shape[2]
    col_count = lax.axis_size("col")
    half_rows = block_width // col_count
    wanted = box_orbitals.reshape(-1)
    wanted_total = wanted.shape[0]
    block_index = wanted // block_width
    within = wanted % block_width
    source = block_index // BR_DEV * col_count + within // half_rows
    local_row = block_index % BR_DEV * half_rows + within % half_rows
    start_rows = jnp.zeros((wanted_total, columns), jnp.bfloat16)
    shards = lax.all_gather(density_local[None], ("row", "col"), axis=0, tiled=True)
    count = shards.shape[0]
    inside = (source >= 0) & (source < count)
    clipped = jnp.clip(source, 0, count - 1)
    fetched = shards[clipped, local_row]
    picked = jnp.where(inside[:, None], fetched, start_rows)
    picked = picked.reshape(box_basis.shape[0], box_basis.shape[1], columns)
    projected = jnp.einsum("nas,nap->nsp", picked, box_basis, preferred_element_type=jnp.float32)
    density = jnp.sum(supernode_basis.astype(jnp.float32) * projected, axis=1)
    return (inverse_column, density)


def solution(mesh):
    return jax.shard_map(
        local,
        mesh=mesh,
        in_specs=(
            P(("pole", "col"), None, None, "row", None),
            P(("pole", "row", "col"), None, None, None),
            P(("pole", "row", "col")),
            P(("pole", "row", "col")),
            P("pole"),
            P(("pole", "row", "col"), None),
            P(("pole", "row", "col"), None, None),
            P(("pole", "row", "col"), None, None),
        ),
        out_specs=(P(("pole", "row"), None, "col", None), P(("pole", "row", "col"), None)),
        check_vma=False,
    )
```

profile of v0, /device:TPU:0, one launch (start us, length us, event | category | flops | bytes accessed | tf_op | source)
XLA Modules:
  0.0 160.3 jit_solution(1189421149225466076)
XLA Ops:
  7.2 0.0 copy-start
  7.2 0.0 all-gather.3.cloned.1.call-start
  7.2 1.9 %copy.27 = bf16[1,8,2,64,128]{4,1,3,2,0:T(8,128)(2,1)} copy(bf16[1,8,2,64,128]{4,3,2,1,0:T(8,128)(2,1)} %param.8) | data formatting | bytes 524288 | tf_op args[0]
  9.1 0.0 all-gather.3.cloned.1.call-update
  9.1 0.0 reduce-scatter.2.cloned.1.call-start
  9.2 0.7 broadcast_compare_fusion
  9.8 52.9 %all-gather.3.cloned.1.call-done = bf16[1,8,2,512,128]{4,1,3,2,0:T(8,128)(2,1)} async-done(((bf16[1,8,2,64,128]{4,1,3,2,0:T(8,128)(2,1)}), bf16[1,8,2,512,128]{4,1,3,2,0:T(8,128)(2,1)}) %all-gather.3.cloned.1.call-update) | async-done | bytes 2097168 | tf_op jit(solution)/shard_map/all_gather | solution.py:10
  62.8 2.9 %convolution_convert_fusion = bf16[11,2,512,128]{3,0,2,1:T(8,128)(2,1)S(1)} fusion(bf16[1,8,2,512,128]{4,1,3,2,0:T(8,128)(2,1)} %all-gather.3.cloned.1.call-done, s32[11]{0:T(128)} %param.11), kind=kOutput, calls=%fused_computation.18 | convolution fusion | flops 24510552 | bytes 4980780 | tf_op jit(solution)/shard_map/tj,jcbs->tcbs/dot_general | solution.py:15
  65.7 2.7 %slice_bitcast_fusion = (bf16[11,512,128]{2,0,1:T(8,128)(2,1)}, bf16[11,512,128]{2,0,1:T(8,128)(2,1)}) fusion(bf16[11,2,512,128]{3,0,2,1:T(8,128)(2,1)S(1)} %convolution_convert_fusion), kind=kLoop, calls=%fused_computation.19 | loop fusion | bytes 5767168 | tf_op jit(solution)/shard_map/squeeze | solution.py:22
  68.4 3.2 %copy.31 = bf16[11,512,128]{1,2,0:T(8,128)(2,1)S(1)} copy(bf16[11,512,128]{2,0,1:T(8,128)(2,1)} %get-tuple-element.8) | data formatting | bytes 2883584 | tf_op jit(solution)/shard_map/squeeze | solution.py:22
  71.6 3.2 %copy.29 = bf16[11,512,128]{1,2,0:T(8,128)(2,1)S(1)} copy(bf16[11,512,128]{2,0,1:T(8,128)(2,1)} %get-tuple-element.9) | data formatting | bytes 2883584 | tf_op jit(solution)/shard_map/squeeze | solution.py:19
  74.8 4.6 %fusion.2 = f32[11,128,512]{2,1,0:T(8,128)S(1)} fusion(bf16[11,512,128]{1,2,0:T(8,128)(2,1)S(1)} %copy.31, bf16[11,2,512,512]{3,2,1,0:T(8,128)(2,1)} %param.9), kind=kOutput, calls=%fused_computation.4 | convolution fusion | flops 738197504 | bytes 10092544 | tf_op jit(solution)/shard_map/tab,tbs->tas/dot_general | solution.py:21
  79.5 0.0 slice-start
  79.5 0.0 slice-start.1
  79.5 4.8 %fusion = f32[11,128,512]{2,1,0:T(8,128)S(1)} fusion(bf16[11,512,128]{1,2,0:T(8,128)(2,1)S(1)} %copy.29, bf16[11,2,512,512]{3,2,1,0:T(8,128)(2,1)} %param.9), kind=kOutput, calls=%fused_computation.2 | convolution fusion | flops 738197504 | bytes 10092544 | tf_op jit(solution)/shard_map/tab,tbs->tas/dot_general | solution.py:27
  84.3 0.0 slice-start.2
  84.3 4.8 %subtract_bitcast_fusion = f32[11,1,512,128]{2,3,0,1:T(8,128)S(1)} fusion(f32[11,128,512]{2,1,0:T(8,128)S(1)} %fusion.2, bf16[11,512,128]{1,2,0:T(8,128)(2,1)S(1)} %copy.29, bf16[11,2,512,512]{3,2,1,0:T(8,128)(2,1)} %param.9), kind=kOutput, calls=%fused_computation.17 | convolution fusion | flops 738918400 | bytes 12976128 | tf_op jit(solution)/shard_map/tab,tbs->tas/dot_general | solution.py:18
  89.1 0.0 slice-done
  89.1 0.0 slice-done.1
  89.1 0.0 slice-done.2
  89.1 2.0 %add_bitcast_fusion = f32[11,1,512,128]{2,3,0,1:T(8,128)S(1)} fusion(f32[11,128,512]{2,1,0:T(8,128)S(1)} %fusion, bf16[11,512,128]{1,2,0:T(8,128)(2,1)S(1)} %copy.31, bf16[11,2,512,512]{3,2,1,0:T(8,128)(2,1)S(1)} %bitcast.55), kind=kOutput, calls=%fused_computation.16 | convolution fusion | flops 738918400 | bytes 12976128 | tf_op jit(solution)/shard_map/tab,tbs->tas/dot_general | solution.py:24
  91.1 1.0 select_reduce_fusion.1
  92.2 0.0 copy-start.2
  92.2 0.0 copy-start.1
  92.2 1.0 pad_maximum_fusion.1
  93.2 0.0 copy-start.3
  93.2 0.0 reduce-scatter.2.cloned.1.call-update
  93.3 0.0 all-gather.5.cloned.1.call-start
  93.3 0.0 copy-done.2
  93.3 0.6 fusion.34
  93.9 6.6 %reduce-scatter.2.cloned.1.call-done = f32[2,2,256,128]{2,3,1,0:T(8,128)} async-done(((f32[2,2,512,128]{2,3,1,0:T(8,128)}), f32[2,2,256,128]{2,3,1,0:T(8,128)}) %reduce-scatter.2.cloned.1.call-update) | async-done | bytes 524304 | tf_op jit(solution)/shard_map/reduce_scatter | solution.py:37
  100.5 1.1 neg.3
  101.6 1.3 fusion.19
  102.9 0.8 copy.34
  103.7 0.0 all-gather.5.cloned.1.call-update
  103.7 0.0 copy-done.1
  103.7 0.1 fusion.29
  103.8 1.0 copy.36
  104.8 41.6 %all-gather.5.cloned.1.call-done = bf16[16,512,128]{2,1,0:T(8,128)(2,1)} async-done(((bf16[1,512,128]{2,1,0:T(8,128)(2,1)}), bf16[16,512,128]{2,1,0:T(8,128)(2,1)}) %all-gather.5.cloned.1.call-update) | async-done | bytes 2097168 | tf_op jit(solution)/shard_map/all_gather | solution.py:54
  146.4 6.4 %gather_fusion = bf16[512,128]{1,0:T(8,128)(2,1)S(1)} fusion(bf16[16,512,128]{2,1,0:T(8,128)(2,1)} %all-gather.5.cloned.1.call-done, s32[512]{0:T(512)S(1)} %bitcast.56), kind=kCustom, calls=%fused_computation | custom fusion | bytes 266240 | tf_op jit(solution)/shard_map/gather | solution.py:58
  152.8 0.1 copy.35
  152.9 0.0 copy-done
  152.9 0.0 copy-done.3
  153.0 0.8 fusion.17
  (3 shorter events, 0.0 us)
Async XLA Ops:
  7.2 145.8 %copy-start = (bf16[2,256,512]{2,1,0:T(8,128)(2,1)S(1)}, bf16[2,256,512]{2,1,0:T(8,128)(2,1)}, u32[]{:S(2)}) copy-start(bf16[2,256,512]{2,1,0:T(8,128)(2,1)} %param.14) | copy-start | bytes 1572868
  7.2 55.6 %all-gather.3.cloned.1.call-start = ((), (), s32[]{:S(2)}) async-start(), calls=%async_computation.1 | async-start | bytes 2359296 | tf_op jit(solution)/shard_map/all_gather | solution.py:10
  9.1 91.3 %reduce-scatter.2.cloned.1.call-start = ((), (), s32[]{:S(2)}) async-start(), calls=%async_computation.2 | async-start | bytes 1572864 | tf_op jit(solution)/shard_map/reduce_scatter | solution.py:37
  79.5 9.6 %slice-start = ((s8[11534336]{0:T(1024)(128)(4,1)}), s8[4194304]{0:T(1024)(128)(4,1)S(1)}, s32[]{:S(2)}) async-start(s8[11534336]{0:T(1024)(128)(4,1)} %bitcast.54), calls=%async_computation.4 | async-start | bytes 8388608
  79.5 9.6 %slice-start.1 = ((s8[11534336]{0:T(1024)(128)(4,1)}), s8[4194304]{0:T(1024)(128)(4,1)S(1)}, s32[]{:S(2)}) async-start(s8[11534336]{0:T(1024)(128)(4,1)} %bitcast.54), calls=%async_computation.5 | async-start | bytes 8388608
  84.3 4.9 %slice-start.2 = ((s8[11534336]{0:T(1024)(128)(4,1)}), s8[3145728]{0:T(1024)(128)(4,1)S(1)}, s32[]{:S(2)}) async-start(s8[11534336]{0:T(1024)(128)(4,1)} %bitcast.54), calls=%async_computation.6 | async-start | bytes 6291456
  92.2 1.1 copy-start.2
  92.2 11.5 %copy-start.1 = (s32[2,256]{1,0:T(2,128)S(1)}, s32[2,256]{1,0:T(2,128)}, u32[]{:S(2)}) copy-start(s32[2,256]{1,0:T(2,128)} %param.13) | copy-start | bytes 6148
  93.2 59.7 %copy-start.3 = (bf16[2,128,512]{2,1,0:T(8,128)(2,1)S(1)}, bf16[2,128,512]{2,1,0:T(8,128)(2,1)}, u32[]{:S(2)}) copy-start(bf16[2,128,512]{2,1,0:T(8,128)(2,1)} %param.15) | copy-start | bytes 786436
  93.3 53.1 %all-gather.5.cloned.1.call-start = ((), (), s32[]{:S(2)}) async-start(), calls=%async_computation.3 | async-start | bytes 2228224 | tf_op jit(solution)/shard_map/all_gather | solution.py:54
Sparse Core Ops, SparseCore 0:
  10.8 51.9 all-gather.2
  93.4 7.0 reduce-scatter.1
  103.8 42.5 all-gather.4
where the time goes:
time: 161 us; the launch traced here: 160 us
  waiting for transfers between devices  101 us (63%)
  local copies, waits for them, and re-layouts  20 us (12%)
  matrix products  19.9 us (12%)
  between operations  14 us (9%)
  other arithmetic  5.24 us (3%)
    all_gather x1, waiting for transfers between devices, local(): gathered = lax.all_gather(panel, 'row', axis=3, tiled=True)  52.9 us
    all_gather x1, waiting for transfers between devices, local(): lax.all_gather(density_local[None], ('row', 'col'), axis=0, tiled=True)  41.6 us
    reduce_scatter x1, waiting for transfers between devices, local(): lax.psum_scatter(partial_value, 'col', scatter_dimension=2, tiled=True)  6.56 us
    gather x2, local copies, waits for them, and re-layouts, local(): fetched = shards[clipped, local_row]  6.55 us
    squeeze x2, local copies, waits for them, and re-layouts, local(): chosen[:, 1]  5.91 us
    dot_general x1, matrix products, local(): jnp.einsum('tab,tbs->tas', tiles[:, 0], chosen[:, 0], preferred_element_t...  4.82 us
    dot_general x1, matrix products, local(): jnp.einsum('tab,tbs->tas', tiles[:, 1], chosen[:, 0], preferred_element_t...  4.77 us
    dot_general x1, matrix products, local(): jnp.einsum('tab,tbs->tas', tiles[:, 1], chosen[:, 1], preferred_element_t...  4.61 us
  transfers between devices with their start and end apart: 3, of which 3 were waited for; matrix products, arithmetic and copies ran while one was open for 1% of the time, Pallas kernels for 0%

commit v1 on v0

v1 whole, which is shorter than its diff:
```python
import functools

import jax
import jax.numpy as jnp
from jax import lax
from jax.experimental import pallas as pl
from jax.experimental.pallas import tpu as pltpu
from jax.sharding import PartitionSpec as P

BR_DEV = 2
LANES = 128
F32 = jnp.float32
BF16 = jnp.bfloat16
VMEM_LIMIT = 48 * 1024 * 1024


def ring_order(n):
    if n <= 8 and n % 2 == 0:
        return list(range(0, n, 2)) + list(range(n - 1, 0, -2))
    return list(range(n))


def full_spec(shape):
    zeros = (0,) * len(shape)
    return pl.BlockSpec(shape, lambda *_: zeros)


def place(factor, first, count):
    depth = factor.shape[1]
    reps = LANES // depth
    row = lax.broadcasted_iota(jnp.int32, (LANES, factor.shape[2]), 0)
    inside = (row // depth) == first
    spread = [
        jnp.where(inside, jnp.concatenate([factor[p].astype(F32)] * reps, axis=0), 0.0)
        for p in range(2)
    ]
    upper = jnp.concatenate([spread[0], spread[1]], axis=1)
    lower = jnp.concatenate([-spread[1], spread[0]], axis=1)
    return jnp.concatenate([upper, lower], axis=0).astype(BF16)


def accumulate(meta, where, factors, blocks, acc, weights, tile_count, reps):
    step = pl.program_id(0)
    for s, parts in enumerate(factors):
        done = 0
        for part in parts:
            for j in range(part.shape[0]):
                @pl.when(step == 0)
                def _(part=part, j=j, s=s, at=done + j):
                    weights[at, s * 2 * LANES:(s + 1) * 2 * LANES, :] = place(
                        part[j], meta[where[s]] % reps, reps
                    )
            done += part.shape[0]
    slot = meta[step]
    block = meta[tile_count + step]
    left = jnp.concatenate([b[0, p] for b in blocks for p in range(2)], axis=1)
    acc[slot] += jnp.dot(left, weights[block], preferred_element_type=F32)


def hop_first(meta, own, tile, out, weights, *, tile_count, where, reps):
    @pl.when(pl.program_id(0) == 0)
    def _():
        out[...] = jnp.zeros_like(out)
    accumulate(meta, where, [[own]], [tile], out, weights, tile_count, reps)


def hop_middle(meta, from_left, from_right, tile_a, tile_b, start, out, weights, *, tile_count, where, reps):
    @pl.when(pl.program_id(0) == 0)
    def _():
        out[...] = start[...]
    accumulate(meta, where, [[from_left], [from_right]], [tile_a, tile_b], out, weights, tile_count, reps)


def hop_last(meta, pole_weight, low, high, tile, start, dens, mine, other, acc, weights, *, tile_count, where, reps, col_at):
    step = pl.program_id(0)

    @pl.when(step == 0)
    def _():
        acc[...] = start[...]
    accumulate(meta, where, [[low, high]], [tile], acc, weights, tile_count, reps)

    @pl.when(step == tile_count - 1)
    def _():
        col = meta[col_at]
        half = mine.shape[2]
        width = mine.shape[3]
        for slot in range(acc.shape[0]):
            real = -acc[slot, :, :width]
            imag = -acc[slot, :, width:]
            dens[slot] = pole_weight[0] * imag + pole_weight[1] * real
            for p in range(2):
                cols = slice(p * width, (p + 1) * width)
                mine[slot, p] = -acc[slot, pl.ds(pl.multiple_of(col * half, half), half), cols]
                other[slot, p] = -acc[slot, pl.ds(pl.multiple_of((1 - col) * half, half), half), cols]


def basis_kernel(wanted_row, wanted_col, basis, out, *, rows_chip, slots):
    total = wanted_row.shape[1]
    src_row = wanted_row[...] // rows_chip
    src_col = wanted_col[...] // rows_chip
    at_col = lax.broadcasted_iota(jnp.int32, (total, total), 0)
    at_row = lax.broadcasted_iota(jnp.int32, (total, total), 1)
    before = ((src_col == src_row) & (at_col < at_row)).astype(F32)
    rank = jnp.sum(before, axis=0, keepdims=True).astype(jnp.int32)
    slot = src_row * slots + rank
    boxes, orbitals, _ = basis.shape
    arrive = out.shape[1]
    for n in range(boxes):
        index = lax.broadcasted_iota(jnp.int32, (arrive, orbitals), 0)
        pick = (index == slot[:, n * orbitals:(n + 1) * orbitals]).astype(F32).astype(BF16)
        out[n] = jnp.dot(pick, basis[n], preferred_element_type=F32).astype(BF16)


def pick_kernel(me, wanted, out, *, rows_chip, slots):
    dests, total = wanted.shape
    asked = wanted[...]
    here = (asked // rows_chip) == me[0]
    local = (asked % rows_chip).astype(F32)
    at_col = lax.broadcasted_iota(jnp.int32, (total, total), 0)
    at_row = lax.broadcasted_iota(jnp.int32, (total, total), 1)
    earlier = (at_col < at_row).astype(F32).astype(BF16)
    rank = jnp.dot(here.astype(F32).astype(BF16), earlier, preferred_element_type=F32).astype(jnp.int32)
    rank = jnp.where(here, rank, -1)
    index = lax.broadcasted_iota(jnp.int32, (slots, total), 0)
    lane = lax.broadcasted_iota(jnp.int32, (slots, rows_chip), 1)
    for d in range(dests):
        chosen = jnp.where(index == rank[d:d + 1], local[d:d + 1], 0.0)
        row = jnp.sum(chosen, axis=1, keepdims=True).astype(jnp.int32)
        out[d * slots:(d + 1) * slots, :] = (lane == row).astype(F32).astype(BF16)


def select_kernel(pick, mine, theirs, out):
    rows = pick.shape[1]
    total = (mine[...] + theirs[...]).reshape(rows, mine.shape[2]).astype(BF16)
    out[...] = jnp.dot(pick[...], total, preferred_element_type=F32).astype(BF16)


def density_kernel(arrived, basis, supernode, out):
    for n in range(basis.shape[0]):
        projected = lax.dot_general(
            arrived[...], basis[n], (((0,), (0,)), ((), ())), preferred_element_type=F32
        )
        out[n:n + 1, :] = jnp.sum(supernode[n].astype(F32) * projected, axis=0, keepdims=True)


def local(n_row, panel, tiles, tile_slot, tile_col, pole_weight, box_orbitals, box_basis, supernode_basis):
    order = ring_order(n_row)
    half_ring = n_row // 2
    to_right = [(order[i], order[(i + 1) % n_row]) for i in range(n_row)]
    to_left = [(order[(i + 1) % n_row], order[i]) for i in range(n_row)]
    row = lax.axis_index("row").astype(jnp.int32)
    col = lax.axis_index("col").astype(jnp.int32)

    own = panel[0]
    blocks, parts, depth, width = own.shape
    tile_count, _, order_b, _ = tiles.shape
    reps = LANES // depth
    boxes, orbitals = box_orbitals.shape
    wanted_total = boxes * orbitals
    rows_chip = BR_DEV * order_b
    slots = 2 * wanted_total // n_row
    half = order_b // 2

    table = jnp.asarray(order, jnp.int32)
    position = jnp.sum(jnp.where(table == row, jnp.arange(n_row, dtype=jnp.int32), 0))
    offsets = [0]
    for h in range(1, half_ring):
        offsets += [-h, h]
    offsets.append(half_ring)
    at = (position + jnp.asarray(offsets, jnp.int32)) % n_row
    shard_rows = jnp.sum(jnp.where(at[:, None] == jnp.arange(n_row)[None], table[None], 0), axis=1)
    meta = jnp.concatenate([tile_slot, tile_col, shard_rows.astype(jnp.int32), col[None]])
    base = 2 * tile_count
    col_at = base + len(offsets)

    factor_spec = full_spec(own.shape)
    acc_shape = (BR_DEV, order_b, 2 * width)

    def tile_spec(where):
        return pl.BlockSpec(
            (1, 2, order_b, LANES), lambda t, meta: (t, 0, 0, meta[where] // reps)
        )

    def call(body, in_specs, out_specs, out_shape, scratch, shards, aliases=None):
        return pl.pallas_call(
            body,
            grid_spec=pltpu.PrefetchScalarGridSpec(
                num_scalar_prefetch=1,
                grid=(tile_count,),
                in_specs=in_specs,
                out_specs=out_specs,
                scratch_shapes=scratch,
            ),
            out_shape=out_shape,
            compiler_params=pltpu.CompilerParams(
                dimension_semantics=("arbitrary",), vmem_limit_bytes=VMEM_LIMIT
            ),
            cost_estimate=pl.CostEstimate(
                flops=shards * tile_count * order_b * 256 * 256 * 4,
                bytes_accessed=shards * tile_count * order_b * 256 * 2,
                transcendentals=0,
            ),
        )

    acc_out = jax.ShapeDtypeStruct(acc_shape, F32)

    wanted = box_orbitals.reshape(1, wanted_total)
    asked = wanted
    left, right = own, own
    acc = None
    distance = 1
    for h in range(1, half_ring + 1):
        if h < half_ring:
            next_left = lax.ppermute(left, "row", to_right)
            next_right = lax.ppermute(right, "row", to_left)
        else:
            cut = blocks // 2
            next_left = lax.ppermute(left[:cut], "row", to_right)
            next_right = lax.ppermute(right[cut:], "row", to_left)
        if distance < n_row:
            got = lax.ppermute(asked, "row", [(i, i ^ distance) for i in range(n_row)])
            low = (row // distance) % 2 == 0
            asked = jnp.concatenate(
                [jnp.where(low, asked, got), jnp.where(low, got, asked)], axis=0
            )
            distance *= 2
        if h == 1:
            acc = call(
                functools.partial(hop_first, tile_count=tile_count, where=[base], reps=reps),
                [factor_spec, tile_spec(base)],
                full_spec(acc_shape),
                acc_out,
                [pltpu.VMEM((blocks, 2 * LANES, 2 * width), BF16)],
                1,
            )(meta, own, tiles)
        else:
            at_h = [base + 2 * h - 3, base + 2 * h - 2]
            acc = call(
                functools.partial(hop_middle, tile_count=tile_count, where=at_h, reps=reps),
                [factor_spec, factor_spec, tile_spec(at_h[0]), tile_spec(at_h[1]), full_spec(acc_shape)],
                full_spec(acc_shape),
                acc_out,
                [pltpu.VMEM((blocks, 4 * LANES, 2 * width), BF16)],
                2,
            )(meta, left, right, tiles, tiles, acc)
        left, right = next_left, next_right

    half_shape = (BR_DEV, 2, half, width)
    dens_shape = (BR_DEV, order_b, width)
    last = base + len(offsets) - 1
    dens, mine, other = call(
        functools.partial(hop_last, tile_count=tile_count, where=[last], reps=reps, col_at=col_at),
        [
            pl.BlockSpec(memory_space=pltpu.SMEM),
            full_spec(left.shape),
            full_spec(right.shape),
            tile_spec(last),
            full_spec(acc_shape),
        ],
        [full_spec(dens_shape), full_spec(half_shape), full_spec(half_shape)],
        [
            jax.ShapeDtypeStruct(dens_shape, F32),
            jax.ShapeDtypeStruct(half_shape, F32),
            jax.ShapeDtypeStruct(half_shape, F32),
        ],
        [pltpu.VMEM(acc_shape, F32), pltpu.VMEM((blocks, 2 * LANES, 2 * width), BF16)],
        1,
    )(meta, pole_weight, left, right, tiles, acc)

    arrive = n_row * slots
    params = pltpu.CompilerParams(vmem_limit_bytes=VMEM_LIMIT)
    basis_here = pl.pallas_call(
        functools.partial(basis_kernel, rows_chip=rows_chip, slots=slots),
        out_shape=jax.ShapeDtypeStruct((boxes, arrive, box_basis.shape[2]), BF16),
        compiler_params=params,
        cost_estimate=pl.CostEstimate(
            flops=2 * arrive * wanted_total * box_basis.shape[2], bytes_accessed=2 ** 21, transcendentals=0
        ),
    )(wanted, box_orbitals.reshape(wanted_total, 1), box_basis)
    pick = pl.pallas_call(
        functools.partial(pick_kernel, rows_chip=rows_chip, slots=slots),
        in_specs=[pl.BlockSpec(memory_space=pltpu.SMEM), pl.BlockSpec(memory_space=pltpu.VMEM)],
        out_shape=jax.ShapeDtypeStruct((arrive, rows_chip), BF16),
        compiler_params=params,
        cost_estimate=pl.CostEstimate(
            flops=2 * arrive * wanted_total * 512, bytes_accessed=2 ** 21, transcendentals=0
        ),
    )(row[None], asked)

    swap = [(0, 1), (1, 0)]
    dens_other = lax.ppermute(dens, "col", swap)
    inverse_other = lax.ppermute(other, "col", swap)
    send = pl.pallas_call(
        select_kernel,
        out_shape=jax.ShapeDtypeStruct((arrive, width), BF16),
        compiler_params=params,
    )(pick, dens, dens_other)
    arrived = lax.all_to_all(send, "row", 0, 0, tiled=True)
    density = pl.pallas_call(
        density_kernel,
        out_shape=jax.ShapeDtypeStruct((boxes, box_basis.shape[2]), F32),
        compiler_params=params,
    )(arrived, basis_here, supernode_basis)
    return mine + inverse_other, density


def solution(mesh):
    return jax.shard_map(
        functools.partial(local, mesh.shape["row"]),
        mesh=mesh,
        in_specs=(
            P(("pole", "col"), None, None, "row", None),
            P(("pole", "row", "col"), None, None, None),
            P(("pole", "row", "col")),
            P(("pole", "row", "col")),
            P("pole"),
            P(("pole", "row", "col"), None),
            P(("pole", "row", "col"), None, None),
            P(("pole", "row", "col"), None, None),
        ),
        out_specs=(P(("pole", "row"), None, "col", None), P(("pole", "row", "col"), None)),
        check_vma=False,
    )
```

time: 161 us -> 87.1 us (0.54)
  waiting for transfers between devices: 101 us -> 8.39 us
  Pallas kernels: 0 us -> 48.3 us
  matrix products: 19.9 us -> 0 us
  starting transfers between devices: 0.12 us -> 19.5 us
  local copies, waits for them, and re-layouts: 20 us -> 2.62 us
  between operations: 14 us -> 0.88 us
    all_gather x2 -> x0, waiting for transfers between devices: 94.5 us -> none  [the longest x1 52.9 us: local(): gathered = lax.all_gather(panel, 'row', axis=3, tiled=True)]
    pallas_call x0 -> x9, Pallas kernels: none -> 48.3 us  [the longest x3 27.1 us: local(): call(functools.partial(hop_middle, tile_count=tile_count, where=at_h, rep...]
    dot_general x6 -> x0, matrix products: 19.9 us -> none  [the longest x1 4.82 us: local(): jnp.einsum('tab,tbs->tas', tiles[:, 0], chosen[:, 0], preferred_element_t...]
    ppermute x0 -> x13, starting transfers between devices: none -> 15.7 us  [the longest x3 6.25 us: local(): got = lax.ppermute(asked, 'row', [(i, i ^ distance) for i in range(n_row)])]
    squeeze x3 -> x0, local copies, waits for them, and re-layouts: 9.15 us -> none  [the longest x2 5.91 us: local(): chosen[:, 1]]
    reduce_scatter x1 -> x0, waiting for transfers between devices: 6.56 us -> none  [local(): lax.psum_scatter(partial_value, 'col', scatter_dimension=2, tiled=True)]
    gather x2 -> x0, local copies, waits for them, and re-layouts: 6.55 us -> none  [local(): fetched = shards[clipped, local_row]]
    all_to_all x0 -> x1, waiting for transfers between devices: none -> 6.4 us  [local(): arrived = lax.all_to_all(send, 'row', 0, 0, tiled=True)]
  transfers between devices with their start and end apart: 3 -> 14, of which waited for: 3 -> 2; matrix products, arithmetic and copies ran while one was open for 1% -> 8% of each run, Pallas kernels for 0% -> 55%
where the time goes in v1:
time: 87.1 us; the launch traced here: 86 us
  Pallas kernels  48.3 us (55%)
  starting transfers between devices  19.5 us (22%)
  waiting for transfers between devices  8.39 us (10%)
  other arithmetic  6.29 us (7%)
  local copies, waits for them, and re-layouts  2.62 us (3%)
  between operations  0.88 us (1%)
    pallas_call x3, Pallas kernels, local(): call(functools.partial(hop_middle, tile_count=tile_count, where=at_h, rep...  27.1 us
    pallas_call x1, Pallas kernels, local(): call(functools.partial(hop_last, tile_count=tile_count, where=[last], rep...  8.97 us
    pallas_call x1, Pallas kernels, local(): call(functools.partial(hop_first, tile_count=tile_count, where=[base], re...  7.94 us
    all_to_all x1, waiting for transfers between devices, local(): arrived = lax.all_to_all(send, 'row', 0, 0, tiled=True)  6.4 us
    ppermute x3, starting transfers between devices, local(): got = lax.ppermute(asked, 'row', [(i, i ^ distance) for i in range(n_row)])  6.25 us
    ppermute x3, starting transfers between devices, local(): next_left = lax.ppermute(left, 'row', to_right)  4.71 us
    all_to_all x1, starting transfers between devices, local(): arrived = lax.all_to_all(send, 'row', 0, 0, tiled=True)  3.87 us
    unnamed x12, local copies, waits for them, and re-layouts  2.6 us
  transfers between devices with their start and end apart: 14, of which 2 were waited for; matrix products, arithmetic and copies ran while one was open for 8% of the time, Pallas kernels for 55%

profile of v1, /device:TPU:0, one launch (start us, length us, event | category | flops | bytes accessed | tf_op | source)
XLA Modules:
  0.0 86.0 jit_solution(3406195220972038479)
XLA Ops:
  0.6 3.1 %collective-permute-start = (bf16[8,2,64,128]{3,2,1,0:T(8,128)(2,1)}, bf16[8,2,64,128]{3,2,1,0:T(8,128)(2,1)S(1)}, u32[]{:S(2)}, u32[]{:S(2)}) collective-permute-start(bf16[8,2,64,128]{3,2,1,0:T(8,128)(2,1)} %bitcast.14), channel_id=1, source_target_pairs={{0,4},{4,8},{8,12},{12,14},{14,10},{10,6},{6,2},{2,0},{1,5},{5,9},... | collective-permute-start | bytes 786440 | tf_op jit(solution)/shard_map/ppermute | solution.py:214
  3.7 0.0 collective-permute-start.4
  3.7 0.7 copy.14
  4.4 2.0 %collective-permute-start.9 = (s32[1,512]{1,0:T(1,128)S(1)}, s32[1,512]{1,0:T(1,128)S(1)}, u32[]{:S(2)}, u32[]{:S(2)}) collective-permute-start(s32[1,512]{1,0:T(1,128)S(1)} %bitcast.17), channel_id=1, source_target_pairs={{0,2},{2,0},{4,6},{6,4},{8,10},{10,8},{12,14},{14,12},{1,3},{3,1},... | collective-permute-start | bytes 6152 | tf_op jit(solution)/shard_map/ppermute | solution.py:221
  6.4 1.3 %fusion.1 = s32[]{:T(128)} fusion(s32[8]{0:T(128)} %constant.78.clone, s32[]{:T(128)} %axis_index.23), kind=kLoop, calls=%fused_computation.16 | loop fusion | flops 23 | bytes 40 | tf_op jit(solution)/shard_map/reduce_sum | solution.py:165
  7.7 1.3 %and_select_fusion = s32[8]{0:T(128)S(1)} fusion(s32[8]{0:T(128)} %constant.79.clone, s32[]{:T(128)} %fusion.1), kind=kLoop, calls=%fused_computation.13 | loop fusion | flops 96 | bytes 68 | tf_op jit(solution)/shard_map/jit(remainder)/select_n | solution.py:170
  9.0 0.8 select_reduce_fusion
  9.8 0.8 pad_add_fusion.3.meta
  10.6 0.9 %copy-done.2 = bf16[1,8,2,64,128]{4,3,2,1,0:T(8,128)(2,1)S(1)} copy-done((bf16[1,8,2,64,128]{4,3,2,1,0:T(8,128)(2,1)S(1)}, bf16[1,8,2,64,128]{4,3,2,1,0:T(8,128)(2,1)}, u32[]{:S(2)}) %copy-start.2) | copy-done | bytes 262168
  11.5 7.9 %shard_map.113.start = f32[2,512,256]{2,1,0:T(8,128)S(1)} custom-call(s32[31]{0:T(128)S(1)} %pad_add_fusion.3.meta, bf16[8,2,64,128]{3,2,1,0:T(8,128)(2,1)S(1)} %bitcast.16, bf16[11,2,512,512]{3,2,1,0:T(8,128)(2,1)} %tile.3), custom_call_target="tpu_custom_call" | custom-call | flops 1476395008 | bytes 2883584 | tf_op jit(solution)/shard_map/pallas_call | solution.py:228
  19.5 0.0 collective-permute-done.9
  19.5 1.6 %collective-permute-start.10 = (s32[2,512]{1,0:T(2,128)S(1)}, s32[2,512]{1,0:T(2,128)S(1)}, u32[]{:S(2)}, u32[]{:S(2)}) collective-permute-start(s32[2,512]{1,0:T(2,128)S(1)} %pad_add_fusion.2), channel_id=1, source_target_pairs={{0,4},{2,6},{4,0},{6,2},{8,12},{10,14},{12,8},{14,10},{1,5},{3,7},... | collective-permute-start | bytes 12296 | tf_op jit(solution)/shard_map/ppermute | solution.py:221
  21.2 0.0 collective-permute-done.from_left
  21.2 0.5 collective-permute-start.1
  21.6 0.0 collective-permute-done.4.from_right
  21.6 1.6 %collective-permute-start.5 = (bf16[8,2,64,128]{3,2,1,0:T(8,128)(2,1)S(1)}, bf16[8,2,64,128]{3,2,1,0:T(8,128)(2,1)S(1)}, u32[]{:S(2)}, u32[]{:S(2)}) collective-permute-start(bf16[8,2,64,128]{3,2,1,0:T(8,128)(2,1)S(1)} %collective-permute-done.4.from_right), channel_id=1, source_target_pairs={{4,0},{8,4},{12,8},{14,12},{10,14},{6,10},{2,6},{0,2},{5,1},{9,5},... | collective-permute-start | bytes 786440 | tf_op jit(solution)/shard_map/ppermute | solution.py:215
  23.2 9.0 %shard_map.114.start = f32[2,512,256]{2,1,0:T(8,128)S(1)} custom-call(s32[31]{0:T(128)S(1)} %pad_add_fusion.3.meta, bf16[8,2,64,128]{3,2,1,0:T(8,128)(2,1)S(1)} %collective-permute-done.from_left, bf16[8,2,64,128]{3,2,1,0:T(8,128)(2,1)S(1)} %collective-permute-done.4.from_right, bf16[11,2,512,512]{3,2,1,0:T(8,128)(2,1)} %tile.3, ...), custom_call_target="tpu_custom_call" | custom-call | flops 2952790016 | bytes 5767168 | tf_op jit(solution)/shard_map/pallas_call | solution.py:238
  32.2 0.0 collective-permute-done.1.from_left
  32.3 1.2 %collective-permute-start.2 = (bf16[8,2,64,128]{3,2,1,0:T(8,128)(2,1)S(1)}, bf16[8,2,64,128]{3,2,1,0:T(8,128)(2,1)S(1)}, u32[]{:S(2)}, u32[]{:S(2)}) collective-permute-start(bf16[8,2,64,128]{3,2,1,0:T(8,128)(2,1)S(1)} %collective-permute-done.1.from_left), channel_id=1, source_target_pairs={{0,4},{4,8},{8,12},{12,14},{14,10},{10,6},{6,2},{2,0},{1,5},{5,9},... | collective-permute-start | bytes 786440 | tf_op jit(solution)/shard_map/ppermute | solution.py:214
  33.4 0.0 collective-permute-done.5.from_right
  33.4 0.9 %collective-permute-start.6 = (bf16[8,2,64,128]{3,2,1,0:T(8,128)(2,1)S(1)}, bf16[8,2,64,128]{3,2,1,0:T(8,128)(2,1)S(1)}, u32[]{:S(2)}, u32[]{:S(2)}) collective-permute-start(bf16[8,2,64,128]{3,2,1,0:T(8,128)(2,1)S(1)} %collective-permute-done.5.from_right), channel_id=1, source_target_pairs={{4,0},{8,4},{12,8},{14,12},{10,14},{6,10},{2,6},{0,2},{5,1},{9,5},... | collective-permute-start | bytes 786440 | tf_op jit(solution)/shard_map/ppermute | solution.py:215
  34.3 9.0 %shard_map.115.start = f32[2,512,256]{2,1,0:T(8,128)S(1)} custom-call(s32[31]{0:T(128)S(1)} %pad_add_fusion.3.meta, bf16[8,2,64,128]{3,2,1,0:T(8,128)(2,1)S(1)} %collective-permute-done.1.from_left, bf16[8,2,64,128]{3,2,1,0:T(8,128)(2,1)S(1)} %collective-permute-done.5.from_right, bf16[11,2,512,512]{3,2,1,0:T(8,128)(2,1)} %tile.3, ...), custom_call_target="tpu_custom_call" | custom-call | flops 2952790016 | bytes 5767168 | tf_op jit(solution)/shard_map/pallas_call | solution.py:238
  43.4 0.0 collective-permute-done.2.from_left
  43.4 1.2 %collective-permute-start.3 = (bf16[4,2,64,128]{3,2,1,0:T(8,128)(2,1)S(1)}, bf16[4,2,64,128]{3,2,1,0:T(8,128)(2,1)S(1)}, u32[]{:S(2)}, u32[]{:S(2)}) collective-permute-start(bf16[4,2,64,128]{3,2,1,0:T(8,128)(2,1)S(1)} %slice.8), channel_id=1, source_target_pairs={{0,4},{4,8},{8,12},{12,14},{14,10},{10,6},{6,2},{2,0},{1,5},{5,9},... | collective-permute-start | bytes 393224 | tf_op jit(solution)/shard_map/ppermute | solution.py:218
  44.6 0.0 collective-permute-done.6.from_right
  44.6 0.0 copy-start.4
  44.6 0.9 %collective-permute-start.7 = (bf16[4,2,64,128]{3,2,1,0:T(8,128)(2,1)S(1)}, bf16[4,2,64,128]{3,2,1,0:T(8,128)(2,1)S(1)}, u32[]{:S(2)}, u32[]{:S(2)}) collective-permute-start(bf16[4,2,64,128]{3,2,1,0:T(8,128)(2,1)S(1)} %slice.9), channel_id=1, source_target_pairs={{4,0},{8,4},{12,8},{14,12},{10,14},{6,10},{2,6},{0,2},{5,1},{9,5},... | collective-permute-start | bytes 393224 | tf_op jit(solution)/shard_map/ppermute | solution.py:219
  45.6 9.0 %shard_map.116.start = f32[2,512,256]{2,1,0:T(8,128)S(1)} custom-call(s32[31]{0:T(128)S(1)} %pad_add_fusion.3.meta, bf16[8,2,64,128]{3,2,1,0:T(8,128)(2,1)S(1)} %collective-permute-done.2.from_left, bf16[8,2,64,128]{3,2,1,0:T(8,128)(2,1)S(1)} %collective-permute-done.6.from_right, bf16[11,2,512,512]{3,2,1,0:T(8,128)(2,1)} %tile.3, ...), custom_call_target="tpu_custom_call" | custom-call | flops 2952790016 | bytes 5767168 | tf_op jit(solution)/shard_map/pallas_call | solution.py:238
  54.6 0.0 collective-permute-done.3.low
  54.6 0.0 collective-permute-done.7.high
  54.7 9.0 %shard_map.117 = (f32[2,512,128]{2,1,0:T(8,128)S(1)}, f32[2,2,256,128]{3,2,1,0:T(8,128)S(1)}, f32[2,2,256,128]{3,2,1,0:T(8,128)}) custom-call(s32[31]{0:T(128)S(1)} %pad_add_fusion.3.meta, f32[2]{0:T(128)S(1)} %copy-done.4, bf16[4,2,64,128]{3,2,1,0:T(8,128)(2,1)S(1)} %collective-permute-done.3.low, bf16[4,2,64,128]{3,2,1,0:T(8,128)(2,1)S(1)} %collective-permute-done.7.high, ...), custom_call_target="tpu_custom_call" | custom-call | flops 1476395008 | bytes 2883584 | tf_op jit(solution)/shard_map/pallas_call | solution.py:251
  63.6 0.8 copy-done.1
  64.4 0.0 collective-permute-start.12
  64.4 0.0 collective-permute-done.10
  64.5 2.7 %collective-permute-start.11 = (s32[4,512]{1,0:T(4,128)S(1)}, s32[4,512]{1,0:T(4,128)S(1)}, u32[]{:S(2)}, u32[]{:S(2)}) collective-permute-start(s32[4,512]{1,0:T(4,128)S(1)} %pad_add_fusion.1), channel_id=1, source_target_pairs={{0,8},{2,10},{4,12},{6,14},{8,0},{10,2},{12,4},{14,6},{1,9},{3,11}... | collective-permute-start | bytes 24584 | tf_op jit(solution)/shard_map/ppermute | solution.py:221
  67.1 2.0 %collective-permute-done.11 = s32[4,512]{1,0:T(4,128)S(1)} collective-permute-done((s32[4,512]{1,0:T(4,128)S(1)}, s32[4,512]{1,0:T(4,128)S(1)}, u32[]{:S(2)}, u32[]{:S(2)}) %collective-permute-start.11) | collective-permute-done | bytes 8224 | tf_op jit(solution)/shard_map/ppermute | solution.py:221
  69.1 0.1 collective-permute-start.8
  69.2 0.8 shard_map.118.pick
  70.0 0.0 copy-start
  70.1 1.4 %shard_map.119 = bf16[1024,128]{1,0:T(8,128)(2,1)} custom-call(bf16[1024,1024]{1,0:T(8,128)(2,1)S(1)} %shard_map.118.pick, f32[2,512,128]{2,1,0:T(8,128)S(1)} %get-tuple-element.7.mine, f32[2,512,128]{2,1,0:T(8,128)S(1)} %collective-permute-done.12.theirs), custom_call_target="tpu_custom_call" | custom-call | tf_op jit(solution)/shard_map/pallas_call | solution.py:293
  71.5 3.9 %all-to-all-start = ((bf16[8,128,128]{2,1,0:T(8,128)(2,1)}), bf16[8,128,128]{2,1,0:T(8,128)(2,1)S(1)}, u32[]{:S(2)}, u32[]{:S(2)}) async-start(bf16[8,128,128]{2,1,0:T(8,128)(2,1)} %bitcast.3), calls=%async_computation | async-start | bytes 524288 | tf_op jit(solution)/shard_map/all_to_all | solution.py:298
  75.3 0.1 copy.16
  75.5 0.0 copy-start.3
  75.5 0.9 %shard_map.120.basis = bf16[2,1024,512]{2,1,0:T(8,128)(2,1)S(1)} custom-call(s32[1,512]{1,0:T(1,128)S(1)} %bitcast.20, s32[512,1]{1,0:T(8,128)S(1)} %bitcast.13, bf16[2,256,512]{2,1,0:T(8,128)(2,1)S(1)} %copy-done), custom_call_target="tpu_custom_call" | custom-call | flops 536870912 | bytes 2097152 | tf_op jit(solution)/shard_map/pallas_call | solution.py:272
  76.5 0.0 collective-permute-done.8
  76.5 2.0 %add.31 = f32[2,2,256,128]{3,2,1,0:T(8,128)} add(f32[2,2,256,128]{3,2,1,0:T(8,128)} %copy-done.1, f32[2,2,256,128]{3,2,1,0:T(8,128)} %collective-permute-done.8) | non-fusion elementwise | flops 131072 | bytes 1572864 | tf_op jit(solution)/shard_map/add | solution.py:304
  78.5 6.4 %all-to-all-done = bf16[8,128,128]{2,1,0:T(8,128)(2,1)S(1)} async-done(((bf16[8,128,128]{2,1,0:T(8,128)(2,1)}), bf16[8,128,128]{2,1,0:T(8,128)(2,1)S(1)}, u32[]{:S(2)}, u32[]{:S(2)}) %all-to-all-start) | async-done | bytes 262176 | tf_op jit(solution)/shard_map/all_to_all | solution.py:298
  84.9 1.1 %shard_map.121 = f32[2,512]{1,0:T(2,128)} custom-call(bf16[1024,128]{1,0:T(8,128)(2,1)S(1)} %bitcast.12, bf16[2,1024,512]{2,1,0:T(8,128)(2,1)S(1)} %shard_map.120.basis, bf16[2,128,512]{2,1,0:T(8,128)(2,1)S(1)} %copy-done.3), custom_call_target="tpu_custom_call" | custom-call | tf_op jit(solution)/shard_map/pallas_call | solution.py:299
  (14 shorter events, 0.1 us)
Async XLA Ops:
  0.6 20.5 %collective-permute-start = (bf16[8,2,64,128]{3,2,1,0:T(8,128)(2,1)}, bf16[8,2,64,128]{3,2,1,0:T(8,128)(2,1)S(1)}, u32[]{:S(2)}, u32[]{:S(2)}) collective-permute-start(bf16[8,2,64,128]{3,2,1,0:T(8,128)(2,1)} %bitcast.14), channel_id=1, source_target_pairs={{0,4},{4,8},{8,12},{12,14},{14,10},{10,6},{6,2},{2,0},{1,5},{5,9},... | collective-permute-start | bytes 786440 | tf_op jit(solution)/shard_map/ppermute | solution.py:214
  3.7 17.9 %collective-permute-start.4 = (bf16[8,2,64,128]{3,2,1,0:T(8,128)(2,1)}, bf16[8,2,64,128]{3,2,1,0:T(8,128)(2,1)S(1)}, u32[]{:S(2)}, u32[]{:S(2)}) collective-permute-start(bf16[8,2,64,128]{3,2,1,0:T(8,128)(2,1)} %bitcast.15), channel_id=1, source_target_pairs={{4,0},{8,4},{12,8},{14,12},{10,14},{6,10},{2,6},{0,2},{5,1},{9,5},... | collective-permute-start | bytes 786440 | tf_op jit(solution)/shard_map/ppermute | solution.py:215
  4.4 15.1 %collective-permute-start.9 = (s32[1,512]{1,0:T(1,128)S(1)}, s32[1,512]{1,0:T(1,128)S(1)}, u32[]{:S(2)}, u32[]{:S(2)}) collective-permute-start(s32[1,512]{1,0:T(1,128)S(1)} %bitcast.17), channel_id=1, source_target_pairs={{0,2},{2,0},{4,6},{6,4},{8,10},{10,8},{12,14},{14,12},{1,3},{3,1},... | collective-permute-start | bytes 6152 | tf_op jit(solution)/shard_map/ppermute | solution.py:221
  10.5 1.0 %copy-start.2 = (bf16[1,8,2,64,128]{4,3,2,1,0:T(8,128)(2,1)S(1)}, bf16[1,8,2,64,128]{4,3,2,1,0:T(8,128)(2,1)}, u32[]{:S(2)}) copy-start(bf16[1,8,2,64,128]{4,3,2,1,0:T(8,128)(2,1)} %param.10) | copy-start | bytes 786436
  19.5 44.9 %collective-permute-start.10 = (s32[2,512]{1,0:T(2,128)S(1)}, s32[2,512]{1,0:T(2,128)S(1)}, u32[]{:S(2)}, u32[]{:S(2)}) collective-permute-start(s32[2,512]{1,0:T(2,128)S(1)} %pad_add_fusion.2), channel_id=1, source_target_pairs={{0,4},{2,6},{4,0},{6,2},{8,12},{10,14},{12,8},{14,10},{1,5},{3,7},... | collective-permute-start | bytes 12296 | tf_op jit(solution)/shard_map/ppermute | solution.py:221
  21.2 11.1 %collective-permute-start.1 = (bf16[8,2,64,128]{3,2,1,0:T(8,128)(2,1)S(1)}, bf16[8,2,64,128]{3,2,1,0:T(8,128)(2,1)S(1)}, u32[]{:S(2)}, u32[]{:S(2)}) collective-permute-start(bf16[8,2,64,128]{3,2,1,0:T(8,128)(2,1)S(1)} %collective-permute-done.from_left), channel_id=1, source_target_pairs={{0,4},{4,8},{8,12},{12,14},{14,10},{10,6},{6,2},{2,0},{1,5},{5,9},... | collective-permute-start | bytes 786440 | tf_op jit(solution)/shard_map/ppermute | solution.py:214
  21.6 11.8 %collective-permute-start.5 = (bf16[8,2,64,128]{3,2,1,0:T(8,128)(2,1)S(1)}, bf16[8,2,64,128]{3,2,1,0:T(8,128)(2,1)S(1)}, u32[]{:S(2)}, u32[]{:S(2)}) collective-permute-start(bf16[8,2,64,128]{3,2,1,0:T(8,128)(2,1)S(1)} %collective-permute-done.4.from_right), channel_id=1, source_target_pairs={{4,0},{8,4},{12,8},{14,12},{10,14},{6,10},{2,6},{0,2},{5,1},{9,5},... | collective-permute-start | bytes 786440 | tf_op jit(solution)/shard_map/ppermute | solution.py:215
  32.3 11.1 %collective-permute-start.2 = (bf16[8,2,64,128]{3,2,1,0:T(8,128)(2,1)S(1)}, bf16[8,2,64,128]{3,2,1,0:T(8,128)(2,1)S(1)}, u32[]{:S(2)}, u32[]{:S(2)}) collective-permute-start(bf16[8,2,64,128]{3,2,1,0:T(8,128)(2,1)S(1)} %collective-permute-done.1.from_left), channel_id=1, source_target_pairs={{0,4},{4,8},{8,12},{12,14},{14,10},{10,6},{6,2},{2,0},{1,5},{5,9},... | collective-permute-start | bytes 786440 | tf_op jit(solution)/shard_map/ppermute | solution.py:214
  33.4 11.2 %collective-permute-start.6 = (bf16[8,2,64,128]{3,2,1,0:T(8,128)(2,1)S(1)}, bf16[8,2,64,128]{3,2,1,0:T(8,128)(2,1)S(1)}, u32[]{:S(2)}, u32[]{:S(2)}) collective-permute-start(bf16[8,2,64,128]{3,2,1,0:T(8,128)(2,1)S(1)} %collective-permute-done.5.from_right), channel_id=1, source_target_pairs={{4,0},{8,4},{12,8},{14,12},{10,14},{6,10},{2,6},{0,2},{5,1},{9,5},... | collective-permute-start | bytes 786440 | tf_op jit(solution)/shard_map/ppermute | solution.py:215
  43.4 11.2 %collective-permute-start.3 = (bf16[4,2,64,128]{3,2,1,0:T(8,128)(2,1)S(1)}, bf16[4,2,64,128]{3,2,1,0:T(8,128)(2,1)S(1)}, u32[]{:S(2)}, u32[]{:S(2)}) collective-permute-start(bf16[4,2,64,128]{3,2,1,0:T(8,128)(2,1)S(1)} %slice.8), channel_id=1, source_target_pairs={{0,4},{4,8},{8,12},{12,14},{14,10},{10,6},{6,2},{2,0},{1,5},{5,9},... | collective-permute-start | bytes 393224 | tf_op jit(solution)/shard_map/ppermute | solution.py:218
  44.6 10.0 %copy-start.4 = (f32[2]{0:T(128)S(1)}, f32[2]{0:T(128)}, u32[]{:S(2)}) copy-start(f32[2]{0:T(128)} %pole_weight.1) | copy-start | bytes 28
  44.6 10.0 %collective-permute-start.7 = (bf16[4,2,64,128]{3,2,1,0:T(8,128)(2,1)S(1)}, bf16[4,2,64,128]{3,2,1,0:T(8,128)(2,1)S(1)}, u32[]{:S(2)}, u32[]{:S(2)}) collective-permute-start(bf16[4,2,64,128]{3,2,1,0:T(8,128)(2,1)S(1)} %slice.9), channel_id=1, source_target_pairs={{4,0},{8,4},{12,8},{14,12},{10,14},{6,10},{2,6},{0,2},{5,1},{9,5},... | collective-permute-start | bytes 393224 | tf_op jit(solution)/shard_map/ppermute | solution.py:219
  63.6 0.8 copy-start.1
  64.4 5.6 %collective-permute-start.12 = (f32[2,512,128]{2,1,0:T(8,128)S(1)}, f32[2,512,128]{2,1,0:T(8,128)S(1)}, u32[]{:S(2)}, u32[]{:S(2)}) collective-permute-start(f32[2,512,128]{2,1,0:T(8,128)S(1)} %get-tuple-element.7.mine), channel_id=1, source_target_pairs={{0,1},{1,0},{2,3},{3,2},{4,5},{5,4},{6,7},{7,6},{8,9},{9,8},{10,11... | collective-permute-start | bytes 1572872 | tf_op jit(solution)/shard_map/ppermute | solution.py:291
  64.5 4.6 %collective-permute-start.11 = (s32[4,512]{1,0:T(4,128)S(1)}, s32[4,512]{1,0:T(4,128)S(1)}, u32[]{:S(2)}, u32[]{:S(2)}) collective-permute-start(s32[4,512]{1,0:T(4,128)S(1)} %pad_add_fusion.1), channel_id=1, source_target_pairs={{0,8},{2,10},{4,12},{6,14},{8,0},{10,2},{12,4},{14,6},{1,9},{3,11}... | collective-permute-start | bytes 24584 | tf_op jit(solution)/shard_map/ppermute | solution.py:221
  69.1 7.4 %collective-permute-start.8 = (f32[2,2,256,128]{3,2,1,0:T(8,128)}, f32[2,2,256,128]{3,2,1,0:T(8,128)}, u32[]{:S(2)}, u32[]{:S(2)}) collective-permute-start(f32[2,2,256,128]{3,2,1,0:T(8,128)} %get-tuple-element.6), channel_id=1, source_target_pairs={{0,1},{1,0},{2,3},{3,2},{4,5},{5,4},{6,7},{7,6},{8,9},{9,8},{10,11... | collective-permute-start | bytes 1572872 | tf_op jit(solution)/shard_map/ppermute | solution.py:292
  70.0 5.5 %copy-start = (bf16[2,256,512]{2,1,0:T(8,128)(2,1)S(1)}, bf16[2,256,512]{2,1,0:T(8,128)(2,1)}, u32[]{:S(2)}) copy-start(bf16[2,256,512]{2,1,0:T(8,128)(2,1)} %basis.1) | copy-start | bytes 1572868
  71.5 13.4 %all-to-all-start = ((bf16[8,128,128]{2,1,0:T(8,128)(2,1)}), bf16[8,128,128]{2,1,0:T(8,128)(2,1)S(1)}, u32[]{:S(2)}, u32[]{:S(2)}) async-start(bf16[8,128,128]{2,1,0:T(8,128)(2,1)} %bitcast.3), calls=%async_computation | async-start | bytes 524288 | tf_op jit(solution)/shard_map/all_to_all | solution.py:298
  75.5 9.4 %copy-start.3 = (bf16[2,128,512]{2,1,0:T(8,128)(2,1)S(1)}, bf16[2,128,512]{2,1,0:T(8,128)(2,1)}, u32[]{:S(2)}) copy-start(bf16[2,128,512]{2,1,0:T(8,128)(2,1)} %supernode.1) | copy-start | bytes 786436

commit v2 on v1

v2 whole, which is shorter than its diff:
```python
import functools

import jax
import jax.numpy as jnp
from jax import lax
from jax.experimental import pallas as pl
from jax.experimental.pallas import tpu as pltpu
from jax.sharding import PartitionSpec as P

BR_DEV = 2
LANES = 128
F32 = jnp.float32
BF16 = jnp.bfloat16
VMEM_LIMIT = 16 * 1024 * 1024


def ring_order(n):
    if n <= 8 and n % 2 == 0:
        return list(range(0, n, 2)) + list(range(n - 1, 0, -2))
    return list(range(n))


def shard_row(n, hop):
    row = lax.axis_index("row")
    if ring_order(n) == list(range(n)):
        return lax.rem(row + hop + n, n)
    at = jnp.where(row % 2 == 0, row // 2, n - 1 - row // 2)
    at = lax.rem(at + hop + n, n)
    return jnp.where(at < n // 2, 2 * at, 2 * (n - 1 - at) + 1)


def place(factor, first):
    depth = factor.shape[1]
    reps = LANES // depth
    row = lax.broadcasted_iota(jnp.int32, (LANES, factor.shape[2]), 0)
    inside = (row // depth) == first
    spread = [
        jnp.where(inside, jnp.concatenate([factor[p].astype(F32)] * reps, axis=0), 0.0)
        for p in range(2)
    ]
    upper = jnp.concatenate([spread[0], spread[1]], axis=1)
    lower = jnp.concatenate([-spread[1], spread[0]], axis=1)
    return jnp.concatenate([upper, lower], axis=0).astype(BF16)


def accumulate(slots, cols, tiles, shards, acc, weights):
    starts = []
    for s, (row, parts) in enumerate(shards):
        reps = LANES // parts[0].shape[2]
        starts.append(pl.multiple_of(row // reps * LANES, LANES))
        at = 0
        for part in parts:
            for j in range(part.shape[0]):
                weights[at, s * 2 * LANES:(s + 1) * 2 * LANES, :] = place(part[j], row % reps)
                at += 1
    for t in range(tiles.shape[0]):
        left = jnp.concatenate(
            [tiles[t, p, :, pl.ds(start, LANES)] for start in starts for p in range(2)], axis=1
        )
        acc[slots[t]] += jnp.dot(left, weights[cols[t]], preferred_element_type=F32)


def hop_first(slots, cols, own, tiles, out, weights, *, n):
    out[...] = jnp.zeros_like(out)
    accumulate(slots, cols, tiles, [(shard_row(n, 0), [own])], out, weights)


def hop_middle(slots, cols, from_left, from_right, tiles, start, out, weights, *, n, hop):
    out[...] = start[...]
    shards = [(shard_row(n, -hop), [from_left]), (shard_row(n, hop), [from_right])]
    accumulate(slots, cols, tiles, shards, out, weights)


def hop_last(slots, cols, pole_weight, low, high, tiles, start, dens, mine, other, acc, weights, *, n):
    acc[...] = start[...]
    accumulate(slots, cols, tiles, [(shard_row(n, n // 2), [low, high])], acc, weights)
    col = lax.axis_index("col")
    half = mine.shape[2]
    width = mine.shape[3]
    for slot in range(acc.shape[0]):
        real = -acc[slot, :, :width]
        imag = -acc[slot, :, width:]
        dens[slot] = pole_weight[0] * imag + pole_weight[1] * real
        for p in range(2):
            cut = slice(p * width, (p + 1) * width)
            mine[slot, p] = -acc[slot, pl.ds(pl.multiple_of(col * half, half), half), cut]
            other[slot, p] = -acc[slot, pl.ds(pl.multiple_of((1 - col) * half, half), half), cut]


def basis_kernel(wanted_row, wanted_col, basis, out, *, rows_chip, slots):
    total = wanted_row.shape[1]
    src_row = wanted_row[...] // rows_chip
    src_col = wanted_col[...] // rows_chip
    at_col = lax.broadcasted_iota(jnp.int32, (total, total), 0)
    at_row = lax.broadcasted_iota(jnp.int32, (total, total), 1)
    before = ((src_col == src_row) & (at_col < at_row)).astype(F32)
    rank = jnp.sum(before, axis=0, keepdims=True).astype(jnp.int32)
    slot = src_row * slots + rank
    boxes, orbitals, _ = basis.shape
    arrive = out.shape[1]
    for n in range(boxes):
        index = lax.broadcasted_iota(jnp.int32, (arrive, orbitals), 0)
        pick = (index == slot[:, n * orbitals:(n + 1) * orbitals]).astype(F32).astype(BF16)
        out[n] = jnp.dot(pick, basis[n], preferred_element_type=F32).astype(BF16)


def pick_kernel(wanted, out, *, rows_chip, slots):
    dests, total = wanted.shape
    asked = wanted[...]
    here = (asked // rows_chip) == lax.axis_index("row")
    local = (asked % rows_chip).astype(F32)
    at_col = lax.broadcasted_iota(jnp.int32, (total, total), 0)
    at_row = lax.broadcasted_iota(jnp.int32, (total, total), 1)
    earlier = (at_col < at_row).astype(F32).astype(BF16)
    rank = jnp.dot(here.astype(F32).astype(BF16), earlier, preferred_element_type=F32).astype(jnp.int32)
    rank = jnp.where(here, rank, -1)
    index = lax.broadcasted_iota(jnp.int32, (slots, total), 0)
    lane = lax.broadcasted_iota(jnp.int32, (slots, rows_chip), 1)
    for d in range(dests):
        chosen = jnp.where(index == rank[d:d + 1], local[d:d + 1], 0.0)
        row = jnp.sum(chosen, axis=1, keepdims=True).astype(jnp.int32)
        out[d * slots:(d + 1) * slots, :] = (lane == row).astype(F32).astype(BF16)


def select_kernel(pick, mine, theirs, out):
    rows = pick.shape[1]
    total = (mine[...] + theirs[...]).reshape(rows, mine.shape[2]).astype(BF16)
    out[...] = jnp.dot(pick[...], total, preferred_element_type=F32).astype(BF16)


def density_kernel(arrived, basis, supernode, out):
    for n in range(basis.shape[0]):
        projected = lax.dot_general(
            arrived[...], basis[n], (((0,), (0,)), ((), ())), preferred_element_type=F32
        )
        out[n:n + 1, :] = jnp.sum(supernode[n].astype(F32) * projected, axis=0, keepdims=True)


def local(n_row, panel, tiles, tile_slot, tile_col, pole_weight, box_orbitals, box_basis, supernode_basis):
    order = ring_order(n_row)
    half_ring = n_row // 2
    to_right = [(order[i], order[(i + 1) % n_row]) for i in range(n_row)]
    to_left = [(order[(i + 1) % n_row], order[i]) for i in range(n_row)]
    row = lax.axis_index("row").astype(jnp.int32)

    own = panel[0]
    blocks, parts, depth, width = own.shape
    tile_count, _, order_b, _ = tiles.shape
    boxes, orbitals = box_orbitals.shape
    wanted_total = boxes * orbitals
    rows_chip = BR_DEV * order_b
    slots = 2 * wanted_total // n_row
    half = order_b // 2
    acc_shape = (BR_DEV, order_b, 2 * width)
    acc_out = jax.ShapeDtypeStruct(acc_shape, F32)
    in_vmem = pl.BlockSpec(memory_space=pltpu.VMEM)
    in_smem = pl.BlockSpec(memory_space=pltpu.SMEM)
    params = pltpu.CompilerParams(vmem_limit_bytes=VMEM_LIMIT)

    def call(body, n_smem, n_vmem, out_shape, scratch, shards):
        return pl.pallas_call(
            body,
            in_specs=[in_smem] * n_smem + [in_vmem] * n_vmem,
            out_shape=out_shape,
            scratch_shapes=scratch + [pltpu.VMEM((blocks, shards * 2 * LANES, 2 * width), BF16)],
            compiler_params=params,
            cost_estimate=pl.CostEstimate(
                flops=shards * tile_count * order_b * 256 * 256 * 8,
                bytes_accessed=shards * tile_count * order_b * 256 * 2,
                transcendentals=0,
            ),
        )

    wanted = box_orbitals.reshape(1, wanted_total)
    asked = wanted
    left, right = own, own
    acc = None
    pick = None
    arrive = n_row * slots
    distance = 1
    for h in range(1, half_ring + 1):
        if h < half_ring:
            next_left = lax.ppermute(left, "row", to_right)
            next_right = lax.ppermute(right, "row", to_left)
        else:
            cut = blocks // 2
            next_left = lax.ppermute(left[:cut], "row", to_right)
            next_right = lax.ppermute(right[cut:], "row", to_left)
        if distance < n_row:
            got = lax.ppermute(asked, "row", [(i, i ^ distance) for i in range(n_row)])
            low = (row // distance) % 2 == 0
            asked = jnp.concatenate(
                [jnp.where(low, asked, got), jnp.where(low, got, asked)], axis=0
            )
            distance *= 2
        elif pick is None:
            pick = pl.pallas_call(
                functools.partial(pick_kernel, rows_chip=rows_chip, slots=slots),
                out_shape=jax.ShapeDtypeStruct((arrive, rows_chip), BF16),
                compiler_params=params,
                cost_estimate=pl.CostEstimate(
                    flops=2 * arrive * wanted_total * 512, bytes_accessed=2 ** 21, transcendentals=0
                ),
            )(asked)
            acc, pick = lax.optimization_barrier((acc, pick))
        if h == 1:
            acc = call(functools.partial(hop_first, n=n_row), 2, 2, acc_out, [], 1)(
                tile_slot, tile_col, own, tiles
            )
        else:
            acc, asked = lax.optimization_barrier((acc, asked))
            acc = call(functools.partial(hop_middle, n=n_row, hop=h - 1), 2, 4, acc_out, [], 2)(
                tile_slot, tile_col, left, right, tiles, acc
            )
        left, right = next_left, next_right

    half_shape = (BR_DEV, 2, half, width)
    dens_shape = (BR_DEV, order_b, width)
    dens, mine, other = call(
        functools.partial(hop_last, n=n_row),
        3,
        4,
        [
            jax.ShapeDtypeStruct(dens_shape, F32),
            jax.ShapeDtypeStruct(half_shape, F32),
            jax.ShapeDtypeStruct(half_shape, F32),
        ],
        [pltpu.VMEM(acc_shape, F32)],
        1,
    )(tile_slot, tile_col, pole_weight, left, right, tiles, acc)

    basis_here = pl.pallas_call(
        functools.partial(basis_kernel, rows_chip=rows_chip, slots=slots),
        out_shape=jax.ShapeDtypeStruct((boxes, arrive, box_basis.shape[2]), BF16),
        compiler_params=params,
        cost_estimate=pl.CostEstimate(
            flops=2 * arrive * wanted_total * box_basis.shape[2], bytes_accessed=2 ** 21, transcendentals=0
        ),
    )(wanted, box_orbitals.reshape(wanted_total, 1), box_basis)
    swap = [(0, 1), (1, 0)]
    dens_other = lax.ppermute(dens, "col", swap)
    inverse_other = lax.ppermute(other, "col", swap)
    send = pl.pallas_call(
        select_kernel,
        out_shape=jax.ShapeDtypeStruct((arrive, width), BF16),
        compiler_params=params,
    )(pick, dens, dens_other)
    arrived = lax.all_to_all(send, "row", 0, 0, tiled=True)
    density = pl.pallas_call(
        density_kernel,
        out_shape=jax.ShapeDtypeStruct((boxes, box_basis.shape[2]), F32),
        compiler_params=params,
    )(arrived, basis_here, supernode_basis)
    return mine + inverse_other, density


def solution(mesh):
    return jax.shard_map(
        functools.partial(local, mesh.shape["row"]),
        mesh=mesh,
        in_specs=(
            P(("pole", "col"), None, None, "row", None),
            P(("pole", "row", "col"), None, None, None),
            P(("pole", "row", "col")),
            P(("pole", "row", "col")),
            P("pole"),
            P(("pole", "row", "col"), None),
            P(("pole", "row", "col"), None, None),
            P(("pole", "row", "col"), None, None),
        ),
        out_specs=(P(("pole", "row"), None, "col", None), P(("pole", "row", "col"), None)),
        check_vma=False,
    )
```

time: 87.1 us -> 70 us (0.80)
  Pallas kernels: 48.3 us -> 17.2 us
  local copies, waits for them, and re-layouts: 2.62 us -> 11.8 us
  waiting for transfers between devices: 8.39 us -> 17.4 us
  other arithmetic: 6.29 us -> 1.96 us
  starting transfers between devices: 19.5 us -> 20.4 us
    pallas_call x5, Pallas kernels: 44 us -> 13 us  [the longest x3 8.35 us: local(): call(functools.partial(hop_middle, n=n_row, hop=h - 1), 2, 4, acc_out, []...]
    unnamed x12 -> x30, local copies, waits for them, and re-layouts: 2.6 us -> 11.7 us
    ppermute x3, waiting for transfers between devices: 0.01 us -> 7.51 us  [local(): next_left = lax.ppermute(left, 'row', to_right)]
    ppermute x3, starting transfers between devices: 4.71 us -> 1.51 us  [local(): next_left = lax.ppermute(left, 'row', to_right)]
    ppermute x3, starting transfers between devices: 2.48 us -> 4.62 us  [local(): next_right = lax.ppermute(right, 'row', to_left)]
    reduce_sum x2 -> x0, other arithmetic: 2.13 us -> none  [the longest x1 1.29 us: local(): jnp.sum(jnp.where(table == row, jnp.arange(n_row, dtype=jnp.int32), 0))]
    ppermute x3, starting transfers between devices: 6.25 us -> 7.89 us  [local(): got = lax.ppermute(asked, 'row', [(i, i ^ distance) for i in range(n_row)])]
    ppermute x1, waiting for transfers between devices: 0.01 us -> 1.42 us  [local(): dens_other = lax.ppermute(dens, 'col', swap)]
  transfers between devices with their start and end apart: 14 -> 14, of which waited for: 2 -> 7; matrix products, arithmetic and copies ran while one was open for 8% -> 3% of each run, Pallas kernels for 55% -> 19%
where the time goes in v2:
time: 70 us; the launch traced here: 69.6 us
  starting transfers between devices  20.4 us (29%)
  waiting for transfers between devices  17.4 us (25%)
  Pallas kernels  17.2 us (25%)
  local copies, waits for them, and re-layouts  11.8 us (17%)
  other arithmetic  1.96 us (3%)
  between operations  0.83 us (1%)
    unnamed x30, local copies, waits for them, and re-layouts  11.7 us
    pallas_call x3, Pallas kernels, local(): call(functools.partial(hop_middle, n=n_row, hop=h - 1), 2, 4, acc_out, []...  8.35 us
    ppermute x3, starting transfers between devices, local(): got = lax.ppermute(asked, 'row', [(i, i ^ distance) for i in range(n_row)])  7.89 us
    ppermute x3, waiting for transfers between devices, local(): next_left = lax.ppermute(left, 'row', to_right)  7.51 us
    all_to_all x1, waiting for transfers between devices, local(): arrived = lax.all_to_all(send, 'row', 0, 0, tiled=True)  6.13 us
    ppermute x3, starting transfers between devices, local(): next_right = lax.ppermute(right, 'row', to_left)  4.62 us
    all_to_all x1, starting transfers between devices, local(): arrived = lax.all_to_all(send, 'row', 0, 0, tiled=True)  3.74 us
    pallas_call x1, Pallas kernels, local(): call(functools.partial(hop_last, n=n_row), 3, 4, [jax.ShapeDtypeStruct(de...  2.84 us
  transfers between devices with their start and end apart: 14, of which 7 were waited for; matrix products, arithmetic and copies ran while one was open for 3% of the time, Pallas kernels for 19%

profile of v2, /device:TPU:0, one launch (start us, length us, event | category | flops | bytes accessed | tf_op | source)
XLA Modules:
  0.0 69.6 jit_solution(3539933933910445756)
XLA Ops:
  0.6 0.7 copy.11
  1.3 3.0 %collective-permute-start.8 = (s32[1,512]{1,0:T(1,128)S(1)}, s32[1,512]{1,0:T(1,128)S(1)}, u32[]{:S(2)}, u32[]{:S(2)}) collective-permute-start(s32[1,512]{1,0:T(1,128)S(1)} %bitcast.15), channel_id=1, source_target_pairs={{0,2},{2,0},{4,6},{6,4},{8,10},{10,8},{12,14},{14,12},{1,3},{3,1},... | collective-permute-start | bytes 6152 | tf_op jit(solution)/shard_map/ppermute | solution.py:190
  4.3 1.6 %collective-permute-done.8 = s32[1,512]{1,0:T(1,128)S(1)} collective-permute-done((s32[1,512]{1,0:T(1,128)S(1)}, s32[1,512]{1,0:T(1,128)S(1)}, u32[]{:S(2)}, u32[]{:S(2)}) %collective-permute-start.8) | collective-permute-done | bytes 2080 | tf_op jit(solution)/shard_map/ppermute | solution.py:190
  5.9 2.1 %collective-permute-start.9 = (s32[2,512]{1,0:T(2,128)S(1)}, s32[2,512]{1,0:T(2,128)S(1)}, u32[]{:S(2)}, u32[]{:S(2)}) collective-permute-start(s32[2,512]{1,0:T(2,128)S(1)} %pad_add_fusion.2), channel_id=1, source_target_pairs={{0,4},{2,6},{4,0},{6,2},{8,12},{10,14},{12,8},{14,10},{1,5},{3,7},... | collective-permute-start | bytes 12296 | tf_op jit(solution)/shard_map/ppermute | solution.py:190
  8.0 4.3 %copy-done = bf16[11,2,512,512]{3,2,1,0:T(8,128)(2,1)S(1)} copy-done((bf16[11,2,512,512]{3,2,1,0:T(8,128)(2,1)S(1)}, bf16[11,2,512,512]{3,2,1,0:T(8,128)(2,1)}, u32[]{:S(2)}) %copy-start) | copy-done | bytes 11534360
  12.3 0.9 %copy-done.6 = bf16[1,8,2,64,128]{4,3,2,1,0:T(8,128)(2,1)S(1)} copy-done((bf16[1,8,2,64,128]{4,3,2,1,0:T(8,128)(2,1)S(1)}, bf16[1,8,2,64,128]{4,3,2,1,0:T(8,128)(2,1)}, u32[]{:S(2)}) %copy-start.6) | copy-done | bytes 262168
  13.2 0.7 copy-done.9
  13.9 0.7 copy-done.11
  14.6 1.8 %shard_map.95.start = f32[2,512,256]{2,1,0:T(8,128)S(1)} custom-call(s32[11]{0:T(128)S(1)} %copy-done.9, s32[11]{0:T(128)S(1)} %copy-done.11, bf16[8,2,64,128]{3,2,1,0:T(8,128)(2,1)S(1)} %bitcast.12, bf16[11,2,512,512]{3,2,1,0:T(8,128)(2,1)S(1)} %copy-done), custom_call_target="tpu_custom_call" | custom-call | flops 2952790016 | bytes 2883584 | tf_op jit(solution)/shard_map/pallas_call | solution.py:207
  16.4 0.0 collective-permute-done.9
  16.4 2.8 %collective-permute-start.10 = (s32[4,512]{1,0:T(4,128)S(1)}, s32[4,512]{1,0:T(4,128)S(1)}, u32[]{:S(2)}, u32[]{:S(2)}) collective-permute-start(s32[4,512]{1,0:T(4,128)S(1)} %pad_add_fusion.1), channel_id=1, source_target_pairs={{0,8},{2,10},{4,12},{6,14},{8,0},{10,2},{12,4},{14,6},{1,9},{3,11}... | collective-permute-start | bytes 24584 | tf_op jit(solution)/shard_map/ppermute | solution.py:190
  19.2 0.5 collective-permute-start
  19.6 1.6 %collective-permute-start.4 = (bf16[8,2,64,128]{3,2,1,0:T(8,128)(2,1)S(1)}, bf16[8,2,64,128]{3,2,1,0:T(8,128)(2,1)S(1)}, u32[]{:S(2)}, u32[]{:S(2)}) collective-permute-start(bf16[8,2,64,128]{3,2,1,0:T(8,128)(2,1)S(1)} %bitcast.14), channel_id=1, source_target_pairs={{4,0},{8,4},{12,8},{14,12},{10,14},{6,10},{2,6},{0,2},{5,1},{9,5},... | collective-permute-start | bytes 786440 | tf_op jit(solution)/shard_map/ppermute | solution.py:184
  21.2 0.0 collective-permute-done.10
  21.2 4.7 %collective-permute-done.from_left = bf16[8,2,64,128]{3,2,1,0:T(8,128)(2,1)S(1)} collective-permute-done((bf16[8,2,64,128]{3,2,1,0:T(8,128)(2,1)S(1)}, bf16[8,2,64,128]{3,2,1,0:T(8,128)(2,1)S(1)}, u32[]{:S(2)}, u32[]{:S(2)}) %collective-permute-start) | collective-permute-done | bytes 262176 | tf_op jit(solution)/shard_map/ppermute | solution.py:183
  25.9 0.5 collective-permute-start.1
  26.4 0.0 collective-permute-done.4.from_right
  26.4 1.5 %collective-permute-start.5 = (bf16[8,2,64,128]{3,2,1,0:T(8,128)(2,1)S(1)}, bf16[8,2,64,128]{3,2,1,0:T(8,128)(2,1)S(1)}, u32[]{:S(2)}, u32[]{:S(2)}) collective-permute-start(bf16[8,2,64,128]{3,2,1,0:T(8,128)(2,1)S(1)} %collective-permute-done.4.from_right), channel_id=1, source_target_pairs={{4,0},{8,4},{12,8},{14,12},{10,14},{6,10},{2,6},{0,2},{5,1},{9,5},... | collective-permute-start | bytes 786440 | tf_op jit(solution)/shard_map/ppermute | solution.py:184
  28.0 4.3 %copy-done.1 = bf16[11,2,512,512]{3,2,1,0:T(8,128)(2,1)S(1)} copy-done((bf16[11,2,512,512]{3,2,1,0:T(8,128)(2,1)S(1)}, bf16[11,2,512,512]{3,2,1,0:T(8,128)(2,1)}, u32[]{:S(2)}) %copy-start.1) | copy-done | bytes 11534360
  32.2 2.8 %shard_map.96.start = f32[2,512,256]{2,1,0:T(8,128)S(1)} custom-call(s32[11]{0:T(128)S(1)} %copy-done.10, s32[11]{0:T(128)S(1)} %copy-done.12, bf16[8,2,64,128]{3,2,1,0:T(8,128)(2,1)S(1)} %collective-permute-done.from_left, bf16[8,2,64,128]{3,2,1,0:T(8,128)(2,1)S(1)} %collective-permute-done.4.from_right, bf16[11,2,512,512]{3,2,1,0:T(8,128)(2,1)S(1)} %copy-done.1, ...), custom_call_target="tpu_custom_call" | custom-call | flops 5905580032 | bytes 5767168 | tf_op jit(solution)/shard_map/pallas_call | solution.py:212
  35.0 0.8 %shard_map.98.pick = bf16[1024,1024]{1,0:T(8,128)(2,1)S(1)} custom-call(s32[8,512]{1,0:T(8,128)S(1)} %pad_add_fusion.wanted), custom_call_target="tpu_custom_call" | custom-call | flops 536870912 | bytes 2097152 | tf_op jit(solution)/shard_map/pallas_call | solution.py:197
  35.9 0.0 collective-permute-done.1.from_left
  35.9 0.6 collective-permute-start.2
  36.4 0.0 collective-permute-done.5.from_right
  36.4 1.5 %collective-permute-start.6 = (bf16[8,2,64,128]{3,2,1,0:T(8,128)(2,1)S(1)}, bf16[8,2,64,128]{3,2,1,0:T(8,128)(2,1)S(1)}, u32[]{:S(2)}, u32[]{:S(2)}) collective-permute-start(bf16[8,2,64,128]{3,2,1,0:T(8,128)(2,1)S(1)} %collective-permute-done.5.from_right), channel_id=1, source_target_pairs={{4,0},{8,4},{12,8},{14,12},{10,14},{6,10},{2,6},{0,2},{5,1},{9,5},... | collective-permute-start | bytes 786440 | tf_op jit(solution)/shard_map/ppermute | solution.py:184
  38.0 2.9 %shard_map.97.start = f32[2,512,256]{2,1,0:T(8,128)S(1)} custom-call(s32[11]{0:T(128)S(1)} %copy-done.10, s32[11]{0:T(128)S(1)} %copy-done.12, bf16[8,2,64,128]{3,2,1,0:T(8,128)(2,1)S(1)} %collective-permute-done.1.from_left, bf16[8,2,64,128]{3,2,1,0:T(8,128)(2,1)S(1)} %collective-permute-done.5.from_right, bf16[11,2,512,512]{3,2,1,0:T(8,128)(2,1)S(1)} %copy-done.2, ...), custom_call_target="tpu_custom_call" | custom-call | flops 5905580032 | bytes 5767168 | tf_op jit(solution)/shard_map/pallas_call | solution.py:212
  40.9 2.8 %collective-permute-done.2.from_left = bf16[8,2,64,128]{3,2,1,0:T(8,128)(2,1)S(1)} collective-permute-done((bf16[8,2,64,128]{3,2,1,0:T(8,128)(2,1)S(1)}, bf16[8,2,64,128]{3,2,1,0:T(8,128)(2,1)S(1)}, u32[]{:S(2)}, u32[]{:S(2)}) %collective-permute-start.2) | collective-permute-done | bytes 262176 | tf_op jit(solution)/shard_map/ppermute | solution.py:183
  43.7 0.6 collective-permute-start.3
  44.3 0.0 collective-permute-done.6.from_right
  44.3 0.0 copy-start.13
  44.3 1.6 %collective-permute-start.7 = (bf16[4,2,64,128]{3,2,1,0:T(8,128)(2,1)S(1)}, bf16[4,2,64,128]{3,2,1,0:T(8,128)(2,1)S(1)}, u32[]{:S(2)}, u32[]{:S(2)}) collective-permute-start(bf16[4,2,64,128]{3,2,1,0:T(8,128)(2,1)S(1)} %slice.9), channel_id=1, source_target_pairs={{4,0},{8,4},{12,8},{14,12},{10,14},{6,10},{2,6},{0,2},{5,1},{9,5},... | collective-permute-start | bytes 393224 | tf_op jit(solution)/shard_map/ppermute | solution.py:188
  45.9 2.6 %shard_map.99.start = f32[2,512,256]{2,1,0:T(8,128)S(1)} custom-call(s32[11]{0:T(128)S(1)} %copy-done.10, s32[11]{0:T(128)S(1)} %copy-done.12, bf16[8,2,64,128]{3,2,1,0:T(8,128)(2,1)S(1)} %collective-permute-done.2.from_left, bf16[8,2,64,128]{3,2,1,0:T(8,128)(2,1)S(1)} %collective-permute-done.6.from_right, bf16[11,2,512,512]{3,2,1,0:T(8,128)(2,1)S(1)} %copy-done.2, ...), custom_call_target="tpu_custom_call" | custom-call | flops 5905580032 | bytes 5767168 | tf_op jit(solution)/shard_map/pallas_call | solution.py:212
  48.5 0.2 collective-permute-done.3.low
  48.7 0.6 collective-permute-done.7.high
  49.3 2.8 %shard_map.100 = (f32[2,512,128]{2,1,0:T(8,128)S(1)}, f32[2,2,256,128]{3,2,1,0:T(8,128)S(1)}, f32[2,2,256,128]{3,2,1,0:T(8,128)}) custom-call(s32[11]{0:T(128)S(1)} %copy-done.10, s32[11]{0:T(128)S(1)} %copy-done.12, f32[2]{0:T(128)S(1)} %copy-done.13, bf16[4,2,64,128]{3,2,1,0:T(8,128)(2,1)S(1)} %collective-permute-done.3.low, ...), custom_call_target="tpu_custom_call" | custom-call | flops 2952790016 | bytes 2883584 | tf_op jit(solution)/shard_map/pallas_call | solution.py:219
  52.2 0.0 collective-permute-start.12
  52.2 0.5 collective-permute-start.11
  52.7 1.4 %collective-permute-done.12.theirs = f32[2,512,128]{2,1,0:T(8,128)S(1)} collective-permute-done((f32[2,512,128]{2,1,0:T(8,128)S(1)}, f32[2,512,128]{2,1,0:T(8,128)S(1)}, u32[]{:S(2)}, u32[]{:S(2)}) %collective-permute-start.12) | collective-permute-done | bytes 524320 | tf_op jit(solution)/shard_map/ppermute | solution.py:241
  54.1 1.4 %shard_map.101 = bf16[1024,128]{1,0:T(8,128)(2,1)} custom-call(bf16[1024,1024]{1,0:T(8,128)(2,1)S(1)} %shard_map.98.pick, f32[2,512,128]{2,1,0:T(8,128)S(1)} %get-tuple-element.21.mine, f32[2,512,128]{2,1,0:T(8,128)S(1)} %collective-permute-done.12.theirs), custom_call_target="tpu_custom_call" | custom-call | tf_op jit(solution)/shard_map/pallas_call | solution.py:243
  55.5 3.7 %all-to-all-start = ((bf16[8,128,128]{2,1,0:T(8,128)(2,1)}), bf16[8,128,128]{2,1,0:T(8,128)(2,1)S(1)}, u32[]{:S(2)}, u32[]{:S(2)}) async-start(bf16[8,128,128]{2,1,0:T(8,128)(2,1)} %bitcast.1), calls=%async_computation | async-start | bytes 524288 | tf_op jit(solution)/shard_map/all_to_all | solution.py:248
  59.3 0.1 copy.13
  59.5 0.0 copy-start.8
  59.5 0.9 %shard_map.102.basis = bf16[2,1024,512]{2,1,0:T(8,128)(2,1)S(1)} custom-call(s32[1,512]{1,0:T(1,128)S(1)} %bitcast.18, s32[512,1]{1,0:T(8,128)S(1)} %bitcast.11, bf16[2,256,512]{2,1,0:T(8,128)(2,1)S(1)} %copy-done.3), custom_call_target="tpu_custom_call" | custom-call | flops 536870912 | bytes 2097152 | tf_op jit(solution)/shard_map/pallas_call | solution.py:232
  60.4 0.0 collective-permute-done.11
  60.4 0.1 copy-done.5
  60.5 1.9 %add.19 = f32[2,2,256,128]{3,2,1,0:T(8,128)} add(f32[2,2,256,128]{3,2,1,0:T(8,128)S(1)} %copy-done.5, f32[2,2,256,128]{3,2,1,0:T(8,128)} %collective-permute-done.11) | non-fusion elementwise | flops 131072 | bytes 1572864 | tf_op jit(solution)/shard_map/add | solution.py:254
  62.4 6.1 %all-to-all-done = bf16[8,128,128]{2,1,0:T(8,128)(2,1)S(1)} async-done(((bf16[8,128,128]{2,1,0:T(8,128)(2,1)}), bf16[8,128,128]{2,1,0:T(8,128)(2,1)S(1)}, u32[]{:S(2)}, u32[]{:S(2)}) %all-to-all-start) | async-done | bytes 262176 | tf_op jit(solution)/shard_map/all_to_all | solution.py:248
  68.5 1.1 %shard_map.103 = f32[2,512]{1,0:T(2,128)} custom-call(bf16[1024,128]{1,0:T(8,128)(2,1)S(1)} %bitcast.10, bf16[2,1024,512]{2,1,0:T(8,128)(2,1)S(1)} %shard_map.102.basis, bf16[2,128,512]{2,1,0:T(8,128)(2,1)S(1)} %copy-done.8), custom_call_target="tpu_custom_call" | custom-call | tf_op jit(solution)/shard_map/pallas_call | solution.py:249
  (28 shorter events, 0.1 us)
Async XLA Ops:
  1.3 4.5 %collective-permute-start.8 = (s32[1,512]{1,0:T(1,128)S(1)}, s32[1,512]{1,0:T(1,128)S(1)}, u32[]{:S(2)}, u32[]{:S(2)}) collective-permute-start(s32[1,512]{1,0:T(1,128)S(1)} %bitcast.15), channel_id=1, source_target_pairs={{0,2},{2,0},{4,6},{6,4},{8,10},{10,8},{12,14},{14,12},{1,3},{3,1},... | collective-permute-start | bytes 6152 | tf_op jit(solution)/shard_map/ppermute | solution.py:190
  5.9 10.5 %collective-permute-start.9 = (s32[2,512]{1,0:T(2,128)S(1)}, s32[2,512]{1,0:T(2,128)S(1)}, u32[]{:S(2)}, u32[]{:S(2)}) collective-permute-start(s32[2,512]{1,0:T(2,128)S(1)} %pad_add_fusion.2), channel_id=1, source_target_pairs={{0,4},{2,6},{4,0},{6,2},{8,12},{10,14},{12,8},{14,10},{1,5},{3,7},... | collective-permute-start | bytes 12296 | tf_op jit(solution)/shard_map/ppermute | solution.py:190
  8.0 4.3 %copy-start = (bf16[11,2,512,512]{3,2,1,0:T(8,128)(2,1)S(1)}, bf16[11,2,512,512]{3,2,1,0:T(8,128)(2,1)}, u32[]{:S(2)}) copy-start(bf16[11,2,512,512]{3,2,1,0:T(8,128)(2,1)} %tiles.9) | copy-start | bytes 34603012
  12.3 0.9 %copy-start.6 = (bf16[1,8,2,64,128]{4,3,2,1,0:T(8,128)(2,1)S(1)}, bf16[1,8,2,64,128]{4,3,2,1,0:T(8,128)(2,1)}, u32[]{:S(2)}) copy-start(bf16[1,8,2,64,128]{4,3,2,1,0:T(8,128)(2,1)} %param.8) | copy-start | bytes 786436
  13.2 0.7 copy-start.9
  13.9 0.7 copy-start.11
  14.5 4.6 %copy-start.7 = (bf16[1,8,2,64,128]{4,3,2,1,0:T(8,128)(2,1)S(1)}, bf16[1,8,2,64,128]{4,3,2,1,0:T(8,128)(2,1)}, u32[]{:S(2)}) copy-start(bf16[1,8,2,64,128]{4,3,2,1,0:T(8,128)(2,1)} %param.8) | copy-start | bytes 786436
  14.5 13.4 %copy-start.10 = (s32[11]{0:T(128)S(1)}, s32[11]{0:T(128)}, u32[]{:S(2)}) copy-start(s32[11]{0:T(128)} %slots.9) | copy-start | bytes 136
  14.6 13.4 %copy-start.12 = (s32[11]{0:T(128)S(1)}, s32[11]{0:T(128)}, u32[]{:S(2)}) copy-start(s32[11]{0:T(128)} %cols.9) | copy-start | bytes 136
  16.4 4.8 %collective-permute-start.10 = (s32[4,512]{1,0:T(4,128)S(1)}, s32[4,512]{1,0:T(4,128)S(1)}, u32[]{:S(2)}, u32[]{:S(2)}) collective-permute-start(s32[4,512]{1,0:T(4,128)S(1)} %pad_add_fusion.1), channel_id=1, source_target_pairs={{0,8},{2,10},{4,12},{6,14},{8,0},{10,2},{12,4},{14,6},{1,9},{3,11}... | collective-permute-start | bytes 24584 | tf_op jit(solution)/shard_map/ppermute | solution.py:190
  19.2 6.7 %collective-permute-start = (bf16[8,2,64,128]{3,2,1,0:T(8,128)(2,1)S(1)}, bf16[8,2,64,128]{3,2,1,0:T(8,128)(2,1)S(1)}, u32[]{:S(2)}, u32[]{:S(2)}) collective-permute-start(bf16[8,2,64,128]{3,2,1,0:T(8,128)(2,1)S(1)} %bitcast.13), channel_id=1, source_target_pairs={{0,4},{4,8},{8,12},{12,14},{14,10},{10,6},{6,2},{2,0},{1,5},{5,9},... | collective-permute-start | bytes 786440 | tf_op jit(solution)/shard_map/ppermute | solution.py:183
  19.6 6.8 %collective-permute-start.4 = (bf16[8,2,64,128]{3,2,1,0:T(8,128)(2,1)S(1)}, bf16[8,2,64,128]{3,2,1,0:T(8,128)(2,1)S(1)}, u32[]{:S(2)}, u32[]{:S(2)}) collective-permute-start(bf16[8,2,64,128]{3,2,1,0:T(8,128)(2,1)S(1)} %bitcast.14), channel_id=1, source_target_pairs={{4,0},{8,4},{12,8},{14,12},{10,14},{6,10},{2,6},{0,2},{5,1},{9,5},... | collective-permute-start | bytes 786440 | tf_op jit(solution)/shard_map/ppermute | solution.py:184
  25.9 9.9 %collective-permute-start.1 = (bf16[8,2,64,128]{3,2,1,0:T(8,128)(2,1)S(1)}, bf16[8,2,64,128]{3,2,1,0:T(8,128)(2,1)S(1)}, u32[]{:S(2)}, u32[]{:S(2)}) collective-permute-start(bf16[8,2,64,128]{3,2,1,0:T(8,128)(2,1)S(1)} %collective-permute-done.from_left), channel_id=1, source_target_pairs={{0,4},{4,8},{8,12},{12,14},{14,10},{10,6},{6,2},{2,0},{1,5},{5,9},... | collective-permute-start | bytes 786440 | tf_op jit(solution)/shard_map/ppermute | solution.py:183
  26.4 10.0 %collective-permute-start.5 = (bf16[8,2,64,128]{3,2,1,0:T(8,128)(2,1)S(1)}, bf16[8,2,64,128]{3,2,1,0:T(8,128)(2,1)S(1)}, u32[]{:S(2)}, u32[]{:S(2)}) collective-permute-start(bf16[8,2,64,128]{3,2,1,0:T(8,128)(2,1)S(1)} %collective-permute-done.4.from_right), channel_id=1, source_target_pairs={{4,0},{8,4},{12,8},{14,12},{10,14},{6,10},{2,6},{0,2},{5,1},{9,5},... | collective-permute-start | bytes 786440 | tf_op jit(solution)/shard_map/ppermute | solution.py:184
  28.0 4.3 %copy-start.1 = (bf16[11,2,512,512]{3,2,1,0:T(8,128)(2,1)S(1)}, bf16[11,2,512,512]{3,2,1,0:T(8,128)(2,1)}, u32[]{:S(2)}) copy-start(bf16[11,2,512,512]{3,2,1,0:T(8,128)(2,1)} %tiles.9) | copy-start | bytes 34603012
  32.2 5.7 %copy-start.2 = (bf16[11,2,512,512]{3,2,1,0:T(8,128)(2,1)S(1)}, bf16[11,2,512,512]{3,2,1,0:T(8,128)(2,1)}, u32[]{:S(2)}) copy-start(bf16[11,2,512,512]{3,2,1,0:T(8,128)(2,1)} %tiles.9) | copy-start | bytes 34603012
  35.9 7.8 %collective-permute-start.2 = (bf16[8,2,64,128]{3,2,1,0:T(8,128)(2,1)S(1)}, bf16[8,2,64,128]{3,2,1,0:T(8,128)(2,1)S(1)}, u32[]{:S(2)}, u32[]{:S(2)}) collective-permute-start(bf16[8,2,64,128]{3,2,1,0:T(8,128)(2,1)S(1)} %collective-permute-done.1.from_left), channel_id=1, source_target_pairs={{0,4},{4,8},{8,12},{12,14},{14,10},{10,6},{6,2},{2,0},{1,5},{5,9},... | collective-permute-start | bytes 786440 | tf_op jit(solution)/shard_map/ppermute | solution.py:183
  36.4 7.8 %collective-permute-start.6 = (bf16[8,2,64,128]{3,2,1,0:T(8,128)(2,1)S(1)}, bf16[8,2,64,128]{3,2,1,0:T(8,128)(2,1)S(1)}, u32[]{:S(2)}, u32[]{:S(2)}) collective-permute-start(bf16[8,2,64,128]{3,2,1,0:T(8,128)(2,1)S(1)} %collective-permute-done.5.from_right), channel_id=1, source_target_pairs={{4,0},{8,4},{12,8},{14,12},{10,14},{6,10},{2,6},{0,2},{5,1},{9,5},... | collective-permute-start | bytes 786440 | tf_op jit(solution)/shard_map/ppermute | solution.py:184
  43.7 5.0 %collective-permute-start.3 = (bf16[4,2,64,128]{3,2,1,0:T(8,128)(2,1)S(1)}, bf16[4,2,64,128]{3,2,1,0:T(8,128)(2,1)S(1)}, u32[]{:S(2)}, u32[]{:S(2)}) collective-permute-start(bf16[4,2,64,128]{3,2,1,0:T(8,128)(2,1)S(1)} %slice.8), channel_id=1, source_target_pairs={{0,4},{4,8},{8,12},{12,14},{14,10},{10,6},{6,2},{2,0},{1,5},{5,9},... | collective-permute-start | bytes 393224 | tf_op jit(solution)/shard_map/ppermute | solution.py:187
  44.3 5.0 %copy-start.13 = (f32[2]{0:T(128)S(1)}, f32[2]{0:T(128)}, u32[]{:S(2)}) copy-start(f32[2]{0:T(128)} %pole_weight.1) | copy-start | bytes 28
  44.3 5.0 %collective-permute-start.7 = (bf16[4,2,64,128]{3,2,1,0:T(8,128)(2,1)S(1)}, bf16[4,2,64,128]{3,2,1,0:T(8,128)(2,1)S(1)}, u32[]{:S(2)}, u32[]{:S(2)}) collective-permute-start(bf16[4,2,64,128]{3,2,1,0:T(8,128)(2,1)S(1)} %slice.9), channel_id=1, source_target_pairs={{4,0},{8,4},{12,8},{14,12},{10,14},{6,10},{2,6},{0,2},{5,1},{9,5},... | collective-permute-start | bytes 393224 | tf_op jit(solution)/shard_map/ppermute | solution.py:188
  52.2 3.4 %copy-start.4 = (f32[2,2,256,128]{3,2,1,0:T(8,128)}, f32[2,2,256,128]{3,2,1,0:T(8,128)S(1)}, u32[]{:S(2)}) copy-start(f32[2,2,256,128]{3,2,1,0:T(8,128)S(1)} %get-tuple-element.18) | copy-start | bytes 1572868
  52.2 1.9 %collective-permute-start.12 = (f32[2,512,128]{2,1,0:T(8,128)S(1)}, f32[2,512,128]{2,1,0:T(8,128)S(1)}, u32[]{:S(2)}, u32[]{:S(2)}) collective-permute-start(f32[2,512,128]{2,1,0:T(8,128)S(1)} %get-tuple-element.21.mine), channel_id=1, source_target_pairs={{0,1},{1,0},{2,3},{3,2},{4,5},{5,4},{6,7},{7,6},{8,9},{9,8},{10,11... | collective-permute-start | bytes 1572872 | tf_op jit(solution)/shard_map/ppermute | solution.py:241
  52.2 7.3 %copy-start.3 = (bf16[2,256,512]{2,1,0:T(8,128)(2,1)S(1)}, bf16[2,256,512]{2,1,0:T(8,128)(2,1)}, u32[]{:S(2)}) copy-start(bf16[2,256,512]{2,1,0:T(8,128)(2,1)} %basis.1) | copy-start | bytes 1572868
  52.2 8.2 %collective-permute-start.11 = (f32[2,2,256,128]{3,2,1,0:T(8,128)}, f32[2,2,256,128]{3,2,1,0:T(8,128)}, u32[]{:S(2)}, u32[]{:S(2)}) collective-permute-start(f32[2,2,256,128]{3,2,1,0:T(8,128)} %get-tuple-element.19), channel_id=1, source_target_pairs={{0,1},{1,0},{2,3},{3,2},{4,5},{5,4},{6,7},{7,6},{8,9},{9,8},{10,11... | collective-permute-start | bytes 1572872 | tf_op jit(solution)/shard_map/ppermute | solution.py:242
  55.5 13.0 %all-to-all-start = ((bf16[8,128,128]{2,1,0:T(8,128)(2,1)}), bf16[8,128,128]{2,1,0:T(8,128)(2,1)S(1)}, u32[]{:S(2)}, u32[]{:S(2)}) async-start(bf16[8,128,128]{2,1,0:T(8,128)(2,1)} %bitcast.1), calls=%async_computation | async-start | bytes 524288 | tf_op jit(solution)/shard_map/all_to_all | solution.py:248
  59.4 1.0 %copy-start.5 = (f32[2,2,256,128]{3,2,1,0:T(8,128)S(1)}, f32[2,2,256,128]{3,2,1,0:T(8,128)}, u32[]{:S(2)}) copy-start(f32[2,2,256,128]{3,2,1,0:T(8,128)} %copy-done.4) | copy-start | bytes 1572868
  59.5 9.1 %copy-start.8 = (bf16[2,128,512]{2,1,0:T(8,128)(2,1)S(1)}, bf16[2,128,512]{2,1,0:T(8,128)(2,1)}, u32[]{:S(2)}) copy-start(bf16[2,128,512]{2,1,0:T(8,128)(2,1)} %supernode.1) | copy-start | bytes 786436

commit v3 on v2

v3 whole, which is shorter than its diff:
```python
import functools

import jax
import jax.numpy as jnp
from jax import lax
from jax.experimental import pallas as pl
from jax.experimental.pallas import tpu as pltpu
from jax.sharding import PartitionSpec as P

BR_DEV = 2
LANES = 128
F32 = jnp.float32
BF16 = jnp.bfloat16
VMEM_LIMIT = 8 * 1024 * 1024


def ring_order(n):
    if n <= 8 and n % 2 == 0:
        return list(range(0, n, 2)) + list(range(n - 1, 0, -2))
    return list(range(n))


def shard_row(n, hop):
    row = lax.axis_index("row")
    if ring_order(n) == list(range(n)):
        return lax.rem(row + hop + n, n)
    at = jnp.where(row % 2 == 0, row // 2, n - 1 - row // 2)
    at = lax.rem(at + hop + n, n)
    return jnp.where(at < n // 2, 2 * at, 2 * (n - 1 - at) + 1)


def digits(rows):
    boxes, orbitals = rows.shape
    pieces = [rows[n:n + 1, c:c + LANES] for n in range(boxes) for c in range(0, orbitals, LANES)]
    lines = [piece // 256 for piece in pieces] + [piece % 256 for piece in pieces]
    pad = -len(lines) % 16
    lines.append(jnp.zeros((pad, LANES), jnp.int32))
    return jnp.concatenate(lines, axis=0).astype(F32).astype(BF16)


def undigits(lines, total):
    count = total // LANES
    lines = lines.astype(F32)
    whole = lines[:count] * 256.0 + lines[count:2 * count]
    return jnp.concatenate([whole[i:i + 1] for i in range(count)], axis=1)


def pack_kernel(panel, wanted, out, sem):
    rows = panel.shape[0]
    copy = pltpu.make_async_copy(panel, out.at[pl.ds(0, rows)], sem)
    copy.start()
    out[rows:, :] = digits(wanted[...])
    copy.wait()


def place(part, block, depth, first):
    reps = LANES // depth
    row = lax.broadcasted_iota(jnp.int32, (LANES, part.shape[1]), 0)
    inside = (row // depth) == first
    spread = []
    for p in range(2):
        rows = part[(2 * block + p) * depth:(2 * block + p + 1) * depth, :].astype(F32)
        spread.append(jnp.where(inside, jnp.concatenate([rows] * reps, axis=0), 0.0))
    upper = jnp.concatenate([spread[0], spread[1]], axis=1)
    lower = jnp.concatenate([-spread[1], spread[0]], axis=1)
    return jnp.concatenate([upper, lower], axis=0).astype(BF16)


def accumulate(slots, cols, tiles, shards, acc, weights):
    blocks = weights.shape[0]
    starts = []
    for s, (row, depth, parts) in enumerate(shards):
        reps = LANES // depth
        starts.append(pl.multiple_of(row // reps * LANES, LANES))
        share = blocks // len(parts)
        for b in range(blocks):
            weights[b, s * 2 * LANES:(s + 1) * 2 * LANES, :] = place(
                parts[b // share], b % share, depth, row % reps
            )
    for t in range(tiles.shape[0]):
        left = jnp.concatenate(
            [tiles[t, p, :, pl.ds(start, LANES)] for start in starts for p in range(2)], axis=1
        )
        acc[slots[t]] += jnp.dot(left, weights[cols[t]], preferred_element_type=F32)


def hop_first(slots, cols, own, tiles, out, weights, *, n, depth):
    out[...] = jnp.zeros_like(out)
    accumulate(slots, cols, tiles, [(shard_row(n, 0), depth, [own])], out, weights)


def hop_middle(slots, cols, from_left, from_right, tiles, start, out, weights, *, n, depth, hop):
    del start
    shards = [
        (shard_row(n, -hop), depth, [from_left]), (shard_row(n, hop), depth, [from_right])
    ]
    accumulate(slots, cols, tiles, shards, out, weights)


def hop_last(
    slots, cols, pole_weight, low, high, tiles, start, dens, mine, other, acc, weights, *, n, depth
):
    acc[...] = start[...]
    accumulate(slots, cols, tiles, [(shard_row(n, n // 2), depth, [low, high])], acc, weights)
    col = lax.axis_index("col")
    half = mine.shape[2]
    width = mine.shape[3]
    for slot in range(acc.shape[0]):
        real = -acc[slot, :, :width]
        imag = -acc[slot, :, width:]
        dens[slot] = pole_weight[0] * imag + pole_weight[1] * real
        for p in range(2):
            cut = slice(p * width, (p + 1) * width)
            mine[slot, p] = -acc[slot, pl.ds(pl.multiple_of(col * half, half), half), cut]
            other[slot, p] = -acc[slot, pl.ds(pl.multiple_of((1 - col) * half, half), half), cut]


def earlier(total):
    first = lax.broadcasted_iota(jnp.int32, (total, total), 0)
    second = lax.broadcasted_iota(jnp.int32, (total, total), 1)
    return (first < second).astype(F32).astype(BF16)


def basis_kernel(wanted, basis, out, *, n, rows_chip, slots):
    boxes, orbitals, _ = basis.shape
    total = boxes * orbitals
    rows = wanted[...]
    asked = jnp.concatenate([rows[b:b + 1] for b in range(boxes)], axis=1)
    source = asked // rows_chip
    marks = (lax.broadcasted_iota(jnp.int32, (n, total), 0) == source).astype(F32)
    counts = jnp.dot(marks.astype(BF16), earlier(total), preferred_element_type=F32)
    rank = jnp.sum(marks * counts, axis=0, keepdims=True).astype(jnp.int32)
    slot = source * slots + rank
    index = lax.broadcasted_iota(jnp.int32, (out.shape[1], orbitals), 0)
    for b in range(boxes):
        pick = (index == slot[:, b * orbitals:(b + 1) * orbitals]).astype(F32).astype(BF16)
        out[b] = jnp.dot(pick, basis[b], preferred_element_type=F32).astype(BF16)


def pick_kernel(*refs, n, hops, total, rows_chip, slots):
    *shards, out = refs
    lines = -(-2 * total // (16 * LANES)) * 16
    asked = jnp.concatenate(
        [undigits(ref[ref.shape[0] - lines:, :], total) for ref in shards], axis=0
    ).astype(jnp.int32)
    here = (asked // rows_chip) == lax.axis_index("row")
    local = (asked % rows_chip).astype(F32)
    rank = jnp.dot(
        here.astype(F32).astype(BF16), earlier(total), preferred_element_type=F32
    ).astype(jnp.int32)
    rank = jnp.where(here, rank, -1)
    index = lax.broadcasted_iota(jnp.int32, (slots, total), 0)
    lane = lax.broadcasted_iota(jnp.int32, (slots, rows_chip), 1)
    for d, hop in enumerate(hops):
        chosen = jnp.where(index == rank[d:d + 1], local[d:d + 1], 0.0)
        row = jnp.sum(chosen, axis=1, keepdims=True).astype(jnp.int32)
        at = pl.multiple_of(shard_row(n, hop) * slots, slots)
        out[pl.ds(at, slots), :] = (lane == row).astype(F32).astype(BF16)


def select_kernel(pick, mine, theirs, out):
    rows = pick.shape[1]
    total = (mine[...] + theirs[...]).reshape(rows, mine.shape[2]).astype(BF16)
    out[...] = jnp.dot(pick[...], total, preferred_element_type=F32).astype(BF16)


def density_kernel(arrived, basis, supernode, out):
    for n in range(basis.shape[0]):
        projected = lax.dot_general(
            arrived[...], basis[n], (((0,), (0,)), ((), ())), preferred_element_type=F32
        )
        out[n:n + 1, :] = jnp.sum(supernode[n].astype(F32) * projected, axis=0, keepdims=True)


def local(n_row, panel, tiles, tile_slot, tile_col, pole_weight, box_orbitals, box_basis, supernode_basis):
    order = ring_order(n_row)
    half_ring = n_row // 2
    to_right = [(order[i], order[(i + 1) % n_row]) for i in range(n_row)]
    to_left = [(order[(i + 1) % n_row], order[i]) for i in range(n_row)]
    _, blocks, parts, depth, width = panel.shape
    tile_count, _, order_b, _ = tiles.shape
    boxes, orbitals = box_orbitals.shape
    total = boxes * orbitals
    rows_chip = BR_DEV * order_b
    slots = 2 * total // n_row
    arrive = n_row * slots
    half = order_b // 2
    shard_rows = blocks * parts * depth
    lines = -(-2 * total // (16 * LANES)) * 16
    acc_shape = (BR_DEV, order_b, 2 * width)
    acc_out = jax.ShapeDtypeStruct(acc_shape, F32)
    in_vmem = pl.BlockSpec(memory_space=pltpu.VMEM)
    in_smem = pl.BlockSpec(memory_space=pltpu.SMEM)
    in_hbm = pl.BlockSpec(memory_space=pltpu.HBM)
    params = pltpu.CompilerParams(vmem_limit_bytes=VMEM_LIMIT)
    cost = pl.CostEstimate(flops=2 ** 20, bytes_accessed=2 ** 20, transcendentals=0)

    def call(body, in_specs, out_shape, before, shards, aliases={}):
        weights = pltpu.VMEM((blocks, shards * 2 * LANES, 2 * width), BF16)
        return pl.pallas_call(
            functools.partial(body, n=n_row, depth=depth),
            in_specs=in_specs,
            out_specs=jax.tree.map(lambda _: in_vmem, out_shape),
            out_shape=out_shape,
            scratch_shapes=[*before, weights],
            input_output_aliases=aliases,
            compiler_params=params,
            cost_estimate=cost,
        )

    own = pl.pallas_call(
        pack_kernel,
        in_specs=[in_hbm, in_vmem],
        out_specs=in_vmem,
        out_shape=jax.ShapeDtypeStruct((shard_rows + lines, width), BF16),
        scratch_shapes=[pltpu.SemaphoreType.DMA],
        compiler_params=params,
        cost_estimate=cost,
    )(panel.reshape(shard_rows, width), box_orbitals)

    left, right = own, own
    seen, hops = [own], [0]
    acc = None
    for h in range(1, half_ring + 1):
        if h < half_ring:
            next_left = lax.ppermute(left, "row", to_right)
            next_right = lax.ppermute(right, "row", to_left)
        else:
            cut = shard_rows // 2
            next_left = lax.ppermute(left[:cut], "row", to_right)
            next_right = lax.ppermute(right[cut:], "row", to_left)
        if h == 1:
            acc = call(hop_first, [in_smem] * 2 + [in_vmem] * 2, acc_out, [], 1)(
                tile_slot, tile_col, own, tiles
            )
        else:
            acc = call(
                functools.partial(hop_middle, hop=h - 1),
                [in_smem] * 2 + [in_vmem] * 4,
                acc_out,
                [],
                2,
                aliases={5: 0},
            )(tile_slot, tile_col, left, right, tiles, acc)
        left, right, acc = lax.optimization_barrier((next_left, next_right, acc))
        if h < half_ring:
            seen += [left, right]
            hops += [-h, h]
        else:
            seen.append(right)
            hops.append(h)

    half_shape = (BR_DEV, 2, half, width)
    dens_shape = (BR_DEV, order_b, width)
    dens, mine, other = call(
        hop_last,
        [in_smem] * 3 + [in_vmem] * 4,
        [
            jax.ShapeDtypeStruct(dens_shape, F32),
            jax.ShapeDtypeStruct(half_shape, F32),
            jax.ShapeDtypeStruct(half_shape, F32),
        ],
        [pltpu.VMEM(acc_shape, F32)],
        1,
    )(tile_slot, tile_col, pole_weight, left, right, tiles, acc)

    basis_here = pl.pallas_call(
        functools.partial(basis_kernel, n=n_row, rows_chip=rows_chip, slots=slots),
        out_shape=jax.ShapeDtypeStruct((boxes, arrive, box_basis.shape[2]), BF16),
        compiler_params=params,
        cost_estimate=cost,
    )(box_orbitals, box_basis)
    pick = pl.pallas_call(
        functools.partial(
            pick_kernel, n=n_row, hops=hops, total=total, rows_chip=rows_chip, slots=slots
        ),
        out_shape=jax.ShapeDtypeStruct((arrive, rows_chip), BF16),
        compiler_params=params,
        cost_estimate=cost,
    )(*seen)

    swap = [(0, 1), (1, 0)]
    dens_other = lax.ppermute(dens, "col", swap)
    inverse_other = lax.ppermute(other, "col", swap)
    send = pl.pallas_call(
        select_kernel,
        out_shape=jax.ShapeDtypeStruct((arrive, width), BF16),
        compiler_params=params,
    )(pick, dens, dens_other)
    arrived = lax.all_to_all(send, "row", 0, 0, tiled=True)
    density = pl.pallas_call(
        density_kernel,
        out_shape=jax.ShapeDtypeStruct((boxes, box_basis.shape[2]), F32),
        compiler_params=params,
    )(arrived, basis_here, supernode_basis)
    return mine + inverse_other, density


def solution(mesh):
    return jax.shard_map(
        functools.partial(local, mesh.shape["row"]),
        mesh=mesh,
        in_specs=(
            P(("pole", "col"), None, None, "row", None),
            P(("pole", "row", "col"), None, None, None),
            P(("pole", "row", "col")),
            P(("pole", "row", "col")),
            P("pole"),
            P(("pole", "row", "col"), None),
            P(("pole", "row", "col"), None, None),
            P(("pole", "row", "col"), None, None),
        ),
        out_specs=(P(("pole", "row"), None, "col", None), P(("pole", "row", "col"), None)),
        check_vma=False,
    )
```

time: 70 us -> 59.5 us (0.85)
  starting transfers between devices: 20.4 us -> 14.4 us
  local copies, waits for them, and re-layouts: 11.8 us -> 8.21 us
  waiting for transfers between devices: 17.4 us -> 16.6 us
    ppermute x3 -> x0, starting transfers between devices: 7.89 us -> none  [local(): got = lax.ppermute(asked, 'row', [(i, i ^ distance) for i in range(n_row)])]
    ppermute x3, starting transfers between devices: 1.51 us -> 6.26 us  [local(): next_left = lax.ppermute(left, 'row', to_right)]
    ppermute x3, starting transfers between devices: 4.62 us -> 0.87 us  [local(): next_right = lax.ppermute(right, 'row', to_left)]
    ppermute x3, waiting for transfers between devices: 0.01 us -> 3.6 us  [local(): next_right = lax.ppermute(right, 'row', to_left)]
    unnamed x30 -> x24, local copies, waits for them, and re-layouts: 11.7 us -> 8.2 us
    ppermute x3, waiting for transfers between devices: 7.51 us -> 4.56 us  [local(): next_left = lax.ppermute(left, 'row', to_right)]
    ppermute x3 -> x0, waiting for transfers between devices: 1.57 us -> none  [local(): got = lax.ppermute(asked, 'row', [(i, i ^ distance) for i in range(n_row)])]
    ppermute x1, starting transfers between devices: 1.57 us -> 0.63 us  [local(): next_right = lax.ppermute(right[cut:], 'row', to_left)]
  transfers between devices with their start and end apart: 14 -> 11, of which waited for: 7 -> 8; matrix products, arithmetic and copies ran while one was open for 3% -> 3% of each run, Pallas kernels for 19% -> 22%
where the time goes in v3:
time: 59.5 us; the launch traced here: 59 us
  Pallas kernels  17.2 us (29%)
  waiting for transfers between devices  16.6 us (28%)
  starting transfers between devices  14.4 us (24%)
  local copies, waits for them, and re-layouts  8.21 us (14%)
  other arithmetic  1.89 us (3%)
  between operations  0.78 us (1%)
    unnamed x24, local copies, waits for them, and re-layouts  8.2 us
    pallas_call x3, Pallas kernels, local(): call(functools.partial(hop_middle, hop=h - 1), [in_smem] * 2 + [in_vmem]...  8.12 us
    all_to_all x1, waiting for transfers between devices, local(): arrived = lax.all_to_all(send, 'row', 0, 0, tiled=True)  6.44 us
    ppermute x3, starting transfers between devices, local(): next_left = lax.ppermute(left, 'row', to_right)  6.26 us
    all_to_all x1, starting transfers between devices, local(): arrived = lax.all_to_all(send, 'row', 0, 0, tiled=True)  4.58 us
    ppermute x3, waiting for transfers between devices, local(): next_left = lax.ppermute(left, 'row', to_right)  4.56 us
    ppermute x3, waiting for transfers between devices, local(): next_right = lax.ppermute(right, 'row', to_left)  3.6 us
    pallas_call x1, Pallas kernels, local(): call(hop_last, [in_smem] * 3 + [in_vmem] * 4, [jax.ShapeDtypeStruct(dens_...  2.95 us
  transfers between devices with their start and end apart: 11, of which 8 were waited for; matrix products, arithmetic and copies ran while one was open for 3% of the time, Pallas kernels for 22%

profile of v3, /device:TPU:0, one launch (start us, length us, event | category | flops | bytes accessed | tf_op | source)
XLA Modules:
  0.0 59.0 jit_solution(15028318471887570338)
XLA Ops:
  0.6 0.0 copy-start.4
  0.6 0.9 %copy-done.4 = bf16[1,8,2,64,128]{4,3,2,1,0:T(8,128)(2,1)S(1)} copy-done((bf16[1,8,2,64,128]{4,3,2,1,0:T(8,128)(2,1)S(1)}, bf16[1,8,2,64,128]{4,3,2,1,0:T(8,128)(2,1)}, u32[]{:S(2)}) %copy-start.4) | copy-done | bytes 262168
  1.6 0.7 %copy-done.9 = s32[2,256]{1,0:T(2,128)S(1)} copy-done((s32[2,256]{1,0:T(2,128)S(1)}, s32[2,256]{1,0:T(2,128)}, u32[]{:S(2)}) %copy-start.9) | copy-done | bytes 2072
  2.3 3.1 %collective-permute-start = (bf16[1040,128]{1,0:T(8,128)(2,1)S(1)}, bf16[1040,128]{1,0:T(8,128)(2,1)S(1)}, u32[]{:S(2)}, u32[]{:S(2)}) collective-permute-start(bf16[1040,128]{1,0:T(8,128)(2,1)S(1)} %shard_map.95.own.refs_0_), channel_id=1, source_target_pairs={{0,4},{4,8},{8,12},{12,14},{14,10},{10,6},{6,2},{2,0},{1,5},{5,9},... | collective-permute-start | bytes 798728 | tf_op jit(solution)/shard_map/ppermute | solution.py:226
  5.4 0.0 collective-permute-start.1
  5.4 4.3 %copy-done = bf16[11,2,512,512]{3,2,1,0:T(8,128)(2,1)S(1)} copy-done((bf16[11,2,512,512]{3,2,1,0:T(8,128)(2,1)S(1)}, bf16[11,2,512,512]{3,2,1,0:T(8,128)(2,1)}, u32[]{:S(2)}) %copy-start) | copy-done | bytes 11534360
  9.7 0.7 %copy-done.5 = s32[11]{0:T(128)S(1)} copy-done((s32[11]{0:T(128)S(1)}, s32[11]{0:T(128)}, u32[]{:S(2)}) %copy-start.5) | copy-done | bytes 68
  10.3 0.7 %copy-done.7 = s32[11]{0:T(128)S(1)} copy-done((s32[11]{0:T(128)S(1)}, s32[11]{0:T(128)}, u32[]{:S(2)}) %copy-start.7) | copy-done | bytes 68
  11.0 1.9 %shard_map.96.start = f32[2,512,256]{2,1,0:T(8,128)S(1)} custom-call(s32[11]{0:T(128)S(1)} %copy-done.5, s32[11]{0:T(128)S(1)} %copy-done.7, bf16[1040,128]{1,0:T(8,128)(2,1)S(1)} %shard_map.95.own.refs_0_, bf16[11,2,512,512]{3,2,1,0:T(8,128)(2,1)S(1)} %copy-done), custom_call_target="tpu_custom_call" | custom-call | flops 1048576 | bytes 1048576 | tf_op jit(solution)/shard_map/pallas_call | solution.py:233
  12.9 0.0 collective-permute-done.from_left.refs_1_
  12.9 0.3 collective-permute-done.1.from_right.refs_2_
  13.2 1.7 %collective-permute-start.2 = (bf16[1040,128]{1,0:T(8,128)(2,1)S(1)}, bf16[1040,128]{1,0:T(8,128)(2,1)S(1)}, u32[]{:S(2)}, u32[]{:S(2)}) collective-permute-start(bf16[1040,128]{1,0:T(8,128)(2,1)S(1)} %collective-permute-done.from_left.refs_1_), channel_id=1, source_target_pairs={{0,4},{4,8},{8,12},{12,14},{14,10},{10,6},{6,2},{2,0},{1,5},{5,9},... | collective-permute-start | bytes 798728 | tf_op jit(solution)/shard_map/ppermute | solution.py:226
  15.0 0.3 collective-permute-start.3
  15.3 0.0 copy-done.1
  15.3 2.6 %shard_map.97.start = f32[2,512,256]{2,1,0:T(8,128)S(1)} custom-call(s32[11]{0:T(128)S(1)} %copy-done.5, s32[11]{0:T(128)S(1)} %copy-done.7, bf16[1040,128]{1,0:T(8,128)(2,1)S(1)} %collective-permute-done.from_left.refs_1_, bf16[1040,128]{1,0:T(8,128)(2,1)S(1)} %collective-permute-done.1.from_right.refs_2_, ...), custom_call_target="tpu_custom_call", output_to_operand_aliasing={{}: (5, {})} | custom-call | flops 1048576 | bytes 1048576 | tf_op jit(solution)/shard_map/pallas_call | solution.py:237
  17.9 0.0 copy-start.6
  17.9 0.0 copy-start.8
  17.9 2.9 %collective-permute-done.2.from_left.refs_3_ = bf16[1040,128]{1,0:T(8,128)(2,1)S(1)} collective-permute-done((bf16[1040,128]{1,0:T(8,128)(2,1)S(1)}, bf16[1040,128]{1,0:T(8,128)(2,1)S(1)}, u32[]{:S(2)}, u32[]{:S(2)}) %collective-permute-start.2) | collective-permute-done | bytes 266272 | tf_op jit(solution)/shard_map/ppermute | solution.py:226
  20.8 1.5 %collective-permute-done.3.from_right.refs_4_ = bf16[1040,128]{1,0:T(8,128)(2,1)S(1)} collective-permute-done((bf16[1040,128]{1,0:T(8,128)(2,1)S(1)}, bf16[1040,128]{1,0:T(8,128)(2,1)S(1)}, u32[]{:S(2)}, u32[]{:S(2)}) %collective-permute-start.3) | collective-permute-done | bytes 266272 | tf_op jit(solution)/shard_map/ppermute | solution.py:227
  22.3 1.4 %collective-permute-start.4 = (bf16[1040,128]{1,0:T(8,128)(2,1)S(1)}, bf16[1040,128]{1,0:T(8,128)(2,1)S(1)}, u32[]{:S(2)}, u32[]{:S(2)}) collective-permute-start(bf16[1040,128]{1,0:T(8,128)(2,1)S(1)} %collective-permute-done.2.from_left.refs_3_), channel_id=1, source_target_pairs={{0,4},{4,8},{8,12},{12,14},{14,10},{10,6},{6,2},{2,0},{1,5},{5,9},... | collective-permute-start | bytes 798728 | tf_op jit(solution)/shard_map/ppermute | solution.py:226
  23.7 0.6 collective-permute-start.5
  24.3 2.7 %shard_map.98.start = f32[2,512,256]{2,1,0:T(8,128)S(1)} custom-call(s32[11]{0:T(128)S(1)} %copy-done.5, s32[11]{0:T(128)S(1)} %copy-done.7, bf16[1040,128]{1,0:T(8,128)(2,1)S(1)} %collective-permute-done.2.from_left.refs_3_, bf16[1040,128]{1,0:T(8,128)(2,1)S(1)} %collective-permute-done.3.from_right.refs_4_, ...), custom_call_target="tpu_custom_call", output_to_operand_aliasing={{}: (5, {})} | custom-call | flops 1048576 | bytes 1048576 | tf_op jit(solution)/shard_map/pallas_call | solution.py:237
  27.0 1.7 %collective-permute-done.4.from_left.refs_5_ = bf16[1040,128]{1,0:T(8,128)(2,1)S(1)} collective-permute-done((bf16[1040,128]{1,0:T(8,128)(2,1)S(1)}, bf16[1040,128]{1,0:T(8,128)(2,1)S(1)}, u32[]{:S(2)}, u32[]{:S(2)}) %collective-permute-start.4) | collective-permute-done | bytes 266272 | tf_op jit(solution)/shard_map/ppermute | solution.py:226
  28.7 1.8 %collective-permute-done.5.from_right.refs_6_ = bf16[1040,128]{1,0:T(8,128)(2,1)S(1)} collective-permute-done((bf16[1040,128]{1,0:T(8,128)(2,1)S(1)}, bf16[1040,128]{1,0:T(8,128)(2,1)S(1)}, u32[]{:S(2)}, u32[]{:S(2)}) %collective-permute-start.5) | collective-permute-done | bytes 266272 | tf_op jit(solution)/shard_map/ppermute | solution.py:227
  30.5 0.6 %collective-permute-start.7 = (bf16[528,128]{1,0:T(8,128)(2,1)S(1)}, bf16[528,128]{1,0:T(8,128)(2,1)S(1)}, u32[]{:S(2)}, u32[]{:S(2)}) collective-permute-start(bf16[528,128]{1,0:T(8,128)(2,1)S(1)} %slice.7), channel_id=1, source_target_pairs={{4,0},{8,4},{12,8},{14,12},{10,14},{6,10},{2,6},{0,2},{5,1},{9,5},... | collective-permute-start | bytes 405512 | tf_op jit(solution)/shard_map/ppermute | solution.py:231
  31.1 0.0 copy-start.11
  31.2 1.5 %collective-permute-start.6 = (bf16[512,128]{1,0:T(8,128)(2,1)S(1)}, bf16[512,128]{1,0:T(8,128)(2,1)S(1)}, u32[]{:S(2)}, u32[]{:S(2)}) collective-permute-start(bf16[512,128]{1,0:T(8,128)(2,1)S(1)} %slice.6), channel_id=1, source_target_pairs={{0,4},{4,8},{8,12},{12,14},{14,10},{10,6},{6,2},{2,0},{1,5},{5,9},... | collective-permute-start | bytes 393224 | tf_op jit(solution)/shard_map/ppermute | solution.py:230
  32.7 0.0 copy-done.6
  32.7 0.0 copy-done.8
  32.7 2.8 %shard_map.99.start = f32[2,512,256]{2,1,0:T(8,128)S(1)} custom-call(s32[11]{0:T(128)S(1)} %copy-done.6, s32[11]{0:T(128)S(1)} %copy-done.8, bf16[1040,128]{1,0:T(8,128)(2,1)S(1)} %collective-permute-done.4.from_left.refs_5_, bf16[1040,128]{1,0:T(8,128)(2,1)S(1)} %collective-permute-done.5.from_right.refs_6_, ...), custom_call_target="tpu_custom_call", output_to_operand_aliasing={{}: (5, {})} | custom-call | flops 1048576 | bytes 1048576 | tf_op jit(solution)/shard_map/pallas_call | solution.py:237
  35.5 0.7 %collective-permute-done.6.low = bf16[512,128]{1,0:T(8,128)(2,1)S(1)} collective-permute-done((bf16[512,128]{1,0:T(8,128)(2,1)S(1)}, bf16[512,128]{1,0:T(8,128)(2,1)S(1)}, u32[]{:S(2)}, u32[]{:S(2)}) %collective-permute-start.6) | collective-permute-done | bytes 131104 | tf_op jit(solution)/shard_map/ppermute | solution.py:230
  36.2 0.0 collective-permute-done.7.high.refs_7_
  36.2 0.0 copy-done.11
  36.2 3.0 %shard_map.100 = (f32[2,512,128]{2,1,0:T(8,128)S(1)}, f32[2,2,256,128]{3,2,1,0:T(8,128)S(1)}, f32[2,2,256,128]{3,2,1,0:T(8,128)}) custom-call(s32[11]{0:T(128)S(1)} %copy-done.6, s32[11]{0:T(128)S(1)} %copy-done.8, f32[2]{0:T(128)S(1)} %copy-done.11, bf16[512,128]{1,0:T(8,128)(2,1)S(1)} %collective-permute-done.6.low, ...), custom_call_target="tpu_custom_call" | custom-call | flops 1048576 | bytes 1048576 | tf_op jit(solution)/shard_map/pallas_call | solution.py:255
  39.1 0.0 collective-permute-start.9
  39.1 0.5 collective-permute-start.8
  39.6 0.8 %shard_map.101.pick = bf16[1024,1024]{1,0:T(8,128)(2,1)S(1)} custom-call(bf16[1040,128]{1,0:T(8,128)(2,1)S(1)} %shard_map.95.own.refs_0_, bf16[1040,128]{1,0:T(8,128)(2,1)S(1)} %collective-permute-done.from_left.refs_1_, bf16[1040,128]{1,0:T(8,128)(2,1)S(1)} %collective-permute-done.1.from_right.refs_2_, ...), custom_call_target="tpu_custom_call" | custom-call | flops 1048576 | bytes 1048576 | tf_op jit(solution)/shard_map/pallas_call | solution.py:273
  40.5 0.0 copy-start.2
  40.5 0.0 copy-start.10
  40.5 1.2 %collective-permute-done.9.theirs = f32[2,512,128]{2,1,0:T(8,128)S(1)} collective-permute-done((f32[2,512,128]{2,1,0:T(8,128)S(1)}, f32[2,512,128]{2,1,0:T(8,128)S(1)}, u32[]{:S(2)}, u32[]{:S(2)}) %collective-permute-start.9) | collective-permute-done | bytes 524320 | tf_op jit(solution)/shard_map/ppermute | solution.py:283
  41.8 1.4 %shard_map.102 = bf16[1024,128]{1,0:T(8,128)(2,1)} custom-call(bf16[1024,1024]{1,0:T(8,128)(2,1)S(1)} %shard_map.101.pick, f32[2,512,128]{2,1,0:T(8,128)S(1)} %get-tuple-element.31.mine, f32[2,512,128]{2,1,0:T(8,128)S(1)} %collective-permute-done.9.theirs), custom_call_target="tpu_custom_call" | custom-call | tf_op jit(solution)/shard_map/pallas_call | solution.py:285
  43.2 4.6 %all-to-all-start = ((bf16[8,128,128]{2,1,0:T(8,128)(2,1)}), bf16[8,128,128]{2,1,0:T(8,128)(2,1)S(1)}, u32[]{:S(2)}, u32[]{:S(2)}) async-start(bf16[8,128,128]{2,1,0:T(8,128)(2,1)} %bitcast.1), calls=%async_computation | async-start | bytes 524288 | tf_op jit(solution)/shard_map/all_to_all | solution.py:290
  47.8 0.9 %shard_map.103.basis = bf16[2,1024,512]{2,1,0:T(8,128)(2,1)S(1)} custom-call(s32[2,256]{1,0:T(2,128)S(1)} %copy-done.10, bf16[2,256,512]{2,1,0:T(8,128)(2,1)S(1)} %copy-done.2), custom_call_target="tpu_custom_call" | custom-call | flops 1048576 | bytes 1048576 | tf_op jit(solution)/shard_map/pallas_call | solution.py:267
  48.7 0.0 collective-permute-done.8
  48.7 1.9 %add.3 = f32[2,2,256,128]{3,2,1,0:T(8,128)} add(f32[2,2,256,128]{3,2,1,0:T(8,128)S(1)} %get-tuple-element.29, f32[2,2,256,128]{3,2,1,0:T(8,128)} %collective-permute-done.8) | non-fusion elementwise | flops 131072 | bytes 1572864 | tf_op jit(solution)/shard_map/add | solution.py:296
  50.6 6.4 %all-to-all-done = bf16[8,128,128]{2,1,0:T(8,128)(2,1)S(1)} async-done(((bf16[8,128,128]{2,1,0:T(8,128)(2,1)}), bf16[8,128,128]{2,1,0:T(8,128)(2,1)S(1)}, u32[]{:S(2)}, u32[]{:S(2)}) %all-to-all-start) | async-done | bytes 262176 | tf_op jit(solution)/shard_map/all_to_all | solution.py:290
  57.0 0.9 %copy-done.3 = bf16[2,128,512]{2,1,0:T(8,128)(2,1)S(1)} copy-done((bf16[2,128,512]{2,1,0:T(8,128)(2,1)S(1)}, bf16[2,128,512]{2,1,0:T(8,128)(2,1)}, u32[]{:S(2)}) %copy-start.3) | copy-done | bytes 262168
  58.0 1.1 %shard_map.104 = f32[2,512]{1,0:T(2,128)} custom-call(bf16[1024,128]{1,0:T(8,128)(2,1)S(1)} %bitcast.3, bf16[2,1024,512]{2,1,0:T(8,128)(2,1)S(1)} %shard_map.103.basis, bf16[2,128,512]{2,1,0:T(8,128)(2,1)S(1)} %copy-done.3), custom_call_target="tpu_custom_call" | custom-call | tf_op jit(solution)/shard_map/pallas_call | solution.py:291
  (11 shorter events, 0.1 us)
Async XLA Ops:
  0.6 1.0 %copy-start.4 = (bf16[1,8,2,64,128]{4,3,2,1,0:T(8,128)(2,1)S(1)}, bf16[1,8,2,64,128]{4,3,2,1,0:T(8,128)(2,1)}, u32[]{:S(2)}) copy-start(bf16[1,8,2,64,128]{4,3,2,1,0:T(8,128)(2,1)} %param.8) | copy-start | bytes 786436
  1.6 0.7 %copy-start.9 = (s32[2,256]{1,0:T(2,128)S(1)}, s32[2,256]{1,0:T(2,128)}, u32[]{:S(2)}) copy-start(s32[2,256]{1,0:T(2,128)} %wanted.3) | copy-start | bytes 6148
  2.3 10.6 %collective-permute-start = (bf16[1040,128]{1,0:T(8,128)(2,1)S(1)}, bf16[1040,128]{1,0:T(8,128)(2,1)S(1)}, u32[]{:S(2)}, u32[]{:S(2)}) collective-permute-start(bf16[1040,128]{1,0:T(8,128)(2,1)S(1)} %shard_map.95.own.refs_0_), channel_id=1, source_target_pairs={{0,4},{4,8},{8,12},{12,14},{14,10},{10,6},{6,2},{2,0},{1,5},{5,9},... | collective-permute-start | bytes 798728 | tf_op jit(solution)/shard_map/ppermute | solution.py:226
  5.4 7.9 %collective-permute-start.1 = (bf16[1040,128]{1,0:T(8,128)(2,1)S(1)}, bf16[1040,128]{1,0:T(8,128)(2,1)S(1)}, u32[]{:S(2)}, u32[]{:S(2)}) collective-permute-start(bf16[1040,128]{1,0:T(8,128)(2,1)S(1)} %shard_map.95.own.refs_0_), channel_id=1, source_target_pairs={{4,0},{8,4},{12,8},{14,12},{10,14},{6,10},{2,6},{0,2},{5,1},{9,5},... | collective-permute-start | bytes 798728 | tf_op jit(solution)/shard_map/ppermute | solution.py:227
  5.4 4.3 %copy-start = (bf16[11,2,512,512]{3,2,1,0:T(8,128)(2,1)S(1)}, bf16[11,2,512,512]{3,2,1,0:T(8,128)(2,1)}, u32[]{:S(2)}) copy-start(bf16[11,2,512,512]{3,2,1,0:T(8,128)(2,1)} %tiles.9) | copy-start | bytes 34603012
  9.7 0.7 %copy-start.5 = (s32[11]{0:T(128)S(1)}, s32[11]{0:T(128)}, u32[]{:S(2)}) copy-start(s32[11]{0:T(128)} %slots.9) | copy-start | bytes 136
  10.3 0.7 %copy-start.7 = (s32[11]{0:T(128)S(1)}, s32[11]{0:T(128)}, u32[]{:S(2)}) copy-start(s32[11]{0:T(128)} %cols.9) | copy-start | bytes 136
  11.0 4.3 %copy-start.1 = (bf16[11,2,512,512]{3,2,1,0:T(8,128)(2,1)S(1)}, bf16[11,2,512,512]{3,2,1,0:T(8,128)(2,1)}, u32[]{:S(2)}) copy-start(bf16[11,2,512,512]{3,2,1,0:T(8,128)(2,1)} %tiles.9) | copy-start | bytes 34603012
  13.2 7.6 %collective-permute-start.2 = (bf16[1040,128]{1,0:T(8,128)(2,1)S(1)}, bf16[1040,128]{1,0:T(8,128)(2,1)S(1)}, u32[]{:S(2)}, u32[]{:S(2)}) collective-permute-start(bf16[1040,128]{1,0:T(8,128)(2,1)S(1)} %collective-permute-done.from_left.refs_1_), channel_id=1, source_target_pairs={{0,4},{4,8},{8,12},{12,14},{14,10},{10,6},{6,2},{2,0},{1,5},{5,9},... | collective-permute-start | bytes 798728 | tf_op jit(solution)/shard_map/ppermute | solution.py:226
  15.0 7.3 %collective-permute-start.3 = (bf16[1040,128]{1,0:T(8,128)(2,1)S(1)}, bf16[1040,128]{1,0:T(8,128)(2,1)S(1)}, u32[]{:S(2)}, u32[]{:S(2)}) collective-permute-start(bf16[1040,128]{1,0:T(8,128)(2,1)S(1)} %collective-permute-done.1.from_right.refs_2_), channel_id=1, source_target_pairs={{4,0},{8,4},{12,8},{14,12},{10,14},{6,10},{2,6},{0,2},{5,1},{9,5},... | collective-permute-start | bytes 798728 | tf_op jit(solution)/shard_map/ppermute | solution.py:227
  17.9 14.7 %copy-start.6 = (s32[11]{0:T(128)S(1)}, s32[11]{0:T(128)}, u32[]{:S(2)}) copy-start(s32[11]{0:T(128)} %slots.9) | copy-start | bytes 136
  17.9 14.7 %copy-start.8 = (s32[11]{0:T(128)S(1)}, s32[11]{0:T(128)}, u32[]{:S(2)}) copy-start(s32[11]{0:T(128)} %cols.9) | copy-start | bytes 136
  22.3 6.4 %collective-permute-start.4 = (bf16[1040,128]{1,0:T(8,128)(2,1)S(1)}, bf16[1040,128]{1,0:T(8,128)(2,1)S(1)}, u32[]{:S(2)}, u32[]{:S(2)}) collective-permute-start(bf16[1040,128]{1,0:T(8,128)(2,1)S(1)} %collective-permute-done.2.from_left.refs_3_), channel_id=1, source_target_pairs={{0,4},{4,8},{8,12},{12,14},{14,10},{10,6},{6,2},{2,0},{1,5},{5,9},... | collective-permute-start | bytes 798728 | tf_op jit(solution)/shard_map/ppermute | solution.py:226
  23.7 6.8 %collective-permute-start.5 = (bf16[1040,128]{1,0:T(8,128)(2,1)S(1)}, bf16[1040,128]{1,0:T(8,128)(2,1)S(1)}, u32[]{:S(2)}, u32[]{:S(2)}) collective-permute-start(bf16[1040,128]{1,0:T(8,128)(2,1)S(1)} %collective-permute-done.3.from_right.refs_4_), channel_id=1, source_target_pairs={{4,0},{8,4},{12,8},{14,12},{10,14},{6,10},{2,6},{0,2},{5,1},{9,5},... | collective-permute-start | bytes 798728 | tf_op jit(solution)/shard_map/ppermute | solution.py:227
  30.5 5.7 %collective-permute-start.7 = (bf16[528,128]{1,0:T(8,128)(2,1)S(1)}, bf16[528,128]{1,0:T(8,128)(2,1)S(1)}, u32[]{:S(2)}, u32[]{:S(2)}) collective-permute-start(bf16[528,128]{1,0:T(8,128)(2,1)S(1)} %slice.7), channel_id=1, source_target_pairs={{4,0},{8,4},{12,8},{14,12},{10,14},{6,10},{2,6},{0,2},{5,1},{9,5},... | collective-permute-start | bytes 405512 | tf_op jit(solution)/shard_map/ppermute | solution.py:231
  31.1 5.0 %copy-start.11 = (f32[2]{0:T(128)S(1)}, f32[2]{0:T(128)}, u32[]{:S(2)}) copy-start(f32[2]{0:T(128)} %pole_weight.1) | copy-start | bytes 28
  31.2 5.0 %collective-permute-start.6 = (bf16[512,128]{1,0:T(8,128)(2,1)S(1)}, bf16[512,128]{1,0:T(8,128)(2,1)S(1)}, u32[]{:S(2)}, u32[]{:S(2)}) collective-permute-start(bf16[512,128]{1,0:T(8,128)(2,1)S(1)} %slice.6), channel_id=1, source_target_pairs={{0,4},{4,8},{8,12},{12,14},{14,10},{10,6},{6,2},{2,0},{1,5},{5,9},... | collective-permute-start | bytes 393224 | tf_op jit(solution)/shard_map/ppermute | solution.py:230
  39.1 2.6 %collective-permute-start.9 = (f32[2,512,128]{2,1,0:T(8,128)S(1)}, f32[2,512,128]{2,1,0:T(8,128)S(1)}, u32[]{:S(2)}, u32[]{:S(2)}) collective-permute-start(f32[2,512,128]{2,1,0:T(8,128)S(1)} %get-tuple-element.31.mine), channel_id=1, source_target_pairs={{0,1},{1,0},{2,3},{3,2},{4,5},{5,4},{6,7},{7,6},{8,9},{9,8},{10,11... | collective-permute-start | bytes 1572872 | tf_op jit(solution)/shard_map/ppermute | solution.py:283
  39.1 9.5 %collective-permute-start.8 = (f32[2,2,256,128]{3,2,1,0:T(8,128)}, f32[2,2,256,128]{3,2,1,0:T(8,128)}, u32[]{:S(2)}, u32[]{:S(2)}) collective-permute-start(f32[2,2,256,128]{3,2,1,0:T(8,128)} %get-tuple-element.30), channel_id=1, source_target_pairs={{0,1},{1,0},{2,3},{3,2},{4,5},{5,4},{6,7},{7,6},{8,9},{9,8},{10,11... | collective-permute-start | bytes 1572872 | tf_op jit(solution)/shard_map/ppermute | solution.py:284
  40.5 7.3 %copy-start.2 = (bf16[2,256,512]{2,1,0:T(8,128)(2,1)S(1)}, bf16[2,256,512]{2,1,0:T(8,128)(2,1)}, u32[]{:S(2)}) copy-start(bf16[2,256,512]{2,1,0:T(8,128)(2,1)} %basis.1) | copy-start | bytes 1572868
  40.5 7.3 %copy-start.10 = (s32[2,256]{1,0:T(2,128)S(1)}, s32[2,256]{1,0:T(2,128)}, u32[]{:S(2)}) copy-start(s32[2,256]{1,0:T(2,128)} %wanted.3) | copy-start | bytes 6148
  43.2 13.8 %all-to-all-start = ((bf16[8,128,128]{2,1,0:T(8,128)(2,1)}), bf16[8,128,128]{2,1,0:T(8,128)(2,1)S(1)}, u32[]{:S(2)}, u32[]{:S(2)}) async-start(bf16[8,128,128]{2,1,0:T(8,128)(2,1)} %bitcast.1), calls=%async_computation | async-start | bytes 524288 | tf_op jit(solution)/shard_map/all_to_all | solution.py:290
  57.0 1.0 %copy-start.3 = (bf16[2,128,512]{2,1,0:T(8,128)(2,1)S(1)}, bf16[2,128,512]{2,1,0:T(8,128)(2,1)}, u32[]{:S(2)}) copy-start(bf16[2,128,512]{2,1,0:T(8,128)(2,1)} %supernode.1) | copy-start | bytes 786436

commit v4 on v3

--- a/solution.py
+++ b/solution.py
@@ -12,6 +12,7 @@
 F32 = jnp.float32
 BF16 = jnp.bfloat16
 VMEM_LIMIT = 8 * 1024 * 1024
+PACK_LIMIT = 56 * 1024 * 1024
 
 
 def ring_order(n):
@@ -45,11 +46,14 @@
     return jnp.concatenate([whole[i:i + 1] for i in range(count)], axis=1)
 
 
-def pack_kernel(panel, wanted, out, sem):
+def pack_kernel(panel, wanted, out, held, sems):
     rows = panel.shape[0]
-    copy = pltpu.make_async_copy(panel, out.at[pl.ds(0, rows)], sem)
+    bring = pltpu.make_async_copy(wanted, held, sems.at[0])
+    copy = pltpu.make_async_copy(panel, out.at[pl.ds(0, rows)], sems.at[1])
+    bring.start()
     copy.start()
-    out[rows:, :] = digits(wanted[...])
+    bring.wait()
+    out[rows:, :] = digits(held[...])
     copy.wait()
 
 
@@ -84,9 +88,22 @@
         acc[slots[t]] += jnp.dot(left, weights[cols[t]], preferred_element_type=F32)
 
 
-def hop_first(slots, cols, own, tiles, out, weights, *, n, depth):
+def stage_kernel(slots, cols, own, tiles, slots_out, cols_out, own_out, out):
+    del tiles
+    slots_out[...] = slots[...]
+    cols_out[...] = cols[...]
+    own_out[...] = own[...]
     out[...] = jnp.zeros_like(out)
-    accumulate(slots, cols, tiles, [(shard_row(n, 0), depth, [own])], out, weights)
+
+
+def hop_early(slots, cols, own, from_left, from_right, tiles, start, out, weights, *, n, depth):
+    del start
+    shards = [
+        (shard_row(n, 0), depth, [own]),
+        (shard_row(n, -1), depth, [from_left]),
+        (shard_row(n, 1), depth, [from_right]),
+    ]
+    accumulate(slots, cols, tiles, shards, out, weights)
 
 
 def hop_middle(slots, cols, from_left, from_right, tiles, start, out, weights, *, n, depth, hop):
@@ -97,18 +114,19 @@
     accumulate(slots, cols, tiles, shards, out, weights)
 
 
-def hop_last(
-    slots, cols, pole_weight, low, high, tiles, start, dens, mine, other, acc, weights, *, n, depth
-):
-    acc[...] = start[...]
-    accumulate(slots, cols, tiles, [(shard_row(n, n // 2), depth, [low, high])], acc, weights)
+def hop_last(slots, cols, pole_weight, low, high, tiles, start, out, dens, weights, *, n, depth):
+    del start
+    accumulate(slots, cols, tiles, [(shard_row(n, n // 2), depth, [low, high])], out, weights)
+    width = dens.shape[2]
+    for slot in range(out.shape[0]):
+        dens[slot] = -(pole_weight[0] * out[slot, :, width:] + pole_weight[1] * out[slot, :, :width])
+
+
+def halves_kernel(acc, mine, other):
     col = lax.axis_index("col")
     half = mine.shape[2]
     width = mine.shape[3]
     for slot in range(acc.shape[0]):
-        real = -acc[slot, :, :width]
-        imag = -acc[slot, :, width:]
-        dens[slot] = pole_weight[0] * imag + pole_weight[1] * real
         for p in range(2):
             cut = slice(p * width, (p + 1) * width)
             mine[slot, p] = -acc[slot, pl.ds(pl.multiple_of(col * half, half), half), cut]
@@ -121,7 +139,8 @@
     return (first < second).astype(F32).astype(BF16)
 
 
-def basis_kernel(wanted, basis, out, *, n, rows_chip, slots):
+def basis_kernel(wanted, basis, supernode, out, wide, *, n, rows_chip, slots):
+    wide[...] = supernode[...].astype(F32)
     boxes, orbitals, _ = basis.shape
     total = boxes * orbitals
     rows = wanted[...]
@@ -158,6 +177,10 @@
         out[pl.ds(at, slots), :] = (lane == row).astype(F32).astype(BF16)
 
 
+def add_kernel(mine, theirs, out):
+    out[...] = mine[...] + theirs[...]
+
+
 def select_kernel(pick, mine, theirs, out):
     rows = pick.shape[1]
     total = (mine[...] + theirs[...]).reshape(rows, mine.shape[2]).astype(BF16)
@@ -169,7 +192,7 @@
         projected = lax.dot_general(
             arrived[...], basis[n], (((0,), (0,)), ((), ())), preferred_element_type=F32
         )
-        out[n:n + 1, :] = jnp.sum(supernode[n].astype(F32) * projected, axis=0, keepdims=True)
+        out[n:n + 1, :] = jnp.sum(supernode[n] * projected, axis=0, keepdims=True)
 
 
 def local(n_row, panel, tiles, tile_slot, tile_col, pole_weight, box_orbitals, box_basis, supernode_basis):
@@ -210,11 +233,11 @@
 
     own = pl.pallas_call(
         pack_kernel,
-        in_specs=[in_hbm, in_vmem],
+        in_specs=[in_hbm, in_hbm],
         out_specs=in_vmem,
         out_shape=jax.ShapeDtypeStruct((shard_rows + lines, width), BF16),
-        scratch_shapes=[pltpu.SemaphoreType.DMA],
-        compiler_params=params,
+        scratch_shapes=[pltpu.VMEM(box_orbitals.shape, jnp.int32), pltpu.SemaphoreType.DMA((2,))],
+        compiler_params=pltpu.CompilerParams(vmem_limit_bytes=PACK_LIMIT),
         cost_estimate=cost,
     )(panel.reshape(shard_rows, width), box_orbitals)
 
@@ -230,10 +253,25 @@
             next_left = lax.ppermute(left[:cut], "row", to_right)
             next_right = lax.ppermute(right[cut:], "row", to_left)
         if h == 1:
-            acc = call(hop_first, [in_smem] * 2 + [in_vmem] * 2, acc_out, [], 1)(
-                tile_slot, tile_col, own, tiles
-            )
-        else:
+            tile_slot, tile_col, own, acc = pl.pallas_call(
+                stage_kernel,
+                in_specs=[in_vmem] * 4,
+                out_specs=[in_vmem] * 4,
+                out_shape=[
+                    jax.ShapeDtypeStruct(tile_slot.shape, jnp.int32),
+                    jax.ShapeDtypeStruct(tile_col.shape, jnp.int32),
+                    jax.ShapeDtypeStruct(own.shape, BF16),
+                    acc_out,
+                ],
+                compiler_params=params,
+                cost_estimate=cost,
+            )(tile_slot, tile_col, own, tiles)
+            seen[0] = own
+        elif h == 2:
+            acc = call(
+                hop_early, [in_smem] * 2 + [in_vmem] * 5, acc_out, [], 3, aliases={6: 0}
+            )(tile_slot, tile_col, own, left, right, tiles, acc)
+        elif h > 2:
             acc = call(
                 functools.partial(hop_middle, hop=h - 1),
                 [in_smem] * 2 + [in_vmem] * 4,
@@ -242,7 +280,9 @@
                 2,
                 aliases={5: 0},
             )(tile_slot, tile_col, left, right, tiles, acc)
-        left, right, acc = lax.optimization_barrier((next_left, next_right, acc))
+        left, done = lax.optimization_barrier((next_left, acc))
+        right, _ = lax.optimization_barrier((next_right, acc))
+        acc = done
         if h < half_ring:
             seen += [left, right]
             hops += [-h, h]
@@ -251,25 +291,30 @@
             hops.append(h)
 
     half_shape = (BR_DEV, 2, half, width)
-    dens_shape = (BR_DEV, order_b, width)
-    dens, mine, other = call(
+    acc, dens = call(
         hop_last,
         [in_smem] * 3 + [in_vmem] * 4,
-        [
-            jax.ShapeDtypeStruct(dens_shape, F32),
-            jax.ShapeDtypeStruct(half_shape, F32),
-            jax.ShapeDtypeStruct(half_shape, F32),
+        [acc_out, jax.ShapeDtypeStruct((BR_DEV, order_b, width), F32)],
+        [],
+        1,
+        aliases={6: 0},
+    )(tile_slot, tile_col, pole_weight, left, right, tiles, acc)
+    mine, other = pl.pallas_call(
+        halves_kernel,
+        out_shape=[jax.ShapeDtypeStruct(half_shape, F32)] * 2,
+        compiler_params=params,
+        cost_estimate=cost,
+    )(acc)
+
+    basis_here, wide = pl.pallas_call(
+        functools.partial(basis_kernel, n=n_row, rows_chip=rows_chip, slots=slots),
+        out_shape=[
+            jax.ShapeDtypeStruct((boxes, arrive, box_basis.shape[2]), BF16),
+            jax.ShapeDtypeStruct(supernode_basis.shape, F32),
         ],
-        [pltpu.VMEM(acc_shape, F32)],
-        1,
-    )(tile_slot, tile_col, pole_weight, left, right, tiles, acc)
-
-    basis_here = pl.pallas_call(
-        functools.partial(basis_kernel, n=n_row, rows_chip=rows_chip, slots=slots),
-        out_shape=jax.ShapeDtypeStruct((boxes, arrive, box_basis.shape[2]), BF16),
-        compiler_params=params,
-        cost_estimate=cost,
-    )(box_orbitals, box_basis)
+        compiler_params=params,
+        cost_estimate=cost,
+    )(box_orbitals, box_basis, supernode_basis)
     pick = pl.pallas_call(
         functools.partial(
             pick_kernel, n=n_row, hops=hops, total=total, rows_chip=rows_chip, slots=slots
@@ -288,12 +333,18 @@
         compiler_params=params,
     )(pick, dens, dens_other)
     arrived = lax.all_to_all(send, "row", 0, 0, tiled=True)
+    inverse = pl.pallas_call(
+        add_kernel,
+        out_shape=jax.ShapeDtypeStruct(half_shape, F32),
+        compiler_params=params,
+        cost_estimate=cost,
+    )(mine, inverse_other)
     density = pl.pallas_call(
         density_kernel,
         out_shape=jax.ShapeDtypeStruct((boxes, box_basis.shape[2]), F32),
         compiler_params=params,
-    )(arrived, basis_here, supernode_basis)
-    return mine + inverse_other, density
+    )(arrived, basis_here, wide)
+    return inverse, density
 
 
 def solution(mesh):

time: 59.5 us -> 57 us (0.958)
  waiting for transfers between devices: 16.6 us -> 9.41 us
  local copies, waits for them, and re-layouts: 8.21 us -> 12.5 us
  other arithmetic: 1.89 us -> 0 us
  Pallas kernels: 17.2 us -> 19 us
    ppermute x3, starting transfers between devices: 0.87 us -> 6.85 us  [local(): next_right = lax.ppermute(right, 'row', to_left)]
    ppermute x3, starting transfers between devices: 6.26 us -> 0.4 us  [local(): next_left = lax.ppermute(left, 'row', to_right)]
    ppermute x3, waiting for transfers between devices: 4.56 us -> 0.01 us  [local(): next_left = lax.ppermute(left, 'row', to_right)]
    pallas_call x3 -> x6, Pallas kernels: 4.88 us -> 9.19 us  [the longest x1 3.64 us: local(): call(hop_early, [in_smem] * 2 + [in_vmem] * 5, acc_out, [], 3, aliases={6...]
    unnamed x24 -> x22, local copies, waits for them, and re-layouts: 8.2 us -> 12.5 us
    pallas_call x3 -> x2, Pallas kernels: 8.12 us -> 5.62 us  [local(): call(functools.partial(hop_middle, hop=h - 1), [in_smem] * 2 + [in_vmem]...]
    add x1 -> x0, other arithmetic: 1.89 us -> none  [local(): return (mine + inverse_other, density)]
    all_to_all x1, waiting for transfers between devices: 6.44 us -> 4.57 us  [local(): arrived = lax.all_to_all(send, 'row', 0, 0, tiled=True)]
  transfers between devices with their start and end apart: 11 -> 11, of which waited for: 8 -> 4; matrix products, arithmetic and copies ran while one was open for 3% -> 0% of each run, Pallas kernels for 22% -> 25%
where the time goes in v4:
time: 57 us; the launch traced here: 56.5 us
  Pallas kernels  19 us (33%)
  starting transfers between devices  14.8 us (26%)
  local copies, waits for them, and re-layouts  12.5 us (22%)
  waiting for transfers between devices  9.41 us (17%)
  between operations  0.77 us (1%)
    unnamed x22, local copies, waits for them, and re-layouts  12.5 us
    ppermute x3, starting transfers between devices, local(): next_right = lax.ppermute(right, 'row', to_left)  6.85 us
    pallas_call x2, Pallas kernels, local(): call(functools.partial(hop_middle, hop=h - 1), [in_smem] * 2 + [in_vmem]...  5.62 us
    all_to_all x1, starting transfers between devices, local(): arrived = lax.all_to_all(send, 'row', 0, 0, tiled=True)  4.9 us
    all_to_all x1, waiting for transfers between devices, local(): arrived = lax.all_to_all(send, 'row', 0, 0, tiled=True)  4.57 us
    pallas_call x1, Pallas kernels, local(): call(hop_early, [in_smem] * 2 + [in_vmem] * 5, acc_out, [], 3, aliases={6...  3.64 us
    ppermute x3, waiting for transfers between devices, local(): next_right = lax.ppermute(right, 'row', to_left)  3.13 us
    pallas_call x1, Pallas kernels, local(): call(hop_last, [in_smem] * 3 + [in_vmem] * 4, [acc_out, jax.ShapeDtypeStr...  2.06 us
  transfers between devices with their start and end apart: 11, of which 4 were waited for; matrix products, arithmetic and copies ran while one was open for 0% of the time, Pallas kernels for 25%

profile of v4, /device:TPU:0, one launch (start us, length us, event | category | flops | bytes accessed | tf_op | source)
XLA Modules:
  0.0 56.5 jit_solution(13208503485459437020)
XLA Ops:
  0.6 1.7 %shard_map.95.own = bf16[1040,128]{1,0:T(8,128)(2,1)} custom-call(bf16[1024,128]{1,0:T(8,128)(2,1)} %bitcast.4, s32[2,256]{1,0:T(2,128)} %wanted.3), custom_call_target="tpu_custom_call" | custom-call | flops 1048576 | bytes 1048576 | tf_op jit(solution)/shard_map/pallas_call | solution.py:234
  2.3 3.0 %collective-permute-start.2 = (bf16[1040,128]{1,0:T(8,128)(2,1)}, bf16[1040,128]{1,0:T(8,128)(2,1)S(1)}, u32[]{:S(2)}, u32[]{:S(2)}) collective-permute-start(bf16[1040,128]{1,0:T(8,128)(2,1)} %shard_map.95.own), channel_id=1, source_target_pairs={{4,0},{8,4},{12,8},{14,12},{10,14},{6,10},{2,6},{0,2},{5,1},{9,5},... | collective-permute-start | bytes 798728 | tf_op jit(solution)/shard_map/ppermute | solution.py:250
  5.3 0.1 collective-permute-start
  5.5 4.3 %copy-done = bf16[11,2,512,512]{3,2,1,0:T(8,128)(2,1)S(1)} copy-done((bf16[11,2,512,512]{3,2,1,0:T(8,128)(2,1)S(1)}, bf16[11,2,512,512]{3,2,1,0:T(8,128)(2,1)}, u32[]{:S(2)}) %copy-start) | copy-done | bytes 11534360
  9.7 0.9 %copy-done.2 = bf16[1040,128]{1,0:T(8,128)(2,1)S(1)} copy-done((bf16[1040,128]{1,0:T(8,128)(2,1)S(1)}, bf16[1040,128]{1,0:T(8,128)(2,1)}, u32[]{:S(2)}) %copy-start.2) | copy-done | bytes 266264
  10.7 0.7 %copy-done.8 = s32[11]{0:T(128)S(1)} copy-done((s32[11]{0:T(128)S(1)}, s32[11]{0:T(128)}, u32[]{:S(2)}) %copy-start.8) | copy-done | bytes 68
  11.4 0.7 %copy-done.9 = s32[11]{0:T(128)S(1)} copy-done((s32[11]{0:T(128)S(1)}, s32[11]{0:T(128)}, u32[]{:S(2)}) %copy-start.9) | copy-done | bytes 68
  12.0 0.1 shard_map.96
  12.1 0.0 collective-permute-done.2.from_right.refs_2_
  12.1 2.0 %collective-permute-start.4 = (bf16[1040,128]{1,0:T(8,128)(2,1)S(1)}, bf16[1040,128]{1,0:T(8,128)(2,1)S(1)}, u32[]{:S(2)}, u32[]{:S(2)}) collective-permute-start(bf16[1040,128]{1,0:T(8,128)(2,1)S(1)} %collective-permute-done.2.from_right.refs_2_), channel_id=1, source_target_pairs={{4,0},{8,4},{12,8},{14,12},{10,14},{6,10},{2,6},{0,2},{5,1},{9,5},... | collective-permute-start | bytes 798728 | tf_op jit(solution)/shard_map/ppermute | solution.py:250
  14.1 0.0 collective-permute-done.from_left.refs_1_
  14.1 0.1 collective-permute-start.1
  14.2 2.1 %copy-done.1 = bf16[11,2,512,512]{3,2,1,0:T(8,128)(2,1)S(1)} copy-done((bf16[11,2,512,512]{3,2,1,0:T(8,128)(2,1)S(1)}, bf16[11,2,512,512]{3,2,1,0:T(8,128)(2,1)}, u32[]{:S(2)}) %copy-start.1) | copy-done | bytes 11534360
  16.3 3.6 %shard_map.97.start = f32[2,512,256]{2,1,0:T(8,128)S(1)} custom-call(s32[11]{0:T(128)S(1)} %get-tuple-element.24.slots, s32[11]{0:T(128)S(1)} %get-tuple-element.25.cols, bf16[1040,128]{1,0:T(8,128)(2,1)S(1)} %get-tuple-element.28.own.refs_0_, bf16[1040,128]{1,0:T(8,128)(2,1)S(1)} %collective-permute-done.from_left.refs_1_, ...), custom_call_target="tpu_custom_call", output_to_operand_aliasing={{}: (6, {})} | custom-call | flops 1048576 | bytes 1048576 | tf_op jit(solution)/shard_map/pallas_call | solution.py:271
  19.9 0.1 collective-permute-done.4.from_right.refs_4_
  20.0 1.9 %collective-permute-start.6 = (bf16[1040,128]{1,0:T(8,128)(2,1)S(1)}, bf16[1040,128]{1,0:T(8,128)(2,1)S(1)}, u32[]{:S(2)}, u32[]{:S(2)}) collective-permute-start(bf16[1040,128]{1,0:T(8,128)(2,1)S(1)} %collective-permute-done.4.from_right.refs_4_), channel_id=1, source_target_pairs={{4,0},{8,4},{12,8},{14,12},{10,14},{6,10},{2,6},{0,2},{5,1},{9,5},... | collective-permute-start | bytes 798728 | tf_op jit(solution)/shard_map/ppermute | solution.py:250
  21.9 0.0 collective-permute-done.1.from_left.refs_3_
  21.9 0.2 collective-permute-start.3
  22.0 2.8 %shard_map.98.start = f32[2,512,256]{2,1,0:T(8,128)S(1)} custom-call(s32[11]{0:T(128)S(1)} %get-tuple-element.24.slots, s32[11]{0:T(128)S(1)} %get-tuple-element.25.cols, bf16[1040,128]{1,0:T(8,128)(2,1)S(1)} %collective-permute-done.1.from_left.refs_3_, ...), custom_call_target="tpu_custom_call", output_to_operand_aliasing={{}: (5, {})} | custom-call | flops 1048576 | bytes 1048576 | tf_op jit(solution)/shard_map/pallas_call | solution.py:275
  24.8 3.0 %collective-permute-done.6.from_right.refs_6_ = bf16[1040,128]{1,0:T(8,128)(2,1)S(1)} collective-permute-done((bf16[1040,128]{1,0:T(8,128)(2,1)S(1)}, bf16[1040,128]{1,0:T(8,128)(2,1)S(1)}, u32[]{:S(2)}, u32[]{:S(2)}) %collective-permute-start.6) | collective-permute-done | bytes 266272 | tf_op jit(solution)/shard_map/ppermute | solution.py:250
  27.9 1.7 %collective-permute-start.7 = (bf16[528,128]{1,0:T(8,128)(2,1)S(1)}, bf16[528,128]{1,0:T(8,128)(2,1)S(1)}, u32[]{:S(2)}, u32[]{:S(2)}) collective-permute-start(bf16[528,128]{1,0:T(8,128)(2,1)S(1)} %slice.7), channel_id=1, source_target_pairs={{4,0},{8,4},{12,8},{14,12},{10,14},{6,10},{2,6},{0,2},{5,1},{9,5},... | collective-permute-start | bytes 405512 | tf_op jit(solution)/shard_map/ppermute | solution.py:254
  29.5 0.0 collective-permute-done.3.from_left.refs_5_
  29.6 0.0 copy-start.10
  29.6 0.5 collective-permute-start.5
  30.0 2.9 %shard_map.99.start = f32[2,512,256]{2,1,0:T(8,128)S(1)} custom-call(s32[11]{0:T(128)S(1)} %get-tuple-element.24.slots, s32[11]{0:T(128)S(1)} %get-tuple-element.25.cols, bf16[1040,128]{1,0:T(8,128)(2,1)S(1)} %collective-permute-done.3.from_left.refs_5_, ...), custom_call_target="tpu_custom_call", output_to_operand_aliasing={{}: (5, {})} | custom-call | flops 1048576 | bytes 1048576 | tf_op jit(solution)/shard_map/pallas_call | solution.py:275
  32.9 1.7 %collective-permute-done.5.low = bf16[512,128]{1,0:T(8,128)(2,1)S(1)} collective-permute-done((bf16[512,128]{1,0:T(8,128)(2,1)S(1)}, bf16[512,128]{1,0:T(8,128)(2,1)S(1)}, u32[]{:S(2)}, u32[]{:S(2)}) %collective-permute-start.5) | collective-permute-done | bytes 131104 | tf_op jit(solution)/shard_map/ppermute | solution.py:253
  34.6 0.0 collective-permute-done.7.high.refs_7_
  34.6 0.0 copy-done.10
  34.6 2.1 %shard_map.100 = (f32[2,512,256]{2,1,0:T(8,128)S(1)}, f32[2,512,128]{2,1,0:T(8,128)S(1)}) custom-call(s32[11]{0:T(128)S(1)} %get-tuple-element.24.slots, s32[11]{0:T(128)S(1)} %get-tuple-element.25.cols, f32[2]{0:T(128)S(1)} %copy-done.10, bf16[512,128]{1,0:T(8,128)(2,1)S(1)} %collective-permute-done.5.low, ...), custom_call_target="tpu_custom_call", output_to_operand_aliasing={{0}: (6, {})} | custom-call | flops 1048576 | bytes 1048576 | tf_op jit(solution)/shard_map/pallas_call | solution.py:294
  36.7 0.1 collective-permute-start.9
  36.7 0.9 %shard_map.101 = (f32[2,2,256,128]{3,2,1,0:T(8,128)S(1)}, f32[2,2,256,128]{3,2,1,0:T(8,128)}) custom-call(f32[2,512,256]{2,1,0:T(8,128)S(1)} %get-tuple-element.40.acc), custom_call_target="tpu_custom_call" | custom-call | flops 1048576 | bytes 1048576 | tf_op jit(solution)/shard_map/pallas_call | solution.py:302
  37.6 0.5 collective-permute-start.8
  38.1 0.8 %shard_map.103.pick = bf16[1024,1024]{1,0:T(8,128)(2,1)S(1)} custom-call(bf16[1040,128]{1,0:T(8,128)(2,1)S(1)} %get-tuple-element.28.own.refs_0_, bf16[1040,128]{1,0:T(8,128)(2,1)S(1)} %collective-permute-done.from_left.refs_1_, bf16[1040,128]{1,0:T(8,128)(2,1)S(1)} %collective-permute-done.2.from_right.refs_2_, ...), custom_call_target="tpu_custom_call" | custom-call | flops 1048576 | bytes 1048576 | tf_op jit(solution)/shard_map/pallas_call | solution.py:318
  38.9 0.0 copy-start.7
  39.0 0.0 collective-permute-done.9.theirs
  39.0 1.4 %shard_map.104 = bf16[1024,128]{1,0:T(8,128)(2,1)} custom-call(bf16[1024,1024]{1,0:T(8,128)(2,1)S(1)} %shard_map.103.pick, f32[2,512,128]{2,1,0:T(8,128)S(1)} %get-tuple-element.43.mine, f32[2,512,128]{2,1,0:T(8,128)S(1)} %collective-permute-done.9.theirs), custom_call_target="tpu_custom_call" | custom-call | tf_op jit(solution)/shard_map/pallas_call | solution.py:330
  40.4 4.9 %all-to-all-start = ((bf16[8,128,128]{2,1,0:T(8,128)(2,1)}), bf16[8,128,128]{2,1,0:T(8,128)(2,1)S(1)}, u32[]{:S(2)}, u32[]{:S(2)}) async-start(bf16[8,128,128]{2,1,0:T(8,128)(2,1)} %bitcast.1), calls=%async_computation | async-start | bytes 524288 | tf_op jit(solution)/shard_map/all_to_all | solution.py:335
  45.3 0.0 copy-done.7
  45.3 0.0 copy-start.3
  45.3 1.0 %copy-done.3 = bf16[2,256,512]{2,1,0:T(8,128)(2,1)S(1)} copy-done((bf16[2,256,512]{2,1,0:T(8,128)(2,1)S(1)}, bf16[2,256,512]{2,1,0:T(8,128)(2,1)}, u32[]{:S(2)}) %copy-start.3) | copy-done | bytes 524312
  46.4 0.9 %copy-done.6 = bf16[2,128,512]{2,1,0:T(8,128)(2,1)S(1)} copy-done((bf16[2,128,512]{2,1,0:T(8,128)(2,1)S(1)}, bf16[2,128,512]{2,1,0:T(8,128)(2,1)}, u32[]{:S(2)}) %copy-start.6) | copy-done | bytes 262168
  47.3 0.9 %shard_map.105 = (bf16[2,1024,512]{2,1,0:T(8,128)(2,1)S(1)}, f32[2,128,512]{2,1,0:T(8,128)S(1)}) custom-call(s32[2,256]{1,0:T(2,128)S(1)} %copy-done.7, bf16[2,256,512]{2,1,0:T(8,128)(2,1)S(1)} %copy-done.3, bf16[2,128,512]{2,1,0:T(8,128)(2,1)S(1)} %copy-done.6), custom_call_target="tpu_custom_call" | custom-call | flops 1048576 | bytes 1048576 | tf_op jit(solution)/shard_map/pallas_call | solution.py:309
  48.2 0.8 %copy-done.4 = f32[2,128,512]{2,1,0:T(8,128)} copy-done((f32[2,128,512]{2,1,0:T(8,128)}, f32[2,128,512]{2,1,0:T(8,128)S(1)}, u32[]{:S(2)}) %copy-start.4) | copy-done | bytes 524312
  49.0 0.0 collective-permute-done.8.theirs
  49.0 0.8 %shard_map.102 = f32[2,2,256,128]{3,2,1,0:T(8,128)} custom-call(f32[2,2,256,128]{3,2,1,0:T(8,128)S(1)} %get-tuple-element.41.mine, f32[2,2,256,128]{3,2,1,0:T(8,128)S(1)} %collective-permute-done.8.theirs), custom_call_target="tpu_custom_call" | custom-call | flops 1048576 | bytes 1048576 | tf_op jit(solution)/shard_map/pallas_call | solution.py:336
  49.8 4.6 %all-to-all-done = bf16[8,128,128]{2,1,0:T(8,128)(2,1)S(1)} async-done(((bf16[8,128,128]{2,1,0:T(8,128)(2,1)}), bf16[8,128,128]{2,1,0:T(8,128)(2,1)S(1)}, u32[]{:S(2)}, u32[]{:S(2)}) %all-to-all-start) | async-done | bytes 262176 | tf_op jit(solution)/shard_map/all_to_all | solution.py:335
  54.4 1.0 %copy-done.5 = f32[2,128,512]{2,1,0:T(8,128)S(1)} copy-done((f32[2,128,512]{2,1,0:T(8,128)S(1)}, f32[2,128,512]{2,1,0:T(8,128)}, u32[]{:S(2)}) %copy-start.5) | copy-done | bytes 524312
  55.5 1.1 %shard_map.106 = f32[2,512]{1,0:T(2,128)} custom-call(bf16[1024,128]{1,0:T(8,128)(2,1)S(1)} %bitcast.3, bf16[2,1024,512]{2,1,0:T(8,128)(2,1)S(1)} %get-tuple-element.44.basis, f32[2,128,512]{2,1,0:T(8,128)S(1)} %copy-done.5), custom_call_target="tpu_custom_call" | custom-call | tf_op jit(solution)/shard_map/pallas_call | solution.py:342
  (10 shorter events, 0.0 us)
Async XLA Ops:
  2.3 9.8 %collective-permute-start.2 = (bf16[1040,128]{1,0:T(8,128)(2,1)}, bf16[1040,128]{1,0:T(8,128)(2,1)S(1)}, u32[]{:S(2)}, u32[]{:S(2)}) collective-permute-start(bf16[1040,128]{1,0:T(8,128)(2,1)} %shard_map.95.own), channel_id=1, source_target_pairs={{4,0},{8,4},{12,8},{14,12},{10,14},{6,10},{2,6},{0,2},{5,1},{9,5},... | collective-permute-start | bytes 798728 | tf_op jit(solution)/shard_map/ppermute | solution.py:250
  5.3 8.7 %collective-permute-start = (bf16[1040,128]{1,0:T(8,128)(2,1)}, bf16[1040,128]{1,0:T(8,128)(2,1)S(1)}, u32[]{:S(2)}, u32[]{:S(2)}) collective-permute-start(bf16[1040,128]{1,0:T(8,128)(2,1)} %shard_map.95.own), channel_id=1, source_target_pairs={{0,4},{4,8},{8,12},{12,14},{14,10},{10,6},{6,2},{2,0},{1,5},{5,9},... | collective-permute-start | bytes 798728 | tf_op jit(solution)/shard_map/ppermute | solution.py:249
  5.5 4.3 %copy-start = (bf16[11,2,512,512]{3,2,1,0:T(8,128)(2,1)S(1)}, bf16[11,2,512,512]{3,2,1,0:T(8,128)(2,1)}, u32[]{:S(2)}) copy-start(bf16[11,2,512,512]{3,2,1,0:T(8,128)(2,1)} %tiles.9) | copy-start | bytes 34603012
  9.7 1.0 %copy-start.2 = (bf16[1040,128]{1,0:T(8,128)(2,1)S(1)}, bf16[1040,128]{1,0:T(8,128)(2,1)}, u32[]{:S(2)}) copy-start(bf16[1040,128]{1,0:T(8,128)(2,1)} %shard_map.95.own) | copy-start | bytes 798724
  10.7 0.7 %copy-start.8 = (s32[11]{0:T(128)S(1)}, s32[11]{0:T(128)}, u32[]{:S(2)}) copy-start(s32[11]{0:T(128)} %slots.1) | copy-start | bytes 136
  11.4 0.7 %copy-start.9 = (s32[11]{0:T(128)S(1)}, s32[11]{0:T(128)}, u32[]{:S(2)}) copy-start(s32[11]{0:T(128)} %cols.1) | copy-start | bytes 136
  12.0 4.3 %copy-start.1 = (bf16[11,2,512,512]{3,2,1,0:T(8,128)(2,1)S(1)}, bf16[11,2,512,512]{3,2,1,0:T(8,128)(2,1)}, u32[]{:S(2)}) copy-start(bf16[11,2,512,512]{3,2,1,0:T(8,128)(2,1)} %tiles.9) | copy-start | bytes 34603012
  12.1 7.9 %collective-permute-start.4 = (bf16[1040,128]{1,0:T(8,128)(2,1)S(1)}, bf16[1040,128]{1,0:T(8,128)(2,1)S(1)}, u32[]{:S(2)}, u32[]{:S(2)}) collective-permute-start(bf16[1040,128]{1,0:T(8,128)(2,1)S(1)} %collective-permute-done.2.from_right.refs_2_), channel_id=1, source_target_pairs={{4,0},{8,4},{12,8},{14,12},{10,14},{6,10},{2,6},{0,2},{5,1},{9,5},... | collective-permute-start | bytes 798728 | tf_op jit(solution)/shard_map/ppermute | solution.py:250
  14.1 7.8 %collective-permute-start.1 = (bf16[1040,128]{1,0:T(8,128)(2,1)S(1)}, bf16[1040,128]{1,0:T(8,128)(2,1)S(1)}, u32[]{:S(2)}, u32[]{:S(2)}) collective-permute-start(bf16[1040,128]{1,0:T(8,128)(2,1)S(1)} %collective-permute-done.from_left.refs_1_), channel_id=1, source_target_pairs={{0,4},{4,8},{8,12},{12,14},{14,10},{10,6},{6,2},{2,0},{1,5},{5,9},... | collective-permute-start | bytes 798728 | tf_op jit(solution)/shard_map/ppermute | solution.py:249
  20.0 7.8 %collective-permute-start.6 = (bf16[1040,128]{1,0:T(8,128)(2,1)S(1)}, bf16[1040,128]{1,0:T(8,128)(2,1)S(1)}, u32[]{:S(2)}, u32[]{:S(2)}) collective-permute-start(bf16[1040,128]{1,0:T(8,128)(2,1)S(1)} %collective-permute-done.4.from_right.refs_4_), channel_id=1, source_target_pairs={{4,0},{8,4},{12,8},{14,12},{10,14},{6,10},{2,6},{0,2},{5,1},{9,5},... | collective-permute-start | bytes 798728 | tf_op jit(solution)/shard_map/ppermute | solution.py:250
  21.9 7.6 %collective-permute-start.3 = (bf16[1040,128]{1,0:T(8,128)(2,1)S(1)}, bf16[1040,128]{1,0:T(8,128)(2,1)S(1)}, u32[]{:S(2)}, u32[]{:S(2)}) collective-permute-start(bf16[1040,128]{1,0:T(8,128)(2,1)S(1)} %collective-permute-done.1.from_left.refs_3_), channel_id=1, source_target_pairs={{0,4},{4,8},{8,12},{12,14},{14,10},{10,6},{6,2},{2,0},{1,5},{5,9},... | collective-permute-start | bytes 798728 | tf_op jit(solution)/shard_map/ppermute | solution.py:249
  27.9 6.7 %collective-permute-start.7 = (bf16[528,128]{1,0:T(8,128)(2,1)S(1)}, bf16[528,128]{1,0:T(8,128)(2,1)S(1)}, u32[]{:S(2)}, u32[]{:S(2)}) collective-permute-start(bf16[528,128]{1,0:T(8,128)(2,1)S(1)} %slice.7), channel_id=1, source_target_pairs={{4,0},{8,4},{12,8},{14,12},{10,14},{6,10},{2,6},{0,2},{5,1},{9,5},... | collective-permute-start | bytes 405512 | tf_op jit(solution)/shard_map/ppermute | solution.py:254
  29.6 5.0 %copy-start.10 = (f32[2]{0:T(128)S(1)}, f32[2]{0:T(128)}, u32[]{:S(2)}) copy-start(f32[2]{0:T(128)} %pole_weight.1) | copy-start | bytes 28
  29.6 5.0 %collective-permute-start.5 = (bf16[512,128]{1,0:T(8,128)(2,1)S(1)}, bf16[512,128]{1,0:T(8,128)(2,1)S(1)}, u32[]{:S(2)}, u32[]{:S(2)}) collective-permute-start(bf16[512,128]{1,0:T(8,128)(2,1)S(1)} %slice.6), channel_id=1, source_target_pairs={{0,4},{4,8},{8,12},{12,14},{14,10},{10,6},{6,2},{2,0},{1,5},{5,9},... | collective-permute-start | bytes 393224 | tf_op jit(solution)/shard_map/ppermute | solution.py:253
  36.7 2.3 %collective-permute-start.9 = (f32[2,512,128]{2,1,0:T(8,128)S(1)}, f32[2,512,128]{2,1,0:T(8,128)S(1)}, u32[]{:S(2)}, u32[]{:S(2)}) collective-permute-start(f32[2,512,128]{2,1,0:T(8,128)S(1)} %get-tuple-element.43.mine), channel_id=1, source_target_pairs={{0,1},{1,0},{2,3},{3,2},{4,5},{5,4},{6,7},{7,6},{8,9},{9,8},{10,11... | collective-permute-start | bytes 1572872 | tf_op jit(solution)/shard_map/ppermute | solution.py:328
  37.6 11.4 %collective-permute-start.8 = (f32[2,2,256,128]{3,2,1,0:T(8,128)}, f32[2,2,256,128]{3,2,1,0:T(8,128)S(1)}, u32[]{:S(2)}, u32[]{:S(2)}) collective-permute-start(f32[2,2,256,128]{3,2,1,0:T(8,128)} %get-tuple-element.42), channel_id=1, source_target_pairs={{0,1},{1,0},{2,3},{3,2},{4,5},{5,4},{6,7},{7,6},{8,9},{9,8},{10,11... | collective-permute-start | bytes 1572872 | tf_op jit(solution)/shard_map/ppermute | solution.py:329
  38.9 6.4 %copy-start.7 = (s32[2,256]{1,0:T(2,128)S(1)}, s32[2,256]{1,0:T(2,128)}, u32[]{:S(2)}) copy-start(s32[2,256]{1,0:T(2,128)} %wanted.3) | copy-start | bytes 6148
  40.4 14.0 %all-to-all-start = ((bf16[8,128,128]{2,1,0:T(8,128)(2,1)}), bf16[8,128,128]{2,1,0:T(8,128)(2,1)S(1)}, u32[]{:S(2)}, u32[]{:S(2)}) async-start(bf16[8,128,128]{2,1,0:T(8,128)(2,1)} %bitcast.1), calls=%async_computation | async-start | bytes 524288 | tf_op jit(solution)/shard_map/all_to_all | solution.py:335
  45.3 1.0 %copy-start.3 = (bf16[2,256,512]{2,1,0:T(8,128)(2,1)S(1)}, bf16[2,256,512]{2,1,0:T(8,128)(2,1)}, u32[]{:S(2)}) copy-start(bf16[2,256,512]{2,1,0:T(8,128)(2,1)} %basis.1) | copy-start | bytes 1572868
  46.4 0.9 %copy-start.6 = (bf16[2,128,512]{2,1,0:T(8,128)(2,1)S(1)}, bf16[2,128,512]{2,1,0:T(8,128)(2,1)}, u32[]{:S(2)}) copy-start(bf16[2,128,512]{2,1,0:T(8,128)(2,1)} %supernode.1) | copy-start | bytes 786436
  48.2 0.8 %copy-start.4 = (f32[2,128,512]{2,1,0:T(8,128)}, f32[2,128,512]{2,1,0:T(8,128)S(1)}, u32[]{:S(2)}) copy-start(f32[2,128,512]{2,1,0:T(8,128)S(1)} %get-tuple-element.45.supernode) | copy-start | bytes 1572868
  54.4 1.0 %copy-start.5 = (f32[2,128,512]{2,1,0:T(8,128)S(1)}, f32[2,128,512]{2,1,0:T(8,128)}, u32[]{:S(2)}) copy-start(f32[2,128,512]{2,1,0:T(8,128)} %copy-done.4) | copy-start | bytes 1572868

commit v5 on v4

--- a/solution.py
+++ b/solution.py
@@ -12,7 +12,7 @@
 F32 = jnp.float32
 BF16 = jnp.bfloat16
 VMEM_LIMIT = 8 * 1024 * 1024
-PACK_LIMIT = 56 * 1024 * 1024
+PACK_LIMIT = 8 * 1024 * 1024
 
 
 def ring_order(n):
@@ -139,6 +139,14 @@
     return (first < second).astype(F32).astype(BF16)
 
 
+def place_of(chip, n):
+    apart = chip ^ lax.axis_index("row")
+    top = (apart >= n // 2).astype(jnp.int32)
+    step = jnp.where(top == 1, apart - n // 2, apart - 1)
+    other = (top != lax.axis_index("col")).astype(jnp.int32)
+    return jnp.where(apart == 0, 0, 1 + other * (n // 2) + step)
+
+
 def basis_kernel(wanted, basis, supernode, out, wide, *, n, rows_chip, slots):
     wide[...] = supernode[...].astype(F32)
     boxes, orbitals, _ = basis.shape
@@ -149,20 +157,36 @@
     marks = (lax.broadcasted_iota(jnp.int32, (n, total), 0) == source).astype(F32)
     counts = jnp.dot(marks.astype(BF16), earlier(total), preferred_element_type=F32)
     rank = jnp.sum(marks * counts, axis=0, keepdims=True).astype(jnp.int32)
-    slot = source * slots + rank
+    slot = place_of(source, n) * slots + rank
     index = lax.broadcasted_iota(jnp.int32, (out.shape[1], orbitals), 0)
     for b in range(boxes):
         pick = (index == slot[:, b * orbitals:(b + 1) * orbitals]).astype(F32).astype(BF16)
         out[b] = jnp.dot(pick, basis[b], preferred_element_type=F32).astype(BF16)
 
 
-def pick_kernel(*refs, n, hops, total, rows_chip, slots):
+def lines_kernel(*refs, n, hops, lines):
     *shards, out = refs
-    lines = -(-2 * total // (16 * LANES)) * 16
-    asked = jnp.concatenate(
-        [undigits(ref[ref.shape[0] - lines:, :], total) for ref in shards], axis=0
-    ).astype(jnp.int32)
-    here = (asked // rows_chip) == lax.axis_index("row")
+    for ref, hop in zip(shards, hops):
+        at = pl.multiple_of(shard_row(n, hop) * lines, lines)
+        out[pl.ds(at, lines), :] = ref[ref.shape[0] - lines:, :]
+
+
+def pick_kernel(mine, theirs, out, *, n, lines, total, rows_chip, slots):
+    row = lax.axis_index("row")
+    col = lax.axis_index("col")
+    first = jnp.where(col == 0, 1, n // 2)
+
+    def asked_by(chip, own):
+        at = pl.ds(pl.multiple_of(chip * lines, lines), lines)
+        return undigits(jnp.where(own, mine[at, :].astype(F32), theirs[at, :].astype(F32)), total)
+
+    asked = [asked_by(row, True)]
+    for step in range(n // 2):
+        chip = row ^ jnp.minimum(first + step, n - 1)
+        asked += [asked_by(chip, col == 0), asked_by(chip, col == 1)]
+    count = len(asked)
+    asked = jnp.concatenate(asked, axis=0).astype(jnp.int32)
+    here = (asked // rows_chip) == row
     local = (asked % rows_chip).astype(F32)
     rank = jnp.dot(
         here.astype(F32).astype(BF16), earlier(total), preferred_element_type=F32
@@ -170,27 +194,35 @@
     rank = jnp.where(here, rank, -1)
     index = lax.broadcasted_iota(jnp.int32, (slots, total), 0)
     lane = lax.broadcasted_iota(jnp.int32, (slots, rows_chip), 1)
-    for d, hop in enumerate(hops):
+    for d in range(count):
         chosen = jnp.where(index == rank[d:d + 1], local[d:d + 1], 0.0)
-        row = jnp.sum(chosen, axis=1, keepdims=True).astype(jnp.int32)
-        at = pl.multiple_of(shard_row(n, hop) * slots, slots)
-        out[pl.ds(at, slots), :] = (lane == row).astype(F32).astype(BF16)
+        at = jnp.sum(chosen, axis=1, keepdims=True).astype(jnp.int32)
+        out[d * slots:(d + 1) * slots, :] = (lane == at).astype(F32).astype(BF16)
 
 
 def add_kernel(mine, theirs, out):
     out[...] = mine[...] + theirs[...]
 
 
-def select_kernel(pick, mine, theirs, out):
+def select_kernel(pick, mine, theirs, *outs):
     rows = pick.shape[1]
     total = (mine[...] + theirs[...]).reshape(rows, mine.shape[2]).astype(BF16)
-    out[...] = jnp.dot(pick[...], total, preferred_element_type=F32).astype(BF16)
-
-
-def density_kernel(arrived, basis, supernode, out):
+    rows_out = jnp.dot(pick[...], total, preferred_element_type=F32).astype(BF16)
+    at = 0
+    for out in outs:
+        out[...] = rows_out[at:at + out.shape[0]]
+        at += out.shape[0]
+
+
+def density_kernel(*refs):
+    *parts, basis, supernode, out = refs
+    own = parts[0]
+    slots = own.shape[0]
+    at = pl.ds(pl.multiple_of(lax.axis_index("col") * slots, slots), slots)
+    arrived = jnp.concatenate([own[...]] + [part[at, :] for part in parts[1:]], axis=0)
     for n in range(basis.shape[0]):
         projected = lax.dot_general(
-            arrived[...], basis[n], (((0,), (0,)), ((), ())), preferred_element_type=F32
+            arrived, basis[n], (((0,), (0,)), ((), ())), preferred_element_type=F32
         )
         out[n:n + 1, :] = jnp.sum(supernode[n] * projected, axis=0, keepdims=True)
 
@@ -206,7 +238,7 @@
     total = boxes * orbitals
     rows_chip = BR_DEV * order_b
     slots = 2 * total // n_row
-    arrive = n_row * slots
+    arrive = (1 + 2 * half_ring) * slots
     half = order_b // 2
     shard_rows = blocks * parts * depth
     lines = -(-2 * total // (16 * LANES)) * 16
@@ -240,6 +272,16 @@
         compiler_params=pltpu.CompilerParams(vmem_limit_bytes=PACK_LIMIT),
         cost_estimate=cost,
     )(panel.reshape(shard_rows, width), box_orbitals)
+
+    basis_here, wide = pl.pallas_call(
+        functools.partial(basis_kernel, n=n_row, rows_chip=rows_chip, slots=slots),
+        out_shape=[
+            jax.ShapeDtypeStruct((boxes, arrive, box_basis.shape[2]), BF16),
+            jax.ShapeDtypeStruct(supernode_basis.shape, F32),
+        ],
+        compiler_params=params,
+        cost_estimate=cost,
+    )(box_orbitals, box_basis, supernode_basis)
 
     left, right = own, own
     seen, hops = [own], [0]
@@ -280,6 +322,8 @@
                 2,
                 aliases={5: 0},
             )(tile_slot, tile_col, left, right, tiles, acc)
+        if h == half_ring - 1:
+            next_left, basis_here, wide = lax.optimization_barrier((next_left, basis_here, wide))
         left, done = lax.optimization_barrier((next_left, acc))
         right, _ = lax.optimization_barrier((next_right, acc))
         acc = done
@@ -290,6 +334,16 @@
             seen.append(right)
             hops.append(h)
 
+    swap = [(0, 1), (1, 0)]
+    wanted = pl.pallas_call(
+        functools.partial(lines_kernel, n=n_row, hops=hops, lines=lines),
+        out_shape=jax.ShapeDtypeStruct((n_row * lines, width), BF16),
+        compiler_params=params,
+        cost_estimate=cost,
+    )(*seen)
+    left, wanted = lax.optimization_barrier((left, wanted))
+    wanted_other = lax.ppermute(wanted, "col", swap)
+
     half_shape = (BR_DEV, 2, half, width)
     acc, dens = call(
         hop_last,
@@ -299,51 +353,51 @@
         1,
         aliases={6: 0},
     )(tile_slot, tile_col, pole_weight, left, right, tiles, acc)
+    dens_other = lax.ppermute(dens, "col", swap)
+    pick = pl.pallas_call(
+        functools.partial(
+            pick_kernel, n=n_row, lines=lines, total=total, rows_chip=rows_chip, slots=slots
+        ),
+        out_shape=jax.ShapeDtypeStruct((arrive, rows_chip), BF16),
+        compiler_params=params,
+        cost_estimate=cost,
+    )(wanted, wanted_other)
+    message = jax.ShapeDtypeStruct((2 * slots, width), BF16)
+    kept, *sent = pl.pallas_call(
+        select_kernel,
+        out_shape=[jax.ShapeDtypeStruct((slots, width), BF16)] + [message] * half_ring,
+        compiler_params=params,
+        cost_estimate=cost,
+    )(pick, dens, dens_other)
+
+    fetched, passed = [], []
+    for step in range(half_ring):
+        pairs = [(2 * r + 1, 2 * (r ^ (half_ring + step)) + 1) for r in range(n_row)]
+        if step + 1 < half_ring:
+            pairs += [(2 * r, 2 * (r ^ (1 + step))) for r in range(n_row)]
+        fetched.append(lax.ppermute(sent[step], ("row", "col"), pairs))
+        passed.append(lax.ppermute(fetched[-1], "col", swap))
+
+    acc, fetched[0] = lax.optimization_barrier((acc, fetched[0]))
     mine, other = pl.pallas_call(
         halves_kernel,
         out_shape=[jax.ShapeDtypeStruct(half_shape, F32)] * 2,
         compiler_params=params,
         cost_estimate=cost,
     )(acc)
-
-    basis_here, wide = pl.pallas_call(
-        functools.partial(basis_kernel, n=n_row, rows_chip=rows_chip, slots=slots),
-        out_shape=[
-            jax.ShapeDtypeStruct((boxes, arrive, box_basis.shape[2]), BF16),
-            jax.ShapeDtypeStruct(supernode_basis.shape, F32),
-        ],
-        compiler_params=params,
-        cost_estimate=cost,
-    )(box_orbitals, box_basis, supernode_basis)
-    pick = pl.pallas_call(
-        functools.partial(
-            pick_kernel, n=n_row, hops=hops, total=total, rows_chip=rows_chip, slots=slots
-        ),
-        out_shape=jax.ShapeDtypeStruct((arrive, rows_chip), BF16),
-        compiler_params=params,
-        cost_estimate=cost,
-    )(*seen)
-
-    swap = [(0, 1), (1, 0)]
-    dens_other = lax.ppermute(dens, "col", swap)
     inverse_other = lax.ppermute(other, "col", swap)
-    send = pl.pallas_call(
-        select_kernel,
-        out_shape=jax.ShapeDtypeStruct((arrive, width), BF16),
-        compiler_params=params,
-    )(pick, dens, dens_other)
-    arrived = lax.all_to_all(send, "row", 0, 0, tiled=True)
     inverse = pl.pallas_call(
         add_kernel,
         out_shape=jax.ShapeDtypeStruct(half_shape, F32),
         compiler_params=params,
         cost_estimate=cost,
     )(mine, inverse_other)
+    kept, inverse = lax.optimization_barrier((kept, inverse))
     density = pl.pallas_call(
         density_kernel,
         out_shape=jax.ShapeDtypeStruct((boxes, box_basis.shape[2]), F32),
         compiler_params=params,
-    )(arrived, basis_here, wide)
+    )(kept, *fetched, *passed, basis_here, wide)
     return inverse, density
 
 

time: 57 us -> 60 us (1.053)
  starting transfers between devices: 14.8 us -> 24.3 us
  local copies, waits for them, and re-layouts: 12.5 us -> 8.76 us
  Pallas kernels: 19 us -> 16.3 us
    ppermute x0 -> x9, starting transfers between devices: none -> 14.3 us  [the longest x4 8.86 us: local(): passed.append(lax.ppermute(fetched[-1], 'col', swap))]
    all_to_all x1 -> x0, starting transfers between devices: 4.9 us -> none  [local(): arrived = lax.all_to_all(send, 'row', 0, 0, tiled=True)]
    all_to_all x1 -> x0, waiting for transfers between devices: 4.57 us -> none  [local(): arrived = lax.all_to_all(send, 'row', 0, 0, tiled=True)]
    ppermute x0 -> x9, waiting for transfers between devices: none -> 4.17 us  [the longest x4 2.68 us: local(): fetched.append(lax.ppermute(sent[step], ('row', 'col'), pairs))]
    unnamed x22 -> x20, local copies, waits for them, and re-layouts: 12.5 us -> 8.74 us
    pallas_call x1, Pallas kernels: 1.69 us -> 0.06 us  [local(): pl.pallas_call(pack_kernel, in_specs=[in_hbm, in_hbm], out_specs=in_vmem,...]
    pallas_call x1, Pallas kernels: 0.87 us -> 0.07 us  [local(): pl.pallas_call(halves_kernel, out_shape=[jax.ShapeDtypeStruct(half_shape,...]
    ppermute x3, waiting for transfers between devices: 3.13 us -> 3.75 us  [local(): next_right = lax.ppermute(right, 'row', to_left)]
  transfers between devices with their start and end apart: 11 -> 19, of which waited for: 4 -> 6; matrix products, arithmetic and copies ran while one was open for 0% -> 0% of each run, Pallas kernels for 25% -> 20%
where the time goes in v5:
time: 60 us; the launch traced here: 59.8 us
  starting transfers between devices  24.3 us (40%)
  Pallas kernels  16.3 us (27%)
  waiting for transfers between devices  9.66 us (16%)
  local copies, waits for them, and re-layouts  8.76 us (15%)
  between operations  0.82 us (1%)
    ppermute x4, starting transfers between devices, local(): passed.append(lax.ppermute(fetched[-1], 'col', swap))  8.86 us
    unnamed x20, local copies, waits for them, and re-layouts  8.74 us
    ppermute x3, starting transfers between devices, local(): next_right = lax.ppermute(right, 'row', to_left)  6.3 us
    pallas_call x2, Pallas kernels, local(): call(functools.partial(hop_middle, hop=h - 1), [in_smem] * 2 + [in_vmem]...  5.63 us
    ppermute x4, starting transfers between devices, local(): fetched.append(lax.ppermute(sent[step], ('row', 'col'), pairs))  4.98 us
    ppermute x3, waiting for transfers between devices, local(): next_right = lax.ppermute(right, 'row', to_left)  3.75 us
    pallas_call x1, Pallas kernels, local(): call(hop_early, [in_smem] * 2 + [in_vmem] * 5, acc_out, [], 3, aliases={6...  3.64 us
    ppermute x4, waiting for transfers between devices, local(): fetched.append(lax.ppermute(sent[step], ('row', 'col'), pairs))  2.68 us
  transfers between devices with their start and end apart: 19, of which 6 were waited for; matrix products, arithmetic and copies ran while one was open for 0% of the time, Pallas kernels for 20%

profile of v5, /device:TPU:0, one launch (start us, length us, event | category | flops | bytes accessed | tf_op | source)
XLA Modules:
  0.0 59.8 jit_solution(11739068903352752412)
XLA Ops:
  0.6 0.9 %copy-done.4 = bf16[1,8,2,64,128]{4,3,2,1,0:T(8,128)(2,1)S(1)} copy-done((bf16[1,8,2,64,128]{4,3,2,1,0:T(8,128)(2,1)S(1)}, bf16[1,8,2,64,128]{4,3,2,1,0:T(8,128)(2,1)}, u32[]{:S(2)}) %copy-start.4) | copy-done | bytes 262168
  1.6 0.7 %copy-done.5 = s32[2,256]{1,0:T(2,128)S(1)} copy-done((s32[2,256]{1,0:T(2,128)S(1)}, s32[2,256]{1,0:T(2,128)}, u32[]{:S(2)}) %copy-start.5) | copy-done | bytes 2072
  2.3 0.1 shard_map.95.own
  2.3 3.0 %collective-permute-start.2 = (bf16[1040,128]{1,0:T(8,128)(2,1)S(1)}, bf16[1040,128]{1,0:T(8,128)(2,1)S(1)}, u32[]{:S(2)}, u32[]{:S(2)}) collective-permute-start(bf16[1040,128]{1,0:T(8,128)(2,1)S(1)} %shard_map.95.own), channel_id=1, source_target_pairs={{4,0},{8,4},{12,8},{14,12},{10,14},{6,10},{2,6},{0,2},{5,1},{9,5},... | collective-permute-start | bytes 798728 | tf_op jit(solution)/shard_map/ppermute | solution.py:292
  5.3 0.1 collective-permute-start
  5.5 4.3 %copy-done = bf16[11,2,512,512]{3,2,1,0:T(8,128)(2,1)S(1)} copy-done((bf16[11,2,512,512]{3,2,1,0:T(8,128)(2,1)S(1)}, bf16[11,2,512,512]{3,2,1,0:T(8,128)(2,1)}, u32[]{:S(2)}) %copy-start) | copy-done | bytes 11534360
  9.7 0.7 %copy-done.7 = s32[11]{0:T(128)S(1)} copy-done((s32[11]{0:T(128)S(1)}, s32[11]{0:T(128)}, u32[]{:S(2)}) %copy-start.7) | copy-done | bytes 68
  10.4 0.7 %copy-done.8 = s32[11]{0:T(128)S(1)} copy-done((s32[11]{0:T(128)S(1)}, s32[11]{0:T(128)}, u32[]{:S(2)}) %copy-start.8) | copy-done | bytes 68
  11.1 0.1 shard_map.96
  11.1 0.6 %collective-permute-done.2.from_right.refs_2_ = bf16[1040,128]{1,0:T(8,128)(2,1)S(1)} collective-permute-done((bf16[1040,128]{1,0:T(8,128)(2,1)S(1)}, bf16[1040,128]{1,0:T(8,128)(2,1)S(1)}, u32[]{:S(2)}, u32[]{:S(2)}) %collective-permute-start.2) | collective-permute-done | bytes 266272 | tf_op jit(solution)/shard_map/ppermute | solution.py:292
  11.8 1.7 %collective-permute-start.4 = (bf16[1040,128]{1,0:T(8,128)(2,1)S(1)}, bf16[1040,128]{1,0:T(8,128)(2,1)S(1)}, u32[]{:S(2)}, u32[]{:S(2)}) collective-permute-start(bf16[1040,128]{1,0:T(8,128)(2,1)S(1)} %collective-permute-done.2.from_right.refs_2_), channel_id=1, source_target_pairs={{4,0},{8,4},{12,8},{14,12},{10,14},{6,10},{2,6},{0,2},{5,1},{9,5},... | collective-permute-start | bytes 798728 | tf_op jit(solution)/shard_map/ppermute | solution.py:292
  13.5 0.3 collective-permute-start.1
  13.8 1.5 %copy-done.1 = bf16[11,2,512,512]{3,2,1,0:T(8,128)(2,1)S(1)} copy-done((bf16[11,2,512,512]{3,2,1,0:T(8,128)(2,1)S(1)}, bf16[11,2,512,512]{3,2,1,0:T(8,128)(2,1)}, u32[]{:S(2)}) %copy-start.1) | copy-done | bytes 11534360
  15.3 3.6 %shard_map.97.start = f32[2,512,256]{2,1,0:T(8,128)S(1)} custom-call(s32[11]{0:T(128)S(1)} %get-tuple-element.40.slots, s32[11]{0:T(128)S(1)} %get-tuple-element.41.cols, bf16[1040,128]{1,0:T(8,128)(2,1)S(1)} %get-tuple-element.42.own.refs_0_, bf16[1040,128]{1,0:T(8,128)(2,1)S(1)} %collective-permute-done.from_left.refs_1_, ...), custom_call_target="tpu_custom_call", output_to_operand_aliasing={{}: (6, {})} | custom-call | flops 1048576 | bytes 1048576 | tf_op jit(solution)/shard_map/pallas_call | solution.py:313
  19.0 0.0 copy-start.2
  19.0 0.0 copy-start.3
  19.0 0.0 copy-start.6
  19.0 0.4 collective-permute-done.4.from_right.refs_4_
  19.4 1.6 %collective-permute-start.6 = (bf16[1040,128]{1,0:T(8,128)(2,1)S(1)}, bf16[1040,128]{1,0:T(8,128)(2,1)S(1)}, u32[]{:S(2)}, u32[]{:S(2)}) collective-permute-start(bf16[1040,128]{1,0:T(8,128)(2,1)S(1)} %collective-permute-done.4.from_right.refs_4_), channel_id=1, source_target_pairs={{4,0},{8,4},{12,8},{14,12},{10,14},{6,10},{2,6},{0,2},{5,1},{9,5},... | collective-permute-start | bytes 798728 | tf_op jit(solution)/shard_map/ppermute | solution.py:292
  21.0 0.4 collective-permute-start.3
  21.4 2.8 %shard_map.99.start = f32[2,512,256]{2,1,0:T(8,128)S(1)} custom-call(s32[11]{0:T(128)S(1)} %get-tuple-element.40.slots, s32[11]{0:T(128)S(1)} %get-tuple-element.41.cols, bf16[1040,128]{1,0:T(8,128)(2,1)S(1)} %collective-permute-done.1.from_left.refs_3_, ...), custom_call_target="tpu_custom_call", output_to_operand_aliasing={{}: (5, {})} | custom-call | flops 1048576 | bytes 1048576 | tf_op jit(solution)/shard_map/pallas_call | solution.py:317
  24.2 2.7 %collective-permute-done.6.from_right.refs_6_ = bf16[1040,128]{1,0:T(8,128)(2,1)S(1)} collective-permute-done((bf16[1040,128]{1,0:T(8,128)(2,1)S(1)}, bf16[1040,128]{1,0:T(8,128)(2,1)S(1)}, u32[]{:S(2)}, u32[]{:S(2)}) %collective-permute-start.6) | collective-permute-done | bytes 266272 | tf_op jit(solution)/shard_map/ppermute | solution.py:292
  27.0 1.7 %collective-permute-start.7 = (bf16[528,128]{1,0:T(8,128)(2,1)S(1)}, bf16[528,128]{1,0:T(8,128)(2,1)S(1)}, u32[]{:S(2)}, u32[]{:S(2)}) collective-permute-start(bf16[528,128]{1,0:T(8,128)(2,1)S(1)} %slice.7), channel_id=1, source_target_pairs={{4,0},{8,4},{12,8},{14,12},{10,14},{6,10},{2,6},{0,2},{5,1},{9,5},... | collective-permute-start | bytes 405512 | tf_op jit(solution)/shard_map/ppermute | solution.py:296
  28.6 1.0 %shard_map.98 = (bf16[2,1152,512]{2,1,0:T(8,128)(2,1)S(1)}, f32[2,128,512]{2,1,0:T(8,128)S(1)}) custom-call(s32[2,256]{1,0:T(2,128)S(1)} %copy-done.6, bf16[2,256,512]{2,1,0:T(8,128)(2,1)S(1)} %copy-done.2, bf16[2,128,512]{2,1,0:T(8,128)(2,1)S(1)} %copy-done.3), custom_call_target="tpu_custom_call" | custom-call | flops 1048576 | bytes 1048576 | tf_op jit(solution)/shard_map/pallas_call | solution.py:276
  29.6 0.4 collective-permute-start.5
  30.1 2.9 %shard_map.100.start = f32[2,512,256]{2,1,0:T(8,128)S(1)} custom-call(s32[11]{0:T(128)S(1)} %get-tuple-element.40.slots, s32[11]{0:T(128)S(1)} %get-tuple-element.41.cols, bf16[1040,128]{1,0:T(8,128)(2,1)S(1)} %collective-permute-done.3.from_left.refs_5_, ...), custom_call_target="tpu_custom_call", output_to_operand_aliasing={{}: (5, {})} | custom-call | flops 1048576 | bytes 1048576 | tf_op jit(solution)/shard_map/pallas_call | solution.py:317
  33.0 1.7 %collective-permute-done.5.low = bf16[512,128]{1,0:T(8,128)(2,1)S(1)} collective-permute-done((bf16[512,128]{1,0:T(8,128)(2,1)S(1)}, bf16[512,128]{1,0:T(8,128)(2,1)S(1)}, u32[]{:S(2)}, u32[]{:S(2)}) %collective-permute-start.5) | collective-permute-done | bytes 131104 | tf_op jit(solution)/shard_map/ppermute | solution.py:295
  34.7 0.1 shard_map.101.mine
  34.7 2.1 %shard_map.103 = (f32[2,512,256]{2,1,0:T(8,128)S(1)}, f32[2,512,128]{2,1,0:T(8,128)S(1)}) custom-call(s32[11]{0:T(128)S(1)} %get-tuple-element.40.slots, s32[11]{0:T(128)S(1)} %get-tuple-element.41.cols, f32[2]{0:T(128)S(1)} %copy-done.9, bf16[512,128]{1,0:T(8,128)(2,1)S(1)} %collective-permute-done.5.low, ...), custom_call_target="tpu_custom_call", output_to_operand_aliasing={{0}: (6, {})} | custom-call | flops 1048576 | bytes 1048576 | tf_op jit(solution)/shard_map/pallas_call | solution.py:348
  36.8 0.1 collective-permute-start.9
  36.9 0.5 collective-permute-start.8
  37.4 1.4 %collective-permute-done.8.theirs = bf16[128,128]{1,0:T(8,128)(2,1)S(1)} collective-permute-done((bf16[128,128]{1,0:T(8,128)(2,1)S(1)}, bf16[128,128]{1,0:T(8,128)(2,1)S(1)}, u32[]{:S(2)}, u32[]{:S(2)}) %collective-permute-start.8) | collective-permute-done | bytes 32800 | tf_op jit(solution)/shard_map/ppermute | solution.py:345
  38.8 0.9 %shard_map.102.pick = bf16[1152,1024]{1,0:T(8,128)(2,1)S(1)} custom-call(bf16[128,128]{1,0:T(8,128)(2,1)S(1)} %shard_map.101.mine, bf16[128,128]{1,0:T(8,128)(2,1)S(1)} %collective-permute-done.8.theirs), custom_call_target="tpu_custom_call" | custom-call | flops 1048576 | bytes 1048576 | tf_op jit(solution)/shard_map/pallas_call | solution.py:357
  39.8 0.8 %shard_map.104 = (bf16[128,128]{1,0:T(8,128)(2,1)S(1)}, bf16[256,128]{1,0:T(8,128)(2,1)S(1)}, bf16[256,128]{1,0:T(8,128)(2,1)S(1)}, bf16[256,128]{1,0:T(8,128)(2,1)S(1)}, bf16[256,128]{1,0:T(8,128)(2,1)S(1)}) custom-call(bf16[1152,1024]{1,0:T(8,128)(2,1)S(1)} %shard_map.102.pick, f32[2,512,128]{2,1,0:T(8,128)S(1)} %get-tuple-element.59.mine, ...), custom_call_target="tpu_custom_call" | custom-call | flops 1048576 | bytes 1048576 | tf_op jit(solution)/shard_map/pallas_call | solution.py:366
  40.6 1.7 %collective-permute-start.10 = (bf16[256,128]{1,0:T(8,128)(2,1)S(1)}, bf16[256,128]{1,0:T(8,128)(2,1)S(1)}, u32[]{:S(2)}, u32[]{:S(2)}) collective-permute-start(bf16[256,128]{1,0:T(8,128)(2,1)S(1)} %get-tuple-element.62), channel_id=1, source_target_pairs={{1,9},{3,11},{5,13},{7,15},{9,1},{11,3},{13,5},{15,7},{0,2},{2,0},... | collective-permute-start | bytes 196616 | tf_op jit(solution)/shard_map/ppermute | solution.py:378
  42.2 2.7 %collective-permute-done.10.refs_1_ = bf16[256,128]{1,0:T(8,128)(2,1)S(1)} collective-permute-done((bf16[256,128]{1,0:T(8,128)(2,1)S(1)}, bf16[256,128]{1,0:T(8,128)(2,1)S(1)}, u32[]{:S(2)}, u32[]{:S(2)}) %collective-permute-start.10) | collective-permute-done | bytes 65568 | tf_op jit(solution)/shard_map/ppermute | solution.py:378
  44.9 0.1 shard_map.105
  45.0 0.5 collective-permute-start.11
  45.5 0.8 %collective-permute-start.12 = (bf16[256,128]{1,0:T(8,128)(2,1)S(1)}, bf16[256,128]{1,0:T(8,128)(2,1)S(1)}, u32[]{:S(2)}, u32[]{:S(2)}) collective-permute-start(bf16[256,128]{1,0:T(8,128)(2,1)S(1)} %get-tuple-element.69), channel_id=1, source_target_pairs={{1,11},{3,9},{5,15},{7,13},{9,3},{11,1},{13,7},{15,5},{0,4},{2,6},... | collective-permute-start | bytes 196616 | tf_op jit(solution)/shard_map/ppermute | solution.py:378
  46.3 1.9 %collective-permute-start.13 = (bf16[256,128]{1,0:T(8,128)(2,1)S(1)}, bf16[256,128]{1,0:T(8,128)(2,1)S(1)}, u32[]{:S(2)}, u32[]{:S(2)}) collective-permute-start(bf16[256,128]{1,0:T(8,128)(2,1)S(1)} %get-tuple-element.70), channel_id=1, source_target_pairs={{1,13},{3,15},{5,9},{7,11},{9,5},{11,7},{13,1},{15,3},{0,6},{2,4},... | collective-permute-start | bytes 196616 | tf_op jit(solution)/shard_map/ppermute | solution.py:378
  48.2 0.7 %collective-permute-start.14 = (bf16[256,128]{1,0:T(8,128)(2,1)S(1)}, bf16[256,128]{1,0:T(8,128)(2,1)S(1)}, u32[]{:S(2)}, u32[]{:S(2)}) collective-permute-start(bf16[256,128]{1,0:T(8,128)(2,1)S(1)} %get-tuple-element.71), channel_id=1, source_target_pairs={{1,15},{3,13},{5,11},{7,9},{9,7},{11,5},{13,3},{15,1},{17,31},{19,... | collective-permute-start | bytes 196616 | tf_op jit(solution)/shard_map/ppermute | solution.py:378
  48.8 4.7 %collective-permute-start.15 = (bf16[256,128]{1,0:T(8,128)(2,1)S(1)}, bf16[256,128]{1,0:T(8,128)(2,1)S(1)}, u32[]{:S(2)}, u32[]{:S(2)}) collective-permute-start(bf16[256,128]{1,0:T(8,128)(2,1)S(1)} %collective-permute-done.10.refs_1_), channel_id=1, source_target_pairs={{0,1},{1,0},{2,3},{3,2},{4,5},{5,4},{6,7},{7,6},{8,9},{9,8},{10,11... | collective-permute-start | bytes 196616 | tf_op jit(solution)/shard_map/ppermute | solution.py:379
  53.6 0.1 collective-permute-start.16
  53.7 0.4 collective-permute-start.17
  54.1 3.6 %collective-permute-start.18 = (bf16[256,128]{1,0:T(8,128)(2,1)S(1)}, bf16[256,128]{1,0:T(8,128)(2,1)S(1)}, u32[]{:S(2)}, u32[]{:S(2)}) collective-permute-start(bf16[256,128]{1,0:T(8,128)(2,1)S(1)} %collective-permute-done.14.refs_4_), channel_id=1, source_target_pairs={{0,1},{1,0},{2,3},{3,2},{4,5},{5,4},{6,7},{7,6},{8,9},{9,8},{10,11... | collective-permute-start | bytes 196616 | tf_op jit(solution)/shard_map/ppermute | solution.py:379
  57.7 0.8 %shard_map.106 = f32[2,2,256,128]{3,2,1,0:T(8,128)} custom-call(f32[2,2,256,128]{3,2,1,0:T(8,128)S(1)} %get-tuple-element.64.mine, f32[2,2,256,128]{3,2,1,0:T(8,128)S(1)} %collective-permute-done.11.theirs), custom_call_target="tpu_custom_call" | custom-call | flops 1048576 | bytes 1048576 | tf_op jit(solution)/shard_map/pallas_call | solution.py:389
  58.6 0.0 collective-permute-done.18.refs_8_
  58.6 1.1 %shard_map.107 = f32[2,512]{1,0:T(2,128)} custom-call(bf16[128,128]{1,0:T(8,128)(2,1)S(1)} %get-tuple-element.67.refs_0_, bf16[256,128]{1,0:T(8,128)(2,1)S(1)} %collective-permute-done.10.refs_1_, bf16[256,128]{1,0:T(8,128)(2,1)S(1)} %collective-permute-done.12.refs_2_, bf16[256,128]{1,0:T(8,128)(2,1)S(1)} %collective-permute-done.13.refs_3_, ...), custom_call_target="tpu_custom_call" | custom-call | tf_op jit(solution)/shard_map/pallas_call | solution.py:396
  (25 shorter events, 0.1 us)
Async XLA Ops:
  0.6 1.0 %copy-start.4 = (bf16[1,8,2,64,128]{4,3,2,1,0:T(8,128)(2,1)S(1)}, bf16[1,8,2,64,128]{4,3,2,1,0:T(8,128)(2,1)}, u32[]{:S(2)}) copy-start(bf16[1,8,2,64,128]{4,3,2,1,0:T(8,128)(2,1)} %param.8) | copy-start | bytes 786436
  1.6 0.7 %copy-start.5 = (s32[2,256]{1,0:T(2,128)S(1)}, s32[2,256]{1,0:T(2,128)}, u32[]{:S(2)}) copy-start(s32[2,256]{1,0:T(2,128)} %wanted.3) | copy-start | bytes 6148
  2.3 9.5 %collective-permute-start.2 = (bf16[1040,128]{1,0:T(8,128)(2,1)S(1)}, bf16[1040,128]{1,0:T(8,128)(2,1)S(1)}, u32[]{:S(2)}, u32[]{:S(2)}) collective-permute-start(bf16[1040,128]{1,0:T(8,128)(2,1)S(1)} %shard_map.95.own), channel_id=1, source_target_pairs={{4,0},{8,4},{12,8},{14,12},{10,14},{6,10},{2,6},{0,2},{5,1},{9,5},... | collective-permute-start | bytes 798728 | tf_op jit(solution)/shard_map/ppermute | solution.py:292
  5.3 8.1 %collective-permute-start = (bf16[1040,128]{1,0:T(8,128)(2,1)S(1)}, bf16[1040,128]{1,0:T(8,128)(2,1)S(1)}, u32[]{:S(2)}, u32[]{:S(2)}) collective-permute-start(bf16[1040,128]{1,0:T(8,128)(2,1)S(1)} %shard_map.95.own), channel_id=1, source_target_pairs={{0,4},{4,8},{8,12},{12,14},{14,10},{10,6},{6,2},{2,0},{1,5},{5,9},... | collective-permute-start | bytes 798728 | tf_op jit(solution)/shard_map/ppermute | solution.py:291
  5.5 4.3 %copy-start = (bf16[11,2,512,512]{3,2,1,0:T(8,128)(2,1)S(1)}, bf16[11,2,512,512]{3,2,1,0:T(8,128)(2,1)}, u32[]{:S(2)}) copy-start(bf16[11,2,512,512]{3,2,1,0:T(8,128)(2,1)} %tiles.9) | copy-start | bytes 34603012
  9.7 0.7 %copy-start.7 = (s32[11]{0:T(128)S(1)}, s32[11]{0:T(128)}, u32[]{:S(2)}) copy-start(s32[11]{0:T(128)} %slots.1) | copy-start | bytes 136
  10.4 0.7 %copy-start.8 = (s32[11]{0:T(128)S(1)}, s32[11]{0:T(128)}, u32[]{:S(2)}) copy-start(s32[11]{0:T(128)} %cols.1) | copy-start | bytes 136
  11.1 4.3 %copy-start.1 = (bf16[11,2,512,512]{3,2,1,0:T(8,128)(2,1)S(1)}, bf16[11,2,512,512]{3,2,1,0:T(8,128)(2,1)}, u32[]{:S(2)}) copy-start(bf16[11,2,512,512]{3,2,1,0:T(8,128)(2,1)} %tiles.9) | copy-start | bytes 34603012
  11.8 7.6 %collective-permute-start.4 = (bf16[1040,128]{1,0:T(8,128)(2,1)S(1)}, bf16[1040,128]{1,0:T(8,128)(2,1)S(1)}, u32[]{:S(2)}, u32[]{:S(2)}) collective-permute-start(bf16[1040,128]{1,0:T(8,128)(2,1)S(1)} %collective-permute-done.2.from_right.refs_2_), channel_id=1, source_target_pairs={{4,0},{8,4},{12,8},{14,12},{10,14},{6,10},{2,6},{0,2},{5,1},{9,5},... | collective-permute-start | bytes 798728 | tf_op jit(solution)/shard_map/ppermute | solution.py:292
  13.5 7.5 %collective-permute-start.1 = (bf16[1040,128]{1,0:T(8,128)(2,1)S(1)}, bf16[1040,128]{1,0:T(8,128)(2,1)S(1)}, u32[]{:S(2)}, u32[]{:S(2)}) collective-permute-start(bf16[1040,128]{1,0:T(8,128)(2,1)S(1)} %collective-permute-done.from_left.refs_1_), channel_id=1, source_target_pairs={{0,4},{4,8},{8,12},{12,14},{14,10},{10,6},{6,2},{2,0},{1,5},{5,9},... | collective-permute-start | bytes 798728 | tf_op jit(solution)/shard_map/ppermute | solution.py:291
  19.0 9.6 %copy-start.2 = (bf16[2,256,512]{2,1,0:T(8,128)(2,1)S(1)}, bf16[2,256,512]{2,1,0:T(8,128)(2,1)}, u32[]{:S(2)}) copy-start(bf16[2,256,512]{2,1,0:T(8,128)(2,1)} %basis.1) | copy-start | bytes 1572868
  19.0 9.6 %copy-start.3 = (bf16[2,128,512]{2,1,0:T(8,128)(2,1)S(1)}, bf16[2,128,512]{2,1,0:T(8,128)(2,1)}, u32[]{:S(2)}) copy-start(bf16[2,128,512]{2,1,0:T(8,128)(2,1)} %supernode.1) | copy-start | bytes 786436
  19.0 9.6 %copy-start.6 = (s32[2,256]{1,0:T(2,128)S(1)}, s32[2,256]{1,0:T(2,128)}, u32[]{:S(2)}) copy-start(s32[2,256]{1,0:T(2,128)} %wanted.3) | copy-start | bytes 6148
  19.4 7.6 %collective-permute-start.6 = (bf16[1040,128]{1,0:T(8,128)(2,1)S(1)}, bf16[1040,128]{1,0:T(8,128)(2,1)S(1)}, u32[]{:S(2)}, u32[]{:S(2)}) collective-permute-start(bf16[1040,128]{1,0:T(8,128)(2,1)S(1)} %collective-permute-done.4.from_right.refs_4_), channel_id=1, source_target_pairs={{4,0},{8,4},{12,8},{14,12},{10,14},{6,10},{2,6},{0,2},{5,1},{9,5},... | collective-permute-start | bytes 798728 | tf_op jit(solution)/shard_map/ppermute | solution.py:292
  21.0 8.6 %collective-permute-start.3 = (bf16[1040,128]{1,0:T(8,128)(2,1)S(1)}, bf16[1040,128]{1,0:T(8,128)(2,1)S(1)}, u32[]{:S(2)}, u32[]{:S(2)}) collective-permute-start(bf16[1040,128]{1,0:T(8,128)(2,1)S(1)} %collective-permute-done.1.from_left.refs_3_), channel_id=1, source_target_pairs={{0,4},{4,8},{8,12},{12,14},{14,10},{10,6},{6,2},{2,0},{1,5},{5,9},... | collective-permute-start | bytes 798728 | tf_op jit(solution)/shard_map/ppermute | solution.py:291
  27.0 7.7 %collective-permute-start.7 = (bf16[528,128]{1,0:T(8,128)(2,1)S(1)}, bf16[528,128]{1,0:T(8,128)(2,1)S(1)}, u32[]{:S(2)}, u32[]{:S(2)}) collective-permute-start(bf16[528,128]{1,0:T(8,128)(2,1)S(1)} %slice.7), channel_id=1, source_target_pairs={{4,0},{8,4},{12,8},{14,12},{10,14},{6,10},{2,6},{0,2},{5,1},{9,5},... | collective-permute-start | bytes 405512 | tf_op jit(solution)/shard_map/ppermute | solution.py:296
  29.6 5.1 %copy-start.9 = (f32[2]{0:T(128)S(1)}, f32[2]{0:T(128)}, u32[]{:S(2)}) copy-start(f32[2]{0:T(128)} %pole_weight.1) | copy-start | bytes 28
  29.6 5.0 %collective-permute-start.5 = (bf16[512,128]{1,0:T(8,128)(2,1)S(1)}, bf16[512,128]{1,0:T(8,128)(2,1)S(1)}, u32[]{:S(2)}, u32[]{:S(2)}) collective-permute-start(bf16[512,128]{1,0:T(8,128)(2,1)S(1)} %slice.6), channel_id=1, source_target_pairs={{0,4},{4,8},{8,12},{12,14},{14,10},{10,6},{6,2},{2,0},{1,5},{5,9},... | collective-permute-start | bytes 393224 | tf_op jit(solution)/shard_map/ppermute | solution.py:295
  36.8 3.0 %collective-permute-start.9 = (f32[2,512,128]{2,1,0:T(8,128)S(1)}, f32[2,512,128]{2,1,0:T(8,128)S(1)}, u32[]{:S(2)}, u32[]{:S(2)}) collective-permute-start(f32[2,512,128]{2,1,0:T(8,128)S(1)} %get-tuple-element.59.mine), channel_id=1, source_target_pairs={{0,1},{1,0},{2,3},{3,2},{4,5},{5,4},{6,7},{7,6},{8,9},{9,8},{10,11... | collective-permute-start | bytes 1572872 | tf_op jit(solution)/shard_map/ppermute | solution.py:356
  36.9 1.9 %collective-permute-start.8 = (bf16[128,128]{1,0:T(8,128)(2,1)S(1)}, bf16[128,128]{1,0:T(8,128)(2,1)S(1)}, u32[]{:S(2)}, u32[]{:S(2)}) collective-permute-start(bf16[128,128]{1,0:T(8,128)(2,1)S(1)} %shard_map.101.mine), channel_id=1, source_target_pairs={{0,1},{1,0},{2,3},{3,2},{4,5},{5,4},{6,7},{7,6},{8,9},{9,8},{10,11... | collective-permute-start | bytes 98312 | tf_op jit(solution)/shard_map/ppermute | solution.py:345
  40.6 4.3 %collective-permute-start.10 = (bf16[256,128]{1,0:T(8,128)(2,1)S(1)}, bf16[256,128]{1,0:T(8,128)(2,1)S(1)}, u32[]{:S(2)}, u32[]{:S(2)}) collective-permute-start(bf16[256,128]{1,0:T(8,128)(2,1)S(1)} %get-tuple-element.62), channel_id=1, source_target_pairs={{1,9},{3,11},{5,13},{7,15},{9,1},{11,3},{13,5},{15,7},{0,2},{2,0},... | collective-permute-start | bytes 196616 | tf_op jit(solution)/shard_map/ppermute | solution.py:378
  45.0 12.7 %collective-permute-start.11 = (f32[2,2,256,128]{3,2,1,0:T(8,128)S(1)}, f32[2,2,256,128]{3,2,1,0:T(8,128)S(1)}, u32[]{:S(2)}, u32[]{:S(2)}) collective-permute-start(f32[2,2,256,128]{3,2,1,0:T(8,128)S(1)} %get-tuple-element.65), channel_id=1, source_target_pairs={{0,1},{1,0},{2,3},{3,2},{4,5},{5,4},{6,7},{7,6},{8,9},{9,8},{10,11... | collective-permute-start | bytes 1572872 | tf_op jit(solution)/shard_map/ppermute | solution.py:388
  45.5 8.1 %collective-permute-start.12 = (bf16[256,128]{1,0:T(8,128)(2,1)S(1)}, bf16[256,128]{1,0:T(8,128)(2,1)S(1)}, u32[]{:S(2)}, u32[]{:S(2)}) collective-permute-start(bf16[256,128]{1,0:T(8,128)(2,1)S(1)} %get-tuple-element.69), channel_id=1, source_target_pairs={{1,11},{3,9},{5,15},{7,13},{9,3},{11,1},{13,7},{15,5},{0,4},{2,6},... | collective-permute-start | bytes 196616 | tf_op jit(solution)/shard_map/ppermute | solution.py:378
  46.3 7.4 %collective-permute-start.13 = (bf16[256,128]{1,0:T(8,128)(2,1)S(1)}, bf16[256,128]{1,0:T(8,128)(2,1)S(1)}, u32[]{:S(2)}, u32[]{:S(2)}) collective-permute-start(bf16[256,128]{1,0:T(8,128)(2,1)S(1)} %get-tuple-element.70), channel_id=1, source_target_pairs={{1,13},{3,15},{5,9},{7,11},{9,5},{11,7},{13,1},{15,3},{0,6},{2,4},... | collective-permute-start | bytes 196616 | tf_op jit(solution)/shard_map/ppermute | solution.py:378
  48.2 5.9 %collective-permute-start.14 = (bf16[256,128]{1,0:T(8,128)(2,1)S(1)}, bf16[256,128]{1,0:T(8,128)(2,1)S(1)}, u32[]{:S(2)}, u32[]{:S(2)}) collective-permute-start(bf16[256,128]{1,0:T(8,128)(2,1)S(1)} %get-tuple-element.71), channel_id=1, source_target_pairs={{1,15},{3,13},{5,11},{7,9},{9,7},{11,5},{13,3},{15,1},{17,31},{19,... | collective-permute-start | bytes 196616 | tf_op jit(solution)/shard_map/ppermute | solution.py:378
  48.8 9.7 %collective-permute-start.15 = (bf16[256,128]{1,0:T(8,128)(2,1)S(1)}, bf16[256,128]{1,0:T(8,128)(2,1)S(1)}, u32[]{:S(2)}, u32[]{:S(2)}) collective-permute-start(bf16[256,128]{1,0:T(8,128)(2,1)S(1)} %collective-permute-done.10.refs_1_), channel_id=1, source_target_pairs={{0,1},{1,0},{2,3},{3,2},{4,5},{5,4},{6,7},{7,6},{8,9},{9,8},{10,11... | collective-permute-start | bytes 196616 | tf_op jit(solution)/shard_map/ppermute | solution.py:379
  53.6 5.0 %collective-permute-start.16 = (bf16[256,128]{1,0:T(8,128)(2,1)S(1)}, bf16[256,128]{1,0:T(8,128)(2,1)S(1)}, u32[]{:S(2)}, u32[]{:S(2)}) collective-permute-start(bf16[256,128]{1,0:T(8,128)(2,1)S(1)} %collective-permute-done.12.refs_2_), channel_id=1, source_target_pairs={{0,1},{1,0},{2,3},{3,2},{4,5},{5,4},{6,7},{7,6},{8,9},{9,8},{10,11... | collective-permute-start | bytes 196616 | tf_op jit(solution)/shard_map/ppermute | solution.py:379
  53.7 4.9 %collective-permute-start.17 = (bf16[256,128]{1,0:T(8,128)(2,1)S(1)}, bf16[256,128]{1,0:T(8,128)(2,1)S(1)}, u32[]{:S(2)}, u32[]{:S(2)}) collective-permute-start(bf16[256,128]{1,0:T(8,128)(2,1)S(1)} %collective-permute-done.13.refs_3_), channel_id=1, source_target_pairs={{0,1},{1,0},{2,3},{3,2},{4,5},{5,4},{6,7},{7,6},{8,9},{9,8},{10,11... | collective-permute-start | bytes 196616 | tf_op jit(solution)/shard_map/ppermute | solution.py:379
  54.1 4.5 %collective-permute-start.18 = (bf16[256,128]{1,0:T(8,128)(2,1)S(1)}, bf16[256,128]{1,0:T(8,128)(2,1)S(1)}, u32[]{:S(2)}, u32[]{:S(2)}) collective-permute-start(bf16[256,128]{1,0:T(8,128)(2,1)S(1)} %collective-permute-done.14.refs_4_), channel_id=1, source_target_pairs={{0,1},{1,0},{2,3},{3,2},{4,5},{5,4},{6,7},{7,6},{8,9},{9,8},{10,11... | collective-permute-start | bytes 196616 | tf_op jit(solution)/shard_map/ppermute | solution.py:379

commit v6 on v5

--- a/solution.py
+++ b/solution.py
@@ -214,12 +214,21 @@
         at += out.shape[0]
 
 
+def turn_kernel(*refs):
+    *parts, out = refs
+    slots = out.shape[0] // len(parts)
+    at = pl.ds(pl.multiple_of((1 - lax.axis_index("col")) * slots, slots), slots)
+    for i, part in enumerate(parts):
+        out[i * slots:(i + 1) * slots] = part[at, :]
+
+
 def density_kernel(*refs):
-    *parts, basis, supernode, out = refs
-    own = parts[0]
+    own, *parts, passed, basis, supernode, out = refs
     slots = own.shape[0]
     at = pl.ds(pl.multiple_of(lax.axis_index("col") * slots, slots), slots)
-    arrived = jnp.concatenate([own[...]] + [part[at, :] for part in parts[1:]], axis=0)
+    arrived = jnp.concatenate(
+        [own[...]] + [part[at, :] for part in parts] + [passed[...]], axis=0
+    )
     for n in range(basis.shape[0]):
         projected = lax.dot_general(
             arrived, basis[n], (((0,), (0,)), ((), ())), preferred_element_type=F32
@@ -353,6 +362,7 @@
         1,
         aliases={6: 0},
     )(tile_slot, tile_col, pole_weight, left, right, tiles, acc)
+    dens, wanted_other = lax.optimization_barrier((dens, wanted_other))
     dens_other = lax.ppermute(dens, "col", swap)
     pick = pl.pallas_call(
         functools.partial(
@@ -360,7 +370,7 @@
         ),
         out_shape=jax.ShapeDtypeStruct((arrive, rows_chip), BF16),
         compiler_params=params,
-        cost_estimate=cost,
+        cost_estimate=pl.CostEstimate(flops=2 ** 32, bytes_accessed=2 ** 20, transcendentals=0),
     )(wanted, wanted_other)
     message = jax.ShapeDtypeStruct((2 * slots, width), BF16)
     kept, *sent = pl.pallas_call(
@@ -370,15 +380,21 @@
         cost_estimate=cost,
     )(pick, dens, dens_other)
 
-    fetched, passed = [], []
+    fetched = []
     for step in range(half_ring):
         pairs = [(2 * r + 1, 2 * (r ^ (half_ring + step)) + 1) for r in range(n_row)]
         if step + 1 < half_ring:
             pairs += [(2 * r, 2 * (r ^ (1 + step))) for r in range(n_row)]
         fetched.append(lax.ppermute(sent[step], ("row", "col"), pairs))
-        passed.append(lax.ppermute(fetched[-1], "col", swap))
-
-    acc, fetched[0] = lax.optimization_barrier((acc, fetched[0]))
+
+    turned = pl.pallas_call(
+        turn_kernel,
+        out_shape=jax.ShapeDtypeStruct((half_ring * slots, width), BF16),
+        compiler_params=params,
+        cost_estimate=cost,
+    )(*fetched)
+    passed = lax.ppermute(turned, "col", swap)
+
     mine, other = pl.pallas_call(
         halves_kernel,
         out_shape=[jax.ShapeDtypeStruct(half_shape, F32)] * 2,
@@ -397,7 +413,7 @@
         density_kernel,
         out_shape=jax.ShapeDtypeStruct((boxes, box_basis.shape[2]), F32),
         compiler_params=params,
-    )(kept, *fetched, *passed, basis_here, wide)
+    )(kept, *fetched, passed, basis_here, wide)
     return inverse, density
 
 

time: 60 us -> 56 us (0.933)
  starting transfers between devices: 24.3 us -> 19 us
  waiting for transfers between devices: 9.66 us -> 10.9 us
    ppermute x4 -> x1, starting transfers between devices: 8.86 us -> 4.74 us  [local(): passed = lax.ppermute(turned, 'col', swap)]
    ppermute x4, waiting for transfers between devices: 2.68 us -> 4.88 us  [local(): fetched.append(lax.ppermute(sent[step], ('row', 'col'), pairs))]
    ppermute x1, waiting for transfers between devices: 1.45 us -> 0.01 us  [local(): wanted_other = lax.ppermute(wanted, 'col', swap)]
    ppermute x4, starting transfers between devices: 4.98 us -> 4.21 us  [local(): fetched.append(lax.ppermute(sent[step], ('row', 'col'), pairs))]
  transfers between devices with their start and end apart: 19 -> 16, of which waited for: 6 -> 9; matrix products, arithmetic and copies ran while one was open for 0% -> 0% of each run, Pallas kernels for 20% -> 27%
where the time goes in v6:
time: 56 us; the launch traced here: 55.8 us
  starting transfers between devices  19 us (34%)
  Pallas kernels  16.3 us (29%)
  waiting for transfers between devices  10.9 us (19%)
  local copies, waits for them, and re-layouts  8.76 us (16%)
  between operations  0.81 us (1%)
    unnamed x20, local copies, waits for them, and re-layouts  8.74 us
    ppermute x3, starting transfers between devices, local(): next_right = lax.ppermute(right, 'row', to_left)  6.3 us
    pallas_call x2, Pallas kernels, local(): call(functools.partial(hop_middle, hop=h - 1), [in_smem] * 2 + [in_vmem]...  5.63 us
    ppermute x4, waiting for transfers between devices, local(): fetched.append(lax.ppermute(sent[step], ('row', 'col'), pairs))  4.88 us
    ppermute x1, starting transfers between devices, local(): passed = lax.ppermute(turned, 'col', swap)  4.74 us
    ppermute x4, starting transfers between devices, local(): fetched.append(lax.ppermute(sent[step], ('row', 'col'), pairs))  4.21 us
    ppermute x3, waiting for transfers between devices, local(): next_right = lax.ppermute(right, 'row', to_left)  3.75 us
    pallas_call x1, Pallas kernels, local(): call(hop_early, [in_smem] * 2 + [in_vmem] * 5, acc_out, [], 3, aliases={6...  3.64 us
  transfers between devices with their start and end apart: 16, of which 9 were waited for; matrix products, arithmetic and copies ran while one was open for 0% of the time, Pallas kernels for 27%

profile of v6, /device:TPU:0, one launch (start us, length us, event | category | flops | bytes accessed | tf_op | source)
XLA Modules:
  0.0 55.8 jit_solution(4562515537509292593)
XLA Ops:
  0.6 0.9 %copy-done.4 = bf16[1,8,2,64,128]{4,3,2,1,0:T(8,128)(2,1)S(1)} copy-done((bf16[1,8,2,64,128]{4,3,2,1,0:T(8,128)(2,1)S(1)}, bf16[1,8,2,64,128]{4,3,2,1,0:T(8,128)(2,1)}, u32[]{:S(2)}) %copy-start.4) | copy-done | bytes 262168
  1.6 0.7 %copy-done.5 = s32[2,256]{1,0:T(2,128)S(1)} copy-done((s32[2,256]{1,0:T(2,128)S(1)}, s32[2,256]{1,0:T(2,128)}, u32[]{:S(2)}) %copy-start.5) | copy-done | bytes 2072
  2.3 0.1 shard_map.95.own
  2.3 3.0 %collective-permute-start.2 = (bf16[1040,128]{1,0:T(8,128)(2,1)S(1)}, bf16[1040,128]{1,0:T(8,128)(2,1)S(1)}, u32[]{:S(2)}, u32[]{:S(2)}) collective-permute-start(bf16[1040,128]{1,0:T(8,128)(2,1)S(1)} %shard_map.95.own), channel_id=1, source_target_pairs={{4,0},{8,4},{12,8},{14,12},{10,14},{6,10},{2,6},{0,2},{5,1},{9,5},... | collective-permute-start | bytes 798728 | tf_op jit(solution)/shard_map/ppermute | solution.py:301
  5.3 0.1 collective-permute-start
  5.5 4.3 %copy-done = bf16[11,2,512,512]{3,2,1,0:T(8,128)(2,1)S(1)} copy-done((bf16[11,2,512,512]{3,2,1,0:T(8,128)(2,1)S(1)}, bf16[11,2,512,512]{3,2,1,0:T(8,128)(2,1)}, u32[]{:S(2)}) %copy-start) | copy-done | bytes 11534360
  9.7 0.7 %copy-done.7 = s32[11]{0:T(128)S(1)} copy-done((s32[11]{0:T(128)S(1)}, s32[11]{0:T(128)}, u32[]{:S(2)}) %copy-start.7) | copy-done | bytes 68
  10.4 0.7 %copy-done.8 = s32[11]{0:T(128)S(1)} copy-done((s32[11]{0:T(128)S(1)}, s32[11]{0:T(128)}, u32[]{:S(2)}) %copy-start.8) | copy-done | bytes 68
  11.1 0.1 shard_map.96
  11.1 0.6 %collective-permute-done.2.from_right.refs_2_ = bf16[1040,128]{1,0:T(8,128)(2,1)S(1)} collective-permute-done((bf16[1040,128]{1,0:T(8,128)(2,1)S(1)}, bf16[1040,128]{1,0:T(8,128)(2,1)S(1)}, u32[]{:S(2)}, u32[]{:S(2)}) %collective-permute-start.2) | collective-permute-done | bytes 266272 | tf_op jit(solution)/shard_map/ppermute | solution.py:301
  11.8 1.7 %collective-permute-start.4 = (bf16[1040,128]{1,0:T(8,128)(2,1)S(1)}, bf16[1040,128]{1,0:T(8,128)(2,1)S(1)}, u32[]{:S(2)}, u32[]{:S(2)}) collective-permute-start(bf16[1040,128]{1,0:T(8,128)(2,1)S(1)} %collective-permute-done.2.from_right.refs_2_), channel_id=1, source_target_pairs={{4,0},{8,4},{12,8},{14,12},{10,14},{6,10},{2,6},{0,2},{5,1},{9,5},... | collective-permute-start | bytes 798728 | tf_op jit(solution)/shard_map/ppermute | solution.py:301
  13.5 0.3 collective-permute-start.1
  13.8 1.5 %copy-done.1 = bf16[11,2,512,512]{3,2,1,0:T(8,128)(2,1)S(1)} copy-done((bf16[11,2,512,512]{3,2,1,0:T(8,128)(2,1)S(1)}, bf16[11,2,512,512]{3,2,1,0:T(8,128)(2,1)}, u32[]{:S(2)}) %copy-start.1) | copy-done | bytes 11534360
  15.3 3.6 %shard_map.97.start = f32[2,512,256]{2,1,0:T(8,128)S(1)} custom-call(s32[11]{0:T(128)S(1)} %get-tuple-element.40.slots, s32[11]{0:T(128)S(1)} %get-tuple-element.41.cols, bf16[1040,128]{1,0:T(8,128)(2,1)S(1)} %get-tuple-element.42.own.refs_0_, bf16[1040,128]{1,0:T(8,128)(2,1)S(1)} %collective-permute-done.from_left.refs_1_, ...), custom_call_target="tpu_custom_call", output_to_operand_aliasing={{}: (6, {})} | custom-call | flops 1048576 | bytes 1048576 | tf_op jit(solution)/shard_map/pallas_call | solution.py:322
  19.0 0.0 copy-start.2
  19.0 0.0 copy-start.3
  19.0 0.0 copy-start.6
  19.0 0.4 collective-permute-done.4.from_right.refs_4_
  19.4 1.6 %collective-permute-start.6 = (bf16[1040,128]{1,0:T(8,128)(2,1)S(1)}, bf16[1040,128]{1,0:T(8,128)(2,1)S(1)}, u32[]{:S(2)}, u32[]{:S(2)}) collective-permute-start(bf16[1040,128]{1,0:T(8,128)(2,1)S(1)} %collective-permute-done.4.from_right.refs_4_), channel_id=1, source_target_pairs={{4,0},{8,4},{12,8},{14,12},{10,14},{6,10},{2,6},{0,2},{5,1},{9,5},... | collective-permute-start | bytes 798728 | tf_op jit(solution)/shard_map/ppermute | solution.py:301
  21.0 0.4 collective-permute-start.3
  21.4 2.8 %shard_map.99.start = f32[2,512,256]{2,1,0:T(8,128)S(1)} custom-call(s32[11]{0:T(128)S(1)} %get-tuple-element.40.slots, s32[11]{0:T(128)S(1)} %get-tuple-element.41.cols, bf16[1040,128]{1,0:T(8,128)(2,1)S(1)} %collective-permute-done.1.from_left.refs_3_, ...), custom_call_target="tpu_custom_call", output_to_operand_aliasing={{}: (5, {})} | custom-call | flops 1048576 | bytes 1048576 | tf_op jit(solution)/shard_map/pallas_call | solution.py:326
  24.2 2.7 %collective-permute-done.6.from_right.refs_6_ = bf16[1040,128]{1,0:T(8,128)(2,1)S(1)} collective-permute-done((bf16[1040,128]{1,0:T(8,128)(2,1)S(1)}, bf16[1040,128]{1,0:T(8,128)(2,1)S(1)}, u32[]{:S(2)}, u32[]{:S(2)}) %collective-permute-start.6) | collective-permute-done | bytes 266272 | tf_op jit(solution)/shard_map/ppermute | solution.py:301
  27.0 1.7 %collective-permute-start.7 = (bf16[528,128]{1,0:T(8,128)(2,1)S(1)}, bf16[528,128]{1,0:T(8,128)(2,1)S(1)}, u32[]{:S(2)}, u32[]{:S(2)}) collective-permute-start(bf16[528,128]{1,0:T(8,128)(2,1)S(1)} %slice.7), channel_id=1, source_target_pairs={{4,0},{8,4},{12,8},{14,12},{10,14},{6,10},{2,6},{0,2},{5,1},{9,5},... | collective-permute-start | bytes 405512 | tf_op jit(solution)/shard_map/ppermute | solution.py:305
  28.6 1.0 %shard_map.98 = (bf16[2,1152,512]{2,1,0:T(8,128)(2,1)S(1)}, f32[2,128,512]{2,1,0:T(8,128)S(1)}) custom-call(s32[2,256]{1,0:T(2,128)S(1)} %copy-done.6, bf16[2,256,512]{2,1,0:T(8,128)(2,1)S(1)} %copy-done.2, bf16[2,128,512]{2,1,0:T(8,128)(2,1)S(1)} %copy-done.3), custom_call_target="tpu_custom_call" | custom-call | flops 1048576 | bytes 1048576 | tf_op jit(solution)/shard_map/pallas_call | solution.py:285
  29.6 0.0 copy-start.9
  29.6 0.4 collective-permute-start.5
  30.1 2.9 %shard_map.100.start = f32[2,512,256]{2,1,0:T(8,128)S(1)} custom-call(s32[11]{0:T(128)S(1)} %get-tuple-element.40.slots, s32[11]{0:T(128)S(1)} %get-tuple-element.41.cols, bf16[1040,128]{1,0:T(8,128)(2,1)S(1)} %collective-permute-done.3.from_left.refs_5_, ...), custom_call_target="tpu_custom_call", output_to_operand_aliasing={{}: (5, {})} | custom-call | flops 1048576 | bytes 1048576 | tf_op jit(solution)/shard_map/pallas_call | solution.py:326
  33.0 1.7 %collective-permute-done.5.low = bf16[512,128]{1,0:T(8,128)(2,1)S(1)} collective-permute-done((bf16[512,128]{1,0:T(8,128)(2,1)S(1)}, bf16[512,128]{1,0:T(8,128)(2,1)S(1)}, u32[]{:S(2)}, u32[]{:S(2)}) %collective-permute-start.5) | collective-permute-done | bytes 131104 | tf_op jit(solution)/shard_map/ppermute | solution.py:304
  34.7 0.1 shard_map.101.mine
  34.7 0.1 collective-permute-start.8
  34.8 2.1 %shard_map.102 = (f32[2,512,256]{2,1,0:T(8,128)S(1)}, f32[2,512,128]{2,1,0:T(8,128)S(1)}) custom-call(s32[11]{0:T(128)S(1)} %get-tuple-element.40.slots, s32[11]{0:T(128)S(1)} %get-tuple-element.41.cols, f32[2]{0:T(128)S(1)} %copy-done.9, bf16[512,128]{1,0:T(8,128)(2,1)S(1)} %collective-permute-done.5.low, ...), custom_call_target="tpu_custom_call", output_to_operand_aliasing={{0}: (6, {})} | custom-call | flops 1048576 | bytes 1048576 | tf_op jit(solution)/shard_map/pallas_call | solution.py:357
  36.9 0.5 collective-permute-start.9
  37.4 0.1 shard_map.105
  37.5 0.1 collective-permute-start.10
  37.6 0.9 %shard_map.103.pick = bf16[1152,1024]{1,0:T(8,128)(2,1)S(1)} custom-call(bf16[128,128]{1,0:T(8,128)(2,1)S(1)} %shard_map.101.mine, bf16[128,128]{1,0:T(8,128)(2,1)S(1)} %collective-permute-done.8.theirs), custom_call_target="tpu_custom_call" | custom-call | flops 4294967296 | bytes 1048576 | tf_op jit(solution)/shard_map/pallas_call | solution.py:367
  38.6 0.4 collective-permute-done.9.theirs
  39.0 0.8 %shard_map.104 = (bf16[128,128]{1,0:T(8,128)(2,1)S(1)}, bf16[256,128]{1,0:T(8,128)(2,1)S(1)}, bf16[256,128]{1,0:T(8,128)(2,1)S(1)}, bf16[256,128]{1,0:T(8,128)(2,1)S(1)}, bf16[256,128]{1,0:T(8,128)(2,1)S(1)}) custom-call(bf16[1152,1024]{1,0:T(8,128)(2,1)S(1)} %shard_map.103.pick, f32[2,512,128]{2,1,0:T(8,128)S(1)} %get-tuple-element.61.mine, ...), custom_call_target="tpu_custom_call" | custom-call | flops 1048576 | bytes 1048576 | tf_op jit(solution)/shard_map/pallas_call | solution.py:376
  39.8 1.7 %collective-permute-start.11 = (bf16[256,128]{1,0:T(8,128)(2,1)S(1)}, bf16[256,128]{1,0:T(8,128)(2,1)S(1)}, u32[]{:S(2)}, u32[]{:S(2)}) collective-permute-start(bf16[256,128]{1,0:T(8,128)(2,1)S(1)} %get-tuple-element.68), channel_id=1, source_target_pairs={{1,9},{3,11},{5,13},{7,15},{9,1},{11,3},{13,5},{15,7},{0,2},{2,0},... | collective-permute-start | bytes 196616 | tf_op jit(solution)/shard_map/ppermute | solution.py:388
  41.4 1.6 %collective-permute-start.12 = (bf16[256,128]{1,0:T(8,128)(2,1)S(1)}, bf16[256,128]{1,0:T(8,128)(2,1)S(1)}, u32[]{:S(2)}, u32[]{:S(2)}) collective-permute-start(bf16[256,128]{1,0:T(8,128)(2,1)S(1)} %get-tuple-element.69), channel_id=1, source_target_pairs={{1,11},{3,9},{5,15},{7,13},{9,3},{11,1},{13,7},{15,5},{0,4},{2,6},... | collective-permute-start | bytes 196616 | tf_op jit(solution)/shard_map/ppermute | solution.py:388
  43.1 0.3 collective-permute-start.13
  43.3 0.7 %collective-permute-start.14 = (bf16[256,128]{1,0:T(8,128)(2,1)S(1)}, bf16[256,128]{1,0:T(8,128)(2,1)S(1)}, u32[]{:S(2)}, u32[]{:S(2)}) collective-permute-start(bf16[256,128]{1,0:T(8,128)(2,1)S(1)} %get-tuple-element.71), channel_id=1, source_target_pairs={{1,15},{3,13},{5,11},{7,9},{9,7},{11,5},{13,3},{15,1},{17,31},{19,... | collective-permute-start | bytes 196616 | tf_op jit(solution)/shard_map/ppermute | solution.py:388
  44.0 0.1 collective-permute-done.11.refs_0_.refs_1_
  44.1 1.6 %collective-permute-done.12.refs_1_.refs_2_ = bf16[256,128]{1,0:T(8,128)(2,1)S(1)} collective-permute-done((bf16[256,128]{1,0:T(8,128)(2,1)S(1)}, bf16[256,128]{1,0:T(8,128)(2,1)S(1)}, u32[]{:S(2)}, u32[]{:S(2)}) %collective-permute-start.12) | collective-permute-done | bytes 65568 | tf_op jit(solution)/shard_map/ppermute | solution.py:388
  45.7 3.2 %collective-permute-done.13.refs_2_.refs_3_ = bf16[256,128]{1,0:T(8,128)(2,1)S(1)} collective-permute-done((bf16[256,128]{1,0:T(8,128)(2,1)S(1)}, bf16[256,128]{1,0:T(8,128)(2,1)S(1)}, u32[]{:S(2)}, u32[]{:S(2)}) %collective-permute-start.13) | collective-permute-done | bytes 65568 | tf_op jit(solution)/shard_map/ppermute | solution.py:388
  48.9 4.7 %collective-permute-start.15 = (bf16[512,128]{1,0:T(8,128)(2,1)S(1)}, bf16[512,128]{1,0:T(8,128)(2,1)S(1)}, u32[]{:S(2)}, u32[]{:S(2)}) collective-permute-start(bf16[512,128]{1,0:T(8,128)(2,1)S(1)} %shard_map.107), channel_id=1, source_target_pairs={{0,1},{1,0},{2,3},{3,2},{4,5},{5,4},{6,7},{7,6},{8,9},{9,8},{10,11... | collective-permute-start | bytes 393224 | tf_op jit(solution)/shard_map/ppermute | solution.py:396
  53.6 0.8 %shard_map.106 = f32[2,2,256,128]{3,2,1,0:T(8,128)} custom-call(f32[2,2,256,128]{3,2,1,0:T(8,128)S(1)} %get-tuple-element.64.mine, f32[2,2,256,128]{3,2,1,0:T(8,128)S(1)} %collective-permute-done.10.theirs), custom_call_target="tpu_custom_call" | custom-call | flops 1048576 | bytes 1048576 | tf_op jit(solution)/shard_map/pallas_call | solution.py:405
  54.5 0.1 collective-permute-done.15.refs_5_
  54.6 1.1 %shard_map.108 = f32[2,512]{1,0:T(2,128)} custom-call(bf16[128,128]{1,0:T(8,128)(2,1)S(1)} %get-tuple-element.67.refs_0_, bf16[256,128]{1,0:T(8,128)(2,1)S(1)} %collective-permute-done.11.refs_0_.refs_1_, bf16[256,128]{1,0:T(8,128)(2,1)S(1)} %collective-permute-done.12.refs_1_.refs_2_, bf16[256,128]{1,0:T(8,128)(2,1)S(1)} %collective-permute-done.13.refs_2_.refs_3_, ...), custom_call_target="tpu_custom_call" | custom-call | tf_op jit(solution)/shard_map/pallas_call | solution.py:412
  (20 shorter events, 0.1 us)
Async XLA Ops:
  0.6 1.0 %copy-start.4 = (bf16[1,8,2,64,128]{4,3,2,1,0:T(8,128)(2,1)S(1)}, bf16[1,8,2,64,128]{4,3,2,1,0:T(8,128)(2,1)}, u32[]{:S(2)}) copy-start(bf16[1,8,2,64,128]{4,3,2,1,0:T(8,128)(2,1)} %param.8) | copy-start | bytes 786436
  1.6 0.7 %copy-start.5 = (s32[2,256]{1,0:T(2,128)S(1)}, s32[2,256]{1,0:T(2,128)}, u32[]{:S(2)}) copy-start(s32[2,256]{1,0:T(2,128)} %wanted.3) | copy-start | bytes 6148
  2.3 9.5 %collective-permute-start.2 = (bf16[1040,128]{1,0:T(8,128)(2,1)S(1)}, bf16[1040,128]{1,0:T(8,128)(2,1)S(1)}, u32[]{:S(2)}, u32[]{:S(2)}) collective-permute-start(bf16[1040,128]{1,0:T(8,128)(2,1)S(1)} %shard_map.95.own), channel_id=1, source_target_pairs={{4,0},{8,4},{12,8},{14,12},{10,14},{6,10},{2,6},{0,2},{5,1},{9,5},... | collective-permute-start | bytes 798728 | tf_op jit(solution)/shard_map/ppermute | solution.py:301
  5.3 8.1 %collective-permute-start = (bf16[1040,128]{1,0:T(8,128)(2,1)S(1)}, bf16[1040,128]{1,0:T(8,128)(2,1)S(1)}, u32[]{:S(2)}, u32[]{:S(2)}) collective-permute-start(bf16[1040,128]{1,0:T(8,128)(2,1)S(1)} %shard_map.95.own), channel_id=1, source_target_pairs={{0,4},{4,8},{8,12},{12,14},{14,10},{10,6},{6,2},{2,0},{1,5},{5,9},... | collective-permute-start | bytes 798728 | tf_op jit(solution)/shard_map/ppermute | solution.py:300
  5.5 4.3 %copy-start = (bf16[11,2,512,512]{3,2,1,0:T(8,128)(2,1)S(1)}, bf16[11,2,512,512]{3,2,1,0:T(8,128)(2,1)}, u32[]{:S(2)}) copy-start(bf16[11,2,512,512]{3,2,1,0:T(8,128)(2,1)} %tiles.9) | copy-start | bytes 34603012
  9.7 0.7 %copy-start.7 = (s32[11]{0:T(128)S(1)}, s32[11]{0:T(128)}, u32[]{:S(2)}) copy-start(s32[11]{0:T(128)} %slots.1) | copy-start | bytes 136
  10.4 0.7 %copy-start.8 = (s32[11]{0:T(128)S(1)}, s32[11]{0:T(128)}, u32[]{:S(2)}) copy-start(s32[11]{0:T(128)} %cols.1) | copy-start | bytes 136
  11.1 4.3 %copy-start.1 = (bf16[11,2,512,512]{3,2,1,0:T(8,128)(2,1)S(1)}, bf16[11,2,512,512]{3,2,1,0:T(8,128)(2,1)}, u32[]{:S(2)}) copy-start(bf16[11,2,512,512]{3,2,1,0:T(8,128)(2,1)} %tiles.9) | copy-start | bytes 34603012
  11.8 7.6 %collective-permute-start.4 = (bf16[1040,128]{1,0:T(8,128)(2,1)S(1)}, bf16[1040,128]{1,0:T(8,128)(2,1)S(1)}, u32[]{:S(2)}, u32[]{:S(2)}) collective-permute-start(bf16[1040,128]{1,0:T(8,128)(2,1)S(1)} %collective-permute-done.2.from_right.refs_2_), channel_id=1, source_target_pairs={{4,0},{8,4},{12,8},{14,12},{10,14},{6,10},{2,6},{0,2},{5,1},{9,5},... | collective-permute-start | bytes 798728 | tf_op jit(solution)/shard_map/ppermute | solution.py:301
  13.5 7.5 %collective-permute-start.1 = (bf16[1040,128]{1,0:T(8,128)(2,1)S(1)}, bf16[1040,128]{1,0:T(8,128)(2,1)S(1)}, u32[]{:S(2)}, u32[]{:S(2)}) collective-permute-start(bf16[1040,128]{1,0:T(8,128)(2,1)S(1)} %collective-permute-done.from_left.refs_1_), channel_id=1, source_target_pairs={{0,4},{4,8},{8,12},{12,14},{14,10},{10,6},{6,2},{2,0},{1,5},{5,9},... | collective-permute-start | bytes 798728 | tf_op jit(solution)/shard_map/ppermute | solution.py:300
  19.0 9.6 %copy-start.2 = (bf16[2,256,512]{2,1,0:T(8,128)(2,1)S(1)}, bf16[2,256,512]{2,1,0:T(8,128)(2,1)}, u32[]{:S(2)}) copy-start(bf16[2,256,512]{2,1,0:T(8,128)(2,1)} %basis.1) | copy-start | bytes 1572868
  19.0 9.6 %copy-start.3 = (bf16[2,128,512]{2,1,0:T(8,128)(2,1)S(1)}, bf16[2,128,512]{2,1,0:T(8,128)(2,1)}, u32[]{:S(2)}) copy-start(bf16[2,128,512]{2,1,0:T(8,128)(2,1)} %supernode.1) | copy-start | bytes 786436
  19.0 9.6 %copy-start.6 = (s32[2,256]{1,0:T(2,128)S(1)}, s32[2,256]{1,0:T(2,128)}, u32[]{:S(2)}) copy-start(s32[2,256]{1,0:T(2,128)} %wanted.3) | copy-start | bytes 6148
  19.4 7.6 %collective-permute-start.6 = (bf16[1040,128]{1,0:T(8,128)(2,1)S(1)}, bf16[1040,128]{1,0:T(8,128)(2,1)S(1)}, u32[]{:S(2)}, u32[]{:S(2)}) collective-permute-start(bf16[1040,128]{1,0:T(8,128)(2,1)S(1)} %collective-permute-done.4.from_right.refs_4_), channel_id=1, source_target_pairs={{4,0},{8,4},{12,8},{14,12},{10,14},{6,10},{2,6},{0,2},{5,1},{9,5},... | collective-permute-start | bytes 798728 | tf_op jit(solution)/shard_map/ppermute | solution.py:301
  21.0 8.6 %collective-permute-start.3 = (bf16[1040,128]{1,0:T(8,128)(2,1)S(1)}, bf16[1040,128]{1,0:T(8,128)(2,1)S(1)}, u32[]{:S(2)}, u32[]{:S(2)}) collective-permute-start(bf16[1040,128]{1,0:T(8,128)(2,1)S(1)} %collective-permute-done.1.from_left.refs_3_), channel_id=1, source_target_pairs={{0,4},{4,8},{8,12},{12,14},{14,10},{10,6},{6,2},{2,0},{1,5},{5,9},... | collective-permute-start | bytes 798728 | tf_op jit(solution)/shard_map/ppermute | solution.py:300
  27.0 7.7 %collective-permute-start.7 = (bf16[528,128]{1,0:T(8,128)(2,1)S(1)}, bf16[528,128]{1,0:T(8,128)(2,1)S(1)}, u32[]{:S(2)}, u32[]{:S(2)}) collective-permute-start(bf16[528,128]{1,0:T(8,128)(2,1)S(1)} %slice.7), channel_id=1, source_target_pairs={{4,0},{8,4},{12,8},{14,12},{10,14},{6,10},{2,6},{0,2},{5,1},{9,5},... | collective-permute-start | bytes 405512 | tf_op jit(solution)/shard_map/ppermute | solution.py:305
  29.6 5.2 %copy-start.9 = (f32[2]{0:T(128)S(1)}, f32[2]{0:T(128)}, u32[]{:S(2)}) copy-start(f32[2]{0:T(128)} %pole_weight.1) | copy-start | bytes 28
  29.6 5.0 %collective-permute-start.5 = (bf16[512,128]{1,0:T(8,128)(2,1)S(1)}, bf16[512,128]{1,0:T(8,128)(2,1)S(1)}, u32[]{:S(2)}, u32[]{:S(2)}) collective-permute-start(bf16[512,128]{1,0:T(8,128)(2,1)S(1)} %slice.6), channel_id=1, source_target_pairs={{0,4},{4,8},{8,12},{12,14},{14,10},{10,6},{6,2},{2,0},{1,5},{5,9},... | collective-permute-start | bytes 393224 | tf_op jit(solution)/shard_map/ppermute | solution.py:304
  34.7 2.2 %collective-permute-start.8 = (bf16[128,128]{1,0:T(8,128)(2,1)S(1)}, bf16[128,128]{1,0:T(8,128)(2,1)S(1)}, u32[]{:S(2)}, u32[]{:S(2)}) collective-permute-start(bf16[128,128]{1,0:T(8,128)(2,1)S(1)} %shard_map.101.mine), channel_id=1, source_target_pairs={{0,1},{1,0},{2,3},{3,2},{4,5},{5,4},{6,7},{7,6},{8,9},{9,8},{10,11... | collective-permute-start | bytes 98312 | tf_op jit(solution)/shard_map/ppermute | solution.py:354
  36.9 2.1 %collective-permute-start.9 = (f32[2,512,128]{2,1,0:T(8,128)S(1)}, f32[2,512,128]{2,1,0:T(8,128)S(1)}, u32[]{:S(2)}, u32[]{:S(2)}) collective-permute-start(f32[2,512,128]{2,1,0:T(8,128)S(1)} %get-tuple-element.61.mine), channel_id=1, source_target_pairs={{0,1},{1,0},{2,3},{3,2},{4,5},{5,4},{6,7},{7,6},{8,9},{9,8},{10,11... | collective-permute-start | bytes 1572872 | tf_op jit(solution)/shard_map/ppermute | solution.py:366
  37.5 16.1 %collective-permute-start.10 = (f32[2,2,256,128]{3,2,1,0:T(8,128)S(1)}, f32[2,2,256,128]{3,2,1,0:T(8,128)S(1)}, u32[]{:S(2)}, u32[]{:S(2)}) collective-permute-start(f32[2,2,256,128]{3,2,1,0:T(8,128)S(1)} %get-tuple-element.65), channel_id=1, source_target_pairs={{0,1},{1,0},{2,3},{3,2},{4,5},{5,4},{6,7},{7,6},{8,9},{9,8},{10,11... | collective-permute-start | bytes 1572872 | tf_op jit(solution)/shard_map/ppermute | solution.py:404
  39.8 4.3 %collective-permute-start.11 = (bf16[256,128]{1,0:T(8,128)(2,1)S(1)}, bf16[256,128]{1,0:T(8,128)(2,1)S(1)}, u32[]{:S(2)}, u32[]{:S(2)}) collective-permute-start(bf16[256,128]{1,0:T(8,128)(2,1)S(1)} %get-tuple-element.68), channel_id=1, source_target_pairs={{1,9},{3,11},{5,13},{7,15},{9,1},{11,3},{13,5},{15,7},{0,2},{2,0},... | collective-permute-start | bytes 196616 | tf_op jit(solution)/shard_map/ppermute | solution.py:388
  41.4 4.3 %collective-permute-start.12 = (bf16[256,128]{1,0:T(8,128)(2,1)S(1)}, bf16[256,128]{1,0:T(8,128)(2,1)S(1)}, u32[]{:S(2)}, u32[]{:S(2)}) collective-permute-start(bf16[256,128]{1,0:T(8,128)(2,1)S(1)} %get-tuple-element.69), channel_id=1, source_target_pairs={{1,11},{3,9},{5,15},{7,13},{9,3},{11,1},{13,7},{15,5},{0,4},{2,6},... | collective-permute-start | bytes 196616 | tf_op jit(solution)/shard_map/ppermute | solution.py:388
  43.1 5.8 %collective-permute-start.13 = (bf16[256,128]{1,0:T(8,128)(2,1)S(1)}, bf16[256,128]{1,0:T(8,128)(2,1)S(1)}, u32[]{:S(2)}, u32[]{:S(2)}) collective-permute-start(bf16[256,128]{1,0:T(8,128)(2,1)S(1)} %get-tuple-element.70), channel_id=1, source_target_pairs={{1,13},{3,15},{5,9},{7,11},{9,5},{11,7},{13,1},{15,3},{0,6},{2,4},... | collective-permute-start | bytes 196616 | tf_op jit(solution)/shard_map/ppermute | solution.py:388
  43.3 5.5 %collective-permute-start.14 = (bf16[256,128]{1,0:T(8,128)(2,1)S(1)}, bf16[256,128]{1,0:T(8,128)(2,1)S(1)}, u32[]{:S(2)}, u32[]{:S(2)}) collective-permute-start(bf16[256,128]{1,0:T(8,128)(2,1)S(1)} %get-tuple-element.71), channel_id=1, source_target_pairs={{1,15},{3,13},{5,11},{7,9},{9,7},{11,5},{13,3},{15,1},{17,31},{19,... | collective-permute-start | bytes 196616 | tf_op jit(solution)/shard_map/ppermute | solution.py:388
  48.9 5.7 %collective-permute-start.15 = (bf16[512,128]{1,0:T(8,128)(2,1)S(1)}, bf16[512,128]{1,0:T(8,128)(2,1)S(1)}, u32[]{:S(2)}, u32[]{:S(2)}) collective-permute-start(bf16[512,128]{1,0:T(8,128)(2,1)S(1)} %shard_map.107), channel_id=1, source_target_pairs={{0,1},{1,0},{2,3},{3,2},{4,5},{5,4},{6,7},{7,6},{8,9},{9,8},{10,11... | collective-permute-start | bytes 393224 | tf_op jit(solution)/shard_map/ppermute | solution.py:396

commit v7 on v6

--- a/solution.py
+++ b/solution.py
@@ -139,12 +139,19 @@
     return (first < second).astype(F32).astype(BF16)
 
 
+def peers(n):
+    half = n // 2
+    return list(range(n - 1, half + 1, -1)) + [half], list(range(1, half)) + [half + 1]
+
+
 def place_of(chip, n):
     apart = chip ^ lax.axis_index("row")
-    top = (apart >= n // 2).astype(jnp.int32)
-    step = jnp.where(top == 1, apart - n // 2, apart - 1)
-    other = (top != lax.axis_index("col")).astype(jnp.int32)
-    return jnp.where(apart == 0, 0, 1 + other * (n // 2) + step)
+    place = jnp.zeros_like(apart)
+    for core, steps in enumerate(peers(n)):
+        first = jnp.where(lax.axis_index("col") == core, 1, 1 + n // 2)
+        for step, k in enumerate(steps):
+            place = jnp.where(apart == k, first + step, place)
+    return place
 
 
 def basis_kernel(wanted, basis, supernode, out, wide, *, n, rows_chip, slots):
@@ -174,7 +181,8 @@
 def pick_kernel(mine, theirs, out, *, n, lines, total, rows_chip, slots):
     row = lax.axis_index("row")
     col = lax.axis_index("col")
-    first = jnp.where(col == 0, 1, n // 2)
+    far, near = peers(n)
+    far = far + near[-1:]
 
     def asked_by(chip, own):
         at = pl.ds(pl.multiple_of(chip * lines, lines), lines)
@@ -182,7 +190,7 @@
 
     asked = [asked_by(row, True)]
     for step in range(n // 2):
-        chip = row ^ jnp.minimum(first + step, n - 1)
+        chip = row ^ jnp.where(col == 0, far[step], near[step])
         asked += [asked_by(chip, col == 0), asked_by(chip, col == 1)]
     count = len(asked)
     asked = jnp.concatenate(asked, axis=0).astype(jnp.int32)
@@ -380,11 +388,12 @@
         cost_estimate=cost,
     )(pick, dens, dens_other)
 
+    far, near = peers(n_row)
     fetched = []
     for step in range(half_ring):
-        pairs = [(2 * r + 1, 2 * (r ^ (half_ring + step)) + 1) for r in range(n_row)]
-        if step + 1 < half_ring:
-            pairs += [(2 * r, 2 * (r ^ (1 + step))) for r in range(n_row)]
+        pairs = [(2 * r + 1, 2 * (r ^ near[step]) + 1) for r in range(n_row)]
+        if step < len(far):
+            pairs += [(2 * r, 2 * (r ^ far[step])) for r in range(n_row)]
         fetched.append(lax.ppermute(sent[step], ("row", "col"), pairs))
 
     turned = pl.pallas_call(

time: 56 us -> 55.1 us (0.984)
  starting transfers between devices: 19 us -> 16.5 us
  waiting for transfers between devices: 10.9 us -> 12.5 us
    ppermute x1, starting transfers between devices: 4.74 us -> 0.07 us  [local(): passed = lax.ppermute(turned, 'col', swap)]
    ppermute x4, starting transfers between devices: 4.21 us -> 6.38 us  [local(): fetched.append(lax.ppermute(sent[step], ('row', 'col'), pairs))]
    ppermute x4, waiting for transfers between devices: 4.88 us -> 6.1 us  [local(): fetched.append(lax.ppermute(sent[step], ('row', 'col'), pairs))]
where the time goes in v7:
time: 55.1 us; the launch traced here: 54.8 us
  starting transfers between devices  16.5 us (30%)
  Pallas kernels  16.3 us (30%)
  waiting for transfers between devices  12.5 us (23%)
  local copies, waits for them, and re-layouts  8.76 us (16%)
  between operations  0.83 us (2%)
    unnamed x20, local copies, waits for them, and re-layouts  8.74 us
    ppermute x4, starting transfers between devices, local(): fetched.append(lax.ppermute(sent[step], ('row', 'col'), pairs))  6.38 us
    ppermute x3, starting transfers between devices, local(): next_right = lax.ppermute(right, 'row', to_left)  6.3 us
    ppermute x4, waiting for transfers between devices, local(): fetched.append(lax.ppermute(sent[step], ('row', 'col'), pairs))  6.1 us
    pallas_call x2, Pallas kernels, local(): call(functools.partial(hop_middle, hop=h - 1), [in_smem] * 2 + [in_vmem]...  5.63 us
    ppermute x3, waiting for transfers between devices, local(): next_right = lax.ppermute(right, 'row', to_left)  3.75 us
    pallas_call x1, Pallas kernels, local(): call(hop_early, [in_smem] * 2 + [in_vmem] * 5, acc_out, [], 3, aliases={6...  3.64 us
    pallas_call x1, Pallas kernels, local(): call(hop_last, [in_smem] * 3 + [in_vmem] * 4, [acc_out, jax.ShapeDtypeStr...  2.05 us
  transfers between devices with their start and end apart: 16, of which 9 were waited for; matrix products, arithmetic and copies ran while one was open for 0% of the time, Pallas kernels for 27%

profile of v7, /device:TPU:0, one launch (start us, length us, event | category | flops | bytes accessed | tf_op | source)
XLA Modules:
  0.0 54.8 jit_solution(1543424704753774428)
XLA Ops:
  0.6 0.9 %copy-done.4 = bf16[1,8,2,64,128]{4,3,2,1,0:T(8,128)(2,1)S(1)} copy-done((bf16[1,8,2,64,128]{4,3,2,1,0:T(8,128)(2,1)S(1)}, bf16[1,8,2,64,128]{4,3,2,1,0:T(8,128)(2,1)}, u32[]{:S(2)}) %copy-start.4) | copy-done | bytes 262168
  1.6 0.7 %copy-done.5 = s32[2,256]{1,0:T(2,128)S(1)} copy-done((s32[2,256]{1,0:T(2,128)S(1)}, s32[2,256]{1,0:T(2,128)}, u32[]{:S(2)}) %copy-start.5) | copy-done | bytes 2072
  2.3 0.1 shard_map.95.own
  2.3 3.0 %collective-permute-start.2 = (bf16[1040,128]{1,0:T(8,128)(2,1)S(1)}, bf16[1040,128]{1,0:T(8,128)(2,1)S(1)}, u32[]{:S(2)}, u32[]{:S(2)}) collective-permute-start(bf16[1040,128]{1,0:T(8,128)(2,1)S(1)} %shard_map.95.own), channel_id=1, source_target_pairs={{4,0},{8,4},{12,8},{14,12},{10,14},{6,10},{2,6},{0,2},{5,1},{9,5},... | collective-permute-start | bytes 798728 | tf_op jit(solution)/shard_map/ppermute | solution.py:309
  5.3 0.1 collective-permute-start
  5.5 4.3 %copy-done = bf16[11,2,512,512]{3,2,1,0:T(8,128)(2,1)S(1)} copy-done((bf16[11,2,512,512]{3,2,1,0:T(8,128)(2,1)S(1)}, bf16[11,2,512,512]{3,2,1,0:T(8,128)(2,1)}, u32[]{:S(2)}) %copy-start) | copy-done | bytes 11534360
  9.7 0.7 %copy-done.7 = s32[11]{0:T(128)S(1)} copy-done((s32[11]{0:T(128)S(1)}, s32[11]{0:T(128)}, u32[]{:S(2)}) %copy-start.7) | copy-done | bytes 68
  10.4 0.7 %copy-done.8 = s32[11]{0:T(128)S(1)} copy-done((s32[11]{0:T(128)S(1)}, s32[11]{0:T(128)}, u32[]{:S(2)}) %copy-start.8) | copy-done | bytes 68
  11.1 0.1 shard_map.96
  11.1 0.6 %collective-permute-done.2.from_right.refs_2_ = bf16[1040,128]{1,0:T(8,128)(2,1)S(1)} collective-permute-done((bf16[1040,128]{1,0:T(8,128)(2,1)S(1)}, bf16[1040,128]{1,0:T(8,128)(2,1)S(1)}, u32[]{:S(2)}, u32[]{:S(2)}) %collective-permute-start.2) | collective-permute-done | bytes 266272 | tf_op jit(solution)/shard_map/ppermute | solution.py:309
  11.8 1.7 %collective-permute-start.4 = (bf16[1040,128]{1,0:T(8,128)(2,1)S(1)}, bf16[1040,128]{1,0:T(8,128)(2,1)S(1)}, u32[]{:S(2)}, u32[]{:S(2)}) collective-permute-start(bf16[1040,128]{1,0:T(8,128)(2,1)S(1)} %collective-permute-done.2.from_right.refs_2_), channel_id=1, source_target_pairs={{4,0},{8,4},{12,8},{14,12},{10,14},{6,10},{2,6},{0,2},{5,1},{9,5},... | collective-permute-start | bytes 798728 | tf_op jit(solution)/shard_map/ppermute | solution.py:309
  13.5 0.3 collective-permute-start.1
  13.8 1.5 %copy-done.1 = bf16[11,2,512,512]{3,2,1,0:T(8,128)(2,1)S(1)} copy-done((bf16[11,2,512,512]{3,2,1,0:T(8,128)(2,1)S(1)}, bf16[11,2,512,512]{3,2,1,0:T(8,128)(2,1)}, u32[]{:S(2)}) %copy-start.1) | copy-done | bytes 11534360
  15.3 3.6 %shard_map.97.start = f32[2,512,256]{2,1,0:T(8,128)S(1)} custom-call(s32[11]{0:T(128)S(1)} %get-tuple-element.40.slots, s32[11]{0:T(128)S(1)} %get-tuple-element.41.cols, bf16[1040,128]{1,0:T(8,128)(2,1)S(1)} %get-tuple-element.42.own.refs_0_, bf16[1040,128]{1,0:T(8,128)(2,1)S(1)} %collective-permute-done.from_left.refs_1_, ...), custom_call_target="tpu_custom_call", output_to_operand_aliasing={{}: (6, {})} | custom-call | flops 1048576 | bytes 1048576 | tf_op jit(solution)/shard_map/pallas_call | solution.py:330
  19.0 0.0 copy-start.2
  19.0 0.0 copy-start.3
  19.0 0.0 copy-start.6
  19.0 0.4 collective-permute-done.4.from_right.refs_4_
  19.4 1.6 %collective-permute-start.6 = (bf16[1040,128]{1,0:T(8,128)(2,1)S(1)}, bf16[1040,128]{1,0:T(8,128)(2,1)S(1)}, u32[]{:S(2)}, u32[]{:S(2)}) collective-permute-start(bf16[1040,128]{1,0:T(8,128)(2,1)S(1)} %collective-permute-done.4.from_right.refs_4_), channel_id=1, source_target_pairs={{4,0},{8,4},{12,8},{14,12},{10,14},{6,10},{2,6},{0,2},{5,1},{9,5},... | collective-permute-start | bytes 798728 | tf_op jit(solution)/shard_map/ppermute | solution.py:309
  21.0 0.4 collective-permute-start.3
  21.4 2.8 %shard_map.99.start = f32[2,512,256]{2,1,0:T(8,128)S(1)} custom-call(s32[11]{0:T(128)S(1)} %get-tuple-element.40.slots, s32[11]{0:T(128)S(1)} %get-tuple-element.41.cols, bf16[1040,128]{1,0:T(8,128)(2,1)S(1)} %collective-permute-done.1.from_left.refs_3_, ...), custom_call_target="tpu_custom_call", output_to_operand_aliasing={{}: (5, {})} | custom-call | flops 1048576 | bytes 1048576 | tf_op jit(solution)/shard_map/pallas_call | solution.py:334
  24.2 2.7 %collective-permute-done.6.from_right.refs_6_ = bf16[1040,128]{1,0:T(8,128)(2,1)S(1)} collective-permute-done((bf16[1040,128]{1,0:T(8,128)(2,1)S(1)}, bf16[1040,128]{1,0:T(8,128)(2,1)S(1)}, u32[]{:S(2)}, u32[]{:S(2)}) %collective-permute-start.6) | collective-permute-done | bytes 266272 | tf_op jit(solution)/shard_map/ppermute | solution.py:309
  27.0 1.7 %collective-permute-start.7 = (bf16[528,128]{1,0:T(8,128)(2,1)S(1)}, bf16[528,128]{1,0:T(8,128)(2,1)S(1)}, u32[]{:S(2)}, u32[]{:S(2)}) collective-permute-start(bf16[528,128]{1,0:T(8,128)(2,1)S(1)} %slice.7), channel_id=1, source_target_pairs={{4,0},{8,4},{12,8},{14,12},{10,14},{6,10},{2,6},{0,2},{5,1},{9,5},... | collective-permute-start | bytes 405512 | tf_op jit(solution)/shard_map/ppermute | solution.py:313
  28.6 1.0 %shard_map.98 = (bf16[2,1152,512]{2,1,0:T(8,128)(2,1)S(1)}, f32[2,128,512]{2,1,0:T(8,128)S(1)}) custom-call(s32[2,256]{1,0:T(2,128)S(1)} %copy-done.6, bf16[2,256,512]{2,1,0:T(8,128)(2,1)S(1)} %copy-done.2, bf16[2,128,512]{2,1,0:T(8,128)(2,1)S(1)} %copy-done.3), custom_call_target="tpu_custom_call" | custom-call | flops 1048576 | bytes 1048576 | tf_op jit(solution)/shard_map/pallas_call | solution.py:293
  29.6 0.0 copy-start.9
  29.6 0.5 collective-permute-start.5
  30.1 2.9 %shard_map.100.start = f32[2,512,256]{2,1,0:T(8,128)S(1)} custom-call(s32[11]{0:T(128)S(1)} %get-tuple-element.40.slots, s32[11]{0:T(128)S(1)} %get-tuple-element.41.cols, bf16[1040,128]{1,0:T(8,128)(2,1)S(1)} %collective-permute-done.3.from_left.refs_5_, ...), custom_call_target="tpu_custom_call", output_to_operand_aliasing={{}: (5, {})} | custom-call | flops 1048576 | bytes 1048576 | tf_op jit(solution)/shard_map/pallas_call | solution.py:334
  33.0 1.7 %collective-permute-done.5.low = bf16[512,128]{1,0:T(8,128)(2,1)S(1)} collective-permute-done((bf16[512,128]{1,0:T(8,128)(2,1)S(1)}, bf16[512,128]{1,0:T(8,128)(2,1)S(1)}, u32[]{:S(2)}, u32[]{:S(2)}) %collective-permute-start.5) | collective-permute-done | bytes 131104 | tf_op jit(solution)/shard_map/ppermute | solution.py:312
  34.7 0.1 shard_map.101.mine
  34.7 0.1 collective-permute-start.8
  34.8 2.1 %shard_map.102 = (f32[2,512,256]{2,1,0:T(8,128)S(1)}, f32[2,512,128]{2,1,0:T(8,128)S(1)}) custom-call(s32[11]{0:T(128)S(1)} %get-tuple-element.40.slots, s32[11]{0:T(128)S(1)} %get-tuple-element.41.cols, f32[2]{0:T(128)S(1)} %copy-done.9, bf16[512,128]{1,0:T(8,128)(2,1)S(1)} %collective-permute-done.5.low, ...), custom_call_target="tpu_custom_call", output_to_operand_aliasing={{0}: (6, {})} | custom-call | flops 1048576 | bytes 1048576 | tf_op jit(solution)/shard_map/pallas_call | solution.py:365
  36.9 0.6 %collective-permute-start.9 = (f32[2,512,128]{2,1,0:T(8,128)S(1)}, f32[2,512,128]{2,1,0:T(8,128)S(1)}, u32[]{:S(2)}, u32[]{:S(2)}) collective-permute-start(f32[2,512,128]{2,1,0:T(8,128)S(1)} %get-tuple-element.61.mine), channel_id=1, source_target_pairs={{0,1},{1,0},{2,3},{3,2},{4,5},{5,4},{6,7},{7,6},{8,9},{9,8},{10,11... | collective-permute-start | bytes 1572872 | tf_op jit(solution)/shard_map/ppermute | solution.py:374
  37.4 0.1 shard_map.105
  37.5 0.1 collective-permute-start.10
  37.6 0.9 %shard_map.103.pick = bf16[1152,1024]{1,0:T(8,128)(2,1)S(1)} custom-call(bf16[128,128]{1,0:T(8,128)(2,1)S(1)} %shard_map.101.mine, bf16[128,128]{1,0:T(8,128)(2,1)S(1)} %collective-permute-done.8.theirs), custom_call_target="tpu_custom_call" | custom-call | flops 4294967296 | bytes 1048576 | tf_op jit(solution)/shard_map/pallas_call | solution.py:375
  38.6 0.4 collective-permute-done.9.theirs
  39.0 0.8 %shard_map.104 = (bf16[128,128]{1,0:T(8,128)(2,1)S(1)}, bf16[256,128]{1,0:T(8,128)(2,1)S(1)}, bf16[256,128]{1,0:T(8,128)(2,1)S(1)}, bf16[256,128]{1,0:T(8,128)(2,1)S(1)}, bf16[256,128]{1,0:T(8,128)(2,1)S(1)}) custom-call(bf16[1152,1024]{1,0:T(8,128)(2,1)S(1)} %shard_map.103.pick, f32[2,512,128]{2,1,0:T(8,128)S(1)} %get-tuple-element.61.mine, ...), custom_call_target="tpu_custom_call" | custom-call | flops 1048576 | bytes 1048576 | tf_op jit(solution)/shard_map/pallas_call | solution.py:384
  39.8 3.6 %collective-permute-start.11 = (bf16[256,128]{1,0:T(8,128)(2,1)S(1)}, bf16[256,128]{1,0:T(8,128)(2,1)S(1)}, u32[]{:S(2)}, u32[]{:S(2)}) collective-permute-start(bf16[256,128]{1,0:T(8,128)(2,1)S(1)} %get-tuple-element.68), channel_id=1, source_target_pairs={{1,3},{3,1},{5,7},{7,5},{9,11},{11,9},{13,15},{15,13},{0,14},{2,12... | collective-permute-start | bytes 196616 | tf_op jit(solution)/shard_map/ppermute | solution.py:397
  43.4 1.3 %collective-permute-start.12 = (bf16[256,128]{1,0:T(8,128)(2,1)S(1)}, bf16[256,128]{1,0:T(8,128)(2,1)S(1)}, u32[]{:S(2)}, u32[]{:S(2)}) collective-permute-start(bf16[256,128]{1,0:T(8,128)(2,1)S(1)} %get-tuple-element.69), channel_id=1, source_target_pairs={{1,5},{3,7},{5,1},{7,3},{9,13},{11,15},{13,9},{15,11},{0,12},{2,14... | collective-permute-start | bytes 196616 | tf_op jit(solution)/shard_map/ppermute | solution.py:397
  44.7 0.8 %collective-permute-start.13 = (bf16[256,128]{1,0:T(8,128)(2,1)S(1)}, bf16[256,128]{1,0:T(8,128)(2,1)S(1)}, u32[]{:S(2)}, u32[]{:S(2)}) collective-permute-start(bf16[256,128]{1,0:T(8,128)(2,1)S(1)} %get-tuple-element.70), channel_id=1, source_target_pairs={{1,7},{3,5},{5,3},{7,1},{9,15},{11,13},{13,11},{15,9},{0,8},{2,10}... | collective-permute-start | bytes 196616 | tf_op jit(solution)/shard_map/ppermute | solution.py:397
  45.5 0.7 %collective-permute-start.14 = (bf16[256,128]{1,0:T(8,128)(2,1)S(1)}, bf16[256,128]{1,0:T(8,128)(2,1)S(1)}, u32[]{:S(2)}, u32[]{:S(2)}) collective-permute-start(bf16[256,128]{1,0:T(8,128)(2,1)S(1)} %get-tuple-element.71), channel_id=1, source_target_pairs={{1,11},{3,9},{5,15},{7,13},{9,3},{11,1},{13,7},{15,5},{17,27},{19,... | collective-permute-start | bytes 196616 | tf_op jit(solution)/shard_map/ppermute | solution.py:397
  46.2 1.3 %collective-permute-done.11.refs_0_.refs_1_ = bf16[256,128]{1,0:T(8,128)(2,1)S(1)} collective-permute-done((bf16[256,128]{1,0:T(8,128)(2,1)S(1)}, bf16[256,128]{1,0:T(8,128)(2,1)S(1)}, u32[]{:S(2)}, u32[]{:S(2)}) %collective-permute-start.11) | collective-permute-done | bytes 65568 | tf_op jit(solution)/shard_map/ppermute | solution.py:397
  47.5 2.0 %collective-permute-done.12.refs_1_.refs_2_ = bf16[256,128]{1,0:T(8,128)(2,1)S(1)} collective-permute-done((bf16[256,128]{1,0:T(8,128)(2,1)S(1)}, bf16[256,128]{1,0:T(8,128)(2,1)S(1)}, u32[]{:S(2)}, u32[]{:S(2)}) %collective-permute-start.12) | collective-permute-done | bytes 65568 | tf_op jit(solution)/shard_map/ppermute | solution.py:397
  49.5 2.8 %collective-permute-done.13.refs_2_.refs_3_ = bf16[256,128]{1,0:T(8,128)(2,1)S(1)} collective-permute-done((bf16[256,128]{1,0:T(8,128)(2,1)S(1)}, bf16[256,128]{1,0:T(8,128)(2,1)S(1)}, u32[]{:S(2)}, u32[]{:S(2)}) %collective-permute-start.13) | collective-permute-done | bytes 65568 | tf_op jit(solution)/shard_map/ppermute | solution.py:397
  52.3 0.1 collective-permute-start.15
  52.4 0.8 %shard_map.106 = f32[2,2,256,128]{3,2,1,0:T(8,128)} custom-call(f32[2,2,256,128]{3,2,1,0:T(8,128)S(1)} %get-tuple-element.64.mine, f32[2,2,256,128]{3,2,1,0:T(8,128)S(1)} %collective-permute-done.10.theirs), custom_call_target="tpu_custom_call" | custom-call | flops 1048576 | bytes 1048576 | tf_op jit(solution)/shard_map/pallas_call | solution.py:414
  53.2 0.5 collective-permute-done.15.refs_5_
  53.7 1.1 %shard_map.108 = f32[2,512]{1,0:T(2,128)} custom-call(bf16[128,128]{1,0:T(8,128)(2,1)S(1)} %get-tuple-element.67.refs_0_, bf16[256,128]{1,0:T(8,128)(2,1)S(1)} %collective-permute-done.11.refs_0_.refs_1_, bf16[256,128]{1,0:T(8,128)(2,1)S(1)} %collective-permute-done.12.refs_1_.refs_2_, bf16[256,128]{1,0:T(8,128)(2,1)S(1)} %collective-permute-done.13.refs_2_.refs_3_, ...), custom_call_target="tpu_custom_call" | custom-call | tf_op jit(solution)/shard_map/pallas_call | solution.py:421
  (20 shorter events, 0.1 us)
Async XLA Ops:
  0.6 1.0 %copy-start.4 = (bf16[1,8,2,64,128]{4,3,2,1,0:T(8,128)(2,1)S(1)}, bf16[1,8,2,64,128]{4,3,2,1,0:T(8,128)(2,1)}, u32[]{:S(2)}) copy-start(bf16[1,8,2,64,128]{4,3,2,1,0:T(8,128)(2,1)} %param.8) | copy-start | bytes 786436
  1.6 0.7 %copy-start.5 = (s32[2,256]{1,0:T(2,128)S(1)}, s32[2,256]{1,0:T(2,128)}, u32[]{:S(2)}) copy-start(s32[2,256]{1,0:T(2,128)} %wanted.3) | copy-start | bytes 6148
  2.3 9.5 %collective-permute-start.2 = (bf16[1040,128]{1,0:T(8,128)(2,1)S(1)}, bf16[1040,128]{1,0:T(8,128)(2,1)S(1)}, u32[]{:S(2)}, u32[]{:S(2)}) collective-permute-start(bf16[1040,128]{1,0:T(8,128)(2,1)S(1)} %shard_map.95.own), channel_id=1, source_target_pairs={{4,0},{8,4},{12,8},{14,12},{10,14},{6,10},{2,6},{0,2},{5,1},{9,5},... | collective-permute-start | bytes 798728 | tf_op jit(solution)/shard_map/ppermute | solution.py:309
  5.3 8.1 %collective-permute-start = (bf16[1040,128]{1,0:T(8,128)(2,1)S(1)}, bf16[1040,128]{1,0:T(8,128)(2,1)S(1)}, u32[]{:S(2)}, u32[]{:S(2)}) collective-permute-start(bf16[1040,128]{1,0:T(8,128)(2,1)S(1)} %shard_map.95.own), channel_id=1, source_target_pairs={{0,4},{4,8},{8,12},{12,14},{14,10},{10,6},{6,2},{2,0},{1,5},{5,9},... | collective-permute-start | bytes 798728 | tf_op jit(solution)/shard_map/ppermute | solution.py:308
  5.5 4.3 %copy-start = (bf16[11,2,512,512]{3,2,1,0:T(8,128)(2,1)S(1)}, bf16[11,2,512,512]{3,2,1,0:T(8,128)(2,1)}, u32[]{:S(2)}) copy-start(bf16[11,2,512,512]{3,2,1,0:T(8,128)(2,1)} %tiles.9) | copy-start | bytes 34603012
  9.7 0.7 %copy-start.7 = (s32[11]{0:T(128)S(1)}, s32[11]{0:T(128)}, u32[]{:S(2)}) copy-start(s32[11]{0:T(128)} %slots.1) | copy-start | bytes 136
  10.4 0.7 %copy-start.8 = (s32[11]{0:T(128)S(1)}, s32[11]{0:T(128)}, u32[]{:S(2)}) copy-start(s32[11]{0:T(128)} %cols.1) | copy-start | bytes 136
  11.1 4.3 %copy-start.1 = (bf16[11,2,512,512]{3,2,1,0:T(8,128)(2,1)S(1)}, bf16[11,2,512,512]{3,2,1,0:T(8,128)(2,1)}, u32[]{:S(2)}) copy-start(bf16[11,2,512,512]{3,2,1,0:T(8,128)(2,1)} %tiles.9) | copy-start | bytes 34603012
  11.8 7.6 %collective-permute-start.4 = (bf16[1040,128]{1,0:T(8,128)(2,1)S(1)}, bf16[1040,128]{1,0:T(8,128)(2,1)S(1)}, u32[]{:S(2)}, u32[]{:S(2)}) collective-permute-start(bf16[1040,128]{1,0:T(8,128)(2,1)S(1)} %collective-permute-done.2.from_right.refs_2_), channel_id=1, source_target_pairs={{4,0},{8,4},{12,8},{14,12},{10,14},{6,10},{2,6},{0,2},{5,1},{9,5},... | collective-permute-start | bytes 798728 | tf_op jit(solution)/shard_map/ppermute | solution.py:309
  13.5 7.5 %collective-permute-start.1 = (bf16[1040,128]{1,0:T(8,128)(2,1)S(1)}, bf16[1040,128]{1,0:T(8,128)(2,1)S(1)}, u32[]{:S(2)}, u32[]{:S(2)}) collective-permute-start(bf16[1040,128]{1,0:T(8,128)(2,1)S(1)} %collective-permute-done.from_left.refs_1_), channel_id=1, source_target_pairs={{0,4},{4,8},{8,12},{12,14},{14,10},{10,6},{6,2},{2,0},{1,5},{5,9},... | collective-permute-start | bytes 798728 | tf_op jit(solution)/shard_map/ppermute | solution.py:308
  19.0 9.6 %copy-start.2 = (bf16[2,256,512]{2,1,0:T(8,128)(2,1)S(1)}, bf16[2,256,512]{2,1,0:T(8,128)(2,1)}, u32[]{:S(2)}) copy-start(bf16[2,256,512]{2,1,0:T(8,128)(2,1)} %basis.1) | copy-start | bytes 1572868
  19.0 9.6 %copy-start.3 = (bf16[2,128,512]{2,1,0:T(8,128)(2,1)S(1)}, bf16[2,128,512]{2,1,0:T(8,128)(2,1)}, u32[]{:S(2)}) copy-start(bf16[2,128,512]{2,1,0:T(8,128)(2,1)} %supernode.1) | copy-start | bytes 786436
  19.0 9.6 %copy-start.6 = (s32[2,256]{1,0:T(2,128)S(1)}, s32[2,256]{1,0:T(2,128)}, u32[]{:S(2)}) copy-start(s32[2,256]{1,0:T(2,128)} %wanted.3) | copy-start | bytes 6148
  19.4 7.6 %collective-permute-start.6 = (bf16[1040,128]{1,0:T(8,128)(2,1)S(1)}, bf16[1040,128]{1,0:T(8,128)(2,1)S(1)}, u32[]{:S(2)}, u32[]{:S(2)}) collective-permute-start(bf16[1040,128]{1,0:T(8,128)(2,1)S(1)} %collective-permute-done.4.from_right.refs_4_), channel_id=1, source_target_pairs={{4,0},{8,4},{12,8},{14,12},{10,14},{6,10},{2,6},{0,2},{5,1},{9,5},... | collective-permute-start | bytes 798728 | tf_op jit(solution)/shard_map/ppermute | solution.py:309
  21.0 8.6 %collective-permute-start.3 = (bf16[1040,128]{1,0:T(8,128)(2,1)S(1)}, bf16[1040,128]{1,0:T(8,128)(2,1)S(1)}, u32[]{:S(2)}, u32[]{:S(2)}) collective-permute-start(bf16[1040,128]{1,0:T(8,128)(2,1)S(1)} %collective-permute-done.1.from_left.refs_3_), channel_id=1, source_target_pairs={{0,4},{4,8},{8,12},{12,14},{14,10},{10,6},{6,2},{2,0},{1,5},{5,9},... | collective-permute-start | bytes 798728 | tf_op jit(solution)/shard_map/ppermute | solution.py:308
  27.0 7.7 %collective-permute-start.7 = (bf16[528,128]{1,0:T(8,128)(2,1)S(1)}, bf16[528,128]{1,0:T(8,128)(2,1)S(1)}, u32[]{:S(2)}, u32[]{:S(2)}) collective-permute-start(bf16[528,128]{1,0:T(8,128)(2,1)S(1)} %slice.7), channel_id=1, source_target_pairs={{4,0},{8,4},{12,8},{14,12},{10,14},{6,10},{2,6},{0,2},{5,1},{9,5},... | collective-permute-start | bytes 405512 | tf_op jit(solution)/shard_map/ppermute | solution.py:313
  29.6 5.2 %copy-start.9 = (f32[2]{0:T(128)S(1)}, f32[2]{0:T(128)}, u32[]{:S(2)}) copy-start(f32[2]{0:T(128)} %pole_weight.1) | copy-start | bytes 28
  29.6 5.0 %collective-permute-start.5 = (bf16[512,128]{1,0:T(8,128)(2,1)S(1)}, bf16[512,128]{1,0:T(8,128)(2,1)S(1)}, u32[]{:S(2)}, u32[]{:S(2)}) collective-permute-start(bf16[512,128]{1,0:T(8,128)(2,1)S(1)} %slice.6), channel_id=1, source_target_pairs={{0,4},{4,8},{8,12},{12,14},{14,10},{10,6},{6,2},{2,0},{1,5},{5,9},... | collective-permute-start | bytes 393224 | tf_op jit(solution)/shard_map/ppermute | solution.py:312
  34.7 2.2 %collective-permute-start.8 = (bf16[128,128]{1,0:T(8,128)(2,1)S(1)}, bf16[128,128]{1,0:T(8,128)(2,1)S(1)}, u32[]{:S(2)}, u32[]{:S(2)}) collective-permute-start(bf16[128,128]{1,0:T(8,128)(2,1)S(1)} %shard_map.101.mine), channel_id=1, source_target_pairs={{0,1},{1,0},{2,3},{3,2},{4,5},{5,4},{6,7},{7,6},{8,9},{9,8},{10,11... | collective-permute-start | bytes 98312 | tf_op jit(solution)/shard_map/ppermute | solution.py:362
  36.9 2.1 %collective-permute-start.9 = (f32[2,512,128]{2,1,0:T(8,128)S(1)}, f32[2,512,128]{2,1,0:T(8,128)S(1)}, u32[]{:S(2)}, u32[]{:S(2)}) collective-permute-start(f32[2,512,128]{2,1,0:T(8,128)S(1)} %get-tuple-element.61.mine), channel_id=1, source_target_pairs={{0,1},{1,0},{2,3},{3,2},{4,5},{5,4},{6,7},{7,6},{8,9},{9,8},{10,11... | collective-permute-start | bytes 1572872 | tf_op jit(solution)/shard_map/ppermute | solution.py:374
  37.5 14.8 %collective-permute-start.10 = (f32[2,2,256,128]{3,2,1,0:T(8,128)S(1)}, f32[2,2,256,128]{3,2,1,0:T(8,128)S(1)}, u32[]{:S(2)}, u32[]{:S(2)}) collective-permute-start(f32[2,2,256,128]{3,2,1,0:T(8,128)S(1)} %get-tuple-element.65), channel_id=1, source_target_pairs={{0,1},{1,0},{2,3},{3,2},{4,5},{5,4},{6,7},{7,6},{8,9},{9,8},{10,11... | collective-permute-start | bytes 1572872 | tf_op jit(solution)/shard_map/ppermute | solution.py:413
  39.8 7.7 %collective-permute-start.11 = (bf16[256,128]{1,0:T(8,128)(2,1)S(1)}, bf16[256,128]{1,0:T(8,128)(2,1)S(1)}, u32[]{:S(2)}, u32[]{:S(2)}) collective-permute-start(bf16[256,128]{1,0:T(8,128)(2,1)S(1)} %get-tuple-element.68), channel_id=1, source_target_pairs={{1,3},{3,1},{5,7},{7,5},{9,11},{11,9},{13,15},{15,13},{0,14},{2,12... | collective-permute-start | bytes 196616 | tf_op jit(solution)/shard_map/ppermute | solution.py:397
  43.4 6.1 %collective-permute-start.12 = (bf16[256,128]{1,0:T(8,128)(2,1)S(1)}, bf16[256,128]{1,0:T(8,128)(2,1)S(1)}, u32[]{:S(2)}, u32[]{:S(2)}) collective-permute-start(bf16[256,128]{1,0:T(8,128)(2,1)S(1)} %get-tuple-element.69), channel_id=1, source_target_pairs={{1,5},{3,7},{5,1},{7,3},{9,13},{11,15},{13,9},{15,11},{0,12},{2,14... | collective-permute-start | bytes 196616 | tf_op jit(solution)/shard_map/ppermute | solution.py:397
  44.7 7.6 %collective-permute-start.13 = (bf16[256,128]{1,0:T(8,128)(2,1)S(1)}, bf16[256,128]{1,0:T(8,128)(2,1)S(1)}, u32[]{:S(2)}, u32[]{:S(2)}) collective-permute-start(bf16[256,128]{1,0:T(8,128)(2,1)S(1)} %get-tuple-element.70), channel_id=1, source_target_pairs={{1,7},{3,5},{5,3},{7,1},{9,15},{11,13},{13,11},{15,9},{0,8},{2,10}... | collective-permute-start | bytes 196616 | tf_op jit(solution)/shard_map/ppermute | solution.py:397
  45.5 6.8 %collective-permute-start.14 = (bf16[256,128]{1,0:T(8,128)(2,1)S(1)}, bf16[256,128]{1,0:T(8,128)(2,1)S(1)}, u32[]{:S(2)}, u32[]{:S(2)}) collective-permute-start(bf16[256,128]{1,0:T(8,128)(2,1)S(1)} %get-tuple-element.71), channel_id=1, source_target_pairs={{1,11},{3,9},{5,15},{7,13},{9,3},{11,1},{13,7},{15,5},{17,27},{19,... | collective-permute-start | bytes 196616 | tf_op jit(solution)/shard_map/ppermute | solution.py:397
  52.3 1.4 %collective-permute-start.15 = (bf16[512,128]{1,0:T(8,128)(2,1)S(1)}, bf16[512,128]{1,0:T(8,128)(2,1)S(1)}, u32[]{:S(2)}, u32[]{:S(2)}) collective-permute-start(bf16[512,128]{1,0:T(8,128)(2,1)S(1)} %shard_map.107), channel_id=1, source_target_pairs={{0,1},{1,0},{2,3},{3,2},{4,5},{5,4},{6,7},{7,6},{8,9},{9,8},{10,11... | collective-permute-start | bytes 393224 | tf_op jit(solution)/shard_map/ppermute | solution.py:405

commit v8 on v7

--- a/solution.py
+++ b/solution.py
@@ -12,7 +12,6 @@
 F32 = jnp.float32
 BF16 = jnp.bfloat16
 VMEM_LIMIT = 8 * 1024 * 1024
-PACK_LIMIT = 8 * 1024 * 1024
 
 
 def ring_order(n):
@@ -46,15 +45,13 @@
     return jnp.concatenate([whole[i:i + 1] for i in range(count)], axis=1)
 
 
-def pack_kernel(panel, wanted, out, held, sems):
-    rows = panel.shape[0]
-    bring = pltpu.make_async_copy(wanted, held, sems.at[0])
-    copy = pltpu.make_async_copy(panel, out.at[pl.ds(0, rows)], sems.at[1])
-    bring.start()
-    copy.start()
-    bring.wait()
-    out[rows:, :] = digits(held[...])
-    copy.wait()
+def digits_kernel(wanted, out):
+    out[...] = digits(wanted[...])
+
+
+def pack_kernel(rows, lines, out):
+    out[:rows.shape[0], :] = rows[...]
+    out[rows.shape[0]:, :] = lines[...]
 
 
 def place(part, block, depth, first):
@@ -88,16 +85,8 @@
         acc[slots[t]] += jnp.dot(left, weights[cols[t]], preferred_element_type=F32)
 
 
-def stage_kernel(slots, cols, own, tiles, slots_out, cols_out, own_out, out):
-    del tiles
-    slots_out[...] = slots[...]
-    cols_out[...] = cols[...]
-    own_out[...] = own[...]
+def hop_early(slots, cols, own, from_left, from_right, tiles, out, weights, *, n, depth):
     out[...] = jnp.zeros_like(out)
-
-
-def hop_early(slots, cols, own, from_left, from_right, tiles, start, out, weights, *, n, depth):
-    del start
     shards = [
         (shard_row(n, 0), depth, [own]),
         (shard_row(n, -1), depth, [from_left]),
@@ -263,7 +252,6 @@
     acc_out = jax.ShapeDtypeStruct(acc_shape, F32)
     in_vmem = pl.BlockSpec(memory_space=pltpu.VMEM)
     in_smem = pl.BlockSpec(memory_space=pltpu.SMEM)
-    in_hbm = pl.BlockSpec(memory_space=pltpu.HBM)
     params = pltpu.CompilerParams(vmem_limit_bytes=VMEM_LIMIT)
     cost = pl.CostEstimate(flops=2 ** 20, bytes_accessed=2 ** 20, transcendentals=0)
 
@@ -280,15 +268,19 @@
             cost_estimate=cost,
         )
 
-    own = pl.pallas_call(
+    own = panel.reshape(shard_rows, width)
+    own_lines = pl.pallas_call(
+        digits_kernel,
+        out_shape=jax.ShapeDtypeStruct((lines, width), BF16),
+        compiler_params=params,
+        cost_estimate=pl.CostEstimate(flops=2 ** 34, bytes_accessed=2 ** 10, transcendentals=0),
+    )(box_orbitals)
+    pack = pl.pallas_call(
         pack_kernel,
-        in_specs=[in_hbm, in_hbm],
-        out_specs=in_vmem,
         out_shape=jax.ShapeDtypeStruct((shard_rows + lines, width), BF16),
-        scratch_shapes=[pltpu.VMEM(box_orbitals.shape, jnp.int32), pltpu.SemaphoreType.DMA((2,))],
-        compiler_params=pltpu.CompilerParams(vmem_limit_bytes=PACK_LIMIT),
-        cost_estimate=cost,
-    )(panel.reshape(shard_rows, width), box_orbitals)
+        compiler_params=params,
+        cost_estimate=cost,
+    )
 
     basis_here, wide = pl.pallas_call(
         functools.partial(basis_kernel, n=n_row, rows_chip=rows_chip, slots=slots),
@@ -301,7 +293,7 @@
     )(box_orbitals, box_basis, supernode_basis)
 
     left, right = own, own
-    seen, hops = [own], [0]
+    seen, hops = [own_lines], [0]
     acc = None
     for h in range(1, half_ring + 1):
         if h < half_ring:
@@ -312,24 +304,16 @@
             next_left = lax.ppermute(left[:cut], "row", to_right)
             next_right = lax.ppermute(right[cut:], "row", to_left)
         if h == 1:
-            tile_slot, tile_col, own, acc = pl.pallas_call(
-                stage_kernel,
-                in_specs=[in_vmem] * 4,
-                out_specs=[in_vmem] * 4,
-                out_shape=[
-                    jax.ShapeDtypeStruct(tile_slot.shape, jnp.int32),
-                    jax.ShapeDtypeStruct(tile_col.shape, jnp.int32),
-                    jax.ShapeDtypeStruct(own.shape, BF16),
-                    acc_out,
-                ],
-                compiler_params=params,
-                cost_estimate=cost,
-            )(tile_slot, tile_col, own, tiles)
-            seen[0] = own
-        elif h == 2:
-            acc = call(
-                hop_early, [in_smem] * 2 + [in_vmem] * 5, acc_out, [], 3, aliases={6: 0}
-            )(tile_slot, tile_col, own, left, right, tiles, acc)
+            seen += [
+                lax.ppermute(own_lines, "row", to_right), lax.ppermute(own_lines, "row", to_left)
+            ]
+            hops += [-1, 1]
+            left, right = pack(next_left, seen[1]), pack(next_right, seen[2])
+            continue
+        if h == 2:
+            acc = call(hop_early, [in_smem] * 2 + [in_vmem] * 4, acc_out, [], 3)(
+                tile_slot, tile_col, own, left, right, tiles
+            )
         elif h > 2:
             acc = call(
                 functools.partial(hop_middle, hop=h - 1),

time: 55.1 us -> 52.8 us (0.958)
  local copies, waits for them, and re-layouts: 8.76 us -> 1.01 us
  starting transfers between devices: 16.5 us -> 19.4 us
  waiting for transfers between devices: 12.5 us -> 15.1 us
    unnamed x20 -> x22, local copies, waits for them, and re-layouts: 8.74 us -> 0.99 us
    ppermute x0 -> x2, waiting for transfers between devices: none -> 2.99 us  [the longest x1 2.99 us: local(): lax.ppermute(own_lines, 'row', to_left)]
    ppermute x0 -> x2, starting transfers between devices: none -> 2.6 us  [the longest x1 2.47 us: local(): lax.ppermute(own_lines, 'row', to_left)]
    pallas_call x3 -> x4, Pallas kernels: 3.78 us -> 3.79 us  [the longest x1 3.73 us: local(): call(hop_early, [in_smem] * 2 + [in_vmem] * 4, acc_out, [], 3)]
  transfers between devices with their start and end apart: 16 -> 18, of which waited for: 9 -> 9; matrix products, arithmetic and copies ran while one was open for 0% -> 0% of each run, Pallas kernels for 27% -> 29%
where the time goes in v8:
time: 52.8 us; the launch traced here: 52.6 us
  starting transfers between devices  19.4 us (37%)
  Pallas kernels  16.2 us (31%)
  waiting for transfers between devices  15.1 us (29%)
  local copies, waits for them, and re-layouts  1.01 us (2%)
  between operations  0.9 us (2%)
    ppermute x4, starting transfers between devices, local(): fetched.append(lax.ppermute(sent[step], ('row', 'col'), pairs))  6.44 us
    ppermute x3, starting transfers between devices, local(): next_right = lax.ppermute(right, 'row', to_left)  6.12 us
    ppermute x4, waiting for transfers between devices, local(): fetched.append(lax.ppermute(sent[step], ('row', 'col'), pairs))  6.1 us
    pallas_call x2, Pallas kernels, local(): call(functools.partial(hop_middle, hop=h - 1), [in_smem] * 2 + [in_vmem]...  5.63 us
    pallas_call x1, Pallas kernels, local(): call(hop_early, [in_smem] * 2 + [in_vmem] * 4, acc_out, [], 3)  3.73 us
    ppermute x3, waiting for transfers between devices, local(): next_right = lax.ppermute(right, 'row', to_left)  3.4 us
    ppermute x1, waiting for transfers between devices, local(): lax.ppermute(own_lines, 'row', to_left)  2.99 us
    ppermute x1, starting transfers between devices, local(): lax.ppermute(own_lines, 'row', to_left)  2.47 us
  transfers between devices with their start and end apart: 18, of which 9 were waited for; matrix products, arithmetic and copies ran while one was open for 0% of the time, Pallas kernels for 29%

profile of v8, /device:TPU:0, one launch (start us, length us, event | category | flops | bytes accessed | tf_op | source)
XLA Modules:
  0.0 52.6 jit_solution(531712127381799274)
XLA Ops:
  0.6 0.0 slice-start.1
  0.7 0.0 slice-start.2
  0.7 3.0 %collective-permute-start.3 = (bf16[1024,128]{1,0:T(8,128)(2,1)}, bf16[1024,128]{1,0:T(8,128)(2,1)S(1)}, u32[]{:S(2)}, u32[]{:S(2)}) collective-permute-start(bf16[1024,128]{1,0:T(8,128)(2,1)} %bitcast.3), channel_id=1, source_target_pairs={{4,0},{8,4},{12,8},{14,12},{10,14},{6,10},{2,6},{0,2},{5,1},{9,5},... | collective-permute-start | bytes 786440 | tf_op jit(solution)/shard_map/ppermute | solution.py:301
  3.7 0.1 collective-permute-start
  3.8 0.9 %copy-done.5 = s32[2,256]{1,0:T(2,128)S(1)} copy-done((s32[2,256]{1,0:T(2,128)S(1)}, s32[2,256]{1,0:T(2,128)}, u32[]{:S(2)}) %copy-start.5) | copy-done | bytes 2072
  4.8 2.5 %collective-permute-start.4 = (bf16[16,128]{1,0:T(8,128)(2,1)S(1)}, bf16[16,128]{1,0:T(8,128)(2,1)S(1)}, u32[]{:S(2)}, u32[]{:S(2)}) collective-permute-start(bf16[16,128]{1,0:T(8,128)(2,1)S(1)} %shard_map.95.refs_0_), channel_id=1, source_target_pairs={{4,0},{8,4},{12,8},{14,12},{10,14},{6,10},{2,6},{0,2},{5,1},{9,5},... | collective-permute-start | bytes 12296 | tf_op jit(solution)/shard_map/ppermute | solution.py:308
  7.3 0.1 collective-permute-start.1
  7.4 3.0 %collective-permute-done.4.lines.refs_2_ = bf16[16,128]{1,0:T(8,128)(2,1)S(1)} collective-permute-done((bf16[16,128]{1,0:T(8,128)(2,1)S(1)}, bf16[16,128]{1,0:T(8,128)(2,1)S(1)}, u32[]{:S(2)}, u32[]{:S(2)}) %collective-permute-start.4) | collective-permute-done | bytes 4128 | tf_op jit(solution)/shard_map/ppermute | solution.py:308
  10.4 1.7 %collective-permute-start.6 = (bf16[1040,128]{1,0:T(8,128)(2,1)S(1)}, bf16[1040,128]{1,0:T(8,128)(2,1)S(1)}, u32[]{:S(2)}, u32[]{:S(2)}) collective-permute-start(bf16[1040,128]{1,0:T(8,128)(2,1)S(1)} %shard_map.97.from_right), channel_id=1, source_target_pairs={{4,0},{8,4},{12,8},{14,12},{10,14},{6,10},{2,6},{0,2},{5,1},{9,5},... | collective-permute-start | bytes 798728 | tf_op jit(solution)/shard_map/ppermute | solution.py:301
  12.1 0.0 collective-permute-done.1.lines.refs_1_
  12.1 0.0 collective-permute-done.rows
  12.2 0.4 collective-permute-start.2
  12.6 3.7 %shard_map.98.start = f32[2,512,256]{2,1,0:T(8,128)S(1)} custom-call(s32[11]{0:T(128)S(1)} %copy-done.3, s32[11]{0:T(128)S(1)} %copy-done.4, bf16[1024,128]{1,0:T(8,128)(2,1)S(1)} %bitcast.5, bf16[1040,128]{1,0:T(8,128)(2,1)S(1)} %shard_map.96.from_left, bf16[1040,128]{1,0:T(8,128)(2,1)S(1)} %shard_map.97.from_right, bf16[11,2,512,512]{3,2,1,0:T(8,128)(2,1)S(1)} %bitcast.2), custom_call_target="tpu_custom_call" | custom-call | flops 1048576 | bytes 1048576 | tf_op jit(solution)/shard_map/pallas_call | solution.py:314
  16.3 0.0 copy-start
  16.4 0.0 copy-start.2
  16.4 0.0 copy-start.6
  16.4 1.7 %collective-permute-done.6.from_right.refs_4_ = bf16[1040,128]{1,0:T(8,128)(2,1)S(1)} collective-permute-done((bf16[1040,128]{1,0:T(8,128)(2,1)S(1)}, bf16[1040,128]{1,0:T(8,128)(2,1)S(1)}, u32[]{:S(2)}, u32[]{:S(2)}) %collective-permute-start.6) | collective-permute-done | bytes 266272 | tf_op jit(solution)/shard_map/ppermute | solution.py:301
  18.0 1.4 %collective-permute-start.8 = (bf16[1040,128]{1,0:T(8,128)(2,1)S(1)}, bf16[1040,128]{1,0:T(8,128)(2,1)S(1)}, u32[]{:S(2)}, u32[]{:S(2)}) collective-permute-start(bf16[1040,128]{1,0:T(8,128)(2,1)S(1)} %collective-permute-done.6.from_right.refs_4_), channel_id=1, source_target_pairs={{4,0},{8,4},{12,8},{14,12},{10,14},{6,10},{2,6},{0,2},{5,1},{9,5},... | collective-permute-start | bytes 798728 | tf_op jit(solution)/shard_map/ppermute | solution.py:301
  19.4 0.7 %collective-permute-start.5 = (bf16[1040,128]{1,0:T(8,128)(2,1)S(1)}, bf16[1040,128]{1,0:T(8,128)(2,1)S(1)}, u32[]{:S(2)}, u32[]{:S(2)}) collective-permute-start(bf16[1040,128]{1,0:T(8,128)(2,1)S(1)} %collective-permute-done.2.from_left.refs_3_), channel_id=1, source_target_pairs={{0,4},{4,8},{8,12},{12,14},{14,10},{10,6},{6,2},{2,0},{1,5},{5,9},... | collective-permute-start | bytes 798728 | tf_op jit(solution)/shard_map/ppermute | solution.py:300
  20.1 2.9 %shard_map.100.start = f32[2,512,256]{2,1,0:T(8,128)S(1)} custom-call(s32[11]{0:T(128)S(1)} %copy-done.3, s32[11]{0:T(128)S(1)} %copy-done.4, bf16[1040,128]{1,0:T(8,128)(2,1)S(1)} %collective-permute-done.2.from_left.refs_3_, bf16[1040,128]{1,0:T(8,128)(2,1)S(1)} %collective-permute-done.6.from_right.refs_4_, ...), custom_call_target="tpu_custom_call", output_to_operand_aliasing={{}: (5, {})} | custom-call | flops 1048576 | bytes 1048576 | tf_op jit(solution)/shard_map/pallas_call | solution.py:318
  22.9 1.7 %collective-permute-done.8.from_right.refs_6_ = bf16[1040,128]{1,0:T(8,128)(2,1)S(1)} collective-permute-done((bf16[1040,128]{1,0:T(8,128)(2,1)S(1)}, bf16[1040,128]{1,0:T(8,128)(2,1)S(1)}, u32[]{:S(2)}, u32[]{:S(2)}) %collective-permute-start.8) | collective-permute-done | bytes 266272 | tf_op jit(solution)/shard_map/ppermute | solution.py:301
  24.7 1.6 %collective-permute-start.9 = (bf16[528,128]{1,0:T(8,128)(2,1)S(1)}, bf16[528,128]{1,0:T(8,128)(2,1)S(1)}, u32[]{:S(2)}, u32[]{:S(2)}) collective-permute-start(bf16[528,128]{1,0:T(8,128)(2,1)S(1)} %slice.7), channel_id=1, source_target_pairs={{4,0},{8,4},{12,8},{14,12},{10,14},{6,10},{2,6},{0,2},{5,1},{9,5},... | collective-permute-start | bytes 405512 | tf_op jit(solution)/shard_map/ppermute | solution.py:305
  26.3 1.0 %shard_map.99 = (bf16[2,1152,512]{2,1,0:T(8,128)(2,1)S(1)}, f32[2,128,512]{2,1,0:T(8,128)S(1)}) custom-call(s32[2,256]{1,0:T(2,128)S(1)} %copy-done.6, bf16[2,256,512]{2,1,0:T(8,128)(2,1)S(1)} %copy-done, bf16[2,128,512]{2,1,0:T(8,128)(2,1)S(1)} %copy-done.2), custom_call_target="tpu_custom_call" | custom-call | flops 1048576 | bytes 1048576 | tf_op jit(solution)/shard_map/pallas_call | solution.py:285
  27.2 0.0 collective-permute-done.5.from_left.refs_5_
  27.3 0.0 copy-start.7
  27.3 0.8 %collective-permute-start.7 = (bf16[512,128]{1,0:T(8,128)(2,1)S(1)}, bf16[512,128]{1,0:T(8,128)(2,1)S(1)}, u32[]{:S(2)}, u32[]{:S(2)}) collective-permute-start(bf16[512,128]{1,0:T(8,128)(2,1)S(1)} %slice.6), channel_id=1, source_target_pairs={{0,4},{4,8},{8,12},{12,14},{14,10},{10,6},{6,2},{2,0},{1,5},{5,9},... | collective-permute-start | bytes 393224 | tf_op jit(solution)/shard_map/ppermute | solution.py:304
  28.0 2.8 %shard_map.101.start = f32[2,512,256]{2,1,0:T(8,128)S(1)} custom-call(s32[11]{0:T(128)S(1)} %copy-done.3, s32[11]{0:T(128)S(1)} %copy-done.4, bf16[1040,128]{1,0:T(8,128)(2,1)S(1)} %collective-permute-done.5.from_left.refs_5_, bf16[1040,128]{1,0:T(8,128)(2,1)S(1)} %collective-permute-done.8.from_right.refs_6_, ...), custom_call_target="tpu_custom_call", output_to_operand_aliasing={{}: (5, {})} | custom-call | flops 1048576 | bytes 1048576 | tf_op jit(solution)/shard_map/pallas_call | solution.py:318
  30.8 1.7 %collective-permute-done.7.low = bf16[512,128]{1,0:T(8,128)(2,1)S(1)} collective-permute-done((bf16[512,128]{1,0:T(8,128)(2,1)S(1)}, bf16[512,128]{1,0:T(8,128)(2,1)S(1)}, u32[]{:S(2)}, u32[]{:S(2)}) %collective-permute-start.7) | collective-permute-done | bytes 131104 | tf_op jit(solution)/shard_map/ppermute | solution.py:304
  32.5 0.1 shard_map.102.mine
  32.5 0.1 collective-permute-start.10
  32.6 2.0 %shard_map.103 = (f32[2,512,256]{2,1,0:T(8,128)S(1)}, f32[2,512,128]{2,1,0:T(8,128)S(1)}) custom-call(s32[11]{0:T(128)S(1)} %copy-done.3, s32[11]{0:T(128)S(1)} %copy-done.4, f32[2]{0:T(128)S(1)} %copy-done.7, bf16[512,128]{1,0:T(8,128)(2,1)S(1)} %collective-permute-done.7.low, ...), custom_call_target="tpu_custom_call", output_to_operand_aliasing={{0}: (6, {})} | custom-call | flops 1048576 | bytes 1048576 | tf_op jit(solution)/shard_map/pallas_call | solution.py:349
  34.6 0.6 %collective-permute-start.11 = (f32[2,512,128]{2,1,0:T(8,128)S(1)}, f32[2,512,128]{2,1,0:T(8,128)S(1)}, u32[]{:S(2)}, u32[]{:S(2)}) collective-permute-start(f32[2,512,128]{2,1,0:T(8,128)S(1)} %get-tuple-element.47.mine), channel_id=1, source_target_pairs={{0,1},{1,0},{2,3},{3,2},{4,5},{5,4},{6,7},{7,6},{8,9},{9,8},{10,11... | collective-permute-start | bytes 1572872 | tf_op jit(solution)/shard_map/ppermute | solution.py:358
  35.2 0.1 shard_map.106
  35.2 0.1 collective-permute-start.12
  35.3 0.9 %shard_map.104.pick = bf16[1152,1024]{1,0:T(8,128)(2,1)S(1)} custom-call(bf16[128,128]{1,0:T(8,128)(2,1)S(1)} %shard_map.102.mine, bf16[128,128]{1,0:T(8,128)(2,1)S(1)} %collective-permute-done.10.theirs), custom_call_target="tpu_custom_call" | custom-call | flops 4294967296 | bytes 1048576 | tf_op jit(solution)/shard_map/pallas_call | solution.py:359
  36.3 0.4 collective-permute-done.11.theirs
  36.7 0.8 %shard_map.105 = (bf16[128,128]{1,0:T(8,128)(2,1)S(1)}, bf16[256,128]{1,0:T(8,128)(2,1)S(1)}, bf16[256,128]{1,0:T(8,128)(2,1)S(1)}, bf16[256,128]{1,0:T(8,128)(2,1)S(1)}, bf16[256,128]{1,0:T(8,128)(2,1)S(1)}) custom-call(bf16[1152,1024]{1,0:T(8,128)(2,1)S(1)} %shard_map.104.pick, f32[2,512,128]{2,1,0:T(8,128)S(1)} %get-tuple-element.47.mine, ...), custom_call_target="tpu_custom_call" | custom-call | flops 1048576 | bytes 1048576 | tf_op jit(solution)/shard_map/pallas_call | solution.py:368
  37.5 3.7 %collective-permute-start.13 = (bf16[256,128]{1,0:T(8,128)(2,1)S(1)}, bf16[256,128]{1,0:T(8,128)(2,1)S(1)}, u32[]{:S(2)}, u32[]{:S(2)}) collective-permute-start(bf16[256,128]{1,0:T(8,128)(2,1)S(1)} %get-tuple-element.54), channel_id=1, source_target_pairs={{1,3},{3,1},{5,7},{7,5},{9,11},{11,9},{13,15},{15,13},{0,14},{2,12... | collective-permute-start | bytes 196616 | tf_op jit(solution)/shard_map/ppermute | solution.py:381
  41.2 1.2 %collective-permute-start.14 = (bf16[256,128]{1,0:T(8,128)(2,1)S(1)}, bf16[256,128]{1,0:T(8,128)(2,1)S(1)}, u32[]{:S(2)}, u32[]{:S(2)}) collective-permute-start(bf16[256,128]{1,0:T(8,128)(2,1)S(1)} %get-tuple-element.55), channel_id=1, source_target_pairs={{1,5},{3,7},{5,1},{7,3},{9,13},{11,15},{13,9},{15,11},{0,12},{2,14... | collective-permute-start | bytes 196616 | tf_op jit(solution)/shard_map/ppermute | solution.py:381
  42.4 0.9 %collective-permute-start.15 = (bf16[256,128]{1,0:T(8,128)(2,1)S(1)}, bf16[256,128]{1,0:T(8,128)(2,1)S(1)}, u32[]{:S(2)}, u32[]{:S(2)}) collective-permute-start(bf16[256,128]{1,0:T(8,128)(2,1)S(1)} %get-tuple-element.56), channel_id=1, source_target_pairs={{1,7},{3,5},{5,3},{7,1},{9,15},{11,13},{13,11},{15,9},{0,8},{2,10}... | collective-permute-start | bytes 196616 | tf_op jit(solution)/shard_map/ppermute | solution.py:381
  43.3 0.7 %collective-permute-start.16 = (bf16[256,128]{1,0:T(8,128)(2,1)S(1)}, bf16[256,128]{1,0:T(8,128)(2,1)S(1)}, u32[]{:S(2)}, u32[]{:S(2)}) collective-permute-start(bf16[256,128]{1,0:T(8,128)(2,1)S(1)} %get-tuple-element.57), channel_id=1, source_target_pairs={{1,11},{3,9},{5,15},{7,13},{9,3},{11,1},{13,7},{15,5},{17,27},{19,... | collective-permute-start | bytes 196616 | tf_op jit(solution)/shard_map/ppermute | solution.py:381
  43.9 1.3 %collective-permute-done.13.refs_0_.refs_1_ = bf16[256,128]{1,0:T(8,128)(2,1)S(1)} collective-permute-done((bf16[256,128]{1,0:T(8,128)(2,1)S(1)}, bf16[256,128]{1,0:T(8,128)(2,1)S(1)}, u32[]{:S(2)}, u32[]{:S(2)}) %collective-permute-start.13) | collective-permute-done | bytes 65568 | tf_op jit(solution)/shard_map/ppermute | solution.py:381
  45.2 2.1 %collective-permute-done.14.refs_1_.refs_2_ = bf16[256,128]{1,0:T(8,128)(2,1)S(1)} collective-permute-done((bf16[256,128]{1,0:T(8,128)(2,1)S(1)}, bf16[256,128]{1,0:T(8,128)(2,1)S(1)}, u32[]{:S(2)}, u32[]{:S(2)}) %collective-permute-start.14) | collective-permute-done | bytes 65568 | tf_op jit(solution)/shard_map/ppermute | solution.py:381
  47.3 2.8 %collective-permute-done.15.refs_2_.refs_3_ = bf16[256,128]{1,0:T(8,128)(2,1)S(1)} collective-permute-done((bf16[256,128]{1,0:T(8,128)(2,1)S(1)}, bf16[256,128]{1,0:T(8,128)(2,1)S(1)}, u32[]{:S(2)}, u32[]{:S(2)}) %collective-permute-start.15) | collective-permute-done | bytes 65568 | tf_op jit(solution)/shard_map/ppermute | solution.py:381
  50.0 0.1 collective-permute-start.17
  50.1 0.8 %shard_map.107 = f32[2,2,256,128]{3,2,1,0:T(8,128)} custom-call(f32[2,2,256,128]{3,2,1,0:T(8,128)S(1)} %get-tuple-element.50.mine, f32[2,2,256,128]{3,2,1,0:T(8,128)S(1)} %collective-permute-done.12.theirs), custom_call_target="tpu_custom_call" | custom-call | flops 1048576 | bytes 1048576 | tf_op jit(solution)/shard_map/pallas_call | solution.py:398
  51.0 0.5 collective-permute-done.17.refs_5_
  51.5 1.2 %shard_map.109 = f32[2,512]{1,0:T(2,128)} custom-call(bf16[128,128]{1,0:T(8,128)(2,1)S(1)} %get-tuple-element.53.refs_0_, bf16[256,128]{1,0:T(8,128)(2,1)S(1)} %collective-permute-done.13.refs_0_.refs_1_, bf16[256,128]{1,0:T(8,128)(2,1)S(1)} %collective-permute-done.14.refs_1_.refs_2_, bf16[256,128]{1,0:T(8,128)(2,1)S(1)} %collective-permute-done.15.refs_2_.refs_3_, ...), custom_call_target="tpu_custom_call" | custom-call | tf_op jit(solution)/shard_map/pallas_call | solution.py:405
  (28 shorter events, 0.1 us)
Async XLA Ops:
  0.6 11.9 %slice-start = ((s8[11534336]{0:T(1024)(128)(4,1)}), s8[4194304]{0:T(1024)(128)(4,1)S(1)}, s32[]{:S(2)}) async-start(s8[11534336]{0:T(1024)(128)(4,1)} %bitcast.1), calls=%async_computation | async-start | bytes 8388608
  0.6 11.9 %slice-start.1 = ((s8[11534336]{0:T(1024)(128)(4,1)}), s8[4194304]{0:T(1024)(128)(4,1)S(1)}, s32[]{:S(2)}) async-start(s8[11534336]{0:T(1024)(128)(4,1)} %bitcast.1), calls=%async_computation.1 | async-start | bytes 8388608
  0.7 11.9 %slice-start.2 = ((s8[11534336]{0:T(1024)(128)(4,1)}), s8[3145728]{0:T(1024)(128)(4,1)S(1)}, s32[]{:S(2)}) async-start(s8[11534336]{0:T(1024)(128)(4,1)} %bitcast.1), calls=%async_computation.2 | async-start | bytes 6291456
  0.7 11.9 %copy-start.1 = (bf16[1,8,2,64,128]{4,3,2,1,0:T(8,128)(2,1)S(1)}, bf16[1,8,2,64,128]{4,3,2,1,0:T(8,128)(2,1)}, u32[]{:S(2)}) copy-start(bf16[1,8,2,64,128]{4,3,2,1,0:T(8,128)(2,1)} %param.8) | copy-start | bytes 786436
  0.7 11.9 %copy-start.3 = (s32[11]{0:T(128)S(1)}, s32[11]{0:T(128)}, u32[]{:S(2)}) copy-start(s32[11]{0:T(128)} %slots.7) | copy-start | bytes 136
  0.7 11.9 %copy-start.4 = (s32[11]{0:T(128)S(1)}, s32[11]{0:T(128)}, u32[]{:S(2)}) copy-start(s32[11]{0:T(128)} %cols.7) | copy-start | bytes 136
  0.7 9.7 %collective-permute-start.3 = (bf16[1024,128]{1,0:T(8,128)(2,1)}, bf16[1024,128]{1,0:T(8,128)(2,1)S(1)}, u32[]{:S(2)}, u32[]{:S(2)}) collective-permute-start(bf16[1024,128]{1,0:T(8,128)(2,1)} %bitcast.3), channel_id=1, source_target_pairs={{4,0},{8,4},{12,8},{14,12},{10,14},{6,10},{2,6},{0,2},{5,1},{9,5},... | collective-permute-start | bytes 786440 | tf_op jit(solution)/shard_map/ppermute | solution.py:301
  3.7 8.4 %collective-permute-start = (bf16[1024,128]{1,0:T(8,128)(2,1)}, bf16[1024,128]{1,0:T(8,128)(2,1)S(1)}, u32[]{:S(2)}, u32[]{:S(2)}) collective-permute-start(bf16[1024,128]{1,0:T(8,128)(2,1)} %bitcast.4), channel_id=1, source_target_pairs={{0,4},{4,8},{8,12},{12,14},{14,10},{10,6},{6,2},{2,0},{1,5},{5,9},... | collective-permute-start | bytes 786440 | tf_op jit(solution)/shard_map/ppermute | solution.py:300
  3.8 0.9 %copy-start.5 = (s32[2,256]{1,0:T(2,128)S(1)}, s32[2,256]{1,0:T(2,128)}, u32[]{:S(2)}) copy-start(s32[2,256]{1,0:T(2,128)} %wanted.3) | copy-start | bytes 6148
  4.8 5.6 %collective-permute-start.4 = (bf16[16,128]{1,0:T(8,128)(2,1)S(1)}, bf16[16,128]{1,0:T(8,128)(2,1)S(1)}, u32[]{:S(2)}, u32[]{:S(2)}) collective-permute-start(bf16[16,128]{1,0:T(8,128)(2,1)S(1)} %shard_map.95.refs_0_), channel_id=1, source_target_pairs={{4,0},{8,4},{12,8},{14,12},{10,14},{6,10},{2,6},{0,2},{5,1},{9,5},... | collective-permute-start | bytes 12296 | tf_op jit(solution)/shard_map/ppermute | solution.py:308
  7.3 4.9 %collective-permute-start.1 = (bf16[16,128]{1,0:T(8,128)(2,1)S(1)}, bf16[16,128]{1,0:T(8,128)(2,1)S(1)}, u32[]{:S(2)}, u32[]{:S(2)}) collective-permute-start(bf16[16,128]{1,0:T(8,128)(2,1)S(1)} %shard_map.95.refs_0_), channel_id=1, source_target_pairs={{0,4},{4,8},{8,12},{12,14},{14,10},{10,6},{6,2},{2,0},{1,5},{5,9},... | collective-permute-start | bytes 12296 | tf_op jit(solution)/shard_map/ppermute | solution.py:308
  10.4 7.6 %collective-permute-start.6 = (bf16[1040,128]{1,0:T(8,128)(2,1)S(1)}, bf16[1040,128]{1,0:T(8,128)(2,1)S(1)}, u32[]{:S(2)}, u32[]{:S(2)}) collective-permute-start(bf16[1040,128]{1,0:T(8,128)(2,1)S(1)} %shard_map.97.from_right), channel_id=1, source_target_pairs={{4,0},{8,4},{12,8},{14,12},{10,14},{6,10},{2,6},{0,2},{5,1},{9,5},... | collective-permute-start | bytes 798728 | tf_op jit(solution)/shard_map/ppermute | solution.py:301
  12.2 7.2 %collective-permute-start.2 = (bf16[1040,128]{1,0:T(8,128)(2,1)S(1)}, bf16[1040,128]{1,0:T(8,128)(2,1)S(1)}, u32[]{:S(2)}, u32[]{:S(2)}) collective-permute-start(bf16[1040,128]{1,0:T(8,128)(2,1)S(1)} %shard_map.96.from_left), channel_id=1, source_target_pairs={{0,4},{4,8},{8,12},{12,14},{14,10},{10,6},{6,2},{2,0},{1,5},{5,9},... | collective-permute-start | bytes 798728 | tf_op jit(solution)/shard_map/ppermute | solution.py:300
  16.3 9.9 %copy-start = (bf16[2,256,512]{2,1,0:T(8,128)(2,1)S(1)}, bf16[2,256,512]{2,1,0:T(8,128)(2,1)}, u32[]{:S(2)}) copy-start(bf16[2,256,512]{2,1,0:T(8,128)(2,1)} %basis.1) | copy-start | bytes 1572868
  16.4 9.9 %copy-start.2 = (bf16[2,128,512]{2,1,0:T(8,128)(2,1)S(1)}, bf16[2,128,512]{2,1,0:T(8,128)(2,1)}, u32[]{:S(2)}) copy-start(bf16[2,128,512]{2,1,0:T(8,128)(2,1)} %supernode.1) | copy-start | bytes 786436
  16.4 9.9 %copy-start.6 = (s32[2,256]{1,0:T(2,128)S(1)}, s32[2,256]{1,0:T(2,128)}, u32[]{:S(2)}) copy-start(s32[2,256]{1,0:T(2,128)} %wanted.3) | copy-start | bytes 6148
  18.0 6.7 %collective-permute-start.8 = (bf16[1040,128]{1,0:T(8,128)(2,1)S(1)}, bf16[1040,128]{1,0:T(8,128)(2,1)S(1)}, u32[]{:S(2)}, u32[]{:S(2)}) collective-permute-start(bf16[1040,128]{1,0:T(8,128)(2,1)S(1)} %collective-permute-done.6.from_right.refs_4_), channel_id=1, source_target_pairs={{4,0},{8,4},{12,8},{14,12},{10,14},{6,10},{2,6},{0,2},{5,1},{9,5},... | collective-permute-start | bytes 798728 | tf_op jit(solution)/shard_map/ppermute | solution.py:301
  19.4 7.8 %collective-permute-start.5 = (bf16[1040,128]{1,0:T(8,128)(2,1)S(1)}, bf16[1040,128]{1,0:T(8,128)(2,1)S(1)}, u32[]{:S(2)}, u32[]{:S(2)}) collective-permute-start(bf16[1040,128]{1,0:T(8,128)(2,1)S(1)} %collective-permute-done.2.from_left.refs_3_), channel_id=1, source_target_pairs={{0,4},{4,8},{8,12},{12,14},{14,10},{10,6},{6,2},{2,0},{1,5},{5,9},... | collective-permute-start | bytes 798728 | tf_op jit(solution)/shard_map/ppermute | solution.py:300
  24.7 7.8 %collective-permute-start.9 = (bf16[528,128]{1,0:T(8,128)(2,1)S(1)}, bf16[528,128]{1,0:T(8,128)(2,1)S(1)}, u32[]{:S(2)}, u32[]{:S(2)}) collective-permute-start(bf16[528,128]{1,0:T(8,128)(2,1)S(1)} %slice.7), channel_id=1, source_target_pairs={{4,0},{8,4},{12,8},{14,12},{10,14},{6,10},{2,6},{0,2},{5,1},{9,5},... | collective-permute-start | bytes 405512 | tf_op jit(solution)/shard_map/ppermute | solution.py:305
  27.3 5.4 %copy-start.7 = (f32[2]{0:T(128)S(1)}, f32[2]{0:T(128)}, u32[]{:S(2)}) copy-start(f32[2]{0:T(128)} %pole_weight.1) | copy-start | bytes 28
  27.3 5.2 %collective-permute-start.7 = (bf16[512,128]{1,0:T(8,128)(2,1)S(1)}, bf16[512,128]{1,0:T(8,128)(2,1)S(1)}, u32[]{:S(2)}, u32[]{:S(2)}) collective-permute-start(bf16[512,128]{1,0:T(8,128)(2,1)S(1)} %slice.6), channel_id=1, source_target_pairs={{0,4},{4,8},{8,12},{12,14},{14,10},{10,6},{6,2},{2,0},{1,5},{5,9},... | collective-permute-start | bytes 393224 | tf_op jit(solution)/shard_map/ppermute | solution.py:304
  32.5 2.1 %collective-permute-start.10 = (bf16[128,128]{1,0:T(8,128)(2,1)S(1)}, bf16[128,128]{1,0:T(8,128)(2,1)S(1)}, u32[]{:S(2)}, u32[]{:S(2)}) collective-permute-start(bf16[128,128]{1,0:T(8,128)(2,1)S(1)} %shard_map.102.mine), channel_id=1, source_target_pairs={{0,1},{1,0},{2,3},{3,2},{4,5},{5,4},{6,7},{7,6},{8,9},{9,8},{10,11... | collective-permute-start | bytes 98312 | tf_op jit(solution)/shard_map/ppermute | solution.py:346
  34.6 2.1 %collective-permute-start.11 = (f32[2,512,128]{2,1,0:T(8,128)S(1)}, f32[2,512,128]{2,1,0:T(8,128)S(1)}, u32[]{:S(2)}, u32[]{:S(2)}) collective-permute-start(f32[2,512,128]{2,1,0:T(8,128)S(1)} %get-tuple-element.47.mine), channel_id=1, source_target_pairs={{0,1},{1,0},{2,3},{3,2},{4,5},{5,4},{6,7},{7,6},{8,9},{9,8},{10,11... | collective-permute-start | bytes 1572872 | tf_op jit(solution)/shard_map/ppermute | solution.py:358
  35.2 14.9 %collective-permute-start.12 = (f32[2,2,256,128]{3,2,1,0:T(8,128)S(1)}, f32[2,2,256,128]{3,2,1,0:T(8,128)S(1)}, u32[]{:S(2)}, u32[]{:S(2)}) collective-permute-start(f32[2,2,256,128]{3,2,1,0:T(8,128)S(1)} %get-tuple-element.51), channel_id=1, source_target_pairs={{0,1},{1,0},{2,3},{3,2},{4,5},{5,4},{6,7},{7,6},{8,9},{9,8},{10,11... | collective-permute-start | bytes 1572872 | tf_op jit(solution)/shard_map/ppermute | solution.py:397
  37.5 7.7 %collective-permute-start.13 = (bf16[256,128]{1,0:T(8,128)(2,1)S(1)}, bf16[256,128]{1,0:T(8,128)(2,1)S(1)}, u32[]{:S(2)}, u32[]{:S(2)}) collective-permute-start(bf16[256,128]{1,0:T(8,128)(2,1)S(1)} %get-tuple-element.54), channel_id=1, source_target_pairs={{1,3},{3,1},{5,7},{7,5},{9,11},{11,9},{13,15},{15,13},{0,14},{2,12... | collective-permute-start | bytes 196616 | tf_op jit(solution)/shard_map/ppermute | solution.py:381
  41.2 6.1 %collective-permute-start.14 = (bf16[256,128]{1,0:T(8,128)(2,1)S(1)}, bf16[256,128]{1,0:T(8,128)(2,1)S(1)}, u32[]{:S(2)}, u32[]{:S(2)}) collective-permute-start(bf16[256,128]{1,0:T(8,128)(2,1)S(1)} %get-tuple-element.55), channel_id=1, source_target_pairs={{1,5},{3,7},{5,1},{7,3},{9,13},{11,15},{13,9},{15,11},{0,12},{2,14... | collective-permute-start | bytes 196616 | tf_op jit(solution)/shard_map/ppermute | solution.py:381
  42.4 7.6 %collective-permute-start.15 = (bf16[256,128]{1,0:T(8,128)(2,1)S(1)}, bf16[256,128]{1,0:T(8,128)(2,1)S(1)}, u32[]{:S(2)}, u32[]{:S(2)}) collective-permute-start(bf16[256,128]{1,0:T(8,128)(2,1)S(1)} %get-tuple-element.56), channel_id=1, source_target_pairs={{1,7},{3,5},{5,3},{7,1},{9,15},{11,13},{13,11},{15,9},{0,8},{2,10}... | collective-permute-start | bytes 196616 | tf_op jit(solution)/shard_map/ppermute | solution.py:381
  43.3 6.8 %collective-permute-start.16 = (bf16[256,128]{1,0:T(8,128)(2,1)S(1)}, bf16[256,128]{1,0:T(8,128)(2,1)S(1)}, u32[]{:S(2)}, u32[]{:S(2)}) collective-permute-start(bf16[256,128]{1,0:T(8,128)(2,1)S(1)} %get-tuple-element.57), channel_id=1, source_target_pairs={{1,11},{3,9},{5,15},{7,13},{9,3},{11,1},{13,7},{15,5},{17,27},{19,... | collective-permute-start | bytes 196616 | tf_op jit(solution)/shard_map/ppermute | solution.py:381
  50.0 1.4 %collective-permute-start.17 = (bf16[512,128]{1,0:T(8,128)(2,1)S(1)}, bf16[512,128]{1,0:T(8,128)(2,1)S(1)}, u32[]{:S(2)}, u32[]{:S(2)}) collective-permute-start(bf16[512,128]{1,0:T(8,128)(2,1)S(1)} %shard_map.108), channel_id=1, source_target_pairs={{0,1},{1,0},{2,3},{3,2},{4,5},{5,4},{6,7},{7,6},{8,9},{9,8},{10,11... | collective-permute-start | bytes 393224 | tf_op jit(solution)/shard_map/ppermute | solution.py:389

commit v9 on v8

--- a/solution.py
+++ b/solution.py
@@ -219,16 +219,27 @@
         out[i * slots:(i + 1) * slots] = part[at, :]
 
 
-def density_kernel(*refs):
-    own, *parts, passed, basis, supernode, out = refs
+def first_kernel(*refs):
+    own, *parts, basis, out = refs
     slots = own.shape[0]
     at = pl.ds(pl.multiple_of(lax.axis_index("col") * slots, slots), slots)
-    arrived = jnp.concatenate(
-        [own[...]] + [part[at, :] for part in parts] + [passed[...]], axis=0
-    )
+    arrived = jnp.concatenate([own[...]] + [part[at, :] for part in parts], axis=0)
     for n in range(basis.shape[0]):
-        projected = lax.dot_general(
-            arrived, basis[n], (((0,), (0,)), ((), ())), preferred_element_type=F32
+        out[n] = lax.dot_general(
+            arrived,
+            basis[n, :arrived.shape[0], :],
+            (((0,), (0,)), ((), ())),
+            preferred_element_type=F32,
+        )
+
+
+def density_kernel(passed, first, basis, supernode, out):
+    for n in range(basis.shape[0]):
+        projected = first[n] + lax.dot_general(
+            passed[...],
+            basis[n, basis.shape[1] - passed.shape[0]:, :],
+            (((0,), (0,)), ((), ())),
+            preferred_element_type=F32,
         )
         out[n:n + 1, :] = jnp.sum(supernode[n] * projected, axis=0, keepdims=True)
 
@@ -380,14 +391,6 @@
             pairs += [(2 * r, 2 * (r ^ far[step])) for r in range(n_row)]
         fetched.append(lax.ppermute(sent[step], ("row", "col"), pairs))
 
-    turned = pl.pallas_call(
-        turn_kernel,
-        out_shape=jax.ShapeDtypeStruct((half_ring * slots, width), BF16),
-        compiler_params=params,
-        cost_estimate=cost,
-    )(*fetched)
-    passed = lax.ppermute(turned, "col", swap)
-
     mine, other = pl.pallas_call(
         halves_kernel,
         out_shape=[jax.ShapeDtypeStruct(half_shape, F32)] * 2,
@@ -401,12 +404,25 @@
         compiler_params=params,
         cost_estimate=cost,
     )(mine, inverse_other)
-    kept, inverse = lax.optimization_barrier((kept, inverse))
+    fetched[0], inverse = lax.optimization_barrier((fetched[0], inverse))
+    turned = pl.pallas_call(
+        turn_kernel,
+        out_shape=jax.ShapeDtypeStruct((half_ring * slots, width), BF16),
+        compiler_params=params,
+        cost_estimate=cost,
+    )(*fetched)
+    passed = lax.ppermute(turned, "col", swap)
+    first = pl.pallas_call(
+        first_kernel,
+        out_shape=jax.ShapeDtypeStruct((boxes, width, box_basis.shape[2]), F32),
+        compiler_params=params,
+        cost_estimate=cost,
+    )(kept, *fetched, basis_here)
     density = pl.pallas_call(
         density_kernel,
         out_shape=jax.ShapeDtypeStruct((boxes, box_basis.shape[2]), F32),
         compiler_params=params,
-    )(kept, *fetched, passed, basis_here, wide)
+    )(passed, first, basis_here, wide)
     return inverse, density
 
 

time: 52.8 us -> 52.6 us (level)
    ppermute x4, waiting for transfers between devices: 6.1 us -> 5.24 us  [local(): fetched.append(lax.ppermute(sent[step], ('row', 'col'), pairs))]
where the time goes in v9:
time: 52.6 us; the launch traced here: 52.4 us
  starting transfers between devices  19.4 us (37%)
  Pallas kernels  16.4 us (31%)
  waiting for transfers between devices  14.7 us (28%)
  local copies, waits for them, and re-layouts  1.01 us (2%)
  between operations  0.9 us (2%)
    ppermute x4, starting transfers between devices, local(): fetched.append(lax.ppermute(sent[step], ('row', 'col'), pairs))  6.45 us
    ppermute x3, starting transfers between devices, local(): next_right = lax.ppermute(right, 'row', to_left)  6.12 us
    pallas_call x2, Pallas kernels, local(): call(functools.partial(hop_middle, hop=h - 1), [in_smem] * 2 + [in_vmem]...  5.63 us
    ppermute x4, waiting for transfers between devices, local(): fetched.append(lax.ppermute(sent[step], ('row', 'col'), pairs))  5.24 us
    pallas_call x1, Pallas kernels, local(): call(hop_early, [in_smem] * 2 + [in_vmem] * 4, acc_out, [], 3)  3.73 us
    ppermute x3, waiting for transfers between devices, local(): next_right = lax.ppermute(right, 'row', to_left)  3.4 us
    ppermute x1, waiting for transfers between devices, local(): lax.ppermute(own_lines, 'row', to_left)  2.99 us
    ppermute x1, starting transfers between devices, local(): lax.ppermute(own_lines, 'row', to_left)  2.47 us
  transfers between devices with their start and end apart: 18, of which 9 were waited for; matrix products, arithmetic and copies ran while one was open for 0% of the time, Pallas kernels for 29%

profile of v9, /device:TPU:0, one launch (start us, length us, event | category | flops | bytes accessed | tf_op | source)
XLA Modules:
  0.0 52.4 jit_solution(10566311859934255491)
XLA Ops:
  0.6 0.0 slice-start
  0.7 0.0 slice-start.2
  0.7 3.0 %collective-permute-start.3 = (bf16[1024,128]{1,0:T(8,128)(2,1)}, bf16[1024,128]{1,0:T(8,128)(2,1)S(1)}, u32[]{:S(2)}, u32[]{:S(2)}) collective-permute-start(bf16[1024,128]{1,0:T(8,128)(2,1)} %bitcast.3), channel_id=1, source_target_pairs={{4,0},{8,4},{12,8},{14,12},{10,14},{6,10},{2,6},{0,2},{5,1},{9,5},... | collective-permute-start | bytes 786440 | tf_op jit(solution)/shard_map/ppermute | solution.py:312
  3.7 0.1 collective-permute-start
  3.8 0.9 %copy-done.5 = s32[2,256]{1,0:T(2,128)S(1)} copy-done((s32[2,256]{1,0:T(2,128)S(1)}, s32[2,256]{1,0:T(2,128)}, u32[]{:S(2)}) %copy-start.5) | copy-done | bytes 2072
  4.8 2.5 %collective-permute-start.4 = (bf16[16,128]{1,0:T(8,128)(2,1)S(1)}, bf16[16,128]{1,0:T(8,128)(2,1)S(1)}, u32[]{:S(2)}, u32[]{:S(2)}) collective-permute-start(bf16[16,128]{1,0:T(8,128)(2,1)S(1)} %shard_map.95.refs_0_), channel_id=1, source_target_pairs={{4,0},{8,4},{12,8},{14,12},{10,14},{6,10},{2,6},{0,2},{5,1},{9,5},... | collective-permute-start | bytes 12296 | tf_op jit(solution)/shard_map/ppermute | solution.py:319
  7.3 0.1 collective-permute-start.1
  7.4 3.0 %collective-permute-done.4.lines.refs_2_ = bf16[16,128]{1,0:T(8,128)(2,1)S(1)} collective-permute-done((bf16[16,128]{1,0:T(8,128)(2,1)S(1)}, bf16[16,128]{1,0:T(8,128)(2,1)S(1)}, u32[]{:S(2)}, u32[]{:S(2)}) %collective-permute-start.4) | collective-permute-done | bytes 4128 | tf_op jit(solution)/shard_map/ppermute | solution.py:319
  10.4 0.0 collective-permute-done.3.rows
  10.4 1.7 %collective-permute-start.6 = (bf16[1040,128]{1,0:T(8,128)(2,1)S(1)}, bf16[1040,128]{1,0:T(8,128)(2,1)S(1)}, u32[]{:S(2)}, u32[]{:S(2)}) collective-permute-start(bf16[1040,128]{1,0:T(8,128)(2,1)S(1)} %shard_map.97.from_right), channel_id=1, source_target_pairs={{4,0},{8,4},{12,8},{14,12},{10,14},{6,10},{2,6},{0,2},{5,1},{9,5},... | collective-permute-start | bytes 798728 | tf_op jit(solution)/shard_map/ppermute | solution.py:312
  12.2 0.4 collective-permute-start.2
  12.6 3.7 %shard_map.98.start = f32[2,512,256]{2,1,0:T(8,128)S(1)} custom-call(s32[11]{0:T(128)S(1)} %copy-done.3, s32[11]{0:T(128)S(1)} %copy-done.4, bf16[1024,128]{1,0:T(8,128)(2,1)S(1)} %bitcast.5, bf16[1040,128]{1,0:T(8,128)(2,1)S(1)} %shard_map.96.from_left, bf16[1040,128]{1,0:T(8,128)(2,1)S(1)} %shard_map.97.from_right, bf16[11,2,512,512]{3,2,1,0:T(8,128)(2,1)S(1)} %bitcast.2), custom_call_target="tpu_custom_call" | custom-call | flops 1048576 | bytes 1048576 | tf_op jit(solution)/shard_map/pallas_call | solution.py:325
  16.3 0.0 copy-start
  16.4 0.0 copy-start.2
  16.4 0.0 copy-start.6
  16.4 1.7 %collective-permute-done.6.from_right.refs_4_ = bf16[1040,128]{1,0:T(8,128)(2,1)S(1)} collective-permute-done((bf16[1040,128]{1,0:T(8,128)(2,1)S(1)}, bf16[1040,128]{1,0:T(8,128)(2,1)S(1)}, u32[]{:S(2)}, u32[]{:S(2)}) %collective-permute-start.6) | collective-permute-done | bytes 266272 | tf_op jit(solution)/shard_map/ppermute | solution.py:312
  18.0 1.4 %collective-permute-start.8 = (bf16[1040,128]{1,0:T(8,128)(2,1)S(1)}, bf16[1040,128]{1,0:T(8,128)(2,1)S(1)}, u32[]{:S(2)}, u32[]{:S(2)}) collective-permute-start(bf16[1040,128]{1,0:T(8,128)(2,1)S(1)} %collective-permute-done.6.from_right.refs_4_), channel_id=1, source_target_pairs={{4,0},{8,4},{12,8},{14,12},{10,14},{6,10},{2,6},{0,2},{5,1},{9,5},... | collective-permute-start | bytes 798728 | tf_op jit(solution)/shard_map/ppermute | solution.py:312
  19.4 0.0 collective-permute-done.2.from_left.refs_3_
  19.4 0.7 %collective-permute-start.5 = (bf16[1040,128]{1,0:T(8,128)(2,1)S(1)}, bf16[1040,128]{1,0:T(8,128)(2,1)S(1)}, u32[]{:S(2)}, u32[]{:S(2)}) collective-permute-start(bf16[1040,128]{1,0:T(8,128)(2,1)S(1)} %collective-permute-done.2.from_left.refs_3_), channel_id=1, source_target_pairs={{0,4},{4,8},{8,12},{12,14},{14,10},{10,6},{6,2},{2,0},{1,5},{5,9},... | collective-permute-start | bytes 798728 | tf_op jit(solution)/shard_map/ppermute | solution.py:311
  20.1 2.9 %shard_map.100.start = f32[2,512,256]{2,1,0:T(8,128)S(1)} custom-call(s32[11]{0:T(128)S(1)} %copy-done.3, s32[11]{0:T(128)S(1)} %copy-done.4, bf16[1040,128]{1,0:T(8,128)(2,1)S(1)} %collective-permute-done.2.from_left.refs_3_, bf16[1040,128]{1,0:T(8,128)(2,1)S(1)} %collective-permute-done.6.from_right.refs_4_, ...), custom_call_target="tpu_custom_call", output_to_operand_aliasing={{}: (5, {})} | custom-call | flops 1048576 | bytes 1048576 | tf_op jit(solution)/shard_map/pallas_call | solution.py:329
  22.9 1.7 %collective-permute-done.8.from_right.refs_6_ = bf16[1040,128]{1,0:T(8,128)(2,1)S(1)} collective-permute-done((bf16[1040,128]{1,0:T(8,128)(2,1)S(1)}, bf16[1040,128]{1,0:T(8,128)(2,1)S(1)}, u32[]{:S(2)}, u32[]{:S(2)}) %collective-permute-start.8) | collective-permute-done | bytes 266272 | tf_op jit(solution)/shard_map/ppermute | solution.py:312
  24.7 1.6 %collective-permute-start.9 = (bf16[528,128]{1,0:T(8,128)(2,1)S(1)}, bf16[528,128]{1,0:T(8,128)(2,1)S(1)}, u32[]{:S(2)}, u32[]{:S(2)}) collective-permute-start(bf16[528,128]{1,0:T(8,128)(2,1)S(1)} %slice.7), channel_id=1, source_target_pairs={{4,0},{8,4},{12,8},{14,12},{10,14},{6,10},{2,6},{0,2},{5,1},{9,5},... | collective-permute-start | bytes 405512 | tf_op jit(solution)/shard_map/ppermute | solution.py:316
  26.3 1.0 %shard_map.99 = (bf16[2,1152,512]{2,1,0:T(8,128)(2,1)S(1)}, f32[2,128,512]{2,1,0:T(8,128)S(1)}) custom-call(s32[2,256]{1,0:T(2,128)S(1)} %copy-done.6, bf16[2,256,512]{2,1,0:T(8,128)(2,1)S(1)} %copy-done, bf16[2,128,512]{2,1,0:T(8,128)(2,1)S(1)} %copy-done.2), custom_call_target="tpu_custom_call" | custom-call | flops 1048576 | bytes 1048576 | tf_op jit(solution)/shard_map/pallas_call | solution.py:296
  27.3 0.0 copy-start.7
  27.3 0.8 %collective-permute-start.7 = (bf16[512,128]{1,0:T(8,128)(2,1)S(1)}, bf16[512,128]{1,0:T(8,128)(2,1)S(1)}, u32[]{:S(2)}, u32[]{:S(2)}) collective-permute-start(bf16[512,128]{1,0:T(8,128)(2,1)S(1)} %slice.6), channel_id=1, source_target_pairs={{0,4},{4,8},{8,12},{12,14},{14,10},{10,6},{6,2},{2,0},{1,5},{5,9},... | collective-permute-start | bytes 393224 | tf_op jit(solution)/shard_map/ppermute | solution.py:315
  28.0 2.8 %shard_map.101.start = f32[2,512,256]{2,1,0:T(8,128)S(1)} custom-call(s32[11]{0:T(128)S(1)} %copy-done.3, s32[11]{0:T(128)S(1)} %copy-done.4, bf16[1040,128]{1,0:T(8,128)(2,1)S(1)} %collective-permute-done.5.from_left.refs_5_, bf16[1040,128]{1,0:T(8,128)(2,1)S(1)} %collective-permute-done.8.from_right.refs_6_, ...), custom_call_target="tpu_custom_call", output_to_operand_aliasing={{}: (5, {})} | custom-call | flops 1048576 | bytes 1048576 | tf_op jit(solution)/shard_map/pallas_call | solution.py:329
  30.8 1.7 %collective-permute-done.7.low = bf16[512,128]{1,0:T(8,128)(2,1)S(1)} collective-permute-done((bf16[512,128]{1,0:T(8,128)(2,1)S(1)}, bf16[512,128]{1,0:T(8,128)(2,1)S(1)}, u32[]{:S(2)}, u32[]{:S(2)}) %collective-permute-start.7) | collective-permute-done | bytes 131104 | tf_op jit(solution)/shard_map/ppermute | solution.py:315
  32.5 0.1 shard_map.102.mine
  32.5 0.1 collective-permute-start.10
  32.6 2.0 %shard_map.103 = (f32[2,512,256]{2,1,0:T(8,128)S(1)}, f32[2,512,128]{2,1,0:T(8,128)S(1)}) custom-call(s32[11]{0:T(128)S(1)} %copy-done.3, s32[11]{0:T(128)S(1)} %copy-done.4, f32[2]{0:T(128)S(1)} %copy-done.7, bf16[512,128]{1,0:T(8,128)(2,1)S(1)} %collective-permute-done.7.low, ...), custom_call_target="tpu_custom_call", output_to_operand_aliasing={{0}: (6, {})} | custom-call | flops 1048576 | bytes 1048576 | tf_op jit(solution)/shard_map/pallas_call | solution.py:360
  34.6 0.6 %collective-permute-start.11 = (f32[2,512,128]{2,1,0:T(8,128)S(1)}, f32[2,512,128]{2,1,0:T(8,128)S(1)}, u32[]{:S(2)}, u32[]{:S(2)}) collective-permute-start(f32[2,512,128]{2,1,0:T(8,128)S(1)} %get-tuple-element.47.mine), channel_id=1, source_target_pairs={{0,1},{1,0},{2,3},{3,2},{4,5},{5,4},{6,7},{7,6},{8,9},{9,8},{10,11... | collective-permute-start | bytes 1572872 | tf_op jit(solution)/shard_map/ppermute | solution.py:369
  35.2 0.1 shard_map.106
  35.2 0.1 collective-permute-start.13
  35.3 0.9 %shard_map.104.pick = bf16[1152,1024]{1,0:T(8,128)(2,1)S(1)} custom-call(bf16[128,128]{1,0:T(8,128)(2,1)S(1)} %shard_map.102.mine, bf16[128,128]{1,0:T(8,128)(2,1)S(1)} %collective-permute-done.10.theirs), custom_call_target="tpu_custom_call" | custom-call | flops 4294967296 | bytes 1048576 | tf_op jit(solution)/shard_map/pallas_call | solution.py:370
  36.3 0.4 collective-permute-done.11.theirs
  36.7 0.8 %shard_map.105 = (bf16[128,128]{1,0:T(8,128)(2,1)S(1)}, bf16[256,128]{1,0:T(8,128)(2,1)S(1)}, bf16[256,128]{1,0:T(8,128)(2,1)S(1)}, bf16[256,128]{1,0:T(8,128)(2,1)S(1)}, bf16[256,128]{1,0:T(8,128)(2,1)S(1)}) custom-call(bf16[1152,1024]{1,0:T(8,128)(2,1)S(1)} %shard_map.104.pick, f32[2,512,128]{2,1,0:T(8,128)S(1)} %get-tuple-element.47.mine, ...), custom_call_target="tpu_custom_call" | custom-call | flops 1048576 | bytes 1048576 | tf_op jit(solution)/shard_map/pallas_call | solution.py:379
  37.5 3.7 %collective-permute-start.12 = (bf16[256,128]{1,0:T(8,128)(2,1)S(1)}, bf16[256,128]{1,0:T(8,128)(2,1)S(1)}, u32[]{:S(2)}, u32[]{:S(2)}) collective-permute-start(bf16[256,128]{1,0:T(8,128)(2,1)S(1)} %get-tuple-element.48), channel_id=1, source_target_pairs={{1,3},{3,1},{5,7},{7,5},{9,11},{11,9},{13,15},{15,13},{0,14},{2,12... | collective-permute-start | bytes 196616 | tf_op jit(solution)/shard_map/ppermute | solution.py:392
  41.2 1.2 %collective-permute-start.14 = (bf16[256,128]{1,0:T(8,128)(2,1)S(1)}, bf16[256,128]{1,0:T(8,128)(2,1)S(1)}, u32[]{:S(2)}, u32[]{:S(2)}) collective-permute-start(bf16[256,128]{1,0:T(8,128)(2,1)S(1)} %get-tuple-element.54), channel_id=1, source_target_pairs={{1,5},{3,7},{5,1},{7,3},{9,13},{11,15},{13,9},{15,11},{0,12},{2,14... | collective-permute-start | bytes 196616 | tf_op jit(solution)/shard_map/ppermute | solution.py:392
  42.4 0.9 %collective-permute-start.15 = (bf16[256,128]{1,0:T(8,128)(2,1)S(1)}, bf16[256,128]{1,0:T(8,128)(2,1)S(1)}, u32[]{:S(2)}, u32[]{:S(2)}) collective-permute-start(bf16[256,128]{1,0:T(8,128)(2,1)S(1)} %get-tuple-element.55), channel_id=1, source_target_pairs={{1,7},{3,5},{5,3},{7,1},{9,15},{11,13},{13,11},{15,9},{0,8},{2,10}... | collective-permute-start | bytes 196616 | tf_op jit(solution)/shard_map/ppermute | solution.py:392
  43.3 0.7 %collective-permute-start.16 = (bf16[256,128]{1,0:T(8,128)(2,1)S(1)}, bf16[256,128]{1,0:T(8,128)(2,1)S(1)}, u32[]{:S(2)}, u32[]{:S(2)}) collective-permute-start(bf16[256,128]{1,0:T(8,128)(2,1)S(1)} %get-tuple-element.56), channel_id=1, source_target_pairs={{1,11},{3,9},{5,15},{7,13},{9,3},{11,1},{13,7},{15,5},{17,27},{19,... | collective-permute-start | bytes 196616 | tf_op jit(solution)/shard_map/ppermute | solution.py:392
  44.0 0.8 %shard_map.107 = f32[2,2,256,128]{3,2,1,0:T(8,128)} custom-call(f32[2,2,256,128]{3,2,1,0:T(8,128)S(1)} %get-tuple-element.50.mine, f32[2,2,256,128]{3,2,1,0:T(8,128)S(1)} %collective-permute-done.13.theirs), custom_call_target="tpu_custom_call" | custom-call | flops 1048576 | bytes 1048576 | tf_op jit(solution)/shard_map/pallas_call | solution.py:401
  44.8 0.4 collective-permute-done.12.refs_0_.refs_1_
  45.2 2.1 %collective-permute-done.14.refs_1_.refs_2_ = bf16[256,128]{1,0:T(8,128)(2,1)S(1)} collective-permute-done((bf16[256,128]{1,0:T(8,128)(2,1)S(1)}, bf16[256,128]{1,0:T(8,128)(2,1)S(1)}, u32[]{:S(2)}, u32[]{:S(2)}) %collective-permute-start.14) | collective-permute-done | bytes 65568 | tf_op jit(solution)/shard_map/ppermute | solution.py:392
  47.3 2.8 %collective-permute-done.15.refs_2_.refs_3_ = bf16[256,128]{1,0:T(8,128)(2,1)S(1)} collective-permute-done((bf16[256,128]{1,0:T(8,128)(2,1)S(1)}, bf16[256,128]{1,0:T(8,128)(2,1)S(1)}, u32[]{:S(2)}, u32[]{:S(2)}) %collective-permute-start.15) | collective-permute-done | bytes 65568 | tf_op jit(solution)/shard_map/ppermute | solution.py:392
  50.1 0.1 collective-permute-start.17
  50.1 0.4 shard_map.109.first
  50.5 0.9 %collective-permute-done.17.passed = bf16[512,128]{1,0:T(8,128)(2,1)S(1)} collective-permute-done((bf16[512,128]{1,0:T(8,128)(2,1)S(1)}, bf16[512,128]{1,0:T(8,128)(2,1)S(1)}, u32[]{:S(2)}, u32[]{:S(2)}) %collective-permute-start.17) | collective-permute-done | bytes 131104 | tf_op jit(solution)/shard_map/ppermute | solution.py:414
  51.5 0.9 %shard_map.110 = f32[2,512]{1,0:T(2,128)} custom-call(bf16[512,128]{1,0:T(8,128)(2,1)S(1)} %collective-permute-done.17.passed, f32[2,128,512]{2,1,0:T(8,128)S(1)} %shard_map.109.first, bf16[2,1152,512]{2,1,0:T(8,128)(2,1)S(1)} %get-tuple-element.58.refs_5_.basis, f32[2,128,512]{2,1,0:T(8,128)S(1)} %get-tuple-element.59.supernode), custom_call_target="tpu_custom_call" | custom-call | tf_op jit(solution)/shard_map/pallas_call | solution.py:421
  (29 shorter events, 0.1 us)
Async XLA Ops:
  0.6 11.9 %slice-start = ((s8[11534336]{0:T(1024)(128)(4,1)}), s8[4194304]{0:T(1024)(128)(4,1)S(1)}, s32[]{:S(2)}) async-start(s8[11534336]{0:T(1024)(128)(4,1)} %bitcast.1), calls=%async_computation | async-start | bytes 8388608
  0.6 11.9 %slice-start.1 = ((s8[11534336]{0:T(1024)(128)(4,1)}), s8[4194304]{0:T(1024)(128)(4,1)S(1)}, s32[]{:S(2)}) async-start(s8[11534336]{0:T(1024)(128)(4,1)} %bitcast.1), calls=%async_computation.1 | async-start | bytes 8388608
  0.7 11.9 %slice-start.2 = ((s8[11534336]{0:T(1024)(128)(4,1)}), s8[3145728]{0:T(1024)(128)(4,1)S(1)}, s32[]{:S(2)}) async-start(s8[11534336]{0:T(1024)(128)(4,1)} %bitcast.1), calls=%async_computation.2 | async-start | bytes 6291456
  0.7 11.9 %copy-start.1 = (bf16[1,8,2,64,128]{4,3,2,1,0:T(8,128)(2,1)S(1)}, bf16[1,8,2,64,128]{4,3,2,1,0:T(8,128)(2,1)}, u32[]{:S(2)}) copy-start(bf16[1,8,2,64,128]{4,3,2,1,0:T(8,128)(2,1)} %param.8) | copy-start | bytes 786436
  0.7 11.9 %copy-start.3 = (s32[11]{0:T(128)S(1)}, s32[11]{0:T(128)}, u32[]{:S(2)}) copy-start(s32[11]{0:T(128)} %slots.7) | copy-start | bytes 136
  0.7 11.9 %copy-start.4 = (s32[11]{0:T(128)S(1)}, s32[11]{0:T(128)}, u32[]{:S(2)}) copy-start(s32[11]{0:T(128)} %cols.7) | copy-start | bytes 136
  0.7 9.7 %collective-permute-start.3 = (bf16[1024,128]{1,0:T(8,128)(2,1)}, bf16[1024,128]{1,0:T(8,128)(2,1)S(1)}, u32[]{:S(2)}, u32[]{:S(2)}) collective-permute-start(bf16[1024,128]{1,0:T(8,128)(2,1)} %bitcast.3), channel_id=1, source_target_pairs={{4,0},{8,4},{12,8},{14,12},{10,14},{6,10},{2,6},{0,2},{5,1},{9,5},... | collective-permute-start | bytes 786440 | tf_op jit(solution)/shard_map/ppermute | solution.py:312
  3.7 8.4 %collective-permute-start = (bf16[1024,128]{1,0:T(8,128)(2,1)}, bf16[1024,128]{1,0:T(8,128)(2,1)S(1)}, u32[]{:S(2)}, u32[]{:S(2)}) collective-permute-start(bf16[1024,128]{1,0:T(8,128)(2,1)} %bitcast.4), channel_id=1, source_target_pairs={{0,4},{4,8},{8,12},{12,14},{14,10},{10,6},{6,2},{2,0},{1,5},{5,9},... | collective-permute-start | bytes 786440 | tf_op jit(solution)/shard_map/ppermute | solution.py:311
  3.8 0.9 %copy-start.5 = (s32[2,256]{1,0:T(2,128)S(1)}, s32[2,256]{1,0:T(2,128)}, u32[]{:S(2)}) copy-start(s32[2,256]{1,0:T(2,128)} %wanted.3) | copy-start | bytes 6148
  4.8 5.6 %collective-permute-start.4 = (bf16[16,128]{1,0:T(8,128)(2,1)S(1)}, bf16[16,128]{1,0:T(8,128)(2,1)S(1)}, u32[]{:S(2)}, u32[]{:S(2)}) collective-permute-start(bf16[16,128]{1,0:T(8,128)(2,1)S(1)} %shard_map.95.refs_0_), channel_id=1, source_target_pairs={{4,0},{8,4},{12,8},{14,12},{10,14},{6,10},{2,6},{0,2},{5,1},{9,5},... | collective-permute-start | bytes 12296 | tf_op jit(solution)/shard_map/ppermute | solution.py:319
  7.3 4.9 %collective-permute-start.1 = (bf16[16,128]{1,0:T(8,128)(2,1)S(1)}, bf16[16,128]{1,0:T(8,128)(2,1)S(1)}, u32[]{:S(2)}, u32[]{:S(2)}) collective-permute-start(bf16[16,128]{1,0:T(8,128)(2,1)S(1)} %shard_map.95.refs_0_), channel_id=1, source_target_pairs={{0,4},{4,8},{8,12},{12,14},{14,10},{10,6},{6,2},{2,0},{1,5},{5,9},... | collective-permute-start | bytes 12296 | tf_op jit(solution)/shard_map/ppermute | solution.py:319
  10.4 7.6 %collective-permute-start.6 = (bf16[1040,128]{1,0:T(8,128)(2,1)S(1)}, bf16[1040,128]{1,0:T(8,128)(2,1)S(1)}, u32[]{:S(2)}, u32[]{:S(2)}) collective-permute-start(bf16[1040,128]{1,0:T(8,128)(2,1)S(1)} %shard_map.97.from_right), channel_id=1, source_target_pairs={{4,0},{8,4},{12,8},{14,12},{10,14},{6,10},{2,6},{0,2},{5,1},{9,5},... | collective-permute-start | bytes 798728 | tf_op jit(solution)/shard_map/ppermute | solution.py:312
  12.2 7.2 %collective-permute-start.2 = (bf16[1040,128]{1,0:T(8,128)(2,1)S(1)}, bf16[1040,128]{1,0:T(8,128)(2,1)S(1)}, u32[]{:S(2)}, u32[]{:S(2)}) collective-permute-start(bf16[1040,128]{1,0:T(8,128)(2,1)S(1)} %shard_map.96.from_left), channel_id=1, source_target_pairs={{0,4},{4,8},{8,12},{12,14},{14,10},{10,6},{6,2},{2,0},{1,5},{5,9},... | collective-permute-start | bytes 798728 | tf_op jit(solution)/shard_map/ppermute | solution.py:311
  16.3 9.9 %copy-start = (bf16[2,256,512]{2,1,0:T(8,128)(2,1)S(1)}, bf16[2,256,512]{2,1,0:T(8,128)(2,1)}, u32[]{:S(2)}) copy-start(bf16[2,256,512]{2,1,0:T(8,128)(2,1)} %basis.1) | copy-start | bytes 1572868
  16.4 9.9 %copy-start.2 = (bf16[2,128,512]{2,1,0:T(8,128)(2,1)S(1)}, bf16[2,128,512]{2,1,0:T(8,128)(2,1)}, u32[]{:S(2)}) copy-start(bf16[2,128,512]{2,1,0:T(8,128)(2,1)} %supernode.1) | copy-start | bytes 786436
  16.4 9.9 %copy-start.6 = (s32[2,256]{1,0:T(2,128)S(1)}, s32[2,256]{1,0:T(2,128)}, u32[]{:S(2)}) copy-start(s32[2,256]{1,0:T(2,128)} %wanted.3) | copy-start | bytes 6148
  18.0 6.7 %collective-permute-start.8 = (bf16[1040,128]{1,0:T(8,128)(2,1)S(1)}, bf16[1040,128]{1,0:T(8,128)(2,1)S(1)}, u32[]{:S(2)}, u32[]{:S(2)}) collective-permute-start(bf16[1040,128]{1,0:T(8,128)(2,1)S(1)} %collective-permute-done.6.from_right.refs_4_), channel_id=1, source_target_pairs={{4,0},{8,4},{12,8},{14,12},{10,14},{6,10},{2,6},{0,2},{5,1},{9,5},... | collective-permute-start | bytes 798728 | tf_op jit(solution)/shard_map/ppermute | solution.py:312
  19.4 7.8 %collective-permute-start.5 = (bf16[1040,128]{1,0:T(8,128)(2,1)S(1)}, bf16[1040,128]{1,0:T(8,128)(2,1)S(1)}, u32[]{:S(2)}, u32[]{:S(2)}) collective-permute-start(bf16[1040,128]{1,0:T(8,128)(2,1)S(1)} %collective-permute-done.2.from_left.refs_3_), channel_id=1, source_target_pairs={{0,4},{4,8},{8,12},{12,14},{14,10},{10,6},{6,2},{2,0},{1,5},{5,9},... | collective-permute-start | bytes 798728 | tf_op jit(solution)/shard_map/ppermute | solution.py:311
  24.7 7.8 %collective-permute-start.9 = (bf16[528,128]{1,0:T(8,128)(2,1)S(1)}, bf16[528,128]{1,0:T(8,128)(2,1)S(1)}, u32[]{:S(2)}, u32[]{:S(2)}) collective-permute-start(bf16[528,128]{1,0:T(8,128)(2,1)S(1)} %slice.7), channel_id=1, source_target_pairs={{4,0},{8,4},{12,8},{14,12},{10,14},{6,10},{2,6},{0,2},{5,1},{9,5},... | collective-permute-start | bytes 405512 | tf_op jit(solution)/shard_map/ppermute | solution.py:316
  27.3 5.4 %copy-start.7 = (f32[2]{0:T(128)S(1)}, f32[2]{0:T(128)}, u32[]{:S(2)}) copy-start(f32[2]{0:T(128)} %pole_weight.1) | copy-start | bytes 28
  27.3 5.2 %collective-permute-start.7 = (bf16[512,128]{1,0:T(8,128)(2,1)S(1)}, bf16[512,128]{1,0:T(8,128)(2,1)S(1)}, u32[]{:S(2)}, u32[]{:S(2)}) collective-permute-start(bf16[512,128]{1,0:T(8,128)(2,1)S(1)} %slice.6), channel_id=1, source_target_pairs={{0,4},{4,8},{8,12},{12,14},{14,10},{10,6},{6,2},{2,0},{1,5},{5,9},... | collective-permute-start | bytes 393224 | tf_op jit(solution)/shard_map/ppermute | solution.py:315
  32.5 2.1 %collective-permute-start.10 = (bf16[128,128]{1,0:T(8,128)(2,1)S(1)}, bf16[128,128]{1,0:T(8,128)(2,1)S(1)}, u32[]{:S(2)}, u32[]{:S(2)}) collective-permute-start(bf16[128,128]{1,0:T(8,128)(2,1)S(1)} %shard_map.102.mine), channel_id=1, source_target_pairs={{0,1},{1,0},{2,3},{3,2},{4,5},{5,4},{6,7},{7,6},{8,9},{9,8},{10,11... | collective-permute-start | bytes 98312 | tf_op jit(solution)/shard_map/ppermute | solution.py:357
  34.6 2.1 %collective-permute-start.11 = (f32[2,512,128]{2,1,0:T(8,128)S(1)}, f32[2,512,128]{2,1,0:T(8,128)S(1)}, u32[]{:S(2)}, u32[]{:S(2)}) collective-permute-start(f32[2,512,128]{2,1,0:T(8,128)S(1)} %get-tuple-element.47.mine), channel_id=1, source_target_pairs={{0,1},{1,0},{2,3},{3,2},{4,5},{5,4},{6,7},{7,6},{8,9},{9,8},{10,11... | collective-permute-start | bytes 1572872 | tf_op jit(solution)/shard_map/ppermute | solution.py:369
  35.2 8.7 %collective-permute-start.13 = (f32[2,2,256,128]{3,2,1,0:T(8,128)S(1)}, f32[2,2,256,128]{3,2,1,0:T(8,128)S(1)}, u32[]{:S(2)}, u32[]{:S(2)}) collective-permute-start(f32[2,2,256,128]{3,2,1,0:T(8,128)S(1)} %get-tuple-element.51), channel_id=1, source_target_pairs={{0,1},{1,0},{2,3},{3,2},{4,5},{5,4},{6,7},{7,6},{8,9},{9,8},{10,11... | collective-permute-start | bytes 1572872 | tf_op jit(solution)/shard_map/ppermute | solution.py:400
  37.5 7.7 %collective-permute-start.12 = (bf16[256,128]{1,0:T(8,128)(2,1)S(1)}, bf16[256,128]{1,0:T(8,128)(2,1)S(1)}, u32[]{:S(2)}, u32[]{:S(2)}) collective-permute-start(bf16[256,128]{1,0:T(8,128)(2,1)S(1)} %get-tuple-element.48), channel_id=1, source_target_pairs={{1,3},{3,1},{5,7},{7,5},{9,11},{11,9},{13,15},{15,13},{0,14},{2,12... | collective-permute-start | bytes 196616 | tf_op jit(solution)/shard_map/ppermute | solution.py:392
  41.2 6.1 %collective-permute-start.14 = (bf16[256,128]{1,0:T(8,128)(2,1)S(1)}, bf16[256,128]{1,0:T(8,128)(2,1)S(1)}, u32[]{:S(2)}, u32[]{:S(2)}) collective-permute-start(bf16[256,128]{1,0:T(8,128)(2,1)S(1)} %get-tuple-element.54), channel_id=1, source_target_pairs={{1,5},{3,7},{5,1},{7,3},{9,13},{11,15},{13,9},{15,11},{0,12},{2,14... | collective-permute-start | bytes 196616 | tf_op jit(solution)/shard_map/ppermute | solution.py:392
  42.4 7.7 %collective-permute-start.15 = (bf16[256,128]{1,0:T(8,128)(2,1)S(1)}, bf16[256,128]{1,0:T(8,128)(2,1)S(1)}, u32[]{:S(2)}, u32[]{:S(2)}) collective-permute-start(bf16[256,128]{1,0:T(8,128)(2,1)S(1)} %get-tuple-element.55), channel_id=1, source_target_pairs={{1,7},{3,5},{5,3},{7,1},{9,15},{11,13},{13,11},{15,9},{0,8},{2,10}... | collective-permute-start | bytes 196616 | tf_op jit(solution)/shard_map/ppermute | solution.py:392
  43.3 6.8 %collective-permute-start.16 = (bf16[256,128]{1,0:T(8,128)(2,1)S(1)}, bf16[256,128]{1,0:T(8,128)(2,1)S(1)}, u32[]{:S(2)}, u32[]{:S(2)}) collective-permute-start(bf16[256,128]{1,0:T(8,128)(2,1)S(1)} %get-tuple-element.56), channel_id=1, source_target_pairs={{1,11},{3,9},{5,15},{7,13},{9,3},{11,1},{13,7},{15,5},{17,27},{19,... | collective-permute-start | bytes 196616 | tf_op jit(solution)/shard_map/ppermute | solution.py:392
  50.1 1.4 %collective-permute-start.17 = (bf16[512,128]{1,0:T(8,128)(2,1)S(1)}, bf16[512,128]{1,0:T(8,128)(2,1)S(1)}, u32[]{:S(2)}, u32[]{:S(2)}) collective-permute-start(bf16[512,128]{1,0:T(8,128)(2,1)S(1)} %shard_map.108), channel_id=1, source_target_pairs={{0,1},{1,0},{2,3},{3,2},{4,5},{5,4},{6,7},{7,6},{8,9},{9,8},{10,11... | collective-permute-start | bytes 393224 | tf_op jit(solution)/shard_map/ppermute | solution.py:414

commit v10 on v9

--- a/solution.py
+++ b/solution.py
@@ -334,8 +334,6 @@
                 2,
                 aliases={5: 0},
             )(tile_slot, tile_col, left, right, tiles, acc)
-        if h == half_ring - 1:
-            next_left, basis_here, wide = lax.optimization_barrier((next_left, basis_here, wide))
         left, done = lax.optimization_barrier((next_left, acc))
         right, _ = lax.optimization_barrier((next_right, acc))
         acc = done
@@ -353,7 +351,7 @@
         compiler_params=params,
         cost_estimate=cost,
     )(*seen)
-    left, wanted = lax.optimization_barrier((left, wanted))
+    left, wanted, basis_here, wide = lax.optimization_barrier((left, wanted, basis_here, wide))
     wanted_other = lax.ppermute(wanted, "col", swap)
 
     half_shape = (BR_DEV, 2, half, width)

time: 52.6 us -> 51.8 us (0.985)
  waiting for transfers between devices: 14.7 us -> 13.9 us
    ppermute x1, waiting for transfers between devices: 1.68 us -> 0.7 us  [local(): next_left = lax.ppermute(left[:cut], 'row', to_right)]
  transfers between devices with their start and end apart: 18 -> 18, of which waited for: 9 -> 9; matrix products, arithmetic and copies ran while one was open for 0% -> 0% of each run, Pallas kernels for 29% -> 30%
where the time goes in v10:
time: 51.8 us; the launch traced here: 51.6 us
  starting transfers between devices  19.4 us (37%)
  Pallas kernels  16.4 us (32%)
  waiting for transfers between devices  13.9 us (27%)
  local copies, waits for them, and re-layouts  1.01 us (2%)
  between operations  0.89 us (2%)
    ppermute x4, starting transfers between devices, local(): fetched.append(lax.ppermute(sent[step], ('row', 'col'), pairs))  6.44 us
    ppermute x3, starting transfers between devices, local(): next_right = lax.ppermute(right, 'row', to_left)  6.12 us
    pallas_call x2, Pallas kernels, local(): call(functools.partial(hop_middle, hop=h - 1), [in_smem] * 2 + [in_vmem]...  5.63 us
    ppermute x4, waiting for transfers between devices, local(): fetched.append(lax.ppermute(sent[step], ('row', 'col'), pairs))  5.46 us
    pallas_call x1, Pallas kernels, local(): call(hop_early, [in_smem] * 2 + [in_vmem] * 4, acc_out, [], 3)  3.73 us
    ppermute x3, waiting for transfers between devices, local(): next_right = lax.ppermute(right, 'row', to_left)  3.4 us
    ppermute x1, waiting for transfers between devices, local(): lax.ppermute(own_lines, 'row', to_left)  2.99 us
    ppermute x1, starting transfers between devices, local(): lax.ppermute(own_lines, 'row', to_left)  2.47 us
  transfers between devices with their start and end apart: 18, of which 9 were waited for; matrix products, arithmetic and copies ran while one was open for 0% of the time, Pallas kernels for 30%

profile of v10, /device:TPU:0, one launch (start us, length us, event | category | flops | bytes accessed | tf_op | source)
XLA Modules:
  0.0 51.6 jit_solution(5360690897190537697)
XLA Ops:
  0.6 0.0 slice-start.1
  0.7 0.0 slice-start.2
  0.7 3.0 %collective-permute-start.3 = (bf16[1024,128]{1,0:T(8,128)(2,1)}, bf16[1024,128]{1,0:T(8,128)(2,1)S(1)}, u32[]{:S(2)}, u32[]{:S(2)}) collective-permute-start(bf16[1024,128]{1,0:T(8,128)(2,1)} %bitcast.3), channel_id=1, source_target_pairs={{4,0},{8,4},{12,8},{14,12},{10,14},{6,10},{2,6},{0,2},{5,1},{9,5},... | collective-permute-start | bytes 786440 | tf_op jit(solution)/shard_map/ppermute | solution.py:312
  3.7 0.1 collective-permute-start
  3.8 0.9 %copy-done.5 = s32[2,256]{1,0:T(2,128)S(1)} copy-done((s32[2,256]{1,0:T(2,128)S(1)}, s32[2,256]{1,0:T(2,128)}, u32[]{:S(2)}) %copy-start.5) | copy-done | bytes 2072
  4.8 2.5 %collective-permute-start.4 = (bf16[16,128]{1,0:T(8,128)(2,1)S(1)}, bf16[16,128]{1,0:T(8,128)(2,1)S(1)}, u32[]{:S(2)}, u32[]{:S(2)}) collective-permute-start(bf16[16,128]{1,0:T(8,128)(2,1)S(1)} %shard_map.95.refs_0_), channel_id=1, source_target_pairs={{4,0},{8,4},{12,8},{14,12},{10,14},{6,10},{2,6},{0,2},{5,1},{9,5},... | collective-permute-start | bytes 12296 | tf_op jit(solution)/shard_map/ppermute | solution.py:319
  7.3 0.1 collective-permute-start.1
  7.4 3.0 %collective-permute-done.4.lines.refs_2_ = bf16[16,128]{1,0:T(8,128)(2,1)S(1)} collective-permute-done((bf16[16,128]{1,0:T(8,128)(2,1)S(1)}, bf16[16,128]{1,0:T(8,128)(2,1)S(1)}, u32[]{:S(2)}, u32[]{:S(2)}) %collective-permute-start.4) | collective-permute-done | bytes 4128 | tf_op jit(solution)/shard_map/ppermute | solution.py:319
  10.4 1.7 %collective-permute-start.6 = (bf16[1040,128]{1,0:T(8,128)(2,1)S(1)}, bf16[1040,128]{1,0:T(8,128)(2,1)S(1)}, u32[]{:S(2)}, u32[]{:S(2)}) collective-permute-start(bf16[1040,128]{1,0:T(8,128)(2,1)S(1)} %shard_map.97.from_right), channel_id=1, source_target_pairs={{4,0},{8,4},{12,8},{14,12},{10,14},{6,10},{2,6},{0,2},{5,1},{9,5},... | collective-permute-start | bytes 798728 | tf_op jit(solution)/shard_map/ppermute | solution.py:312
  12.1 0.0 collective-permute-done.1.lines.refs_1_
  12.1 0.0 collective-permute-done.rows
  12.2 0.4 collective-permute-start.2
  12.6 3.7 %shard_map.98.start = f32[2,512,256]{2,1,0:T(8,128)S(1)} custom-call(s32[11]{0:T(128)S(1)} %copy-done.3, s32[11]{0:T(128)S(1)} %copy-done.4, bf16[1024,128]{1,0:T(8,128)(2,1)S(1)} %bitcast.5, bf16[1040,128]{1,0:T(8,128)(2,1)S(1)} %shard_map.96.from_left, bf16[1040,128]{1,0:T(8,128)(2,1)S(1)} %shard_map.97.from_right, bf16[11,2,512,512]{3,2,1,0:T(8,128)(2,1)S(1)} %bitcast.2), custom_call_target="tpu_custom_call" | custom-call | flops 1048576 | bytes 1048576 | tf_op jit(solution)/shard_map/pallas_call | solution.py:325
  16.3 0.0 copy-start
  16.4 0.0 copy-start.2
  16.4 0.0 copy-start.6
  16.4 1.7 %collective-permute-done.6.from_right.refs_4_ = bf16[1040,128]{1,0:T(8,128)(2,1)S(1)} collective-permute-done((bf16[1040,128]{1,0:T(8,128)(2,1)S(1)}, bf16[1040,128]{1,0:T(8,128)(2,1)S(1)}, u32[]{:S(2)}, u32[]{:S(2)}) %collective-permute-start.6) | collective-permute-done | bytes 266272 | tf_op jit(solution)/shard_map/ppermute | solution.py:312
  18.0 1.4 %collective-permute-start.8 = (bf16[1040,128]{1,0:T(8,128)(2,1)S(1)}, bf16[1040,128]{1,0:T(8,128)(2,1)S(1)}, u32[]{:S(2)}, u32[]{:S(2)}) collective-permute-start(bf16[1040,128]{1,0:T(8,128)(2,1)S(1)} %collective-permute-done.6.from_right.refs_4_), channel_id=1, source_target_pairs={{4,0},{8,4},{12,8},{14,12},{10,14},{6,10},{2,6},{0,2},{5,1},{9,5},... | collective-permute-start | bytes 798728 | tf_op jit(solution)/shard_map/ppermute | solution.py:312
  19.4 0.7 %collective-permute-start.5 = (bf16[1040,128]{1,0:T(8,128)(2,1)S(1)}, bf16[1040,128]{1,0:T(8,128)(2,1)S(1)}, u32[]{:S(2)}, u32[]{:S(2)}) collective-permute-start(bf16[1040,128]{1,0:T(8,128)(2,1)S(1)} %collective-permute-done.2.from_left.refs_3_), channel_id=1, source_target_pairs={{0,4},{4,8},{8,12},{12,14},{14,10},{10,6},{6,2},{2,0},{1,5},{5,9},... | collective-permute-start | bytes 798728 | tf_op jit(solution)/shard_map/ppermute | solution.py:311
  20.1 2.9 %shard_map.99.start = f32[2,512,256]{2,1,0:T(8,128)S(1)} custom-call(s32[11]{0:T(128)S(1)} %copy-done.3, s32[11]{0:T(128)S(1)} %copy-done.4, bf16[1040,128]{1,0:T(8,128)(2,1)S(1)} %collective-permute-done.2.from_left.refs_3_, bf16[1040,128]{1,0:T(8,128)(2,1)S(1)} %collective-permute-done.6.from_right.refs_4_, ...), custom_call_target="tpu_custom_call", output_to_operand_aliasing={{}: (5, {})} | custom-call | flops 1048576 | bytes 1048576 | tf_op jit(solution)/shard_map/pallas_call | solution.py:329
  22.9 1.7 %collective-permute-done.8.from_right.refs_6_ = bf16[1040,128]{1,0:T(8,128)(2,1)S(1)} collective-permute-done((bf16[1040,128]{1,0:T(8,128)(2,1)S(1)}, bf16[1040,128]{1,0:T(8,128)(2,1)S(1)}, u32[]{:S(2)}, u32[]{:S(2)}) %collective-permute-start.8) | collective-permute-done | bytes 266272 | tf_op jit(solution)/shard_map/ppermute | solution.py:312
  24.7 1.6 %collective-permute-start.9 = (bf16[528,128]{1,0:T(8,128)(2,1)S(1)}, bf16[528,128]{1,0:T(8,128)(2,1)S(1)}, u32[]{:S(2)}, u32[]{:S(2)}) collective-permute-start(bf16[528,128]{1,0:T(8,128)(2,1)S(1)} %slice.7), channel_id=1, source_target_pairs={{4,0},{8,4},{12,8},{14,12},{10,14},{6,10},{2,6},{0,2},{5,1},{9,5},... | collective-permute-start | bytes 405512 | tf_op jit(solution)/shard_map/ppermute | solution.py:316
  26.3 0.8 %collective-permute-start.7 = (bf16[512,128]{1,0:T(8,128)(2,1)S(1)}, bf16[512,128]{1,0:T(8,128)(2,1)S(1)}, u32[]{:S(2)}, u32[]{:S(2)}) collective-permute-start(bf16[512,128]{1,0:T(8,128)(2,1)S(1)} %slice.6), channel_id=1, source_target_pairs={{0,4},{4,8},{8,12},{12,14},{14,10},{10,6},{6,2},{2,0},{1,5},{5,9},... | collective-permute-start | bytes 393224 | tf_op jit(solution)/shard_map/ppermute | solution.py:315
  27.0 1.0 %shard_map.102 = (bf16[2,1152,512]{2,1,0:T(8,128)(2,1)S(1)}, f32[2,128,512]{2,1,0:T(8,128)S(1)}) custom-call(s32[2,256]{1,0:T(2,128)S(1)} %copy-done.6, bf16[2,256,512]{2,1,0:T(8,128)(2,1)S(1)} %copy-done, bf16[2,128,512]{2,1,0:T(8,128)(2,1)S(1)} %copy-done.2), custom_call_target="tpu_custom_call" | custom-call | flops 1048576 | bytes 1048576 | tf_op jit(solution)/shard_map/pallas_call | solution.py:296
  28.0 0.0 copy-start.7
  28.0 2.8 %shard_map.100.start = f32[2,512,256]{2,1,0:T(8,128)S(1)} custom-call(s32[11]{0:T(128)S(1)} %copy-done.3, s32[11]{0:T(128)S(1)} %copy-done.4, bf16[1040,128]{1,0:T(8,128)(2,1)S(1)} %collective-permute-done.5.from_left.refs_5_, bf16[1040,128]{1,0:T(8,128)(2,1)S(1)} %collective-permute-done.8.from_right.refs_6_, ...), custom_call_target="tpu_custom_call", output_to_operand_aliasing={{}: (5, {})} | custom-call | flops 1048576 | bytes 1048576 | tf_op jit(solution)/shard_map/pallas_call | solution.py:329
  30.8 0.7 %collective-permute-done.7.low = bf16[512,128]{1,0:T(8,128)(2,1)S(1)} collective-permute-done((bf16[512,128]{1,0:T(8,128)(2,1)S(1)}, bf16[512,128]{1,0:T(8,128)(2,1)S(1)}, u32[]{:S(2)}, u32[]{:S(2)}) %collective-permute-start.7) | collective-permute-done | bytes 131104 | tf_op jit(solution)/shard_map/ppermute | solution.py:315
  31.5 0.1 shard_map.101.mine
  31.5 0.1 collective-permute-start.10
  31.6 2.0 %shard_map.103 = (f32[2,512,256]{2,1,0:T(8,128)S(1)}, f32[2,512,128]{2,1,0:T(8,128)S(1)}) custom-call(s32[11]{0:T(128)S(1)} %copy-done.3, s32[11]{0:T(128)S(1)} %copy-done.4, f32[2]{0:T(128)S(1)} %copy-done.7, bf16[512,128]{1,0:T(8,128)(2,1)S(1)} %collective-permute-done.7.low, ...), custom_call_target="tpu_custom_call", output_to_operand_aliasing={{0}: (6, {})} | custom-call | flops 1048576 | bytes 1048576 | tf_op jit(solution)/shard_map/pallas_call | solution.py:358
  33.6 0.6 %collective-permute-start.11 = (f32[2,512,128]{2,1,0:T(8,128)S(1)}, f32[2,512,128]{2,1,0:T(8,128)S(1)}, u32[]{:S(2)}, u32[]{:S(2)}) collective-permute-start(f32[2,512,128]{2,1,0:T(8,128)S(1)} %get-tuple-element.45.mine), channel_id=1, source_target_pairs={{0,1},{1,0},{2,3},{3,2},{4,5},{5,4},{6,7},{7,6},{8,9},{9,8},{10,11... | collective-permute-start | bytes 1572872 | tf_op jit(solution)/shard_map/ppermute | solution.py:367
  34.2 0.1 shard_map.106
  34.2 0.1 collective-permute-start.13
  34.3 0.9 %shard_map.104.pick = bf16[1152,1024]{1,0:T(8,128)(2,1)S(1)} custom-call(bf16[128,128]{1,0:T(8,128)(2,1)S(1)} %shard_map.101.mine, bf16[128,128]{1,0:T(8,128)(2,1)S(1)} %collective-permute-done.10.theirs), custom_call_target="tpu_custom_call" | custom-call | flops 4294967296 | bytes 1048576 | tf_op jit(solution)/shard_map/pallas_call | solution.py:368
  35.3 0.4 collective-permute-done.11.theirs
  35.7 0.8 %shard_map.105 = (bf16[128,128]{1,0:T(8,128)(2,1)S(1)}, bf16[256,128]{1,0:T(8,128)(2,1)S(1)}, bf16[256,128]{1,0:T(8,128)(2,1)S(1)}, bf16[256,128]{1,0:T(8,128)(2,1)S(1)}, bf16[256,128]{1,0:T(8,128)(2,1)S(1)}) custom-call(bf16[1152,1024]{1,0:T(8,128)(2,1)S(1)} %shard_map.104.pick, f32[2,512,128]{2,1,0:T(8,128)S(1)} %get-tuple-element.45.mine, ...), custom_call_target="tpu_custom_call" | custom-call | flops 1048576 | bytes 1048576 | tf_op jit(solution)/shard_map/pallas_call | solution.py:377
  36.5 4.1 %collective-permute-start.12 = (bf16[256,128]{1,0:T(8,128)(2,1)S(1)}, bf16[256,128]{1,0:T(8,128)(2,1)S(1)}, u32[]{:S(2)}, u32[]{:S(2)}) collective-permute-start(bf16[256,128]{1,0:T(8,128)(2,1)S(1)} %get-tuple-element.46), channel_id=1, source_target_pairs={{1,3},{3,1},{5,7},{7,5},{9,11},{11,9},{13,15},{15,13},{0,14},{2,12... | collective-permute-start | bytes 196616 | tf_op jit(solution)/shard_map/ppermute | solution.py:390
  40.6 0.8 %collective-permute-start.14 = (bf16[256,128]{1,0:T(8,128)(2,1)S(1)}, bf16[256,128]{1,0:T(8,128)(2,1)S(1)}, u32[]{:S(2)}, u32[]{:S(2)}) collective-permute-start(bf16[256,128]{1,0:T(8,128)(2,1)S(1)} %get-tuple-element.52), channel_id=1, source_target_pairs={{1,5},{3,7},{5,1},{7,3},{9,13},{11,15},{13,9},{15,11},{0,12},{2,14... | collective-permute-start | bytes 196616 | tf_op jit(solution)/shard_map/ppermute | solution.py:390
  41.4 0.9 %collective-permute-start.15 = (bf16[256,128]{1,0:T(8,128)(2,1)S(1)}, bf16[256,128]{1,0:T(8,128)(2,1)S(1)}, u32[]{:S(2)}, u32[]{:S(2)}) collective-permute-start(bf16[256,128]{1,0:T(8,128)(2,1)S(1)} %get-tuple-element.53), channel_id=1, source_target_pairs={{1,7},{3,5},{5,3},{7,1},{9,15},{11,13},{13,11},{15,9},{0,8},{2,10}... | collective-permute-start | bytes 196616 | tf_op jit(solution)/shard_map/ppermute | solution.py:390
  42.3 0.7 %collective-permute-start.16 = (bf16[256,128]{1,0:T(8,128)(2,1)S(1)}, bf16[256,128]{1,0:T(8,128)(2,1)S(1)}, u32[]{:S(2)}, u32[]{:S(2)}) collective-permute-start(bf16[256,128]{1,0:T(8,128)(2,1)S(1)} %get-tuple-element.54), channel_id=1, source_target_pairs={{1,11},{3,9},{5,15},{7,13},{9,3},{11,1},{13,7},{15,5},{17,27},{19,... | collective-permute-start | bytes 196616 | tf_op jit(solution)/shard_map/ppermute | solution.py:390
  43.0 0.8 %shard_map.107 = f32[2,2,256,128]{3,2,1,0:T(8,128)} custom-call(f32[2,2,256,128]{3,2,1,0:T(8,128)S(1)} %get-tuple-element.48.mine, f32[2,2,256,128]{3,2,1,0:T(8,128)S(1)} %collective-permute-done.13.theirs), custom_call_target="tpu_custom_call" | custom-call | flops 1048576 | bytes 1048576 | tf_op jit(solution)/shard_map/pallas_call | solution.py:399
  43.8 0.4 collective-permute-done.12.refs_0_.refs_1_
  44.3 2.5 %collective-permute-done.14.refs_1_.refs_2_ = bf16[256,128]{1,0:T(8,128)(2,1)S(1)} collective-permute-done((bf16[256,128]{1,0:T(8,128)(2,1)S(1)}, bf16[256,128]{1,0:T(8,128)(2,1)S(1)}, u32[]{:S(2)}, u32[]{:S(2)}) %collective-permute-start.14) | collective-permute-done | bytes 65568 | tf_op jit(solution)/shard_map/ppermute | solution.py:390
  46.8 2.5 %collective-permute-done.15.refs_2_.refs_3_ = bf16[256,128]{1,0:T(8,128)(2,1)S(1)} collective-permute-done((bf16[256,128]{1,0:T(8,128)(2,1)S(1)}, bf16[256,128]{1,0:T(8,128)(2,1)S(1)}, u32[]{:S(2)}, u32[]{:S(2)}) %collective-permute-start.15) | collective-permute-done | bytes 65568 | tf_op jit(solution)/shard_map/ppermute | solution.py:390
  49.3 0.1 collective-permute-start.17
  49.4 0.4 shard_map.109.first
  49.8 0.9 %collective-permute-done.17.passed = bf16[512,128]{1,0:T(8,128)(2,1)S(1)} collective-permute-done((bf16[512,128]{1,0:T(8,128)(2,1)S(1)}, bf16[512,128]{1,0:T(8,128)(2,1)S(1)}, u32[]{:S(2)}, u32[]{:S(2)}) %collective-permute-start.17) | collective-permute-done | bytes 131104 | tf_op jit(solution)/shard_map/ppermute | solution.py:412
  50.7 0.9 %shard_map.110 = f32[2,512]{1,0:T(2,128)} custom-call(bf16[512,128]{1,0:T(8,128)(2,1)S(1)} %collective-permute-done.17.passed, f32[2,128,512]{2,1,0:T(8,128)S(1)} %shard_map.109.first, bf16[2,1152,512]{2,1,0:T(8,128)(2,1)S(1)} %get-tuple-element.56.refs_5_.basis, f32[2,128,512]{2,1,0:T(8,128)S(1)} %get-tuple-element.57.supernode), custom_call_target="tpu_custom_call" | custom-call | tf_op jit(solution)/shard_map/pallas_call | solution.py:419
  (29 shorter events, 0.1 us)
Async XLA Ops:
  0.6 11.9 %slice-start = ((s8[11534336]{0:T(1024)(128)(4,1)}), s8[4194304]{0:T(1024)(128)(4,1)S(1)}, s32[]{:S(2)}) async-start(s8[11534336]{0:T(1024)(128)(4,1)} %bitcast.1), calls=%async_computation | async-start | bytes 8388608
  0.6 11.9 %slice-start.1 = ((s8[11534336]{0:T(1024)(128)(4,1)}), s8[4194304]{0:T(1024)(128)(4,1)S(1)}, s32[]{:S(2)}) async-start(s8[11534336]{0:T(1024)(128)(4,1)} %bitcast.1), calls=%async_computation.1 | async-start | bytes 8388608
  0.7 11.9 %slice-start.2 = ((s8[11534336]{0:T(1024)(128)(4,1)}), s8[3145728]{0:T(1024)(128)(4,1)S(1)}, s32[]{:S(2)}) async-start(s8[11534336]{0:T(1024)(128)(4,1)} %bitcast.1), calls=%async_computation.2 | async-start | bytes 6291456
  0.7 11.9 %copy-start.1 = (bf16[1,8,2,64,128]{4,3,2,1,0:T(8,128)(2,1)S(1)}, bf16[1,8,2,64,128]{4,3,2,1,0:T(8,128)(2,1)}, u32[]{:S(2)}) copy-start(bf16[1,8,2,64,128]{4,3,2,1,0:T(8,128)(2,1)} %param.8) | copy-start | bytes 786436
  0.7 11.9 %copy-start.3 = (s32[11]{0:T(128)S(1)}, s32[11]{0:T(128)}, u32[]{:S(2)}) copy-start(s32[11]{0:T(128)} %slots.7) | copy-start | bytes 136
  0.7 11.9 %copy-start.4 = (s32[11]{0:T(128)S(1)}, s32[11]{0:T(128)}, u32[]{:S(2)}) copy-start(s32[11]{0:T(128)} %cols.7) | copy-start | bytes 136
  0.7 9.7 %collective-permute-start.3 = (bf16[1024,128]{1,0:T(8,128)(2,1)}, bf16[1024,128]{1,0:T(8,128)(2,1)S(1)}, u32[]{:S(2)}, u32[]{:S(2)}) collective-permute-start(bf16[1024,128]{1,0:T(8,128)(2,1)} %bitcast.3), channel_id=1, source_target_pairs={{4,0},{8,4},{12,8},{14,12},{10,14},{6,10},{2,6},{0,2},{5,1},{9,5},... | collective-permute-start | bytes 786440 | tf_op jit(solution)/shard_map/ppermute | solution.py:312
  3.7 8.4 %collective-permute-start = (bf16[1024,128]{1,0:T(8,128)(2,1)}, bf16[1024,128]{1,0:T(8,128)(2,1)S(1)}, u32[]{:S(2)}, u32[]{:S(2)}) collective-permute-start(bf16[1024,128]{1,0:T(8,128)(2,1)} %bitcast.4), channel_id=1, source_target_pairs={{0,4},{4,8},{8,12},{12,14},{14,10},{10,6},{6,2},{2,0},{1,5},{5,9},... | collective-permute-start | bytes 786440 | tf_op jit(solution)/shard_map/ppermute | solution.py:311
  3.8 0.9 %copy-start.5 = (s32[2,256]{1,0:T(2,128)S(1)}, s32[2,256]{1,0:T(2,128)}, u32[]{:S(2)}) copy-start(s32[2,256]{1,0:T(2,128)} %wanted.3) | copy-start | bytes 6148
  4.8 5.6 %collective-permute-start.4 = (bf16[16,128]{1,0:T(8,128)(2,1)S(1)}, bf16[16,128]{1,0:T(8,128)(2,1)S(1)}, u32[]{:S(2)}, u32[]{:S(2)}) collective-permute-start(bf16[16,128]{1,0:T(8,128)(2,1)S(1)} %shard_map.95.refs_0_), channel_id=1, source_target_pairs={{4,0},{8,4},{12,8},{14,12},{10,14},{6,10},{2,6},{0,2},{5,1},{9,5},... | collective-permute-start | bytes 12296 | tf_op jit(solution)/shard_map/ppermute | solution.py:319
  7.3 4.9 %collective-permute-start.1 = (bf16[16,128]{1,0:T(8,128)(2,1)S(1)}, bf16[16,128]{1,0:T(8,128)(2,1)S(1)}, u32[]{:S(2)}, u32[]{:S(2)}) collective-permute-start(bf16[16,128]{1,0:T(8,128)(2,1)S(1)} %shard_map.95.refs_0_), channel_id=1, source_target_pairs={{0,4},{4,8},{8,12},{12,14},{14,10},{10,6},{6,2},{2,0},{1,5},{5,9},... | collective-permute-start | bytes 12296 | tf_op jit(solution)/shard_map/ppermute | solution.py:319
  10.4 7.6 %collective-permute-start.6 = (bf16[1040,128]{1,0:T(8,128)(2,1)S(1)}, bf16[1040,128]{1,0:T(8,128)(2,1)S(1)}, u32[]{:S(2)}, u32[]{:S(2)}) collective-permute-start(bf16[1040,128]{1,0:T(8,128)(2,1)S(1)} %shard_map.97.from_right), channel_id=1, source_target_pairs={{4,0},{8,4},{12,8},{14,12},{10,14},{6,10},{2,6},{0,2},{5,1},{9,5},... | collective-permute-start | bytes 798728 | tf_op jit(solution)/shard_map/ppermute | solution.py:312
  12.2 7.2 %collective-permute-start.2 = (bf16[1040,128]{1,0:T(8,128)(2,1)S(1)}, bf16[1040,128]{1,0:T(8,128)(2,1)S(1)}, u32[]{:S(2)}, u32[]{:S(2)}) collective-permute-start(bf16[1040,128]{1,0:T(8,128)(2,1)S(1)} %shard_map.96.from_left), channel_id=1, source_target_pairs={{0,4},{4,8},{8,12},{12,14},{14,10},{10,6},{6,2},{2,0},{1,5},{5,9},... | collective-permute-start | bytes 798728 | tf_op jit(solution)/shard_map/ppermute | solution.py:311
  16.3 10.7 %copy-start = (bf16[2,256,512]{2,1,0:T(8,128)(2,1)S(1)}, bf16[2,256,512]{2,1,0:T(8,128)(2,1)}, u32[]{:S(2)}) copy-start(bf16[2,256,512]{2,1,0:T(8,128)(2,1)} %basis.1) | copy-start | bytes 1572868
  16.4 10.7 %copy-start.2 = (bf16[2,128,512]{2,1,0:T(8,128)(2,1)S(1)}, bf16[2,128,512]{2,1,0:T(8,128)(2,1)}, u32[]{:S(2)}) copy-start(bf16[2,128,512]{2,1,0:T(8,128)(2,1)} %supernode.1) | copy-start | bytes 786436
  16.4 10.7 %copy-start.6 = (s32[2,256]{1,0:T(2,128)S(1)}, s32[2,256]{1,0:T(2,128)}, u32[]{:S(2)}) copy-start(s32[2,256]{1,0:T(2,128)} %wanted.3) | copy-start | bytes 6148
  18.0 6.7 %collective-permute-start.8 = (bf16[1040,128]{1,0:T(8,128)(2,1)S(1)}, bf16[1040,128]{1,0:T(8,128)(2,1)S(1)}, u32[]{:S(2)}, u32[]{:S(2)}) collective-permute-start(bf16[1040,128]{1,0:T(8,128)(2,1)S(1)} %collective-permute-done.6.from_right.refs_4_), channel_id=1, source_target_pairs={{4,0},{8,4},{12,8},{14,12},{10,14},{6,10},{2,6},{0,2},{5,1},{9,5},... | collective-permute-start | bytes 798728 | tf_op jit(solution)/shard_map/ppermute | solution.py:312
  19.4 6.9 %collective-permute-start.5 = (bf16[1040,128]{1,0:T(8,128)(2,1)S(1)}, bf16[1040,128]{1,0:T(8,128)(2,1)S(1)}, u32[]{:S(2)}, u32[]{:S(2)}) collective-permute-start(bf16[1040,128]{1,0:T(8,128)(2,1)S(1)} %collective-permute-done.2.from_left.refs_3_), channel_id=1, source_target_pairs={{0,4},{4,8},{8,12},{12,14},{14,10},{10,6},{6,2},{2,0},{1,5},{5,9},... | collective-permute-start | bytes 798728 | tf_op jit(solution)/shard_map/ppermute | solution.py:311
  24.7 6.8 %collective-permute-start.9 = (bf16[528,128]{1,0:T(8,128)(2,1)S(1)}, bf16[528,128]{1,0:T(8,128)(2,1)S(1)}, u32[]{:S(2)}, u32[]{:S(2)}) collective-permute-start(bf16[528,128]{1,0:T(8,128)(2,1)S(1)} %slice.7), channel_id=1, source_target_pairs={{4,0},{8,4},{12,8},{14,12},{10,14},{6,10},{2,6},{0,2},{5,1},{9,5},... | collective-permute-start | bytes 405512 | tf_op jit(solution)/shard_map/ppermute | solution.py:316
  26.3 5.2 %collective-permute-start.7 = (bf16[512,128]{1,0:T(8,128)(2,1)S(1)}, bf16[512,128]{1,0:T(8,128)(2,1)S(1)}, u32[]{:S(2)}, u32[]{:S(2)}) collective-permute-start(bf16[512,128]{1,0:T(8,128)(2,1)S(1)} %slice.6), channel_id=1, source_target_pairs={{0,4},{4,8},{8,12},{12,14},{14,10},{10,6},{6,2},{2,0},{1,5},{5,9},... | collective-permute-start | bytes 393224 | tf_op jit(solution)/shard_map/ppermute | solution.py:315
  28.0 3.6 %copy-start.7 = (f32[2]{0:T(128)S(1)}, f32[2]{0:T(128)}, u32[]{:S(2)}) copy-start(f32[2]{0:T(128)} %pole_weight.1) | copy-start | bytes 28
  31.5 2.1 %collective-permute-start.10 = (bf16[128,128]{1,0:T(8,128)(2,1)S(1)}, bf16[128,128]{1,0:T(8,128)(2,1)S(1)}, u32[]{:S(2)}, u32[]{:S(2)}) collective-permute-start(bf16[128,128]{1,0:T(8,128)(2,1)S(1)} %shard_map.101.mine), channel_id=1, source_target_pairs={{0,1},{1,0},{2,3},{3,2},{4,5},{5,4},{6,7},{7,6},{8,9},{9,8},{10,11... | collective-permute-start | bytes 98312 | tf_op jit(solution)/shard_map/ppermute | solution.py:355
  33.6 2.1 %collective-permute-start.11 = (f32[2,512,128]{2,1,0:T(8,128)S(1)}, f32[2,512,128]{2,1,0:T(8,128)S(1)}, u32[]{:S(2)}, u32[]{:S(2)}) collective-permute-start(f32[2,512,128]{2,1,0:T(8,128)S(1)} %get-tuple-element.45.mine), channel_id=1, source_target_pairs={{0,1},{1,0},{2,3},{3,2},{4,5},{5,4},{6,7},{7,6},{8,9},{9,8},{10,11... | collective-permute-start | bytes 1572872 | tf_op jit(solution)/shard_map/ppermute | solution.py:367
  34.2 8.7 %collective-permute-start.13 = (f32[2,2,256,128]{3,2,1,0:T(8,128)S(1)}, f32[2,2,256,128]{3,2,1,0:T(8,128)S(1)}, u32[]{:S(2)}, u32[]{:S(2)}) collective-permute-start(f32[2,2,256,128]{3,2,1,0:T(8,128)S(1)} %get-tuple-element.49), channel_id=1, source_target_pairs={{0,1},{1,0},{2,3},{3,2},{4,5},{5,4},{6,7},{7,6},{8,9},{9,8},{10,11... | collective-permute-start | bytes 1572872 | tf_op jit(solution)/shard_map/ppermute | solution.py:398
  36.5 7.8 %collective-permute-start.12 = (bf16[256,128]{1,0:T(8,128)(2,1)S(1)}, bf16[256,128]{1,0:T(8,128)(2,1)S(1)}, u32[]{:S(2)}, u32[]{:S(2)}) collective-permute-start(bf16[256,128]{1,0:T(8,128)(2,1)S(1)} %get-tuple-element.46), channel_id=1, source_target_pairs={{1,3},{3,1},{5,7},{7,5},{9,11},{11,9},{13,15},{15,13},{0,14},{2,12... | collective-permute-start | bytes 196616 | tf_op jit(solution)/shard_map/ppermute | solution.py:390
  40.6 6.2 %collective-permute-start.14 = (bf16[256,128]{1,0:T(8,128)(2,1)S(1)}, bf16[256,128]{1,0:T(8,128)(2,1)S(1)}, u32[]{:S(2)}, u32[]{:S(2)}) collective-permute-start(bf16[256,128]{1,0:T(8,128)(2,1)S(1)} %get-tuple-element.52), channel_id=1, source_target_pairs={{1,5},{3,7},{5,1},{7,3},{9,13},{11,15},{13,9},{15,11},{0,12},{2,14... | collective-permute-start | bytes 196616 | tf_op jit(solution)/shard_map/ppermute | solution.py:390
  41.4 7.9 %collective-permute-start.15 = (bf16[256,128]{1,0:T(8,128)(2,1)S(1)}, bf16[256,128]{1,0:T(8,128)(2,1)S(1)}, u32[]{:S(2)}, u32[]{:S(2)}) collective-permute-start(bf16[256,128]{1,0:T(8,128)(2,1)S(1)} %get-tuple-element.53), channel_id=1, source_target_pairs={{1,7},{3,5},{5,3},{7,1},{9,15},{11,13},{13,11},{15,9},{0,8},{2,10}... | collective-permute-start | bytes 196616 | tf_op jit(solution)/shard_map/ppermute | solution.py:390
  42.3 7.0 %collective-permute-start.16 = (bf16[256,128]{1,0:T(8,128)(2,1)S(1)}, bf16[256,128]{1,0:T(8,128)(2,1)S(1)}, u32[]{:S(2)}, u32[]{:S(2)}) collective-permute-start(bf16[256,128]{1,0:T(8,128)(2,1)S(1)} %get-tuple-element.54), channel_id=1, source_target_pairs={{1,11},{3,9},{5,15},{7,13},{9,3},{11,1},{13,7},{15,5},{17,27},{19,... | collective-permute-start | bytes 196616 | tf_op jit(solution)/shard_map/ppermute | solution.py:390
  49.3 1.4 %collective-permute-start.17 = (bf16[512,128]{1,0:T(8,128)(2,1)S(1)}, bf16[512,128]{1,0:T(8,128)(2,1)S(1)}, u32[]{:S(2)}, u32[]{:S(2)}) collective-permute-start(bf16[512,128]{1,0:T(8,128)(2,1)S(1)} %shard_map.108), channel_id=1, source_target_pairs={{0,1},{1,0},{2,3},{3,2},{4,5},{5,4},{6,7},{7,6},{8,9},{9,8},{10,11... | collective-permute-start | bytes 393224 | tf_op jit(solution)/shard_map/ppermute | solution.py:412

commit v11 on v10

--- a/solution.py
+++ b/solution.py
@@ -130,7 +130,7 @@
 
 def peers(n):
     half = n // 2
-    return list(range(n - 1, half + 1, -1)) + [half], list(range(1, half)) + [half + 1]
+    return list(range(half, n - 2)) + [n - 1], list(range(1, half)) + [n - 2]
 
 
 def place_of(chip, n):

time: 51.8 us -> 50.7 us (0.979)
  waiting for transfers between devices: 13.9 us -> 11.6 us
  starting transfers between devices: 19.4 us -> 20.6 us
    ppermute x4, waiting for transfers between devices: 5.46 us -> 3.16 us  [local(): fetched.append(lax.ppermute(sent[step], ('row', 'col'), pairs))]
    ppermute x4, starting transfers between devices: 6.44 us -> 7.62 us  [local(): fetched.append(lax.ppermute(sent[step], ('row', 'col'), pairs))]
  transfers between devices with their start and end apart: 18 -> 18, of which waited for: 9 -> 7; matrix products, arithmetic and copies ran while one was open for 0% -> 0% of each run, Pallas kernels for 30% -> 30%
where the time goes in v11:
time: 50.7 us; the launch traced here: 50.5 us
  starting transfers between devices  20.6 us (41%)
  Pallas kernels  16.4 us (32%)
  waiting for transfers between devices  11.6 us (23%)
  local copies, waits for them, and re-layouts  1.01 us (2%)
  between operations  0.89 us (2%)
    ppermute x4, starting transfers between devices, local(): fetched.append(lax.ppermute(sent[step], ('row', 'col'), pairs))  7.62 us
    ppermute x3, starting transfers between devices, local(): next_right = lax.ppermute(right, 'row', to_left)  6.12 us
    pallas_call x2, Pallas kernels, local(): call(functools.partial(hop_middle, hop=h - 1), [in_smem] * 2 + [in_vmem]...  5.63 us
    pallas_call x1, Pallas kernels, local(): call(hop_early, [in_smem] * 2 + [in_vmem] * 4, acc_out, [], 3)  3.73 us
    ppermute x3, waiting for transfers between devices, local(): next_right = lax.ppermute(right, 'row', to_left)  3.4 us
    ppermute x4, waiting for transfers between devices, local(): fetched.append(lax.ppermute(sent[step], ('row', 'col'), pairs))  3.16 us
    ppermute x1, waiting for transfers between devices, local(): lax.ppermute(own_lines, 'row', to_left)  2.99 us
    ppermute x1, starting transfers between devices, local(): lax.ppermute(own_lines, 'row', to_left)  2.47 us
  transfers between devices with their start and end apart: 18, of which 7 were waited for; matrix products, arithmetic and copies ran while one was open for 0% of the time, Pallas kernels for 30%

profile of v11, /device:TPU:0, one launch (start us, length us, event | category | flops | bytes accessed | tf_op | source)
XLA Modules:
  0.0 50.5 jit_solution(14499652287444987145)
XLA Ops:
  0.6 0.0 slice-start
  0.7 0.0 slice-start.2
  0.7 3.0 %collective-permute-start.3 = (bf16[1024,128]{1,0:T(8,128)(2,1)}, bf16[1024,128]{1,0:T(8,128)(2,1)S(1)}, u32[]{:S(2)}, u32[]{:S(2)}) collective-permute-start(bf16[1024,128]{1,0:T(8,128)(2,1)} %bitcast.3), channel_id=1, source_target_pairs={{4,0},{8,4},{12,8},{14,12},{10,14},{6,10},{2,6},{0,2},{5,1},{9,5},... | collective-permute-start | bytes 786440 | tf_op jit(solution)/shard_map/ppermute | solution.py:312
  3.7 0.1 collective-permute-start
  3.8 0.9 %copy-done.5 = s32[2,256]{1,0:T(2,128)S(1)} copy-done((s32[2,256]{1,0:T(2,128)S(1)}, s32[2,256]{1,0:T(2,128)}, u32[]{:S(2)}) %copy-start.5) | copy-done | bytes 2072
  4.8 2.5 %collective-permute-start.4 = (bf16[16,128]{1,0:T(8,128)(2,1)S(1)}, bf16[16,128]{1,0:T(8,128)(2,1)S(1)}, u32[]{:S(2)}, u32[]{:S(2)}) collective-permute-start(bf16[16,128]{1,0:T(8,128)(2,1)S(1)} %shard_map.95.refs_0_), channel_id=1, source_target_pairs={{4,0},{8,4},{12,8},{14,12},{10,14},{6,10},{2,6},{0,2},{5,1},{9,5},... | collective-permute-start | bytes 12296 | tf_op jit(solution)/shard_map/ppermute | solution.py:319
  7.3 0.1 collective-permute-start.1
  7.4 3.0 %collective-permute-done.4.lines.refs_2_ = bf16[16,128]{1,0:T(8,128)(2,1)S(1)} collective-permute-done((bf16[16,128]{1,0:T(8,128)(2,1)S(1)}, bf16[16,128]{1,0:T(8,128)(2,1)S(1)}, u32[]{:S(2)}, u32[]{:S(2)}) %collective-permute-start.4) | collective-permute-done | bytes 4128 | tf_op jit(solution)/shard_map/ppermute | solution.py:319
  10.4 0.0 collective-permute-done.3.rows
  10.4 1.7 %collective-permute-start.6 = (bf16[1040,128]{1,0:T(8,128)(2,1)S(1)}, bf16[1040,128]{1,0:T(8,128)(2,1)S(1)}, u32[]{:S(2)}, u32[]{:S(2)}) collective-permute-start(bf16[1040,128]{1,0:T(8,128)(2,1)S(1)} %shard_map.97.from_right), channel_id=1, source_target_pairs={{4,0},{8,4},{12,8},{14,12},{10,14},{6,10},{2,6},{0,2},{5,1},{9,5},... | collective-permute-start | bytes 798728 | tf_op jit(solution)/shard_map/ppermute | solution.py:312
  12.2 0.4 collective-permute-start.2
  12.6 3.7 %shard_map.98.start = f32[2,512,256]{2,1,0:T(8,128)S(1)} custom-call(s32[11]{0:T(128)S(1)} %copy-done.3, s32[11]{0:T(128)S(1)} %copy-done.4, bf16[1024,128]{1,0:T(8,128)(2,1)S(1)} %bitcast.5, bf16[1040,128]{1,0:T(8,128)(2,1)S(1)} %shard_map.96.from_left, bf16[1040,128]{1,0:T(8,128)(2,1)S(1)} %shard_map.97.from_right, bf16[11,2,512,512]{3,2,1,0:T(8,128)(2,1)S(1)} %bitcast.2), custom_call_target="tpu_custom_call" | custom-call | flops 1048576 | bytes 1048576 | tf_op jit(solution)/shard_map/pallas_call | solution.py:325
  16.3 0.0 copy-start
  16.4 0.0 copy-start.2
  16.4 0.0 copy-start.6
  16.4 1.7 %collective-permute-done.6.from_right.refs_4_ = bf16[1040,128]{1,0:T(8,128)(2,1)S(1)} collective-permute-done((bf16[1040,128]{1,0:T(8,128)(2,1)S(1)}, bf16[1040,128]{1,0:T(8,128)(2,1)S(1)}, u32[]{:S(2)}, u32[]{:S(2)}) %collective-permute-start.6) | collective-permute-done | bytes 266272 | tf_op jit(solution)/shard_map/ppermute | solution.py:312
  18.0 1.4 %collective-permute-start.8 = (bf16[1040,128]{1,0:T(8,128)(2,1)S(1)}, bf16[1040,128]{1,0:T(8,128)(2,1)S(1)}, u32[]{:S(2)}, u32[]{:S(2)}) collective-permute-start(bf16[1040,128]{1,0:T(8,128)(2,1)S(1)} %collective-permute-done.6.from_right.refs_4_), channel_id=1, source_target_pairs={{4,0},{8,4},{12,8},{14,12},{10,14},{6,10},{2,6},{0,2},{5,1},{9,5},... | collective-permute-start | bytes 798728 | tf_op jit(solution)/shard_map/ppermute | solution.py:312
  19.4 0.0 collective-permute-done.2.from_left.refs_3_
  19.4 0.7 %collective-permute-start.5 = (bf16[1040,128]{1,0:T(8,128)(2,1)S(1)}, bf16[1040,128]{1,0:T(8,128)(2,1)S(1)}, u32[]{:S(2)}, u32[]{:S(2)}) collective-permute-start(bf16[1040,128]{1,0:T(8,128)(2,1)S(1)} %collective-permute-done.2.from_left.refs_3_), channel_id=1, source_target_pairs={{0,4},{4,8},{8,12},{12,14},{14,10},{10,6},{6,2},{2,0},{1,5},{5,9},... | collective-permute-start | bytes 798728 | tf_op jit(solution)/shard_map/ppermute | solution.py:311
  20.1 2.9 %shard_map.99.start = f32[2,512,256]{2,1,0:T(8,128)S(1)} custom-call(s32[11]{0:T(128)S(1)} %copy-done.3, s32[11]{0:T(128)S(1)} %copy-done.4, bf16[1040,128]{1,0:T(8,128)(2,1)S(1)} %collective-permute-done.2.from_left.refs_3_, bf16[1040,128]{1,0:T(8,128)(2,1)S(1)} %collective-permute-done.6.from_right.refs_4_, ...), custom_call_target="tpu_custom_call", output_to_operand_aliasing={{}: (5, {})} | custom-call | flops 1048576 | bytes 1048576 | tf_op jit(solution)/shard_map/pallas_call | solution.py:329
  22.9 1.7 %collective-permute-done.8.from_right.refs_6_ = bf16[1040,128]{1,0:T(8,128)(2,1)S(1)} collective-permute-done((bf16[1040,128]{1,0:T(8,128)(2,1)S(1)}, bf16[1040,128]{1,0:T(8,128)(2,1)S(1)}, u32[]{:S(2)}, u32[]{:S(2)}) %collective-permute-start.8) | collective-permute-done | bytes 266272 | tf_op jit(solution)/shard_map/ppermute | solution.py:312
  24.7 1.6 %collective-permute-start.9 = (bf16[528,128]{1,0:T(8,128)(2,1)S(1)}, bf16[528,128]{1,0:T(8,128)(2,1)S(1)}, u32[]{:S(2)}, u32[]{:S(2)}) collective-permute-start(bf16[528,128]{1,0:T(8,128)(2,1)S(1)} %slice.7), channel_id=1, source_target_pairs={{4,0},{8,4},{12,8},{14,12},{10,14},{6,10},{2,6},{0,2},{5,1},{9,5},... | collective-permute-start | bytes 405512 | tf_op jit(solution)/shard_map/ppermute | solution.py:316
  26.3 0.0 collective-permute-done.5.from_left.refs_5_
  26.3 0.8 %collective-permute-start.7 = (bf16[512,128]{1,0:T(8,128)(2,1)S(1)}, bf16[512,128]{1,0:T(8,128)(2,1)S(1)}, u32[]{:S(2)}, u32[]{:S(2)}) collective-permute-start(bf16[512,128]{1,0:T(8,128)(2,1)S(1)} %slice.6), channel_id=1, source_target_pairs={{0,4},{4,8},{8,12},{12,14},{14,10},{10,6},{6,2},{2,0},{1,5},{5,9},... | collective-permute-start | bytes 393224 | tf_op jit(solution)/shard_map/ppermute | solution.py:315
  27.0 1.0 %shard_map.102 = (bf16[2,1152,512]{2,1,0:T(8,128)(2,1)S(1)}, f32[2,128,512]{2,1,0:T(8,128)S(1)}) custom-call(s32[2,256]{1,0:T(2,128)S(1)} %copy-done.6, bf16[2,256,512]{2,1,0:T(8,128)(2,1)S(1)} %copy-done, bf16[2,128,512]{2,1,0:T(8,128)(2,1)S(1)} %copy-done.2), custom_call_target="tpu_custom_call" | custom-call | flops 1048576 | bytes 1048576 | tf_op jit(solution)/shard_map/pallas_call | solution.py:296
  28.0 0.0 copy-start.7
  28.0 2.8 %shard_map.100.start = f32[2,512,256]{2,1,0:T(8,128)S(1)} custom-call(s32[11]{0:T(128)S(1)} %copy-done.3, s32[11]{0:T(128)S(1)} %copy-done.4, bf16[1040,128]{1,0:T(8,128)(2,1)S(1)} %collective-permute-done.5.from_left.refs_5_, bf16[1040,128]{1,0:T(8,128)(2,1)S(1)} %collective-permute-done.8.from_right.refs_6_, ...), custom_call_target="tpu_custom_call", output_to_operand_aliasing={{}: (5, {})} | custom-call | flops 1048576 | bytes 1048576 | tf_op jit(solution)/shard_map/pallas_call | solution.py:329
  30.8 0.7 %collective-permute-done.7.low = bf16[512,128]{1,0:T(8,128)(2,1)S(1)} collective-permute-done((bf16[512,128]{1,0:T(8,128)(2,1)S(1)}, bf16[512,128]{1,0:T(8,128)(2,1)S(1)}, u32[]{:S(2)}, u32[]{:S(2)}) %collective-permute-start.7) | collective-permute-done | bytes 131104 | tf_op jit(solution)/shard_map/ppermute | solution.py:315
  31.5 0.1 shard_map.101.mine
  31.5 0.1 collective-permute-start.10
  31.6 2.0 %shard_map.103 = (f32[2,512,256]{2,1,0:T(8,128)S(1)}, f32[2,512,128]{2,1,0:T(8,128)S(1)}) custom-call(s32[11]{0:T(128)S(1)} %copy-done.3, s32[11]{0:T(128)S(1)} %copy-done.4, f32[2]{0:T(128)S(1)} %copy-done.7, bf16[512,128]{1,0:T(8,128)(2,1)S(1)} %collective-permute-done.7.low, ...), custom_call_target="tpu_custom_call", output_to_operand_aliasing={{0}: (6, {})} | custom-call | flops 1048576 | bytes 1048576 | tf_op jit(solution)/shard_map/pallas_call | solution.py:358
  33.6 0.6 %collective-permute-start.11 = (f32[2,512,128]{2,1,0:T(8,128)S(1)}, f32[2,512,128]{2,1,0:T(8,128)S(1)}, u32[]{:S(2)}, u32[]{:S(2)}) collective-permute-start(f32[2,512,128]{2,1,0:T(8,128)S(1)} %get-tuple-element.45.mine), channel_id=1, source_target_pairs={{0,1},{1,0},{2,3},{3,2},{4,5},{5,4},{6,7},{7,6},{8,9},{9,8},{10,11... | collective-permute-start | bytes 1572872 | tf_op jit(solution)/shard_map/ppermute | solution.py:367
  34.2 0.1 shard_map.106
  34.2 0.1 collective-permute-start.13
  34.3 0.9 %shard_map.104.pick = bf16[1152,1024]{1,0:T(8,128)(2,1)S(1)} custom-call(bf16[128,128]{1,0:T(8,128)(2,1)S(1)} %shard_map.101.mine, bf16[128,128]{1,0:T(8,128)(2,1)S(1)} %collective-permute-done.10.theirs), custom_call_target="tpu_custom_call" | custom-call | flops 4294967296 | bytes 1048576 | tf_op jit(solution)/shard_map/pallas_call | solution.py:368
  35.3 0.4 collective-permute-done.11.theirs
  35.7 0.8 %shard_map.105 = (bf16[128,128]{1,0:T(8,128)(2,1)S(1)}, bf16[256,128]{1,0:T(8,128)(2,1)S(1)}, bf16[256,128]{1,0:T(8,128)(2,1)S(1)}, bf16[256,128]{1,0:T(8,128)(2,1)S(1)}, bf16[256,128]{1,0:T(8,128)(2,1)S(1)}) custom-call(bf16[1152,1024]{1,0:T(8,128)(2,1)S(1)} %shard_map.104.pick, f32[2,512,128]{2,1,0:T(8,128)S(1)} %get-tuple-element.45.mine, ...), custom_call_target="tpu_custom_call" | custom-call | flops 1048576 | bytes 1048576 | tf_op jit(solution)/shard_map/pallas_call | solution.py:377
  36.5 2.1 %collective-permute-start.12 = (bf16[256,128]{1,0:T(8,128)(2,1)S(1)}, bf16[256,128]{1,0:T(8,128)(2,1)S(1)}, u32[]{:S(2)}, u32[]{:S(2)}) collective-permute-start(bf16[256,128]{1,0:T(8,128)(2,1)S(1)} %get-tuple-element.46), channel_id=1, source_target_pairs={{1,3},{3,1},{5,7},{7,5},{9,11},{11,9},{13,15},{15,13},{0,8},{2,10}... | collective-permute-start | bytes 196616 | tf_op jit(solution)/shard_map/ppermute | solution.py:390
  38.6 1.9 %collective-permute-start.14 = (bf16[256,128]{1,0:T(8,128)(2,1)S(1)}, bf16[256,128]{1,0:T(8,128)(2,1)S(1)}, u32[]{:S(2)}, u32[]{:S(2)}) collective-permute-start(bf16[256,128]{1,0:T(8,128)(2,1)S(1)} %get-tuple-element.52), channel_id=1, source_target_pairs={{1,5},{3,7},{5,1},{7,3},{9,13},{11,15},{13,9},{15,11},{0,10},{2,8}... | collective-permute-start | bytes 196616 | tf_op jit(solution)/shard_map/ppermute | solution.py:390
  40.5 3.0 %collective-permute-start.15 = (bf16[256,128]{1,0:T(8,128)(2,1)S(1)}, bf16[256,128]{1,0:T(8,128)(2,1)S(1)}, u32[]{:S(2)}, u32[]{:S(2)}) collective-permute-start(bf16[256,128]{1,0:T(8,128)(2,1)S(1)} %get-tuple-element.53), channel_id=1, source_target_pairs={{1,7},{3,5},{5,3},{7,1},{9,15},{11,13},{13,11},{15,9},{0,14},{2,12... | collective-permute-start | bytes 196616 | tf_op jit(solution)/shard_map/ppermute | solution.py:390
  43.5 0.7 %collective-permute-start.16 = (bf16[256,128]{1,0:T(8,128)(2,1)S(1)}, bf16[256,128]{1,0:T(8,128)(2,1)S(1)}, u32[]{:S(2)}, u32[]{:S(2)}) collective-permute-start(bf16[256,128]{1,0:T(8,128)(2,1)S(1)} %get-tuple-element.54), channel_id=1, source_target_pairs={{1,13},{3,15},{5,9},{7,11},{9,5},{11,7},{13,1},{15,3},{17,29},{19,... | collective-permute-start | bytes 196616 | tf_op jit(solution)/shard_map/ppermute | solution.py:390
  44.1 0.0 collective-permute-done.13.theirs
  44.1 0.8 %shard_map.107 = f32[2,2,256,128]{3,2,1,0:T(8,128)} custom-call(f32[2,2,256,128]{3,2,1,0:T(8,128)S(1)} %get-tuple-element.48.mine, f32[2,2,256,128]{3,2,1,0:T(8,128)S(1)} %collective-permute-done.13.theirs), custom_call_target="tpu_custom_call" | custom-call | flops 1048576 | bytes 1048576 | tf_op jit(solution)/shard_map/pallas_call | solution.py:399
  45.0 3.2 %collective-permute-done.15.refs_2_.refs_3_ = bf16[256,128]{1,0:T(8,128)(2,1)S(1)} collective-permute-done((bf16[256,128]{1,0:T(8,128)(2,1)S(1)}, bf16[256,128]{1,0:T(8,128)(2,1)S(1)}, u32[]{:S(2)}, u32[]{:S(2)}) %collective-permute-start.15) | collective-permute-done | bytes 65568 | tf_op jit(solution)/shard_map/ppermute | solution.py:390
  48.2 0.1 collective-permute-start.17
  48.3 0.4 shard_map.109.first
  48.7 0.9 %collective-permute-done.17.passed = bf16[512,128]{1,0:T(8,128)(2,1)S(1)} collective-permute-done((bf16[512,128]{1,0:T(8,128)(2,1)S(1)}, bf16[512,128]{1,0:T(8,128)(2,1)S(1)}, u32[]{:S(2)}, u32[]{:S(2)}) %collective-permute-start.17) | collective-permute-done | bytes 131104 | tf_op jit(solution)/shard_map/ppermute | solution.py:412
  49.6 0.9 %shard_map.110 = f32[2,512]{1,0:T(2,128)} custom-call(bf16[512,128]{1,0:T(8,128)(2,1)S(1)} %collective-permute-done.17.passed, f32[2,128,512]{2,1,0:T(8,128)S(1)} %shard_map.109.first, bf16[2,1152,512]{2,1,0:T(8,128)(2,1)S(1)} %get-tuple-element.56.refs_5_.basis, f32[2,128,512]{2,1,0:T(8,128)S(1)} %get-tuple-element.57.supernode), custom_call_target="tpu_custom_call" | custom-call | tf_op jit(solution)/shard_map/pallas_call | solution.py:419
  (29 shorter events, 0.1 us)
Async XLA Ops:
  0.6 11.9 %slice-start = ((s8[11534336]{0:T(1024)(128)(4,1)}), s8[4194304]{0:T(1024)(128)(4,1)S(1)}, s32[]{:S(2)}) async-start(s8[11534336]{0:T(1024)(128)(4,1)} %bitcast.1), calls=%async_computation | async-start | bytes 8388608
  0.6 11.9 %slice-start.1 = ((s8[11534336]{0:T(1024)(128)(4,1)}), s8[4194304]{0:T(1024)(128)(4,1)S(1)}, s32[]{:S(2)}) async-start(s8[11534336]{0:T(1024)(128)(4,1)} %bitcast.1), calls=%async_computation.1 | async-start | bytes 8388608
  0.7 11.9 %slice-start.2 = ((s8[11534336]{0:T(1024)(128)(4,1)}), s8[3145728]{0:T(1024)(128)(4,1)S(1)}, s32[]{:S(2)}) async-start(s8[11534336]{0:T(1024)(128)(4,1)} %bitcast.1), calls=%async_computation.2 | async-start | bytes 6291456
  0.7 11.9 %copy-start.1 = (bf16[1,8,2,64,128]{4,3,2,1,0:T(8,128)(2,1)S(1)}, bf16[1,8,2,64,128]{4,3,2,1,0:T(8,128)(2,1)}, u32[]{:S(2)}) copy-start(bf16[1,8,2,64,128]{4,3,2,1,0:T(8,128)(2,1)} %param.8) | copy-start | bytes 786436
  0.7 11.9 %copy-start.3 = (s32[11]{0:T(128)S(1)}, s32[11]{0:T(128)}, u32[]{:S(2)}) copy-start(s32[11]{0:T(128)} %slots.7) | copy-start | bytes 136
  0.7 11.9 %copy-start.4 = (s32[11]{0:T(128)S(1)}, s32[11]{0:T(128)}, u32[]{:S(2)}) copy-start(s32[11]{0:T(128)} %cols.7) | copy-start | bytes 136
  0.7 9.7 %collective-permute-start.3 = (bf16[1024,128]{1,0:T(8,128)(2,1)}, bf16[1024,128]{1,0:T(8,128)(2,1)S(1)}, u32[]{:S(2)}, u32[]{:S(2)}) collective-permute-start(bf16[1024,128]{1,0:T(8,128)(2,1)} %bitcast.3), channel_id=1, source_target_pairs={{4,0},{8,4},{12,8},{14,12},{10,14},{6,10},{2,6},{0,2},{5,1},{9,5},... | collective-permute-start | bytes 786440 | tf_op jit(solution)/shard_map/ppermute | solution.py:312
  3.7 8.4 %collective-permute-start = (bf16[1024,128]{1,0:T(8,128)(2,1)}, bf16[1024,128]{1,0:T(8,128)(2,1)S(1)}, u32[]{:S(2)}, u32[]{:S(2)}) collective-permute-start(bf16[1024,128]{1,0:T(8,128)(2,1)} %bitcast.4), channel_id=1, source_target_pairs={{0,4},{4,8},{8,12},{12,14},{14,10},{10,6},{6,2},{2,0},{1,5},{5,9},... | collective-permute-start | bytes 786440 | tf_op jit(solution)/shard_map/ppermute | solution.py:311
  3.8 0.9 %copy-start.5 = (s32[2,256]{1,0:T(2,128)S(1)}, s32[2,256]{1,0:T(2,128)}, u32[]{:S(2)}) copy-start(s32[2,256]{1,0:T(2,128)} %wanted.3) | copy-start | bytes 6148
  4.8 5.6 %collective-permute-start.4 = (bf16[16,128]{1,0:T(8,128)(2,1)S(1)}, bf16[16,128]{1,0:T(8,128)(2,1)S(1)}, u32[]{:S(2)}, u32[]{:S(2)}) collective-permute-start(bf16[16,128]{1,0:T(8,128)(2,1)S(1)} %shard_map.95.refs_0_), channel_id=1, source_target_pairs={{4,0},{8,4},{12,8},{14,12},{10,14},{6,10},{2,6},{0,2},{5,1},{9,5},... | collective-permute-start | bytes 12296 | tf_op jit(solution)/shard_map/ppermute | solution.py:319
  7.3 4.9 %collective-permute-start.1 = (bf16[16,128]{1,0:T(8,128)(2,1)S(1)}, bf16[16,128]{1,0:T(8,128)(2,1)S(1)}, u32[]{:S(2)}, u32[]{:S(2)}) collective-permute-start(bf16[16,128]{1,0:T(8,128)(2,1)S(1)} %shard_map.95.refs_0_), channel_id=1, source_target_pairs={{0,4},{4,8},{8,12},{12,14},{14,10},{10,6},{6,2},{2,0},{1,5},{5,9},... | collective-permute-start | bytes 12296 | tf_op jit(solution)/shard_map/ppermute | solution.py:319
  10.4 7.6 %collective-permute-start.6 = (bf16[1040,128]{1,0:T(8,128)(2,1)S(1)}, bf16[1040,128]{1,0:T(8,128)(2,1)S(1)}, u32[]{:S(2)}, u32[]{:S(2)}) collective-permute-start(bf16[1040,128]{1,0:T(8,128)(2,1)S(1)} %shard_map.97.from_right), channel_id=1, source_target_pairs={{4,0},{8,4},{12,8},{14,12},{10,14},{6,10},{2,6},{0,2},{5,1},{9,5},... | collective-permute-start | bytes 798728 | tf_op jit(solution)/shard_map/ppermute | solution.py:312
  12.2 7.2 %collective-permute-start.2 = (bf16[1040,128]{1,0:T(8,128)(2,1)S(1)}, bf16[1040,128]{1,0:T(8,128)(2,1)S(1)}, u32[]{:S(2)}, u32[]{:S(2)}) collective-permute-start(bf16[1040,128]{1,0:T(8,128)(2,1)S(1)} %shard_map.96.from_left), channel_id=1, source_target_pairs={{0,4},{4,8},{8,12},{12,14},{14,10},{10,6},{6,2},{2,0},{1,5},{5,9},... | collective-permute-start | bytes 798728 | tf_op jit(solution)/shard_map/ppermute | solution.py:311
  16.3 10.7 %copy-start = (bf16[2,256,512]{2,1,0:T(8,128)(2,1)S(1)}, bf16[2,256,512]{2,1,0:T(8,128)(2,1)}, u32[]{:S(2)}) copy-start(bf16[2,256,512]{2,1,0:T(8,128)(2,1)} %basis.1) | copy-start | bytes 1572868
  16.4 10.7 %copy-start.2 = (bf16[2,128,512]{2,1,0:T(8,128)(2,1)S(1)}, bf16[2,128,512]{2,1,0:T(8,128)(2,1)}, u32[]{:S(2)}) copy-start(bf16[2,128,512]{2,1,0:T(8,128)(2,1)} %supernode.1) | copy-start | bytes 786436
  16.4 10.7 %copy-start.6 = (s32[2,256]{1,0:T(2,128)S(1)}, s32[2,256]{1,0:T(2,128)}, u32[]{:S(2)}) copy-start(s32[2,256]{1,0:T(2,128)} %wanted.3) | copy-start | bytes 6148
  18.0 6.7 %collective-permute-start.8 = (bf16[1040,128]{1,0:T(8,128)(2,1)S(1)}, bf16[1040,128]{1,0:T(8,128)(2,1)S(1)}, u32[]{:S(2)}, u32[]{:S(2)}) collective-permute-start(bf16[1040,128]{1,0:T(8,128)(2,1)S(1)} %collective-permute-done.6.from_right.refs_4_), channel_id=1, source_target_pairs={{4,0},{8,4},{12,8},{14,12},{10,14},{6,10},{2,6},{0,2},{5,1},{9,5},... | collective-permute-start | bytes 798728 | tf_op jit(solution)/shard_map/ppermute | solution.py:312
  19.4 6.9 %collective-permute-start.5 = (bf16[1040,128]{1,0:T(8,128)(2,1)S(1)}, bf16[1040,128]{1,0:T(8,128)(2,1)S(1)}, u32[]{:S(2)}, u32[]{:S(2)}) collective-permute-start(bf16[1040,128]{1,0:T(8,128)(2,1)S(1)} %collective-permute-done.2.from_left.refs_3_), channel_id=1, source_target_pairs={{0,4},{4,8},{8,12},{12,14},{14,10},{10,6},{6,2},{2,0},{1,5},{5,9},... | collective-permute-start | bytes 798728 | tf_op jit(solution)/shard_map/ppermute | solution.py:311
  24.7 6.8 %collective-permute-start.9 = (bf16[528,128]{1,0:T(8,128)(2,1)S(1)}, bf16[528,128]{1,0:T(8,128)(2,1)S(1)}, u32[]{:S(2)}, u32[]{:S(2)}) collective-permute-start(bf16[528,128]{1,0:T(8,128)(2,1)S(1)} %slice.7), channel_id=1, source_target_pairs={{4,0},{8,4},{12,8},{14,12},{10,14},{6,10},{2,6},{0,2},{5,1},{9,5},... | collective-permute-start | bytes 405512 | tf_op jit(solution)/shard_map/ppermute | solution.py:316
  26.3 5.2 %collective-permute-start.7 = (bf16[512,128]{1,0:T(8,128)(2,1)S(1)}, bf16[512,128]{1,0:T(8,128)(2,1)S(1)}, u32[]{:S(2)}, u32[]{:S(2)}) collective-permute-start(bf16[512,128]{1,0:T(8,128)(2,1)S(1)} %slice.6), channel_id=1, source_target_pairs={{0,4},{4,8},{8,12},{12,14},{14,10},{10,6},{6,2},{2,0},{1,5},{5,9},... | collective-permute-start | bytes 393224 | tf_op jit(solution)/shard_map/ppermute | solution.py:315
  28.0 3.6 %copy-start.7 = (f32[2]{0:T(128)S(1)}, f32[2]{0:T(128)}, u32[]{:S(2)}) copy-start(f32[2]{0:T(128)} %pole_weight.1) | copy-start | bytes 28
  31.5 2.1 %collective-permute-start.10 = (bf16[128,128]{1,0:T(8,128)(2,1)S(1)}, bf16[128,128]{1,0:T(8,128)(2,1)S(1)}, u32[]{:S(2)}, u32[]{:S(2)}) collective-permute-start(bf16[128,128]{1,0:T(8,128)(2,1)S(1)} %shard_map.101.mine), channel_id=1, source_target_pairs={{0,1},{1,0},{2,3},{3,2},{4,5},{5,4},{6,7},{7,6},{8,9},{9,8},{10,11... | collective-permute-start | bytes 98312 | tf_op jit(solution)/shard_map/ppermute | solution.py:355
  33.6 2.1 %collective-permute-start.11 = (f32[2,512,128]{2,1,0:T(8,128)S(1)}, f32[2,512,128]{2,1,0:T(8,128)S(1)}, u32[]{:S(2)}, u32[]{:S(2)}) collective-permute-start(f32[2,512,128]{2,1,0:T(8,128)S(1)} %get-tuple-element.45.mine), channel_id=1, source_target_pairs={{0,1},{1,0},{2,3},{3,2},{4,5},{5,4},{6,7},{7,6},{8,9},{9,8},{10,11... | collective-permute-start | bytes 1572872 | tf_op jit(solution)/shard_map/ppermute | solution.py:367
  34.2 9.9 %collective-permute-start.13 = (f32[2,2,256,128]{3,2,1,0:T(8,128)S(1)}, f32[2,2,256,128]{3,2,1,0:T(8,128)S(1)}, u32[]{:S(2)}, u32[]{:S(2)}) collective-permute-start(f32[2,2,256,128]{3,2,1,0:T(8,128)S(1)} %get-tuple-element.49), channel_id=1, source_target_pairs={{0,1},{1,0},{2,3},{3,2},{4,5},{5,4},{6,7},{7,6},{8,9},{9,8},{10,11... | collective-permute-start | bytes 1572872 | tf_op jit(solution)/shard_map/ppermute | solution.py:398
  36.5 8.5 %collective-permute-start.12 = (bf16[256,128]{1,0:T(8,128)(2,1)S(1)}, bf16[256,128]{1,0:T(8,128)(2,1)S(1)}, u32[]{:S(2)}, u32[]{:S(2)}) collective-permute-start(bf16[256,128]{1,0:T(8,128)(2,1)S(1)} %get-tuple-element.46), channel_id=1, source_target_pairs={{1,3},{3,1},{5,7},{7,5},{9,11},{11,9},{13,15},{15,13},{0,8},{2,10}... | collective-permute-start | bytes 196616 | tf_op jit(solution)/shard_map/ppermute | solution.py:390
  38.6 6.4 %collective-permute-start.14 = (bf16[256,128]{1,0:T(8,128)(2,1)S(1)}, bf16[256,128]{1,0:T(8,128)(2,1)S(1)}, u32[]{:S(2)}, u32[]{:S(2)}) collective-permute-start(bf16[256,128]{1,0:T(8,128)(2,1)S(1)} %get-tuple-element.52), channel_id=1, source_target_pairs={{1,5},{3,7},{5,1},{7,3},{9,13},{11,15},{13,9},{15,11},{0,10},{2,8}... | collective-permute-start | bytes 196616 | tf_op jit(solution)/shard_map/ppermute | solution.py:390
  40.5 7.7 %collective-permute-start.15 = (bf16[256,128]{1,0:T(8,128)(2,1)S(1)}, bf16[256,128]{1,0:T(8,128)(2,1)S(1)}, u32[]{:S(2)}, u32[]{:S(2)}) collective-permute-start(bf16[256,128]{1,0:T(8,128)(2,1)S(1)} %get-tuple-element.53), channel_id=1, source_target_pairs={{1,7},{3,5},{5,3},{7,1},{9,15},{11,13},{13,11},{15,9},{0,14},{2,12... | collective-permute-start | bytes 196616 | tf_op jit(solution)/shard_map/ppermute | solution.py:390
  43.5 4.7 %collective-permute-start.16 = (bf16[256,128]{1,0:T(8,128)(2,1)S(1)}, bf16[256,128]{1,0:T(8,128)(2,1)S(1)}, u32[]{:S(2)}, u32[]{:S(2)}) collective-permute-start(bf16[256,128]{1,0:T(8,128)(2,1)S(1)} %get-tuple-element.54), channel_id=1, source_target_pairs={{1,13},{3,15},{5,9},{7,11},{9,5},{11,7},{13,1},{15,3},{17,29},{19,... | collective-permute-start | bytes 196616 | tf_op jit(solution)/shard_map/ppermute | solution.py:390
  48.2 1.4 %collective-permute-start.17 = (bf16[512,128]{1,0:T(8,128)(2,1)S(1)}, bf16[512,128]{1,0:T(8,128)(2,1)S(1)}, u32[]{:S(2)}, u32[]{:S(2)}) collective-permute-start(bf16[512,128]{1,0:T(8,128)(2,1)S(1)} %shard_map.108), channel_id=1, source_target_pairs={{0,1},{1,0},{2,3},{3,2},{4,5},{5,4},{6,7},{7,6},{8,9},{9,8},{10,11... | collective-permute-start | bytes 393224 | tf_op jit(solution)/shard_map/ppermute | solution.py:412
